TPU v7x, 32 devices: a whole 2x2x4 slice. The times are simulated.
32 devices in a mesh: ctx: 8 (over y, x, core), head: 4 (over z).
Axes of the slice: x: 2, y: 2, z: 4, core: 2. Of those that a mesh axis runs over, the one named last changes fastest.
Arguments:
- kda_inputs: bfloat16 [3, 1024, 4096], P(None, 'ctx', 'head'), may hold values from -4 to 4
- gate_log: float32 [1024, 4096], P('ctx', 'head'), may hold values from -2.2 to 0
- beta: float32 [1024, 32], P('ctx', 'head'), may hold values from 0.1 to 0.9
- conv_weight: float32 [3, 4, 4096], P(None, None, 'head'), may hold values from -3 to 3
- kda_out_weight: bfloat16 [4096, 2304], P('head'), may hold values from -3 to 3
- residual: bfloat16 [1024, 2304], P('ctx'), may hold values from -3 to 3
- norm_gain: float32 [2304], replicated, may hold values from 0.1 to 1.9
- latent_weight: bfloat16 [2304, 512], replicated, may hold values from -0.125 to 0.125
- latent_gain: float32 [512], replicated, may hold values from 0.1 to 1.9
- query_weight: bfloat16 [2304, 2048], P(None, 'head'), may hold values from -0.27083333 to 0.27083333
- up_weight: bfloat16 [512, 2, 2048], P(None, None, 'head'), may hold values from -0.5745243 to 0.5745243
Outputs:
- stream_out: bfloat16 [1024, 2304], P('ctx')
- attention_out: bfloat16 [1024, 2048], P('ctx', 'head')
All inputs are finite; a program needn't handle non-finite values.
Results may differ from a plain program's by a relative error of at most 0.04.
Values may be sent and summed in bfloat16 or wider, within the bound.
No kernel may reach another device: no remote copies, remote signals or barrier semaphores. Data moves between devices by JAX's collectives and lax.ppermute only.
A program may use at most 128 MiB of HBM per device.

v0:
```python
import math

import jax
import jax.numpy as jnp
from jax import lax
from jax.sharding import PartitionSpec as P

DK = 128
CONV = 4
DH = 128


eps_norm = 1e-06
highest_precision = lax.Precision.HIGHEST


def passed_along(block, axis, distance):
    devices = range(lax.axis_size(axis))
    route = [(i - distance, i) for i in devices if i - distance in devices]
    return lax.ppermute(block, axis, route)


def rounded(values):
    return lax.optimization_barrier(values.astype(jnp.bfloat16))


def unit_heads(activated):
    grouped = activated.reshape(activated.shape[0], -1, DK)
    scaled = grouped * lax.rsqrt(jnp.sum(grouped * grouped, axis=-1, keepdims=True) + eps_norm)
    return scaled.reshape(activated.shape)


def prepare(stream, norm_gain, latent_weight, latent_gain):
    widened = stream.astype(jnp.float32)
    normed = (
        widened
        * lax.rsqrt(jnp.mean(widened * widened, axis=-1, keepdims=True) + eps_norm)
        * norm_gain
    ).astype(jnp.bfloat16)
    latent_pre = jnp.dot(normed, latent_weight, preferred_element_type=jnp.float32)
    latent = (
        latent_pre
        * lax.rsqrt(jnp.mean(latent_pre * latent_pre, axis=-1, keepdims=True) + eps_norm)
        * latent_gain
    ).astype(jnp.bfloat16)
    return (normed, latent)


def span_layout(values, span_rows):
    length, channel_count = values.shape
    return values.reshape(length // span_rows, span_rows, channel_count // DK, DK).transpose(
        0, 2, 1, 3
    )


def matmul_heads(left, right):
    return jnp.einsum("hij,hjk->hik", left, right, precision=highest_precision)


def delta_rule(kda_query, kda_key, kda_value, gate_log, beta):
    span_rows = 32
    length, channel_count = gate_log.shape
    heads = channel_count // DK
    queries = span_layout(kda_query.astype(jnp.float32), span_rows)
    keys_unit = span_layout(kda_key.astype(jnp.float32), span_rows)
    values_new = span_layout(kda_value.astype(jnp.float32), span_rows)
    cumulative = jnp.cumsum(span_layout(gate_log, span_rows), axis=2)
    rates = beta.reshape(length // span_rows, span_rows, heads).transpose(0, 2, 1)[..., None]
    growth = jnp.exp(cumulative)
    final_log = cumulative[:, :, -1:, :]
    keys_grown = keys_unit * growth
    keys_shrunk = keys_unit * jnp.exp(-cumulative)
    queries_grown = queries * growth
    keys_final = keys_unit * jnp.exp(final_log - cumulative)
    strict = jnp.tril(jnp.ones((span_rows, span_rows), jnp.float32), -1)
    inclusive = jnp.tril(jnp.ones((span_rows, span_rows), jnp.float32))
    coupling = (
        jnp.einsum("nhtc,nhsc->nhts", keys_grown, keys_shrunk, precision=highest_precision)
        * jnp.swapaxes(rates, -1, -2)
        * strict
    )
    system = coupling + jnp.eye(span_rows, dtype=jnp.float32)
    solved = jax.scipy.linalg.solve_triangular(
        system, jnp.concatenate([values_new, keys_grown], axis=-1), lower=True, unit_diagonal=True
    )
    fresh = solved[..., :DK] * rates
    carried = solved[..., DK:] * rates
    eye_key = jnp.eye(DK, dtype=jnp.float32)
    transition = jnp.exp(final_log[:, :, 0, :])[..., :, None] * eye_key - jnp.einsum(
        "nhsk,nhsv->nhkv", keys_final, carried, precision=highest_precision
    )
    offset = jnp.einsum("nhsk,nhsv->nhkv", keys_final, fresh, precision=highest_precision)
    mixing = (
        jnp.einsum("nhtc,nhsc->nhts", queries_grown, keys_shrunk, precision=highest_precision)
        * inclusive
    )

    def compose(accumulated, span_parts):
        span_move, span_shift = span_parts
        return (
            (
                matmul_heads(span_move, accumulated[0]),
                matmul_heads(span_move, accumulated[1]) + span_shift,
            ),
            None,
        )

    identity_map = jnp.broadcast_to(eye_key, (heads, DK, DK))
    zero_map = jnp.zeros((heads, DK, DK), jnp.float32)
    (device_move, device_shift), _ = lax.scan(
        compose, (identity_map, zero_map), (transition, offset)
    )
    return (device_move, device_shift, (transition, offset, fresh, carried, queries_grown, mixing))


def emit_spans(start_state, span_data):

    def emit(recurrent_state, span_parts):
        span_move, span_shift, fresh_state_term, carried_state_term, query_term, mixing_part = (
            span_parts
        )
        state_update = fresh_state_term - jnp.einsum(
            "orm,omj->orj", carried_state_term, recurrent_state, precision=highest_precision
        )
        produced_output = jnp.einsum(
            "fmb,fbi->fmi", query_term, recurrent_state, precision=highest_precision
        ) + jnp.einsum("hts,hsv->htv", mixing_part, state_update, precision=highest_precision)
        return (matmul_heads(span_move, recurrent_state) + span_shift, produced_output)

    _, outputs = lax.scan(emit, start_state, span_data)
    block_count, heads, span_rows, _ = outputs.shape
    return (
        outputs.transpose(0, 2, 1, 3)
        .reshape(block_count * span_rows, heads * DK)
        .astype(jnp.bfloat16)
    )


def per_device(
    kda_inputs,
    gate_log,
    beta,
    conv_weight,
    kda_out_weight,
    residual,
    norm_gain,
    latent_weight,
    latent_gain,
    query_weight,
    up_weight,
):
    length = residual.shape[0]
    edge_rows = kda_inputs[:, length - (CONV - 1) :, :]
    earlier_rows = passed_along(edge_rows, "ctx", 1)
    extended = jnp.concatenate([earlier_rows, kda_inputs], axis=1).astype(jnp.float32)
    running = jnp.zeros(kda_inputs.shape, jnp.float32)
    for tap_index in range(CONV):
        running = (
            running
            + conv_weight[:, tap_index, None, :] * extended[:, tap_index : tap_index + length, :]
        )
    activated = jax.nn.silu(running)
    kda_query = rounded(unit_heads(activated[0]) * DK ** (-0.5))
    kda_key = rounded(unit_heads(activated[1]))
    kda_value = rounded(activated[2])
    device_move, device_shift, span_data = delta_rule(kda_query, kda_key, kda_value, gate_log, beta)
    heads = device_move.shape[0]

    def relay(step_index, incoming):
        leaving = matmul_heads(device_move, incoming) + device_shift
        return passed_along(leaving, "ctx", 1)

    start_state = lax.fori_loop(
        0, lax.axis_size("ctx") - 1, relay, jnp.zeros((heads, DK, DK), jnp.float32)
    )
    kda_core = emit_spans(start_state, span_data)
    partial_proj = jnp.dot(kda_core, kda_out_weight, preferred_element_type=jnp.float32)
    summed = lax.psum(partial_proj, "head")
    stream_out = (residual.astype(jnp.float32) + summed).astype(jnp.bfloat16)
    normed, latent = prepare(stream_out, norm_gain, latent_weight, latent_gain)
    mla_query = jnp.dot(normed, query_weight, preferred_element_type=jnp.float32).astype(
        jnp.bfloat16
    )
    query_heads = mla_query.reshape(length, -1, DH)
    heads_mla = query_heads.shape[1]
    flat_up = up_weight.reshape(up_weight.shape[0], -1)
    my_first = lax.axis_index("ctx") * length
    query_positions = my_first + jnp.arange(length, dtype=jnp.int32)
    initial = (
        jnp.full((heads_mla, length), -1e30, jnp.float32),
        jnp.zeros((heads_mla, length), jnp.float32),
        jnp.zeros((heads_mla, length, DH), jnp.float32),
    )
    piece = lax.all_gather(latent, "ctx", axis=0, tiled=True)
    piece_rows = piece.shape[0]
    block_rows = math.gcd(piece_rows, 512)
    blocks = piece.reshape(piece_rows // block_rows, block_rows, piece.shape[1])

    def one_block(state_parts, block_parts):
        block_index, latent_block = block_parts
        running_peak, running_total, running_mixed = state_parts
        paired = (
            jnp.dot(latent_block, flat_up, preferred_element_type=jnp.float32)
            .astype(jnp.bfloat16)
            .reshape(block_rows, 2, heads_mla, DH)
        )
        scores = jnp.einsum(
            "qhd,khd->hqk", query_heads, paired[:, 0], preferred_element_type=jnp.float32
        ) * DH ** (-0.5)
        key_positions = block_index * block_rows + jnp.arange(block_rows, dtype=jnp.int32)
        allowed = key_positions[None, :] <= query_positions[:, None]
        new_peak = jnp.maximum(running_peak, jnp.max(jnp.where(allowed, scores, -1e30), axis=-1))
        weights = jnp.where(allowed, jnp.exp(scores - new_peak[..., None]), 0.0)
        factor = jnp.exp(running_peak - new_peak)
        new_total = running_total * factor + jnp.sum(weights, axis=-1)
        new_mixed = running_mixed * factor[..., None] + jnp.einsum(
            "hqk,khd->hqd",
            weights.astype(jnp.bfloat16),
            paired[:, 1],
            preferred_element_type=jnp.float32,
        )
        return ((new_peak, new_total, new_mixed), None)

    def attend(state_parts):
        return lax.scan(
            one_block, state_parts, (jnp.arange(piece_rows // block_rows, dtype=jnp.int32), blocks)
        )[0]

    final_peak, final_total, final_mixed = lax.cond(
        jnp.int32(0) < my_first + length, attend, lambda state_parts: state_parts, initial
    )
    attention_out = (
        (final_mixed / final_total[..., None])
        .transpose(1, 0, 2)
        .reshape(length, heads_mla * DH)
        .astype(jnp.bfloat16)
    )
    return (stream_out, attention_out)


def solution(mesh):
    in_specs = (
        P(None, "ctx", "head"),
        P("ctx", "head"),
        P("ctx", "head"),
        P(None, None, "head"),
        P("head", None),
        P("ctx", None),
        P(),
        P(),
        P(),
        P(None, "head"),
        P(None, None, "head"),
    )
    out_specs = (P("ctx", None), P("ctx", "head"))
    return jax.shard_map(
        per_device, mesh=mesh, in_specs=in_specs, out_specs=out_specs, check_vma=False
    )
```

profile of v0, /device:TPU:0, one launch (start us, length us, event | category | flops | bytes accessed | tf_op | source)
XLA Modules:
  0.0 402.6 jit_solution(10572172649577620593)
XLA Ops:
  8.8 3.0 collective-permute-start.1
  14.8 7.6 %fusion.56 = f32[4,8,32,128]{3,1,2,0:T(8,128)S(1)} fusion(f32[4,32,8,128]{3,2,1,0:T(8,128)S(1)} %bitcast.216), kind=kOutput, calls=%fused_computation.90 | output fusion | flops 4063232 | bytes 1048576 | tf_op jit(solution)/shard_map/jit(cumsum)/reduce_window_sum | solution.py:67
  31.5 1.9 reduce_sum.45
  34.3 1.9 copy.53
  36.2 1.9 reduce_sum.46
  43.1 1.9 fusion.45
  45.0 80.2 %custom-call.4 = f32[4,8,1,32,32]{3,4,2,1,0:T(8,128)} custom-call(f32[4,8,1,32,32]{4,3,2,1,0:T(8,128)} %fusion.45), custom_call_target="InvertDiagBlocksLowerTriangular" | custom-call | tf_op jit(solution)/shard_map/jit(_solve_triangular)/vmap(vmap())/triangular_solve | solution.py:83
  128.6 4.8 %fusion.66 = f32[4,8,128,128]{3,2,1,0:T(8,128)} fusion(f32[4,8,32,128]{3,2,1,0:T(8,128)S(1)} %get-tuple-element.578, f32[4,32,8,128]{3,2,1,0:T(8,128)S(1)} %bitcast.207, f32[4,8,32,128]{3,1,2,0:T(8,128)S(1)} %fusion.56, f32[4,8,128]{2,1,0:T(8,128)S(1)} %slice_bitcast_fusion), kind=kOutput, calls=%fused_computation.116 | convolution fusion | flops 201588736 | bytes 3686400 | tf_op jit(solution)/shard_map/nhsk,nhsv->nhkv/dot_general | solution.py:92
  133.4 5.2 %multiply_subtract_fusion = f32[4,8,128,128]{3,2,1,0:T(8,128)} fusion(f32[4,8,32,128]{3,2,1,0:T(8,128)S(1)} %get-tuple-element.579, f32[128,128]{1,0:T(8,128)S(1)} %fusion.67, f32[4,8,128]{2,1,0:T(8,128)S(1)} %copy-done.19, f32[4,32,8,128]{3,2,1,0:T(8,128)S(1)} %bitcast.208, f32[4,8,32,128]{3,1,2,0:T(8,128)S(1)} %fusion.56, ...), kind=kOutput, calls=%fused_computation.56 | convolution fusion | flops 202637312 | bytes 3768320 | tf_op jit(solution)/shard_map/nhsk,nhsv->nhkv/dot_general | solution.py:89
  138.6 14.7 %while.52 = (s32[]{:T(128)}, f32[8,128,128]{2,1,0:T(8,128)S(1)}, f32[8,128,128]{2,1,0:T(8,128)S(1)}, f32[4,8,128,128]{3,2,1,0:T(8,128)}, f32[4,8,128,128]{3,2,1,0:T(8,128)}, /*index=5*/s32[]{:T(128)}, s32[]{:T(128)}) while((s32[]{:T(128)}, f32[8,128,128]{2,1,0:T(8,128)S(1)}, f32[8,128,128]{2,1,0:T(8,128)S(1)}, ...), condition=%wide.region_3.4_spmd.clone, body=%wide.region_2.3_spmd.clone.sunk | while | flops 402915328 | bytes 5768791 | solution.py:110
  138.7 1.8 convolution_add_fusion.11
  142.4 1.8 convolution_add_fusion.11
  146.0 1.8 convolution_add_fusion.11
  149.7 1.8 convolution_add_fusion.11
  153.4 3.4 convolution_multiply_fusion.1
  156.8 85.3 %while.50 = (s32[]{:T(128)}, f32[8,128,128]{2,1,0:T(8,128)S(1)}, f32[8,128,128]{2,1,0:T(8,128)S(1)}, f32[8,128,128]{2,1,0:T(8,128)}, s32[]{:T(128)}) while((s32[]{:T(128)}, f32[8,128,128]{2,1,0:T(8,128)S(1)}, f32[8,128,128]{2,1,0:T(8,128)S(1)}, f32[8,128,128]{2,1,0:T(8,128)}, s32[]{:T(128)}) %tuple.119), condition=%wide.region_5.6_spmd, body=%wide.region_4.5_spmd.sunk | while | flops 201457664 | bytes 4194405 | solution.py:173
  157.1 2.5 convolution_add_fusion.9
  159.6 3.9 collective-permute-start
  165.2 2.5 convolution_add_fusion.9
  167.7 6.6 %collective-permute-start = (f32[8,128,128]{2,1,0:T(8,128)}, f32[8,128,128]{2,1,0:T(8,128)S(1)}, u32[]{:S(2)}, u32[]{:S(2)}) collective-permute-start(f32[8,128,128]{2,1,0:T(8,128)} %convolution_add_fusion.9), channel_id=1, source_target_pairs={{0,4},{4,8},{8,12},{12,16},{16,20},{20,24},{24,28},{1,5},{5,9},{9,... | collective-permute-start | bytes 1572872 | tf_op jit(solution)/shard_map/while/body/eval_jaxpr/ppermute | solution.py:20
  176.1 2.5 convolution_add_fusion.9
  178.6 9.0 %collective-permute-start = (f32[8,128,128]{2,1,0:T(8,128)}, f32[8,128,128]{2,1,0:T(8,128)S(1)}, u32[]{:S(2)}, u32[]{:S(2)}) collective-permute-start(f32[8,128,128]{2,1,0:T(8,128)} %convolution_add_fusion.9), channel_id=1, source_target_pairs={{0,4},{4,8},{8,12},{12,16},{16,20},{20,24},{24,28},{1,5},{5,9},{9,... | collective-permute-start | bytes 1572872 | tf_op jit(solution)/shard_map/while/body/eval_jaxpr/ppermute | solution.py:20
  189.3 2.5 convolution_add_fusion.9
  191.8 9.0 %collective-permute-start = (f32[8,128,128]{2,1,0:T(8,128)}, f32[8,128,128]{2,1,0:T(8,128)S(1)}, u32[]{:S(2)}, u32[]{:S(2)}) collective-permute-start(f32[8,128,128]{2,1,0:T(8,128)} %convolution_add_fusion.9), channel_id=1, source_target_pairs={{0,4},{4,8},{8,12},{12,16},{16,20},{20,24},{24,28},{1,5},{5,9},{9,... | collective-permute-start | bytes 1572872 | tf_op jit(solution)/shard_map/while/body/eval_jaxpr/ppermute | solution.py:20
  202.5 2.5 convolution_add_fusion.9
  205.0 9.0 %collective-permute-start = (f32[8,128,128]{2,1,0:T(8,128)}, f32[8,128,128]{2,1,0:T(8,128)S(1)}, u32[]{:S(2)}, u32[]{:S(2)}) collective-permute-start(f32[8,128,128]{2,1,0:T(8,128)} %convolution_add_fusion.9), channel_id=1, source_target_pairs={{0,4},{4,8},{8,12},{12,16},{16,20},{20,24},{24,28},{1,5},{5,9},{9,... | collective-permute-start | bytes 1572872 | tf_op jit(solution)/shard_map/while/body/eval_jaxpr/ppermute | solution.py:20
  215.7 2.5 convolution_add_fusion.9
  218.2 9.0 %collective-permute-start = (f32[8,128,128]{2,1,0:T(8,128)}, f32[8,128,128]{2,1,0:T(8,128)S(1)}, u32[]{:S(2)}, u32[]{:S(2)}) collective-permute-start(f32[8,128,128]{2,1,0:T(8,128)} %convolution_add_fusion.9), channel_id=1, source_target_pairs={{0,4},{4,8},{8,12},{12,16},{16,20},{20,24},{24,28},{1,5},{5,9},{9,... | collective-permute-start | bytes 1572872 | tf_op jit(solution)/shard_map/while/body/eval_jaxpr/ppermute | solution.py:20
  228.9 2.5 convolution_add_fusion.9
  231.4 9.0 %collective-permute-start = (f32[8,128,128]{2,1,0:T(8,128)}, f32[8,128,128]{2,1,0:T(8,128)S(1)}, u32[]{:S(2)}, u32[]{:S(2)}) collective-permute-start(f32[8,128,128]{2,1,0:T(8,128)} %convolution_add_fusion.9), channel_id=1, source_target_pairs={{0,4},{4,8},{8,12},{12,16},{16,20},{20,24},{24,28},{1,5},{5,9},{9,... | collective-permute-start | bytes 1572872 | tf_op jit(solution)/shard_map/while/body/eval_jaxpr/ppermute | solution.py:20
  242.1 25.0 %while.51 = (s32[]{:T(128)}, f32[8,128,128]{2,1,0:T(8,128)S(1)}, bf16[4,8,32,128]{3,2,1,0:T(8,128)(2,1)}, f32[4,8,128,128]{3,2,1,0:T(8,128)}, f32[4,8,128,128]{3...) while((s32[]{:T(128)}, f32[8,128,128]{2,1,0:T(8,128)S(1)}, ...), condition=%wide.region_8.9_spmd, body=%wide.region_7.8_spmd.sunk | while | flops 314769408 | bytes 7474845 | solution.py:130
  246.4 1.9 convolution_add_fusion.10
  252.7 1.9 convolution_add_fusion.10
  258.9 1.9 convolution_add_fusion.10
  265.2 1.9 convolution_add_fusion.10
  268.2 4.1 %fusion.59 = f32[128,2304]{1,0:T(8,128)} fusion(bf16[1024,2304]{1,0:T(8,128)(2,1)} %param.25, bf16[16,8,8,128]{3,2,1,0:T(8,128)(2,1)S(1)} %bitcast.217), kind=kOutput, calls=%fused_computation.106 | convolution fusion | flops 603979776 | bytes 6160384 | tf_op jit(solution)/shard_map/dot_general | solution.py:177
  272.4 70.5 %all-reduce.2.cloned.1.call-done = f32[128,2304]{1,0:T(8,128)} async-done(((f32[128,2304]{1,0:T(8,128)}), f32[128,2304]{1,0:T(8,128)}) %all-reduce.2.cloned.1.call-update) | async-done | bytes 1179664 | tf_op jit(solution)/shard_map/psum | solution.py:178
  346.1 2.5 convolution_convert_fusion.1
  348.5 20.7 %all-gather.2.cloned.1.call-done = bf16[1024,512]{1,0:T(8,128)(2,1)} async-done(((bf16[128,512]{1,0:T(8,128)(2,1)}), bf16[1024,512]{1,0:T(8,128)(2,1)}) %all-gather.2.cloned.1.call-update) | async-done | bytes 1048592 | tf_op jit(solution)/shard_map/all_gather | solution.py:194
  369.2 24.8 %conditional.1 = (f32[4,128]{1,0:T(4,128)}, f32[4,128,128]{2,1,0:T(8,128)}) conditional(s32[]{:T(128)} %convert_element_type.88, () %tuple.35, (bf16[1024,512]{1,0:T(8,128)(2,1)}, bf16[512,2,512]{2,1,0:T(2,128)(2,1)S(1)}, bf16[128,512]{1,0:T(8,128)(2,1)S(1)}, s32[]{:T(128)}, s32[128]{0:T(128)S(1)}) %tuple.124), branch_computations={%region_12.13_spmd, %region_13.18_spmd} | conditional | flops 674237568 | bytes 15112509 | solution.py:229
  371.4 22.7 %while.49 = (s32[]{:T(128)}, f32[4,128]{1,0:T(4,128)S(1)}, f32[4,128]{1,0:T(4,128)}, f32[4,128,128]{2,1,0:T(8,128)}, s32[2]{0:T(128)S(1)}, /*index=5*/s32[128]{0...) while((s32[]{:T(128)}, f32[4,128]{1,0:T(4,128)S(1)}, ...), condition=%wide.region_17.17_spmd.clone, body=%wide.region_14.16_spmd.clone.sunk | while | flops 674237440 | bytes 12489913 | solution.py:225
  372.9 3.1 convolution_convert_fusion.3
  376.0 1.8 reshape.155
  380.1 2.2 convolution_add_fusion.12
  383.8 3.1 convolution_convert_fusion.3
  386.9 1.8 reshape.155
  391.8 2.3 convolution_add_fusion.12
  394.0 1.7 copy_bitcast_fusion.5
  (180 shorter events, 72.0 us)
Async XLA Ops:
  7.2 337.3 %copy-start = (bf16[2304,512]{1,0:T(8,128)(2,1)S(1)}, bf16[2304,512]{1,0:T(8,128)(2,1)}, u32[]{:S(2)}) copy-start(bf16[2304,512]{1,0:T(8,128)(2,1)} %param.28) | copy-start | bytes 7077892
  7.2 16.0 %copy-start.23 = (f32[3,4,1024]{2,1,0:T(4,128)S(1)}, f32[3,4,1024]{2,1,0:T(4,128)}, u32[]{:S(2)}) copy-start(f32[3,4,1024]{2,1,0:T(4,128)} %param.24) | copy-start | bytes 147460
  7.2 335.7 %all-reduce.2.cloned.1.call-start = ((), (), s32[]{:S(2)}) async-start(), calls=%async_computation | async-start | bytes 2359296 | tf_op jit(solution)/shard_map/psum | solution.py:178
  8.8 17.8 %collective-permute-start.1 = (bf16[3,3,1024]{2,1,0:T(4,128)(2,1)}, bf16[3,3,1024]{2,1,0:T(4,128)(2,1)}, u32[]{:S(2)}, u32[]{:S(2)}) collective-permute-start(bf16[3,3,1024]{2,1,0:T(4,128)(2,1)} %slice.60), channel_id=1, source_target_pairs={{0,4},{4,8},{8,12},{12,16},{16,20},{20,24},{24,28},{1,5},{5,9},{9,... | collective-permute-start | bytes 55304 | tf_op jit(solution)/shard_map/ppermute | solution.py:20
  22.5 110.9 %copy-start.2 = (f32[4,8,32,128]{3,1,2,0:T(8,128)}, f32[4,8,32,128]{3,1,2,0:T(8,128)S(1)}, u32[]{:S(2)}) copy-start(f32[4,8,32,128]{3,1,2,0:T(8,128)S(1)} %fusion.56) | copy-start | bytes 1572868
  28.9 2.6 copy-start.5
  40.9 1.3 copy-start.3
  41.1 1.9 copy-start.16
  41.1 1.9 copy-start.20
  41.1 1.9 copy-start.21
  41.1 1.9 copy-start.22
  41.1 1.9 copy-start.24
  42.2 0.8 copy-start.8
  125.2 1.3 copy-start.9
  125.2 1.3 copy-start.13
  127.5 1.0 copy-start.4
  127.7 5.6 %copy-start.6 = (f32[4,8,32,128]{3,2,1,0:T(8,128)}, f32[4,8,32,128]{3,2,1,0:T(8,128)S(1)}, u32[]{:S(2)}) copy-start(f32[4,8,32,128]{3,2,1,0:T(8,128)S(1)} %get-tuple-element.578) | copy-start | bytes 1572868
  127.8 5.6 %copy-start.7 = (f32[4,8,32,128]{3,2,1,0:T(8,128)}, f32[4,8,32,128]{3,2,1,0:T(8,128)S(1)}, u32[]{:S(2)}) copy-start(f32[4,8,32,128]{3,2,1,0:T(8,128)S(1)} %get-tuple-element.579) | copy-start | bytes 1572868
  128.6 4.8 %copy-start.19 = (f32[4,8,128]{2,1,0:T(8,128)S(1)}, f32[4,8,128]{2,1,0:T(8,128)}, u32[]{:S(2)}) copy-start(f32[4,8,128]{2,1,0:T(8,128)} %fusion.72) | copy-start | bytes 49156
  138.6 14.7 %copy-start.18 = (f32[32,32]{1,0:T(8,128)S(1)}, f32[32,32]{1,0:T(8,128)}, u32[]{:S(2)}) copy-start(f32[32,32]{1,0:T(8,128)} %fusion.70) | copy-start | bytes 12292
  153.3 3.4 copy-start.1
  159.6 5.6 %collective-permute-start = (f32[8,128,128]{2,1,0:T(8,128)}, f32[8,128,128]{2,1,0:T(8,128)S(1)}, u32[]{:S(2)}, u32[]{:S(2)}) collective-permute-start(f32[8,128,128]{2,1,0:T(8,128)} %convolution_add_fusion.9), channel_id=1, source_target_pairs={{0,4},{4,8},{8,12},{12,16},{16,20},{20,24},{24,28},{1,5},{5,9},{9,... | collective-permute-start | bytes 1572872 | tf_op jit(solution)/shard_map/while/body/eval_jaxpr/ppermute | solution.py:20
  167.7 8.3 %collective-permute-start = (f32[8,128,128]{2,1,0:T(8,128)}, f32[8,128,128]{2,1,0:T(8,128)S(1)}, u32[]{:S(2)}, u32[]{:S(2)}) collective-permute-start(f32[8,128,128]{2,1,0:T(8,128)} %convolution_add_fusion.9), channel_id=1, source_target_pairs={{0,4},{4,8},{8,12},{12,16},{16,20},{20,24},{24,28},{1,5},{5,9},{9,... | collective-permute-start | bytes 1572872 | tf_op jit(solution)/shard_map/while/body/eval_jaxpr/ppermute | solution.py:20
  178.6 10.7 %collective-permute-start = (f32[8,128,128]{2,1,0:T(8,128)}, f32[8,128,128]{2,1,0:T(8,128)S(1)}, u32[]{:S(2)}, u32[]{:S(2)}) collective-permute-start(f32[8,128,128]{2,1,0:T(8,128)} %convolution_add_fusion.9), channel_id=1, source_target_pairs={{0,4},{4,8},{8,12},{12,16},{16,20},{20,24},{24,28},{1,5},{5,9},{9,... | collective-permute-start | bytes 1572872 | tf_op jit(solution)/shard_map/while/body/eval_jaxpr/ppermute | solution.py:20
  191.8 10.7 %collective-permute-start = (f32[8,128,128]{2,1,0:T(8,128)}, f32[8,128,128]{2,1,0:T(8,128)S(1)}, u32[]{:S(2)}, u32[]{:S(2)}) collective-permute-start(f32[8,128,128]{2,1,0:T(8,128)} %convolution_add_fusion.9), channel_id=1, source_target_pairs={{0,4},{4,8},{8,12},{12,16},{16,20},{20,24},{24,28},{1,5},{5,9},{9,... | collective-permute-start | bytes 1572872 | tf_op jit(solution)/shard_map/while/body/eval_jaxpr/ppermute | solution.py:20
  205.0 10.7 %collective-permute-start = (f32[8,128,128]{2,1,0:T(8,128)}, f32[8,128,128]{2,1,0:T(8,128)S(1)}, u32[]{:S(2)}, u32[]{:S(2)}) collective-permute-start(f32[8,128,128]{2,1,0:T(8,128)} %convolution_add_fusion.9), channel_id=1, source_target_pairs={{0,4},{4,8},{8,12},{12,16},{16,20},{20,24},{24,28},{1,5},{5,9},{9,... | collective-permute-start | bytes 1572872 | tf_op jit(solution)/shard_map/while/body/eval_jaxpr/ppermute | solution.py:20
  218.2 10.7 %collective-permute-start = (f32[8,128,128]{2,1,0:T(8,128)}, f32[8,128,128]{2,1,0:T(8,128)S(1)}, u32[]{:S(2)}, u32[]{:S(2)}) collective-permute-start(f32[8,128,128]{2,1,0:T(8,128)} %convolution_add_fusion.9), channel_id=1, source_target_pairs={{0,4},{4,8},{8,12},{12,16},{16,20},{20,24},{24,28},{1,5},{5,9},{9,... | collective-permute-start | bytes 1572872 | tf_op jit(solution)/shard_map/while/body/eval_jaxpr/ppermute | solution.py:20
  231.4 10.7 %collective-permute-start = (f32[8,128,128]{2,1,0:T(8,128)}, f32[8,128,128]{2,1,0:T(8,128)S(1)}, u32[]{:S(2)}, u32[]{:S(2)}) collective-permute-start(f32[8,128,128]{2,1,0:T(8,128)} %convolution_add_fusion.9), channel_id=1, source_target_pairs={{0,4},{4,8},{8,12},{12,16},{16,20},{20,24},{24,28},{1,5},{5,9},{9,... | collective-permute-start | bytes 1572872 | tf_op jit(solution)/shard_map/while/body/eval_jaxpr/ppermute | solution.py:20
  242.1 2.8 copy-start.14
  246.4 2.0 copy-start.15
  248.4 2.8 copy-start.14
  252.6 2.0 copy-start.15
  254.6 2.8 copy-start.14
  258.9 2.0 copy-start.15
  260.9 2.8 copy-start.14
  265.2 2.0 copy-start.15
  272.4 70.5 %copy-start.11 = (bf16[128,2304]{1,0:T(8,128)(2,1)S(1)}, bf16[128,2304]{1,0:T(8,128)(2,1)}, u32[]{:S(2)}) copy-start(bf16[128,2304]{1,0:T(8,128)(2,1)} %param.26) | copy-start | bytes 1769476
  272.4 72.1 %copy-start.26 = (f32[2304]{0:T(1024)S(1)}, f32[2304]{0:T(1024)}, u32[]{:S(2)}) copy-start(f32[2304]{0:T(1024)} %param.27) | copy-start | bytes 27652
  272.4 96.8 %all-gather.2.cloned.1.call-start = ((), (), s32[]{:S(2)}) async-start(), calls=%async_computation.1 | async-start | bytes 1179648 | tf_op jit(solution)/shard_map/all_gather | solution.py:194
  344.4 0.8 copy-start.12
  344.5 0.8 copy-start.25
  346.0 23.2 %copy-start.10 = (bf16[512,2,512]{2,1,0:T(2,128)(2,1)S(1)}, bf16[512,2,512]{2,1,0:T(2,128)(2,1)}, u32[]{:S(2)}) copy-start(bf16[512,2,512]{2,1,0:T(2,128)(2,1)} %param.31) | copy-start | bytes 3145732
  377.8 1.2 copy-start.17
  388.7 1.2 copy-start.17
Sparse Core Ops, SparseCore 0:
  272.5 70.3 all-reduce.1
  346.2 23.0 all-gather.1
where the time goes:
time: 405 us; the launch traced here: 403 us
  other arithmetic  110 us (27%)
  waiting for transfers between devices  103 us (25%)
  matrix products  91.2 us (23%)
  starting transfers between devices  58.6 us (14%)
  local copies, waits for them, and re-layouts  23.4 us (6%)
  between operations  14.4 us (4%)
    another operation x4, other arithmetic, delta_rule(): jax.scipy.linalg.solve_triangular(system, jnp.concatenate([values_new, ke...  81.5 us
    psum x1, waiting for transfers between devices, per_device(): summed = lax.psum(partial_proj, 'head')  70.5 us
    ppermute x8, starting transfers between devices, passed_along(): return lax.ppermute(block, axis, route)  58.5 us
    dot_general x19, matrix products, matmul_heads(): return jnp.einsum('hij,hjk->hik', left, right, precision=highest_precision)  39.6 us
    all_gather x1, waiting for transfers between devices, per_device(): piece = lax.all_gather(latent, 'ctx', axis=0, tiled=True)  20.7 us
    ppermute x8, waiting for transfers between devices, passed_along(): return lax.ppermute(block, axis, route)  11.9 us
  transfers between devices with their start and end apart: 10, of which 9 were waited for; matrix products, arithmetic and copies ran while one was open for 4% of the time, Pallas kernels for 0%

commit v1 on v0

v1 whole, which is shorter than its diff:
```python
import functools

import jax
import jax.numpy as jnp
from jax import lax
from jax.experimental import pallas as pl
from jax.experimental.pallas import tpu as pltpu
from jax.sharding import PartitionSpec as P

DK = 128
CONV = 4
DH = 128
BETA_ROWS = 16
MIB = 1 << 20

eps_norm = 1e-06
bf16 = jnp.bfloat16
f32 = jnp.float32
VMEM = pl.BlockSpec(memory_space=pltpu.VMEM)
SMEM = pl.BlockSpec(memory_space=pltpu.SMEM)


def mm(left, right):
    return jnp.dot(left.astype(bf16), right.astype(bf16), preferred_element_type=f32)


def mm_nt(left, right):
    return lax.dot_general(
        left.astype(bf16), right.astype(bf16), (((1,), (1,)), ((), ())), preferred_element_type=f32
    )


def mm_tn(left, right):
    return lax.dot_general(
        left.astype(bf16), right.astype(bf16), (((0,), (0,)), ((), ())), preferred_element_type=f32
    )


def call(kernel, outs, args, scratch=(), limit=32):
    return pl.pallas_call(
        kernel,
        out_shape=[jax.ShapeDtypeStruct(shape, dtype) for shape, dtype in outs],
        in_specs=[SMEM if a.dtype == jnp.int32 else VMEM for a in args],
        out_specs=[VMEM for _ in outs],
        scratch_shapes=[pltpu.VMEM(shape, dtype) for shape, dtype in scratch],
        compiler_params=pltpu.CompilerParams(vmem_limit_bytes=limit * MIB),
    )(*args)


def partner(index, step, size):
    return index ^ step if size & (size - 1) == 0 else (size + step - index) % size


def trade(block, axis, step, size):
    route = []
    for i in range(lax.axis_size(axis)):
        base = i // size * size
        route.append((i, base + partner(i - base, step, size)))
    return lax.ppermute(block, axis, route)


def passed_along(block, axis, distance):
    devices = range(lax.axis_size(axis))
    route = [(i - distance, i) for i in devices if i - distance in devices]
    return lax.ppermute(block, axis, route)


def lanes(block_index, width=128):
    return pl.ds(pl.multiple_of(block_index * width, width), width)


def pack_kernel(heads, place, inputs, gate, beta, *packed):
    length = gate.shape[0]
    me = place[0]
    eye = (
        lax.broadcasted_iota(jnp.int32, (length, length), 0)
        == lax.broadcasted_iota(jnp.int32, (length, length), 1)
    ).astype(f32)
    head_lane = lax.broadcasted_iota(jnp.int32, (1, heads), 1)
    for step in range(heads):
        head = partner(me, step, heads)
        out = packed[step]
        for part in range(3):
            out[part * length : (part + 1) * length, :] = inputs[part, :, lanes(head)]
        out[3 * length : 4 * length, :] = gate[:, lanes(head)].astype(bf16)
        column = jnp.sum(jnp.where(head_lane == head, beta[...], 0.0), axis=1, keepdims=True)
        row = jnp.sum(column * eye, axis=0, keepdims=True)
        out[4 * length :, :] = jnp.broadcast_to(row, (BETA_ROWS, length)).astype(bf16)


def delta_kernel(heads, length, grouped, *refs):
    place, taps = refs[:2]
    blocks = refs[2 : 2 + heads]
    rest = refs[2 + heads :]
    if grouped:
        halo, start, rest = rest[0], rest[1], rest[2:]
    cores = rest[:heads]
    rest = rest[heads:]
    if grouped:
        final, rest = rest[0], rest[1:]
    wide, gates, rates, outputs = rest
    me = place[0]
    pad = 8
    for part in range(3):
        if grouped:
            wide[part, :pad, :] = halo[part]
        else:
            wide[part, :pad, :] = jnp.zeros((pad, DK), f32)
    for step in range(heads):
        where = partner(me, step, heads)
        block = blocks[step]
        at = pl.multiple_of(where * length, length)
        for part in range(3):
            wide[part, pl.ds(pl.multiple_of(at + pad, pad), length), :] = block[
                part * length : (part + 1) * length, :
            ].astype(f32)
        gates[pl.ds(at, length), :] = block[3 * length : 4 * length, :]
        rates[where] = block[4 * length :, :]

    rows = lax.broadcasted_iota(jnp.int32, (length, length), 0)
    cols = lax.broadcasted_iota(jnp.int32, (length, length), 1)
    tril = (rows >= cols).astype(bf16)
    half = length // 2
    spread = jnp.full((BETA_ROWS, DK), 1.0 / BETA_ROWS, bf16)
    chunks = range(heads)

    def convolved(part, i):
        total = jnp.zeros((length, DK), f32)
        for tap in range(CONV):
            first = i * length + pad - (CONV - 1) + tap
            total = total + taps[part, tap : tap + 1, :] * wide[part, first : first + length, :]
        return total / (1.0 + jnp.exp(-total))

    def unit(value):
        return value * lax.rsqrt(jnp.sum(value * value, axis=-1, keepdims=True) + eps_norm)

    coupling, mixing, right, finals, queries_grown, decay = [], [], [], [], [], []
    for i in chunks:
        query = (unit(convolved(0, i)) * DK ** (-0.5)).astype(bf16).astype(f32)
        key = unit(convolved(1, i)).astype(bf16).astype(f32)
        value = convolved(2, i).astype(bf16)
        log = jnp.dot(tril, gates[i * length : (i + 1) * length, :], preferred_element_type=f32)
        rate_row = rates[i][:1].astype(f32)
        rate_column = mm_tn(rates[i], spread)
        last = log[length - 1 :]
        kept, mixed = [], []
        for b in range(2):
            own = slice(b * half, (b + 1) * half)
            middle = log[b * half + half // 2 : b * half + half // 2 + 1]
            row_scale = jnp.exp(log[own] - middle)
            shrunk = key * jnp.exp(jnp.minimum(middle - log, 75.0))
            both = jnp.concatenate([query[own] * row_scale, key[own] * row_scale], axis=0)
            product = mm_nt(both, shrunk)
            mixed.append(product[:half])
            kept.append(product[half:])
        coupling.append(
            jnp.where(rows > cols, jnp.concatenate(kept, axis=0) * rate_row, 0.0).astype(bf16)
        )
        mixing.append(
            jnp.where(rows >= cols, jnp.concatenate(mixed, axis=0) * rate_row, 0.0).astype(bf16)
        )
        growth = jnp.exp(log)
        queries_grown.append(query * growth)
        right.append(jnp.concatenate([value, (key * growth).astype(bf16)], axis=1))
        finals.append((key * jnp.exp(last - log) * rate_column).astype(bf16))
        decay.append(jnp.exp(last))

    size = 1
    inverse = None
    while size < length:
        corner = (
            (rows // (2 * size) == cols // (2 * size))
            & ((rows // size) % 2 == 1)
            & ((cols // size) % 2 == 0)
        )
        corners = [jnp.where(corner, coupling[i], jnp.zeros_like(coupling[i])) for i in chunks]
        if inverse is None:
            unit_matrix = (rows == cols).astype(f32)
            inverse = [unit_matrix - corners[i].astype(f32) for i in chunks]
        else:
            short = [inverse[i].astype(bf16) for i in chunks]
            below = [mm(corners[i], short[i]) for i in chunks]
            inverse = [inverse[i] - mm(short[i], below[i]) for i in chunks]
        size *= 2

    short = [inverse[i].astype(bf16) for i in chunks]
    first = [mm(short[i], right[i]).astype(bf16) for i in chunks]
    left = [right[i].astype(f32) - first[i].astype(f32) - mm(coupling[i], first[i]) for i in chunks]
    solved = [(first[i].astype(f32) + mm(short[i], left[i])).astype(bf16) for i in chunks]

    moves = [mm_tn(solved[i], finals[i]) for i in chunks]
    mixes = [mm(mixing[i], solved[i]) for i in chunks]
    reads = [(queries_grown[i] - mixes[i][:, DK:]).astype(bf16) for i in chunks]
    state = start[...] if grouped else jnp.zeros((DK, DK), f32)
    for i in chunks:
        held = state.astype(bf16)
        outputs[i] = (mixes[i][:, :DK] + mm_nt(reads[i], held)).astype(bf16)
        state = state * decay[i] - mm(held, moves[i][DK:]) + moves[i][:DK]
    if grouped:
        final[...] = state
    for step in range(heads):
        cores[step][...] = outputs[partner(me, step, heads)]


def project_kernel(heads, parts, *refs):
    place, residual, weight = refs[:3]
    cores = refs[3 : 3 + heads]
    outs = refs[3 + heads : 3 + heads + parts]
    whole, summed = refs[3 + heads + parts :]
    me, head_me = place[0], place[1]
    for step in range(heads):
        whole[:, lanes(partner(me, step, heads))] = cores[step][...]
    summed[...] = jnp.dot(whole[...], weight[...], preferred_element_type=f32)
    share = summed.shape[0] // parts
    for step in range(parts):
        at = pl.ds(pl.multiple_of(partner(head_me, step, parts) * share, share), share)
        if step == 0:
            outs[0][...] = summed[at, :] + residual[at, :].astype(f32)
        else:
            outs[step][...] = summed[at, :].astype(bf16)


def normalized(values, gain):
    return values * lax.rsqrt(jnp.mean(values * values, axis=-1, keepdims=True) + eps_norm) * gain


def latent_kernel(parts, *refs):
    gain, latent_weight, latent_gain = refs[:3]
    partials = refs[3 : 3 + parts]
    stream, latent = refs[3 + parts :]
    total = partials[0][...]
    for step in range(1, parts):
        total = total + partials[step][...].astype(f32)
    short = total.astype(bf16)
    stream[...] = short
    normed = normalized(short.astype(f32), gain[...]).astype(bf16)
    before = jnp.dot(normed, latent_weight[...], preferred_element_type=f32)
    latent[...] = normalized(before, latent_gain[...]).astype(bf16)


def join_kernel(parts, *refs):
    place = refs[0]
    pieces = refs[1 : 1 + parts]
    out = refs[1 + parts]
    share = out.shape[0] // parts
    for step in range(parts):
        at = pl.ds(pl.multiple_of(partner(place[1], step, parts) * share, share), share)
        out[at, :] = pieces[step][...]


def query_kernel(parts, *refs):
    place, gain, query_weight, up = refs[:4]
    pieces = refs[4 : 4 + parts]
    stream, absorbed = refs[4 + parts :]
    length = stream.shape[0]
    share = length // parts
    for step in range(parts):
        at = pl.ds(pl.multiple_of(partner(place[1], step, parts) * share, share), share)
        stream[at, :] = pieces[step][...]
    normed = normalized(stream[...].astype(f32), gain[...]).astype(bf16)
    query = jnp.dot(normed, query_weight[...], preferred_element_type=f32).astype(bf16)
    for head in range(query.shape[1] // DH):
        own = slice(head * DH, (head + 1) * DH)
        absorbed[head * length : (head + 1) * length, :] = (
            mm_nt(query[:, own], up[:, own]) * DH ** (-0.5)
        ).astype(bf16)


def attend_kernel(count, *refs):
    place, absorbed, up = refs[:3]
    latents = refs[3 : 3 + count]
    out, scores, mixed = refs[3 + count :]
    length = latents[0].shape[0]
    heads = absorbed.shape[0] // length
    me = place[2]
    rows = lax.broadcasted_iota(jnp.int32, (length, length), 0)
    cols = lax.broadcasted_iota(jnp.int32, (length, length), 1)
    causal = jnp.concatenate([rows >= cols] * heads, axis=0)
    peak = None
    for step in range(count):
        part = mm_nt(absorbed[...], latents[step][...])
        if step == 0:
            part = jnp.where(causal, part, -1e30)
        else:
            part = jnp.where(step <= me, part, -1e30)
        scores[:, step * length : (step + 1) * length] = part
        top = jnp.max(part, axis=-1, keepdims=True)
        peak = top if peak is None else jnp.maximum(peak, top)
    total = None
    for step in range(count):
        weights = jnp.exp(scores[:, step * length : (step + 1) * length] - peak)
        added = jnp.sum(weights, axis=-1, keepdims=True)
        share = mm(weights, latents[step][...])
        if total is None:
            total = added
            mixed[...] = share
        else:
            total = total + added
            mixed[...] += share
    for head in range(heads):
        own = slice(head * length, (head + 1) * length)
        value = slice((heads + head) * DH, (heads + head + 1) * DH)
        spread = (mixed[own, :] / total[own, :]).astype(bf16)
        out[:, head * DH : (head + 1) * DH] = jnp.dot(
            spread, up[:, value], preferred_element_type=f32
        ).astype(bf16)


def per_device(
    kda_inputs,
    gate_log,
    beta,
    conv_weight,
    kda_out_weight,
    residual,
    norm_gain,
    latent_weight,
    latent_gain,
    query_weight,
    up_weight,
):
    length, width = residual.shape
    heads = beta.shape[1]
    count, parts = lax.axis_size("ctx"), lax.axis_size("head")
    groups = count // heads
    ctx_me = lax.axis_index("ctx").astype(jnp.int32)
    place = jnp.stack([ctx_me % heads, lax.axis_index("head").astype(jnp.int32), ctx_me])

    message = (4 * length + BETA_ROWS, DK)
    packed = call(
        functools.partial(pack_kernel, heads),
        [(message, bf16)] * heads,
        [place, kda_inputs, gate_log, beta],
    )
    blocks = [packed[0]] + [trade(packed[k], "ctx", k, heads) for k in range(1, heads)]
    taps = lax.dynamic_slice_in_dim(conv_weight, place[0] * DK, DK, axis=2)
    core_outs = [((length, DK), bf16)] * heads
    scratch = [
        ((3, heads * length + 8, DK), f32),
        ((heads * length, DK), bf16),
        ((heads, BETA_ROWS, length), bf16),
        ((heads, length, DK), bf16),
    ]
    if groups == 1:
        cores = call(
            functools.partial(delta_kernel, heads, length, False),
            core_outs,
            [place, taps] + blocks,
            scratch,
        )
    else:
        tails = jnp.stack([b[: 3 * length].reshape(3, length, DK)[:, length - 8 :] for b in blocks])
        order = jnp.stack([partner(heads - 1, k, heads) == place[0] for k in range(heads)])
        tail = jnp.sum(jnp.where(order[:, None, None, None], tails, 0).astype(f32), axis=0)
        halo = passed_along(tail, "ctx", heads)

        def run(start):
            return call(
                functools.partial(delta_kernel, heads, length, True),
                core_outs + [((DK, DK), f32)],
                [place, taps] + blocks + [halo, start],
                scratch,
            )

        def relay(step_index, start):
            return passed_along(run(start)[heads], "ctx", heads)

        start = lax.fori_loop(0, groups - 1, relay, jnp.zeros((DK, DK), f32))
        cores = run(start)[:heads]

    cores = [cores[0]] + [trade(cores[k], "ctx", k, heads) for k in range(1, heads)]
    share = length // parts
    partials = call(
        functools.partial(project_kernel, heads, parts),
        [((share, width), f32)] + [((share, width), bf16)] * (parts - 1),
        [place, residual, kda_out_weight] + list(cores),
        [((length, heads * DK), bf16), ((length, width), f32)],
    )
    partials = [partials[0]] + [trade(partials[k], "head", k, parts) for k in range(1, parts)]
    stream_rows, latent_rows = call(
        functools.partial(latent_kernel, parts),
        [((share, width), bf16), ((share, latent_weight.shape[1]), bf16)],
        [norm_gain[None], latent_weight, latent_gain[None]] + partials,
    )
    latent_parts = [latent_rows] + [trade(latent_rows, "head", k, parts) for k in range(1, parts)]
    stream_parts = [stream_rows] + [trade(stream_rows, "head", k, parts) for k in range(1, parts)]
    latent = call(
        functools.partial(join_kernel, parts),
        [((length, latent_weight.shape[1]), bf16)],
        [place] + latent_parts,
    )[0]
    latents = [latent] + [passed_along(latent, "ctx", k) for k in range(1, count)]
    up = up_weight.reshape(up_weight.shape[0], -1)
    heads_mla = query_weight.shape[1] // DH
    stream_out, absorbed = call(
        functools.partial(query_kernel, parts),
        [((length, width), bf16), ((heads_mla * length, up.shape[0]), bf16)],
        [place, norm_gain[None], query_weight, up] + stream_parts,
    )
    attention_out = call(
        functools.partial(attend_kernel, count),
        [((length, heads_mla * DH), bf16)],
        [place, absorbed, up] + latents,
        [
            ((heads_mla * length, count * length), f32),
            ((heads_mla * length, up.shape[0]), f32),
        ],
        48,
    )[0]
    return (stream_out, attention_out)


def solution(mesh):
    in_specs = (
        P(None, "ctx", "head"),
        P("ctx", "head"),
        P("ctx", "head"),
        P(None, None, "head"),
        P("head", None),
        P("ctx", None),
        P(),
        P(),
        P(),
        P(None, "head"),
        P(None, None, "head"),
    )
    out_specs = (P("ctx", None), P("ctx", "head"))
    return jax.shard_map(
        per_device, mesh=mesh, in_specs=in_specs, out_specs=out_specs, check_vma=False
    )
```

time: 405 us -> 93.7 us (0.23)
  other arithmetic: 110 us -> 0.08 us
  matrix products: 91.2 us -> 0 us
  waiting for transfers between devices: 103 us -> 26.5 us
  local copies, waits for them, and re-layouts: 23.4 us -> 5.59 us
  Pallas kernels: 0 us -> 15.2 us
  starting transfers between devices: 58.6 us -> 44.5 us
  between operations: 14.4 us -> 0.89 us
    dot_general x44 -> x0, matrix products: 90.2 us -> none  [the longest x19 39.6 us: matmul_heads(): return jnp.einsum('hij,hjk->hik', left, right, precision=highest_precision)]
    another operation x5 -> x1, other arithmetic: 89.1 us -> 0.08 us  [per_device(): jnp.stack([ctx_me % heads, lax.axis_index('head').astype(jnp.int32), ctx_...]
    psum x1 -> x0, waiting for transfers between devices: 70.5 us -> none  [per_device(): summed = lax.psum(partial_proj, 'head')]
    ppermute x8 -> x7, starting transfers between devices: 58.5 us -> 14.4 us  [passed_along(): return lax.ppermute(block, axis, route)]
    ppermute x0 -> x23, starting transfers between devices: none -> 30 us  [trade(): return lax.ppermute(block, axis, route)]
    ppermute x0 -> x23, waiting for transfers between devices: none -> 24.8 us  [trade(): return lax.ppermute(block, axis, route)]
    all_gather x1 -> x0, waiting for transfers between devices: 20.7 us -> none  [per_device(): piece = lax.all_gather(latent, 'ctx', axis=0, tiled=True)]
    pallas_call x0 -> x7, Pallas kernels: none -> 15.2 us  [call(): pl.pallas_call(kernel, out_shape=[jax.ShapeDtypeStruct(shape, dtype) for...]
  transfers between devices with their start and end apart: 10 -> 30, of which waited for: 9 -> 11; matrix products, arithmetic and copies ran while one was open for 4% -> 0% of each run, Pallas kernels for 0% -> 2%
where the time goes in v1:
time: 93.7 us; the launch traced here: 92.7 us
  starting transfers between devices  44.5 us (47%)
  waiting for transfers between devices  26.5 us (28%)
  Pallas kernels  15.2 us (16%)
  local copies, waits for them, and re-layouts  5.59 us (6%)
    ppermute x23, starting transfers between devices, trade(): return lax.ppermute(block, axis, route)  30 us
    ppermute x23, waiting for transfers between devices, trade(): return lax.ppermute(block, axis, route)  24.8 us
    pallas_call x7, Pallas kernels, call(): pl.pallas_call(kernel, out_shape=[jax.ShapeDtypeStruct(shape, dtype) for...  15.2 us
    ppermute x7, starting transfers between devices, passed_along(): return lax.ppermute(block, axis, route)  14.4 us
    unnamed x22, local copies, waits for them, and re-layouts  5.58 us
  transfers between devices with their start and end apart: 30, of which 11 were waited for; matrix products, arithmetic and copies ran while one was open for 0% of the time, Pallas kernels for 2%

profile of v1, /device:TPU:0, one launch (start us, length us, event | category | flops | bytes accessed | tf_op | source)
XLA Modules:
  0.0 92.7 jit_solution(14669228572237202605)
XLA Ops:
  0.7 0.8 copy.13.beta
  1.5 1.1 %copy-done.4 = bf16[3,128,1024]{2,1,0:T(8,128)(2,1)S(1)} copy-done((bf16[3,128,1024]{2,1,0:T(8,128)(2,1)S(1)}, bf16[3,128,1024]{2,1,0:T(8,128)(2,1)}, u32[]{:S(2)}) %copy-start.4) | copy-done | bytes 786456
  2.7 1.0 %copy-done.6 = f32[128,1024]{1,0:T(8,128)S(1)} copy-done((f32[128,1024]{1,0:T(8,128)S(1)}, f32[128,1024]{1,0:T(8,128)}, u32[]{:S(2)}) %copy-start.6) | copy-done | bytes 524312
  3.7 1.0 %shard_map.122 = (bf16[528,128]{1,0:T(8,128)(2,1)S(1)}, bf16[528,128]{1,0:T(8,128)(2,1)S(1)}, bf16[528,128]{1,0:T(8,128)(2,1)S(1)}, bf16[528,128]{1,0:T(8,128)(2...) custom-call(s32[3]{0:T(128)S(1)} %pad_add_fusion.place.refs_0_, ...), custom_call_target="tpu_custom_call" | custom-call | tf_op jit(solution)/shard_map/pallas_call | solution.py:40
  4.7 0.5 collective-permute-start
  5.2 2.6 %collective-permute-start.1 = (bf16[528,128]{1,0:T(8,128)(2,1)S(1)}, bf16[528,128]{1,0:T(8,128)(2,1)S(1)}, u32[]{:S(2)}, u32[]{:S(2)}) collective-permute-start(bf16[528,128]{1,0:T(8,128)(2,1)S(1)} %get-tuple-element.28), channel_id=1, source_target_pairs={{0,8},{4,12},{8,0},{12,4},{16,24},{20,28},{24,16},{28,20},{1,9},{5... | collective-permute-start | bytes 405512 | tf_op jit(solution)/shard_map/ppermute | solution.py:59
  7.8 1.8 %collective-permute-start.3 = (bf16[528,128]{1,0:T(8,128)(2,1)S(1)}, bf16[528,128]{1,0:T(8,128)(2,1)S(1)}, u32[]{:S(2)}, u32[]{:S(2)}) collective-permute-start(bf16[528,128]{1,0:T(8,128)(2,1)S(1)} %get-tuple-element.30), channel_id=1, source_target_pairs={{0,16},{4,20},{8,24},{12,28},{16,0},{20,4},{24,8},{28,12},{1,17},{... | collective-permute-start | bytes 405512 | tf_op jit(solution)/shard_map/ppermute | solution.py:59
  9.6 2.6 %collective-permute-start.5 = (bf16[528,128]{1,0:T(8,128)(2,1)S(1)}, bf16[528,128]{1,0:T(8,128)(2,1)S(1)}, u32[]{:S(2)}, u32[]{:S(2)}) collective-permute-start(bf16[528,128]{1,0:T(8,128)(2,1)S(1)} %get-tuple-element.32), channel_id=1, source_target_pairs={{0,24},{4,28},{8,16},{12,20},{16,8},{20,12},{24,0},{28,4},{1,25},{... | collective-permute-start | bytes 405512 | tf_op jit(solution)/shard_map/ppermute | solution.py:59
  12.2 1.7 %collective-permute-start.6 = (bf16[528,128]{1,0:T(8,128)(2,1)S(1)}, bf16[528,128]{1,0:T(8,128)(2,1)S(1)}, u32[]{:S(2)}, u32[]{:S(2)}) collective-permute-start(bf16[528,128]{1,0:T(8,128)(2,1)S(1)} %get-tuple-element.33), channel_id=1, source_target_pairs={{0,28},{4,24},{8,20},{12,16},{16,12},{20,8},{24,4},{28,0},{1,29},{... | collective-permute-start | bytes 405512 | tf_op jit(solution)/shard_map/ppermute | solution.py:59
  13.9 0.7 collective-permute-done.2.refs_5_
  14.6 7.1 %collective-permute-done.4.refs_7_ = bf16[528,128]{1,0:T(8,128)(2,1)S(1)} collective-permute-done((bf16[528,128]{1,0:T(8,128)(2,1)S(1)}, bf16[528,128]{1,0:T(8,128)(2,1)S(1)}, u32[]{:S(2)}, u32[]{:S(2)}) %collective-permute-start.4) | collective-permute-done | bytes 135200 | tf_op jit(solution)/shard_map/ppermute | solution.py:59
  21.6 6.1 %shard_map.123 = (bf16[128,128]{1,0:T(8,128)(2,1)S(1)}, bf16[128,128]{1,0:T(8,128)(2,1)S(1)}, bf16[128,128]{1,0:T(8,128)(2,1)S(1)}, bf16[128,128]{1,0:T(8,128)(2...) custom-call(s32[3]{0:T(128)S(1)} %pad_add_fusion.place.refs_0_, ...), custom_call_target="tpu_custom_call" | custom-call | tf_op jit(solution)/shard_map/pallas_call | solution.py:40
  27.7 0.6 collective-permute-start.7
  28.4 1.7 %collective-permute-start.8 = (bf16[128,128]{1,0:T(8,128)(2,1)S(1)}, bf16[128,128]{1,0:T(8,128)(2,1)S(1)}, u32[]{:S(2)}, u32[]{:S(2)}) collective-permute-start(bf16[128,128]{1,0:T(8,128)(2,1)S(1)} %get-tuple-element.36), channel_id=1, source_target_pairs={{0,8},{4,12},{8,0},{12,4},{16,24},{20,28},{24,16},{28,20},{1,9},{5... | collective-permute-start | bytes 98312 | tf_op jit(solution)/shard_map/ppermute | solution.py:59
  30.1 1.5 %collective-permute-start.10 = (bf16[128,128]{1,0:T(8,128)(2,1)S(1)}, bf16[128,128]{1,0:T(8,128)(2,1)S(1)}, u32[]{:S(2)}, u32[]{:S(2)}) collective-permute-start(bf16[128,128]{1,0:T(8,128)(2,1)S(1)} %get-tuple-element.38), channel_id=1, source_target_pairs={{0,16},{4,20},{8,24},{12,28},{16,0},{20,4},{24,8},{28,12},{1,17},{... | collective-permute-start | bytes 98312 | tf_op jit(solution)/shard_map/ppermute | solution.py:59
  31.6 0.3 collective-permute-start.11
  31.9 2.7 %collective-permute-start.12 = (bf16[128,128]{1,0:T(8,128)(2,1)S(1)}, bf16[128,128]{1,0:T(8,128)(2,1)S(1)}, u32[]{:S(2)}, u32[]{:S(2)}) collective-permute-start(bf16[128,128]{1,0:T(8,128)(2,1)S(1)} %get-tuple-element.40), channel_id=1, source_target_pairs={{0,24},{4,28},{8,16},{12,20},{16,8},{20,12},{24,0},{28,4},{1,25},{... | collective-permute-start | bytes 98312 | tf_op jit(solution)/shard_map/ppermute | solution.py:59
  34.6 0.4 collective-permute-done.11.refs_8_
  35.0 1.7 %collective-permute-done.12.refs_9_ = bf16[128,128]{1,0:T(8,128)(2,1)S(1)} collective-permute-done((bf16[128,128]{1,0:T(8,128)(2,1)S(1)}, bf16[128,128]{1,0:T(8,128)(2,1)S(1)}, u32[]{:S(2)}, u32[]{:S(2)}) %collective-permute-start.12) | collective-permute-done | bytes 32800 | tf_op jit(solution)/shard_map/ppermute | solution.py:59
  36.7 2.4 %collective-permute-done.13.refs_10_ = bf16[128,128]{1,0:T(8,128)(2,1)S(1)} collective-permute-done((bf16[128,128]{1,0:T(8,128)(2,1)S(1)}, bf16[128,128]{1,0:T(8,128)(2,1)S(1)}, u32[]{:S(2)}, u32[]{:S(2)}) %collective-permute-start.13) | collective-permute-done | bytes 32800 | tf_op jit(solution)/shard_map/ppermute | solution.py:59
  39.2 2.3 %copy-done.1 = bf16[1024,2304]{1,0:T(8,128)(2,1)S(1)} copy-done((bf16[1024,2304]{1,0:T(8,128)(2,1)S(1)}, bf16[1024,2304]{1,0:T(8,128)(2,1)}, u32[]{:S(2)}) %copy-start.1) | copy-done | bytes 4718616
  41.5 1.4 %shard_map.124 = (f32[32,2304]{1,0:T(8,128)S(1)}, bf16[32,2304]{1,0:T(8,128)(2,1)S(1)}, bf16[32,2304]{1,0:T(8,128)(2,1)S(1)}, bf16[32,2304]{1,0:T(8,128)(2,1)S(1)}) custom-call(s32[3]{0:T(128)S(1)} %pad_add_fusion.place.refs_0_, bf16[128,2304]{1,0:T(8,128)(2,1)S(1)} %copy-done.5, bf16[1024,2304]{1,0:T(8,128)(2,1)S(1)} %copy-done.1, ...), custom_call_target="tpu_custom_call" | custom-call | tf_op jit(solution)/shard_map/pallas_call | solution.py:40
  43.0 1.6 %collective-permute-start.14 = (bf16[32,2304]{1,0:T(8,128)(2,1)S(1)}, bf16[32,2304]{1,0:T(8,128)(2,1)S(1)}, u32[]{:S(2)}, u32[]{:S(2)}) collective-permute-start(bf16[32,2304]{1,0:T(8,128)(2,1)S(1)} %get-tuple-element.43), channel_id=1, source_target_pairs={{0,1},{1,0},{2,3},{3,2},{4,5},{5,4},{6,7},{7,6},{8,9},{9,8},{10,11... | collective-permute-start | bytes 442376 | tf_op jit(solution)/shard_map/ppermute | solution.py:59
  44.6 2.6 %collective-permute-start.15 = (bf16[32,2304]{1,0:T(8,128)(2,1)S(1)}, bf16[32,2304]{1,0:T(8,128)(2,1)S(1)}, u32[]{:S(2)}, u32[]{:S(2)}) collective-permute-start(bf16[32,2304]{1,0:T(8,128)(2,1)S(1)} %get-tuple-element.44), channel_id=1, source_target_pairs={{0,2},{1,3},{2,0},{3,1},{4,6},{5,7},{6,4},{7,5},{8,10},{9,11},{10,... | collective-permute-start | bytes 442376 | tf_op jit(solution)/shard_map/ppermute | solution.py:59
  47.4 3.8 %collective-permute-done.14.refs_4_ = bf16[32,2304]{1,0:T(8,128)(2,1)S(1)} collective-permute-done((bf16[32,2304]{1,0:T(8,128)(2,1)S(1)}, bf16[32,2304]{1,0:T(8,128)(2,1)S(1)}, u32[]{:S(2)}, u32[]{:S(2)}) %collective-permute-start.14) | collective-permute-done | bytes 147488 | tf_op jit(solution)/shard_map/ppermute | solution.py:59
  51.2 7.3 %collective-permute-done.15.refs_5_ = bf16[32,2304]{1,0:T(8,128)(2,1)S(1)} collective-permute-done((bf16[32,2304]{1,0:T(8,128)(2,1)S(1)}, bf16[32,2304]{1,0:T(8,128)(2,1)S(1)}, u32[]{:S(2)}, u32[]{:S(2)}) %collective-permute-start.15) | collective-permute-done | bytes 147488 | tf_op jit(solution)/shard_map/ppermute | solution.py:59
  58.6 0.8 shard_map.125
  59.3 2.6 %collective-permute-start.20 = (bf16[32,512]{1,0:T(8,128)(2,1)S(1)}, bf16[32,512]{1,0:T(8,128)(2,1)S(1)}, u32[]{:S(2)}, u32[]{:S(2)}) collective-permute-start(bf16[32,512]{1,0:T(8,128)(2,1)S(1)} %get-tuple-element.49.refs_1_), channel_id=1, source_target_pairs={{0,1},{1,0},{2,3},{3,2},{4,5},{5,4},{6,7},{7,6},{8,9},{9,8},{10,11... | collective-permute-start | bytes 98312 | tf_op jit(solution)/shard_map/ppermute | solution.py:59
  62.0 1.1 %collective-permute-start.21 = (bf16[32,512]{1,0:T(8,128)(2,1)S(1)}, bf16[32,512]{1,0:T(8,128)(2,1)S(1)}, u32[]{:S(2)}, u32[]{:S(2)}) collective-permute-start(bf16[32,512]{1,0:T(8,128)(2,1)S(1)} %get-tuple-element.49.refs_1_), channel_id=1, source_target_pairs={{0,2},{1,3},{2,0},{3,1},{4,6},{5,7},{6,4},{7,5},{8,10},{9,11},{10,... | collective-permute-start | bytes 98312 | tf_op jit(solution)/shard_map/ppermute | solution.py:59
  63.1 1.4 %collective-permute-start.22 = (bf16[32,512]{1,0:T(8,128)(2,1)S(1)}, bf16[32,512]{1,0:T(8,128)(2,1)S(1)}, u32[]{:S(2)}, u32[]{:S(2)}) collective-permute-start(bf16[32,512]{1,0:T(8,128)(2,1)S(1)} %get-tuple-element.49.refs_1_), channel_id=1, source_target_pairs={{0,3},{1,2},{2,1},{3,0},{4,7},{5,6},{6,5},{7,4},{8,11},{9,10},{10,... | collective-permute-start | bytes 98312 | tf_op jit(solution)/shard_map/ppermute | solution.py:59
  64.5 1.0 %collective-permute-start.17 = (bf16[32,2304]{1,0:T(8,128)(2,1)S(1)}, bf16[32,2304]{1,0:T(8,128)(2,1)S(1)}, u32[]{:S(2)}, u32[]{:S(2)}) collective-permute-start(bf16[32,2304]{1,0:T(8,128)(2,1)S(1)} %get-tuple-element.46.refs_4_), channel_id=1, source_target_pairs={{0,1},{1,0},{2,3},{3,2},{4,5},{5,4},{6,7},{7,6},{8,9},{9,8},{10,11... | collective-permute-start | bytes 442376 | tf_op jit(solution)/shard_map/ppermute | solution.py:59
  65.5 2.0 %collective-permute-start.18 = (bf16[32,2304]{1,0:T(8,128)(2,1)S(1)}, bf16[32,2304]{1,0:T(8,128)(2,1)S(1)}, u32[]{:S(2)}, u32[]{:S(2)}) collective-permute-start(bf16[32,2304]{1,0:T(8,128)(2,1)S(1)} %get-tuple-element.46.refs_4_), channel_id=1, source_target_pairs={{0,2},{1,3},{2,0},{3,1},{4,6},{5,7},{6,4},{7,5},{8,10},{9,11},{10,... | collective-permute-start | bytes 442376 | tf_op jit(solution)/shard_map/ppermute | solution.py:59
  67.5 1.4 %collective-permute-start.19 = (bf16[32,2304]{1,0:T(8,128)(2,1)S(1)}, bf16[32,2304]{1,0:T(8,128)(2,1)S(1)}, u32[]{:S(2)}, u32[]{:S(2)}) collective-permute-start(bf16[32,2304]{1,0:T(8,128)(2,1)S(1)} %get-tuple-element.46.refs_4_), channel_id=1, source_target_pairs={{0,3},{1,2},{2,1},{3,0},{4,7},{5,6},{6,5},{7,4},{8,11},{9,10},{10,... | collective-permute-start | bytes 442376 | tf_op jit(solution)/shard_map/ppermute | solution.py:59
  68.9 0.4 collective-permute-done.22.refs_4_
  69.3 0.6 shard_map.127.refs_3_
  69.9 1.3 %collective-permute-start.23 = (bf16[128,512]{1,0:T(8,128)(2,1)S(1)}, bf16[128,512]{1,0:T(8,128)(2,1)S(1)}, u32[]{:S(2)}, u32[]{:S(2)}) collective-permute-start(bf16[128,512]{1,0:T(8,128)(2,1)S(1)} %shard_map.127.refs_3_), channel_id=1, source_target_pairs={{0,4},{4,8},{8,12},{12,16},{16,20},{20,24},{24,28},{1,5},{5,9},{9,... | collective-permute-start | bytes 393224 | tf_op jit(solution)/shard_map/ppermute | solution.py:65
  71.2 3.0 %collective-permute-start.24 = (bf16[128,512]{1,0:T(8,128)(2,1)S(1)}, bf16[128,512]{1,0:T(8,128)(2,1)S(1)}, u32[]{:S(2)}, u32[]{:S(2)}) collective-permute-start(bf16[128,512]{1,0:T(8,128)(2,1)S(1)} %shard_map.127.refs_3_), channel_id=1, source_target_pairs={{0,8},{4,12},{8,16},{12,20},{16,24},{20,28},{1,9},{5,13},{9,17},{1... | collective-permute-start | bytes 393224 | tf_op jit(solution)/shard_map/ppermute | solution.py:65
  74.2 3.6 %collective-permute-start.25 = (bf16[128,512]{1,0:T(8,128)(2,1)S(1)}, bf16[128,512]{1,0:T(8,128)(2,1)S(1)}, u32[]{:S(2)}, u32[]{:S(2)}) collective-permute-start(bf16[128,512]{1,0:T(8,128)(2,1)S(1)} %shard_map.127.refs_3_), channel_id=1, source_target_pairs={{0,12},{4,16},{8,20},{12,24},{16,28},{1,13},{5,17},{9,21},{13,25},... | collective-permute-start | bytes 393224 | tf_op jit(solution)/shard_map/ppermute | solution.py:65
  77.8 0.9 collective-permute-done.18.refs_6_
  78.7 2.4 %collective-permute-start.26 = (bf16[128,512]{1,0:T(8,128)(2,1)S(1)}, bf16[128,512]{1,0:T(8,128)(2,1)S(1)}, u32[]{:S(2)}, u32[]{:S(2)}) collective-permute-start(bf16[128,512]{1,0:T(8,128)(2,1)S(1)} %shard_map.127.refs_3_), channel_id=1, source_target_pairs={{0,16},{4,20},{8,24},{12,28},{1,17},{5,21},{9,25},{13,29},{2,18},{... | collective-permute-start | bytes 393224 | tf_op jit(solution)/shard_map/ppermute | solution.py:65
  81.1 1.3 %collective-permute-start.27 = (bf16[128,512]{1,0:T(8,128)(2,1)S(1)}, bf16[128,512]{1,0:T(8,128)(2,1)S(1)}, u32[]{:S(2)}, u32[]{:S(2)}) collective-permute-start(bf16[128,512]{1,0:T(8,128)(2,1)S(1)} %shard_map.127.refs_3_), channel_id=1, source_target_pairs={{0,20},{4,24},{8,28},{1,21},{5,25},{9,29},{2,22},{6,26},{10,30},{3... | collective-permute-start | bytes 393224 | tf_op jit(solution)/shard_map/ppermute | solution.py:65
  82.5 1.5 %collective-permute-start.28 = (bf16[128,512]{1,0:T(8,128)(2,1)S(1)}, bf16[128,512]{1,0:T(8,128)(2,1)S(1)}, u32[]{:S(2)}, u32[]{:S(2)}) collective-permute-start(bf16[128,512]{1,0:T(8,128)(2,1)S(1)} %shard_map.127.refs_3_), channel_id=1, source_target_pairs={{0,24},{4,28},{1,25},{5,29},{2,26},{6,30},{3,27},{7,31}} | collective-permute-start | bytes 393224 | tf_op jit(solution)/shard_map/ppermute | solution.py:65
  84.0 1.3 %collective-permute-start.29 = (bf16[128,512]{1,0:T(8,128)(2,1)S(1)}, bf16[128,512]{1,0:T(8,128)(2,1)S(1)}, u32[]{:S(2)}, u32[]{:S(2)}) collective-permute-start(bf16[128,512]{1,0:T(8,128)(2,1)S(1)} %shard_map.127.refs_3_), channel_id=1, source_target_pairs={{0,28},{1,29},{2,30},{3,31}} | collective-permute-start | bytes 393224 | tf_op jit(solution)/shard_map/ppermute | solution.py:65
  85.3 0.2 copy.14
  85.6 1.5 %shard_map.126 = (bf16[128,2304]{1,0:T(8,128)(2,1)}, bf16[512,512]{1,0:T(8,128)(2,1)S(1)}) custom-call(s32[3]{0:T(128)S(1)} %pad_add_fusion.place.refs_0_, f32[1,2304]{1,0:T(1,128)S(1)} %broadcast_in_dim.7.refs_0_.refs_1_, bf16[2304,512]{1,0:T(8,128)(2,1)S(1)} %copy-done.3, bf16[512,1024]{1,0:T(8,128)(2,1)S(1)} %bitcast.6, ...), custom_call_target="tpu_custom_call" | custom-call | tf_op jit(solution)/shard_map/pallas_call | solution.py:40
  87.1 0.3 collective-permute-done.28.refs_9_
  87.4 1.4 %collective-permute-done.29.refs_10_ = bf16[128,512]{1,0:T(8,128)(2,1)S(1)} collective-permute-done((bf16[128,512]{1,0:T(8,128)(2,1)S(1)}, bf16[128,512]{1,0:T(8,128)(2,1)S(1)}, u32[]{:S(2)}, u32[]{:S(2)}) %collective-permute-start.29) | collective-permute-done | bytes 131104 | tf_op jit(solution)/shard_map/ppermute | solution.py:65
  88.8 3.9 %shard_map.128 = bf16[128,512]{1,0:T(8,128)(2,1)} custom-call(s32[3]{0:T(128)S(1)} %pad_add_fusion.place.refs_0_, bf16[512,512]{1,0:T(8,128)(2,1)S(1)} %get-tuple-element.48.refs_1_, bf16[512,1024]{1,0:T(8,128)(2,1)S(1)} %bitcast.7, bf16[128,512]{1,0:T(8,128)(2,1)S(1)} %shard_map.127.refs_3_, bf16[128,512]{1,0:T(8,128)(2,1)S(1)} %collective-permute-done.23.refs_4_, ...), custom_call_target="tpu_custom_call" | custom-call | tf_op jit(solution)/shard_map/pallas_call | solution.py:40
  (44 shorter events, 0.5 us)
Async XLA Ops:
  0.6 13.3 %copy-start = (f32[3,4,1024]{2,1,0:T(4,128)S(1)}, f32[3,4,1024]{2,1,0:T(4,128)}, u32[]{:S(2)}) copy-start(f32[3,4,1024]{2,1,0:T(4,128)} %param.14) | copy-start | bytes 147460
  1.5 1.1 %copy-start.4 = (bf16[3,128,1024]{2,1,0:T(8,128)(2,1)S(1)}, bf16[3,128,1024]{2,1,0:T(8,128)(2,1)}, u32[]{:S(2)}) copy-start(bf16[3,128,1024]{2,1,0:T(8,128)(2,1)} %inputs.1) | copy-start | bytes 2359300
  2.7 1.0 %copy-start.6 = (f32[128,1024]{1,0:T(8,128)S(1)}, f32[128,1024]{1,0:T(8,128)}, u32[]{:S(2)}) copy-start(f32[128,1024]{1,0:T(8,128)} %gate.1) | copy-start | bytes 1572868
  3.7 35.5 %copy-start.5 = (bf16[128,2304]{1,0:T(8,128)(2,1)S(1)}, bf16[128,2304]{1,0:T(8,128)(2,1)}, u32[]{:S(2)}) copy-start(bf16[128,2304]{1,0:T(8,128)(2,1)} %refs_1_.2) | copy-start | bytes 1769476
  4.7 4.9 %collective-permute-start = (bf16[528,128]{1,0:T(8,128)(2,1)S(1)}, bf16[528,128]{1,0:T(8,128)(2,1)S(1)}, u32[]{:S(2)}, u32[]{:S(2)}) collective-permute-start(bf16[528,128]{1,0:T(8,128)(2,1)S(1)} %get-tuple-element.27), channel_id=1, source_target_pairs={{0,4},{4,0},{8,12},{12,8},{16,20},{20,16},{24,28},{28,24},{1,5},{5... | collective-permute-start | bytes 405512 | tf_op jit(solution)/shard_map/ppermute | solution.py:59
  5.2 7.0 %collective-permute-start.1 = (bf16[528,128]{1,0:T(8,128)(2,1)S(1)}, bf16[528,128]{1,0:T(8,128)(2,1)S(1)}, u32[]{:S(2)}, u32[]{:S(2)}) collective-permute-start(bf16[528,128]{1,0:T(8,128)(2,1)S(1)} %get-tuple-element.28), channel_id=1, source_target_pairs={{0,8},{4,12},{8,0},{12,4},{16,24},{20,28},{24,16},{28,20},{1,9},{5... | collective-permute-start | bytes 405512 | tf_op jit(solution)/shard_map/ppermute | solution.py:59
  7.7 6.8 %collective-permute-start.2 = (bf16[528,128]{1,0:T(8,128)(2,1)S(1)}, bf16[528,128]{1,0:T(8,128)(2,1)S(1)}, u32[]{:S(2)}, u32[]{:S(2)}) collective-permute-start(bf16[528,128]{1,0:T(8,128)(2,1)S(1)} %get-tuple-element.29), channel_id=1, source_target_pairs={{0,12},{4,8},{8,4},{12,0},{16,28},{20,24},{24,20},{28,16},{1,13},{... | collective-permute-start | bytes 405512 | tf_op jit(solution)/shard_map/ppermute | solution.py:59
  7.8 6.7 %collective-permute-start.3 = (bf16[528,128]{1,0:T(8,128)(2,1)S(1)}, bf16[528,128]{1,0:T(8,128)(2,1)S(1)}, u32[]{:S(2)}, u32[]{:S(2)}) collective-permute-start(bf16[528,128]{1,0:T(8,128)(2,1)S(1)} %get-tuple-element.30), channel_id=1, source_target_pairs={{0,16},{4,20},{8,24},{12,28},{16,0},{20,4},{24,8},{28,12},{1,17},{... | collective-permute-start | bytes 405512 | tf_op jit(solution)/shard_map/ppermute | solution.py:59
  9.6 12.0 %collective-permute-start.4 = (bf16[528,128]{1,0:T(8,128)(2,1)S(1)}, bf16[528,128]{1,0:T(8,128)(2,1)S(1)}, u32[]{:S(2)}, u32[]{:S(2)}) collective-permute-start(bf16[528,128]{1,0:T(8,128)(2,1)S(1)} %get-tuple-element.31), channel_id=1, source_target_pairs={{0,20},{4,16},{8,28},{12,24},{16,4},{20,0},{24,12},{28,8},{1,21},{... | collective-permute-start | bytes 405512 | tf_op jit(solution)/shard_map/ppermute | solution.py:59
  9.6 12.0 %collective-permute-start.5 = (bf16[528,128]{1,0:T(8,128)(2,1)S(1)}, bf16[528,128]{1,0:T(8,128)(2,1)S(1)}, u32[]{:S(2)}, u32[]{:S(2)}) collective-permute-start(bf16[528,128]{1,0:T(8,128)(2,1)S(1)} %get-tuple-element.32), channel_id=1, source_target_pairs={{0,24},{4,28},{8,16},{12,20},{16,8},{20,12},{24,0},{28,4},{1,25},{... | collective-permute-start | bytes 405512 | tf_op jit(solution)/shard_map/ppermute | solution.py:59
  12.2 9.4 %collective-permute-start.6 = (bf16[528,128]{1,0:T(8,128)(2,1)S(1)}, bf16[528,128]{1,0:T(8,128)(2,1)S(1)}, u32[]{:S(2)}, u32[]{:S(2)}) collective-permute-start(bf16[528,128]{1,0:T(8,128)(2,1)S(1)} %get-tuple-element.33), channel_id=1, source_target_pairs={{0,28},{4,24},{8,20},{12,16},{16,12},{20,8},{24,4},{28,0},{1,29},{... | collective-permute-start | bytes 405512 | tf_op jit(solution)/shard_map/ppermute | solution.py:59
  27.7 4.1 %collective-permute-start.7 = (bf16[128,128]{1,0:T(8,128)(2,1)S(1)}, bf16[128,128]{1,0:T(8,128)(2,1)S(1)}, u32[]{:S(2)}, u32[]{:S(2)}) collective-permute-start(bf16[128,128]{1,0:T(8,128)(2,1)S(1)} %get-tuple-element.35), channel_id=1, source_target_pairs={{0,4},{4,0},{8,12},{12,8},{16,20},{20,16},{24,28},{28,24},{1,5},{5... | collective-permute-start | bytes 98312 | tf_op jit(solution)/shard_map/ppermute | solution.py:59
  28.4 6.2 %collective-permute-start.8 = (bf16[128,128]{1,0:T(8,128)(2,1)S(1)}, bf16[128,128]{1,0:T(8,128)(2,1)S(1)}, u32[]{:S(2)}, u32[]{:S(2)}) collective-permute-start(bf16[128,128]{1,0:T(8,128)(2,1)S(1)} %get-tuple-element.36), channel_id=1, source_target_pairs={{0,8},{4,12},{8,0},{12,4},{16,24},{20,28},{24,16},{28,20},{1,9},{5... | collective-permute-start | bytes 98312 | tf_op jit(solution)/shard_map/ppermute | solution.py:59
  30.1 4.5 %collective-permute-start.9 = (bf16[128,128]{1,0:T(8,128)(2,1)S(1)}, bf16[128,128]{1,0:T(8,128)(2,1)S(1)}, u32[]{:S(2)}, u32[]{:S(2)}) collective-permute-start(bf16[128,128]{1,0:T(8,128)(2,1)S(1)} %get-tuple-element.37), channel_id=1, source_target_pairs={{0,12},{4,8},{8,4},{12,0},{16,28},{20,24},{24,20},{28,16},{1,13},{... | collective-permute-start | bytes 98312 | tf_op jit(solution)/shard_map/ppermute | solution.py:59
  30.1 4.5 %collective-permute-start.10 = (bf16[128,128]{1,0:T(8,128)(2,1)S(1)}, bf16[128,128]{1,0:T(8,128)(2,1)S(1)}, u32[]{:S(2)}, u32[]{:S(2)}) collective-permute-start(bf16[128,128]{1,0:T(8,128)(2,1)S(1)} %get-tuple-element.38), channel_id=1, source_target_pairs={{0,16},{4,20},{8,24},{12,28},{16,0},{20,4},{24,8},{28,12},{1,17},{... | collective-permute-start | bytes 98312 | tf_op jit(solution)/shard_map/ppermute | solution.py:59
  31.6 3.3 %collective-permute-start.11 = (bf16[128,128]{1,0:T(8,128)(2,1)S(1)}, bf16[128,128]{1,0:T(8,128)(2,1)S(1)}, u32[]{:S(2)}, u32[]{:S(2)}) collective-permute-start(bf16[128,128]{1,0:T(8,128)(2,1)S(1)} %get-tuple-element.39), channel_id=1, source_target_pairs={{0,20},{4,16},{8,28},{12,24},{16,4},{20,0},{24,12},{28,8},{1,21},{... | collective-permute-start | bytes 98312 | tf_op jit(solution)/shard_map/ppermute | solution.py:59
  31.9 4.8 %collective-permute-start.12 = (bf16[128,128]{1,0:T(8,128)(2,1)S(1)}, bf16[128,128]{1,0:T(8,128)(2,1)S(1)}, u32[]{:S(2)}, u32[]{:S(2)}) collective-permute-start(bf16[128,128]{1,0:T(8,128)(2,1)S(1)} %get-tuple-element.40), channel_id=1, source_target_pairs={{0,24},{4,28},{8,16},{12,20},{16,8},{20,12},{24,0},{28,4},{1,25},{... | collective-permute-start | bytes 98312 | tf_op jit(solution)/shard_map/ppermute | solution.py:59
  34.6 4.6 %collective-permute-start.13 = (bf16[128,128]{1,0:T(8,128)(2,1)S(1)}, bf16[128,128]{1,0:T(8,128)(2,1)S(1)}, u32[]{:S(2)}, u32[]{:S(2)}) collective-permute-start(bf16[128,128]{1,0:T(8,128)(2,1)S(1)} %get-tuple-element.41), channel_id=1, source_target_pairs={{0,28},{4,24},{8,20},{12,16},{16,12},{20,8},{24,4},{28,0},{1,29},{... | collective-permute-start | bytes 98312 | tf_op jit(solution)/shard_map/ppermute | solution.py:59
  39.2 2.3 %copy-start.1 = (bf16[1024,2304]{1,0:T(8,128)(2,1)S(1)}, bf16[1024,2304]{1,0:T(8,128)(2,1)}, u32[]{:S(2)}) copy-start(bf16[1024,2304]{1,0:T(8,128)(2,1)} %refs_2_.2) | copy-start | bytes 14155780
  41.5 5.9 %copy-start.9 = (f32[2304]{0:T(1024)S(1)}, f32[2304]{0:T(1024)}, u32[]{:S(2)}) copy-start(f32[2304]{0:T(1024)} %param.17) | copy-start | bytes 27652
  41.5 17.1 %copy-start.2 = (bf16[2304,512]{1,0:T(8,128)(2,1)S(1)}, bf16[2304,512]{1,0:T(8,128)(2,1)}, u32[]{:S(2)}) copy-start(bf16[2304,512]{1,0:T(8,128)(2,1)} %refs_1_.3) | copy-start | bytes 7077892
  41.5 17.1 %copy-start.7 = (f32[512]{0:T(512)S(1)}, f32[512]{0:T(512)}, u32[]{:S(2)}) copy-start(f32[512]{0:T(512)} %param.19) | copy-start | bytes 6148
  43.0 42.3 %copy-start.8 = (bf16[512,2,512]{2,1,0:T(2,128)(2,1)S(1)}, bf16[512,2,512]{2,1,0:T(2,128)(2,1)}, u32[]{:S(2)}) copy-start(bf16[512,2,512]{2,1,0:T(2,128)(2,1)} %param.21) | copy-start | bytes 3145732
  43.0 8.3 %collective-permute-start.14 = (bf16[32,2304]{1,0:T(8,128)(2,1)S(1)}, bf16[32,2304]{1,0:T(8,128)(2,1)S(1)}, u32[]{:S(2)}, u32[]{:S(2)}) collective-permute-start(bf16[32,2304]{1,0:T(8,128)(2,1)S(1)} %get-tuple-element.43), channel_id=1, source_target_pairs={{0,1},{1,0},{2,3},{3,2},{4,5},{5,4},{6,7},{7,6},{8,9},{9,8},{10,11... | collective-permute-start | bytes 442376 | tf_op jit(solution)/shard_map/ppermute | solution.py:59
  44.6 14.0 %collective-permute-start.15 = (bf16[32,2304]{1,0:T(8,128)(2,1)S(1)}, bf16[32,2304]{1,0:T(8,128)(2,1)S(1)}, u32[]{:S(2)}, u32[]{:S(2)}) collective-permute-start(bf16[32,2304]{1,0:T(8,128)(2,1)S(1)} %get-tuple-element.44), channel_id=1, source_target_pairs={{0,2},{1,3},{2,0},{3,1},{4,6},{5,7},{6,4},{7,5},{8,10},{9,11},{10,... | collective-permute-start | bytes 442376 | tf_op jit(solution)/shard_map/ppermute | solution.py:59
  47.2 11.4 %collective-permute-start.16 = (bf16[32,2304]{1,0:T(8,128)(2,1)S(1)}, bf16[32,2304]{1,0:T(8,128)(2,1)S(1)}, u32[]{:S(2)}, u32[]{:S(2)}) collective-permute-start(bf16[32,2304]{1,0:T(8,128)(2,1)S(1)} %get-tuple-element.45), channel_id=1, source_target_pairs={{0,3},{1,2},{2,1},{3,0},{4,7},{5,6},{6,5},{7,4},{8,11},{9,10},{10,... | collective-permute-start | bytes 442376 | tf_op jit(solution)/shard_map/ppermute | solution.py:59
  58.6 27.0 %copy-start.3 = (bf16[2304,512]{1,0:T(8,128)(2,1)S(1)}, bf16[2304,512]{1,0:T(8,128)(2,1)}, u32[]{:S(2)}) copy-start(bf16[2304,512]{1,0:T(8,128)(2,1)} %refs_2_.3) | copy-start | bytes 7077892
  59.3 8.1 %collective-permute-start.20 = (bf16[32,512]{1,0:T(8,128)(2,1)S(1)}, bf16[32,512]{1,0:T(8,128)(2,1)S(1)}, u32[]{:S(2)}, u32[]{:S(2)}) collective-permute-start(bf16[32,512]{1,0:T(8,128)(2,1)S(1)} %get-tuple-element.49.refs_1_), channel_id=1, source_target_pairs={{0,1},{1,0},{2,3},{3,2},{4,5},{5,4},{6,7},{7,6},{8,9},{9,8},{10,11... | collective-permute-start | bytes 98312 | tf_op jit(solution)/shard_map/ppermute | solution.py:59
  62.0 6.9 %collective-permute-start.21 = (bf16[32,512]{1,0:T(8,128)(2,1)S(1)}, bf16[32,512]{1,0:T(8,128)(2,1)S(1)}, u32[]{:S(2)}, u32[]{:S(2)}) collective-permute-start(bf16[32,512]{1,0:T(8,128)(2,1)S(1)} %get-tuple-element.49.refs_1_), channel_id=1, source_target_pairs={{0,2},{1,3},{2,0},{3,1},{4,6},{5,7},{6,4},{7,5},{8,10},{9,11},{10,... | collective-permute-start | bytes 98312 | tf_op jit(solution)/shard_map/ppermute | solution.py:59
  63.1 6.2 %collective-permute-start.22 = (bf16[32,512]{1,0:T(8,128)(2,1)S(1)}, bf16[32,512]{1,0:T(8,128)(2,1)S(1)}, u32[]{:S(2)}, u32[]{:S(2)}) collective-permute-start(bf16[32,512]{1,0:T(8,128)(2,1)S(1)} %get-tuple-element.49.refs_1_), channel_id=1, source_target_pairs={{0,3},{1,2},{2,1},{3,0},{4,7},{5,6},{6,5},{7,4},{8,11},{9,10},{10,... | collective-permute-start | bytes 98312 | tf_op jit(solution)/shard_map/ppermute | solution.py:59
  64.5 9.7 %collective-permute-start.17 = (bf16[32,2304]{1,0:T(8,128)(2,1)S(1)}, bf16[32,2304]{1,0:T(8,128)(2,1)S(1)}, u32[]{:S(2)}, u32[]{:S(2)}) collective-permute-start(bf16[32,2304]{1,0:T(8,128)(2,1)S(1)} %get-tuple-element.46.refs_4_), channel_id=1, source_target_pairs={{0,1},{1,0},{2,3},{3,2},{4,5},{5,4},{6,7},{7,6},{8,9},{9,8},{10,11... | collective-permute-start | bytes 442376 | tf_op jit(solution)/shard_map/ppermute | solution.py:59
  65.5 13.2 %collective-permute-start.18 = (bf16[32,2304]{1,0:T(8,128)(2,1)S(1)}, bf16[32,2304]{1,0:T(8,128)(2,1)S(1)}, u32[]{:S(2)}, u32[]{:S(2)}) collective-permute-start(bf16[32,2304]{1,0:T(8,128)(2,1)S(1)} %get-tuple-element.46.refs_4_), channel_id=1, source_target_pairs={{0,2},{1,3},{2,0},{3,1},{4,6},{5,7},{6,4},{7,5},{8,10},{9,11},{10,... | collective-permute-start | bytes 442376 | tf_op jit(solution)/shard_map/ppermute | solution.py:59
  67.5 13.7 %collective-permute-start.19 = (bf16[32,2304]{1,0:T(8,128)(2,1)S(1)}, bf16[32,2304]{1,0:T(8,128)(2,1)S(1)}, u32[]{:S(2)}, u32[]{:S(2)}) collective-permute-start(bf16[32,2304]{1,0:T(8,128)(2,1)S(1)} %get-tuple-element.46.refs_4_), channel_id=1, source_target_pairs={{0,3},{1,2},{2,1},{3,0},{4,7},{5,6},{6,5},{7,4},{8,11},{9,10},{10,... | collective-permute-start | bytes 442376 | tf_op jit(solution)/shard_map/ppermute | solution.py:59
  69.9 12.6 %collective-permute-start.23 = (bf16[128,512]{1,0:T(8,128)(2,1)S(1)}, bf16[128,512]{1,0:T(8,128)(2,1)S(1)}, u32[]{:S(2)}, u32[]{:S(2)}) collective-permute-start(bf16[128,512]{1,0:T(8,128)(2,1)S(1)} %shard_map.127.refs_3_), channel_id=1, source_target_pairs={{0,4},{4,8},{8,12},{12,16},{16,20},{20,24},{24,28},{1,5},{5,9},{9,... | collective-permute-start | bytes 393224 | tf_op jit(solution)/shard_map/ppermute | solution.py:65
  71.2 12.8 %collective-permute-start.24 = (bf16[128,512]{1,0:T(8,128)(2,1)S(1)}, bf16[128,512]{1,0:T(8,128)(2,1)S(1)}, u32[]{:S(2)}, u32[]{:S(2)}) collective-permute-start(bf16[128,512]{1,0:T(8,128)(2,1)S(1)} %shard_map.127.refs_3_), channel_id=1, source_target_pairs={{0,8},{4,12},{8,16},{12,20},{16,24},{20,28},{1,9},{5,13},{9,17},{1... | collective-permute-start | bytes 393224 | tf_op jit(solution)/shard_map/ppermute | solution.py:65
  74.2 12.9 %collective-permute-start.25 = (bf16[128,512]{1,0:T(8,128)(2,1)S(1)}, bf16[128,512]{1,0:T(8,128)(2,1)S(1)}, u32[]{:S(2)}, u32[]{:S(2)}) collective-permute-start(bf16[128,512]{1,0:T(8,128)(2,1)S(1)} %shard_map.127.refs_3_), channel_id=1, source_target_pairs={{0,12},{4,16},{8,20},{12,24},{16,28},{1,13},{5,17},{9,21},{13,25},... | collective-permute-start | bytes 393224 | tf_op jit(solution)/shard_map/ppermute | solution.py:65
  78.7 8.4 %collective-permute-start.26 = (bf16[128,512]{1,0:T(8,128)(2,1)S(1)}, bf16[128,512]{1,0:T(8,128)(2,1)S(1)}, u32[]{:S(2)}, u32[]{:S(2)}) collective-permute-start(bf16[128,512]{1,0:T(8,128)(2,1)S(1)} %shard_map.127.refs_3_), channel_id=1, source_target_pairs={{0,16},{4,20},{8,24},{12,28},{1,17},{5,21},{9,25},{13,29},{2,18},{... | collective-permute-start | bytes 393224 | tf_op jit(solution)/shard_map/ppermute | solution.py:65
  81.1 5.9 %collective-permute-start.27 = (bf16[128,512]{1,0:T(8,128)(2,1)S(1)}, bf16[128,512]{1,0:T(8,128)(2,1)S(1)}, u32[]{:S(2)}, u32[]{:S(2)}) collective-permute-start(bf16[128,512]{1,0:T(8,128)(2,1)S(1)} %shard_map.127.refs_3_), channel_id=1, source_target_pairs={{0,20},{4,24},{8,28},{1,21},{5,25},{9,29},{2,22},{6,26},{10,30},{3... | collective-permute-start | bytes 393224 | tf_op jit(solution)/shard_map/ppermute | solution.py:65
  82.5 4.9 %collective-permute-start.28 = (bf16[128,512]{1,0:T(8,128)(2,1)S(1)}, bf16[128,512]{1,0:T(8,128)(2,1)S(1)}, u32[]{:S(2)}, u32[]{:S(2)}) collective-permute-start(bf16[128,512]{1,0:T(8,128)(2,1)S(1)} %shard_map.127.refs_3_), channel_id=1, source_target_pairs={{0,24},{4,28},{1,25},{5,29},{2,26},{6,30},{3,27},{7,31}} | collective-permute-start | bytes 393224 | tf_op jit(solution)/shard_map/ppermute | solution.py:65
  84.0 4.8 %collective-permute-start.29 = (bf16[128,512]{1,0:T(8,128)(2,1)S(1)}, bf16[128,512]{1,0:T(8,128)(2,1)S(1)}, u32[]{:S(2)}, u32[]{:S(2)}) collective-permute-start(bf16[128,512]{1,0:T(8,128)(2,1)S(1)} %shard_map.127.refs_3_), channel_id=1, source_target_pairs={{0,28},{1,29},{2,30},{3,31}} | collective-permute-start | bytes 393224 | tf_op jit(solution)/shard_map/ppermute | solution.py:65

commit v2 on v1

v2 whole, which is shorter than its diff:
```python
import functools

import jax
import jax.numpy as jnp
from jax import lax
from jax.experimental import pallas as pl
from jax.experimental.pallas import tpu as pltpu
from jax.sharding import PartitionSpec as P

DK = 128
CONV = 4
DH = 128
HALO = 16
EXTRA = 16
MIB = 1 << 20

eps_norm = 1e-06
bf16 = jnp.bfloat16
f32 = jnp.float32
VMEM = pl.BlockSpec(memory_space=pltpu.VMEM)
SMEM = pl.BlockSpec(memory_space=pltpu.SMEM)
HBM = pl.BlockSpec(memory_space=pltpu.HBM)


def mm(left, right):
    return jnp.dot(left.astype(bf16), right.astype(bf16), preferred_element_type=f32)


def mm_nt(left, right):
    return lax.dot_general(
        left.astype(bf16), right.astype(bf16), (((1,), (1,)), ((), ())), preferred_element_type=f32
    )


def mm_tn(left, right):
    return lax.dot_general(
        left.astype(bf16), right.astype(bf16), (((0,), (0,)), ((), ())), preferred_element_type=f32
    )


def call(kernel, outs, args, scratch=(), limit=32, stored=(), copies=0, cost=1.0):
    scratch_shapes = [pltpu.VMEM(shape, dtype) for shape, dtype in scratch]
    if copies:
        scratch_shapes.append(pltpu.SemaphoreType.DMA((copies,)))
    return pl.pallas_call(
        kernel,
        out_shape=[jax.ShapeDtypeStruct(shape, dtype) for shape, dtype in outs],
        in_specs=[
            HBM if i in stored else SMEM if a.dtype == jnp.int32 else VMEM
            for i, a in enumerate(args)
        ],
        out_specs=[VMEM for _ in outs],
        scratch_shapes=scratch_shapes,
        compiler_params=pltpu.CompilerParams(vmem_limit_bytes=limit * MIB),
        cost_estimate=pl.CostEstimate(flops=int(cost * 1e9), bytes_accessed=0, transcendentals=0),
    )(*args)


def partner(index, step, size):
    return index ^ step if size & (size - 1) == 0 else (size + step - index) % size


def trade(block, axis, step, size):
    route = []
    for i in range(lax.axis_size(axis)):
        base = i // size * size
        route.append((i, base + partner(i - base, step, size)))
    return lax.ppermute(block, axis, route)


def passed_along(block, axis, distance):
    count = lax.axis_size(axis)
    return lax.ppermute(block, axis, [(i, (i + distance) % count) for i in range(count)])


def lanes(block_index, width=128):
    return pl.ds(pl.multiple_of(block_index * width, width), width)


def split_cores(place):
    return place[0] // 2, place[0] % 2


def load_kernel(stored_inputs, stored_gate, stored_taps, inputs, log, taps, gate, sems):
    moves = [
        pltpu.make_async_copy(stored_gate, gate, sems.at[0]),
        pltpu.make_async_copy(stored_inputs, inputs, sems.at[1]),
        pltpu.make_async_copy(stored_taps, taps, sems.at[2]),
    ]
    for move in moves:
        move.start()
    length = gate.shape[0]
    rows = lax.broadcasted_iota(jnp.int32, (length, length), 0)
    cols = lax.broadcasted_iota(jnp.int32, (length, length), 1)
    tril = (rows >= cols).astype(bf16)
    moves[0].wait()
    high = gate[...].astype(bf16)
    low = gate[...] - high.astype(f32)
    log[...] = mm(tril, high) + mm(tril, low)
    moves[1].wait()
    moves[2].wait()


def local_kernel(heads, *refs):
    place, inputs, halo, logs, beta, taps = refs[:6]
    kept, sent, reads, intra = refs[6:10]
    wide, maps = refs[10:]
    length = logs.shape[0]
    pad = wide.shape[1] - length
    before = halo[:, halo.shape[1] - pad :, :].astype(f32)
    wide[:, :pad, :] = jnp.where(place[2] == 0, 0.0, before)
    wide[:, pad:, :] = inputs[...].astype(f32)

    rows = lax.broadcasted_iota(jnp.int32, (length, length), 0)
    cols = lax.broadcasted_iota(jnp.int32, (length, length), 1)
    eye = (rows == cols).astype(f32)
    half = length // 2
    chunks = range(heads)

    def convolved(part, i):
        own = slice(i * DK, (i + 1) * DK)
        total = jnp.zeros((length, DK), f32)
        for tap in range(CONV):
            first = pad - (CONV - 1) + tap
            total = total + taps[part, tap : tap + 1, own] * wide[part, first : first + length, own]
        return total / (1.0 + jnp.exp(-total))

    def unit(value):
        return value * lax.rsqrt(jnp.sum(value * value, axis=-1, keepdims=True) + eps_norm)

    coupling, mixing, right, finals, queries_grown, decay = [], [], [], [], [], []
    for i in chunks:
        own_head = slice(i * DK, (i + 1) * DK)
        query = (unit(convolved(0, i)) * DK ** (-0.5)).astype(bf16).astype(f32)
        key = unit(convolved(1, i)).astype(bf16).astype(f32)
        value = convolved(2, i).astype(bf16)
        log = logs[:, own_head]
        rate_row = beta[i : i + 1, :]
        rate_column = jnp.sum(rate_row * eye, axis=1, keepdims=True)
        last = log[length - 1 :]
        kept_parts, mixed_parts = [], []
        for b in range(2):
            own = slice(b * half, (b + 1) * half)
            middle = log[b * half + half // 2 : b * half + half // 2 + 1]
            row_scale = jnp.exp(log[own] - middle)
            shrunk = key * jnp.exp(jnp.minimum(middle - log, 75.0))
            both = jnp.concatenate([query[own] * row_scale, key[own] * row_scale], axis=0)
            product = mm_nt(both, shrunk)
            mixed_parts.append(product[:half])
            kept_parts.append(product[half:])
        coupling.append(
            jnp.where(rows > cols, jnp.concatenate(kept_parts, axis=0) * rate_row, 0.0).astype(bf16)
        )
        mixing.append(
            jnp.where(rows >= cols, jnp.concatenate(mixed_parts, axis=0) * rate_row, 0.0).astype(
                bf16
            )
        )
        growth = jnp.exp(log)
        queries_grown.append(query * growth)
        right.append(jnp.concatenate([value, (key * growth).astype(bf16)], axis=1))
        finals.append((key * jnp.exp(last - log) * rate_column).astype(bf16))
        decay.append(jnp.exp(last))

    size = 1
    inverse = None
    while size < length:
        corner = (
            (rows // (2 * size) == cols // (2 * size))
            & ((rows // size) % 2 == 1)
            & ((cols // size) % 2 == 0)
        )
        corners = [jnp.where(corner, coupling[i], jnp.zeros_like(coupling[i])) for i in chunks]
        if inverse is None:
            inverse = [eye - corners[i].astype(f32) for i in chunks]
        else:
            short = [inverse[i].astype(bf16) for i in chunks]
            below = [mm(corners[i], short[i]) for i in chunks]
            inverse = [inverse[i] - mm(short[i], below[i]) for i in chunks]
        size *= 2

    short = [inverse[i].astype(bf16) for i in chunks]
    first = [mm(short[i], right[i]).astype(bf16) for i in chunks]
    left = [right[i].astype(f32) - first[i].astype(f32) - mm(coupling[i], first[i]) for i in chunks]
    solved = [(first[i].astype(f32) + mm(short[i], left[i])).astype(bf16) for i in chunks]

    for i in chunks:
        own_head = slice(i * DK, (i + 1) * DK)
        maps[i, : 2 * DK, :] = mm_tn(solved[i], finals[i]).astype(bf16)
        high = decay[i].astype(bf16)
        low = (decay[i] - high.astype(f32)).astype(bf16)
        maps[i, 2 * DK :, :] = jnp.concatenate(
            [jnp.broadcast_to(high, (EXTRA // 2, DK)), jnp.broadcast_to(low, (EXTRA // 2, DK))],
            axis=0,
        )
        mixes = mm(mixing[i], solved[i])
        intra[:, own_head] = mixes[:, :DK]
        reads[:, own_head] = (queries_grown[i] - mixes[:, DK:]).astype(bf16)
    _, core = split_cores(place)
    for pair in range(heads // 2):
        kept[pair] = maps[2 * pair + core]
        sent[pair] = maps[2 * pair + 1 - core]


def parts_of(state_map):
    extra = state_map[2 * DK :].astype(f32)
    decay = extra[:1] + extra[EXTRA // 2 : EXTRA // 2 + 1]
    return state_map[:DK], state_map[DK : 2 * DK], decay


def compose_kernel(pairs, place, kept, got, *refs):
    outs, (maps,) = refs[:pairs], refs[pairs:]
    chip, core = split_cores(place)
    eye = (
        lax.broadcasted_iota(jnp.int32, (DK, DK), 0) == lax.broadcasted_iota(jnp.int32, (DK, DK), 1)
    ).astype(f32)
    for pair in range(pairs):
        mine, other = kept[pair], got[pair]
        offset_a, move_a, decay_a = parts_of(jnp.where(core == 0, mine, other))
        offset_b, move_b, decay_b = parts_of(jnp.where(core == 0, other, mine))
        product = mm(jnp.concatenate([offset_a, move_a], axis=0), move_b)
        column = jnp.sum(eye * decay_a, axis=1, keepdims=True)
        maps[pair, :DK, :] = (
            offset_a.astype(f32) * decay_b - product[:DK] + offset_b.astype(f32)
        ).astype(bf16)
        maps[pair, DK : 2 * DK, :] = (
            move_a.astype(f32) * decay_b + column * move_b.astype(f32) - product[DK:]
        ).astype(bf16)
        decay = decay_a * decay_b
        high = decay.astype(bf16)
        low = (decay - high.astype(f32)).astype(bf16)
        maps[pair, 2 * DK :, :] = jnp.concatenate(
            [jnp.broadcast_to(high, (EXTRA // 2, DK)), jnp.broadcast_to(low, (EXTRA // 2, DK))],
            axis=0,
        )
    for step in range(pairs):
        outs[step][...] = maps[partner(chip, step, pairs)]


def apply_map(state, state_map):
    offset, move, decay = parts_of(state_map)
    return state.astype(f32) * decay - mm(state, move) + offset.astype(f32)


def scan_kernel(pairs, grouped, *refs):
    place, blocks, rest = refs[0], refs[1 : 1 + pairs], refs[1 + pairs :]
    if grouped:
        start, rest = rest[0], rest[1:]
    outs, rest = rest[:pairs], rest[pairs:]
    if grouped:
        final, rest = rest[0], rest[1:]
    maps, starts = rest
    chip, _ = split_cores(place)
    for step in range(pairs):
        maps[partner(chip, step, pairs)] = blocks[step][...]
    state = start[...] if grouped else jnp.zeros((DK, DK), f32)
    for i in range(pairs):
        starts[i] = state.astype(bf16)
        if i < pairs - 1 or grouped:
            if i == 0 and not grouped:
                state = maps[i, :DK, :].astype(f32)
            else:
                state = apply_map(state, maps[i])
    if grouped:
        final[...] = state
    for step in range(pairs):
        outs[step][...] = starts[partner(chip, step, pairs)]


def share_kernel(pairs, place, kept, got, *refs):
    starts, (mine, other) = refs[:pairs], refs[pairs:]
    chip, core = split_cores(place)
    for step in range(pairs):
        pair = partner(chip, step, pairs)
        state = starts[step][...]
        later = apply_map(state, jnp.where(core == 0, kept[pair], got[pair])).astype(bf16)
        mine[pair] = jnp.where(core == 0, state, later)
        other[pair] = jnp.where(core == 0, later, state)


def project_kernel(parts, *refs):
    place, residual, weight, reads, intra, mine, other = refs[:7]
    outs = refs[7 : 7 + parts]
    whole, summed = refs[7 + parts :]
    _, core = split_cores(place)
    head_me = place[1]
    for pair in range(mine.shape[0]):
        for states, head in ((mine, 2 * pair + core), (other, 2 * pair + 1 - core)):
            own = lanes(head)
            whole[:, own] = (intra[:, own] + mm_nt(reads[:, own], states[pair])).astype(bf16)
    summed[...] = jnp.dot(whole[...], weight[...], preferred_element_type=f32)
    share = summed.shape[0] // parts
    for step in range(parts):
        at = pl.ds(pl.multiple_of(partner(head_me, step, parts) * share, share), share)
        if step == 0:
            outs[0][...] = summed[at, :] + residual[at, :].astype(f32)
        else:
            outs[step][...] = summed[at, :].astype(bf16)


def normalized(values, gain):
    return values * lax.rsqrt(jnp.mean(values * values, axis=-1, keepdims=True) + eps_norm) * gain


def latent_kernel(parts, *refs):
    gain, latent_weight, latent_gain = refs[:3]
    partials = refs[3 : 3 + parts]
    stream, latent = refs[3 + parts :]
    total = partials[0][...]
    for step in range(1, parts):
        total = total + partials[step][...].astype(f32)
    short = total.astype(bf16)
    stream[...] = short
    normed = normalized(short.astype(f32), gain[...]).astype(bf16)
    before = jnp.dot(normed, latent_weight[...], preferred_element_type=f32)
    latent[...] = normalized(before, latent_gain[...]).astype(bf16)


def join_kernel(parts, *refs):
    place = refs[0]
    pieces = refs[1 : 1 + parts]
    out = refs[1 + parts]
    share = out.shape[0] // parts
    for step in range(parts):
        at = pl.ds(pl.multiple_of(partner(place[1], step, parts) * share, share), share)
        out[at, :] = pieces[step][...]


def query_kernel(parts, *refs):
    place, gain, query_weight, up = refs[:4]
    pieces = refs[4 : 4 + parts]
    stream, absorbed = refs[4 + parts :]
    length = stream.shape[0]
    share = length // parts
    for step in range(parts):
        at = pl.ds(pl.multiple_of(partner(place[1], step, parts) * share, share), share)
        stream[at, :] = pieces[step][...]
    normed = normalized(stream[...].astype(f32), gain[...]).astype(bf16)
    query = jnp.dot(normed, query_weight[...], preferred_element_type=f32).astype(bf16)
    for head in range(query.shape[1] // DH):
        own = slice(head * DH, (head + 1) * DH)
        absorbed[head * length : (head + 1) * length, :] = (
            mm_nt(query[:, own], up[:, own]) * DH ** (-0.5)
        ).astype(bf16)


def attend_kernel(order, *refs):
    place, absorbed, up = refs[:3]
    latents = refs[3 : 3 + len(order)]
    out, scores, mixed = refs[3 + len(order) :]
    length = latents[0].shape[0]
    heads = absorbed.shape[0] // length
    me = place[2]
    rows = lax.broadcasted_iota(jnp.int32, (length, length), 0)
    cols = lax.broadcasted_iota(jnp.int32, (length, length), 1)
    causal = jnp.concatenate([rows >= cols] * heads, axis=0)
    peak = None
    for place_in, distance in enumerate(order):
        part = mm_nt(absorbed[...], latents[place_in][...])
        allowed = causal if distance == 0 else (me ^ distance) < me
        part = jnp.where(allowed, part, -1e30)
        scores[:, place_in * length : (place_in + 1) * length] = part
        top = jnp.max(part, axis=-1, keepdims=True)
        peak = top if peak is None else jnp.maximum(peak, top)
    total = None
    for place_in in range(len(order)):
        weights = jnp.exp(scores[:, place_in * length : (place_in + 1) * length] - peak)
        added = jnp.sum(weights, axis=-1, keepdims=True)
        share = mm(weights, latents[place_in][...])
        if total is None:
            total = added
            mixed[...] = share
        else:
            total = total + added
            mixed[...] += share
    for head in range(heads):
        own = slice(head * length, (head + 1) * length)
        value = slice((heads + head) * DH, (heads + head + 1) * DH)
        spread = (mixed[own, :] / total[own, :]).astype(bf16)
        out[:, head * DH : (head + 1) * DH] = jnp.dot(
            spread, up[:, value], preferred_element_type=f32
        ).astype(bf16)


def far_first(count):
    return sorted(range(1, count), key=lambda step: (-bin(step).count("1"), -step))


def per_device(
    kda_inputs,
    gate_log,
    beta,
    conv_weight,
    kda_out_weight,
    residual,
    norm_gain,
    latent_weight,
    latent_gain,
    query_weight,
    up_weight,
):
    length, width = residual.shape
    heads = beta.shape[1]
    pairs = heads // 2
    count, parts = lax.axis_size("ctx"), lax.axis_size("head")
    groups = count // heads
    ctx_me = lax.axis_index("ctx").astype(jnp.int32)
    place = jnp.stack([ctx_me % heads, lax.axis_index("head").astype(jnp.int32), ctx_me])

    halo = passed_along(kda_inputs[:, length - HALO :, :], "ctx", 1)
    inputs, logs, taps = call(
        load_kernel,
        [(kda_inputs.shape, bf16), (gate_log.shape, f32), (conv_weight.shape, f32)],
        [kda_inputs, gate_log, conv_weight],
        [(gate_log.shape, f32)],
        24,
        stored=(0, 1, 2),
        copies=3,
    )
    map_shape = (2 * DK + EXTRA, DK)
    kept, sent, reads, intra = call(
        functools.partial(local_kernel, heads),
        [
            ((pairs,) + map_shape, bf16),
            ((pairs,) + map_shape, bf16),
            ((length, heads * DK), bf16),
            ((length, heads * DK), f32),
        ],
        [place, inputs, halo, logs, beta.T, taps],
        [((3, length + 8, heads * DK), f32), ((heads,) + map_shape, bf16)],
        16,
        cost=6.0,
    )

    got = trade(sent, "ctx", 1, heads)
    chip_maps = call(
        functools.partial(compose_kernel, pairs),
        [(map_shape, bf16)] * pairs,
        [place, kept, got],
        [((pairs,) + map_shape, bf16)],
        8,
    )

    def across_chips(pieces):
        moved = {step: trade(pieces[step], "ctx", 2 * step, heads) for step in far_first(pairs)}
        return [pieces[0]] + [moved[step] for step in range(1, pairs)]

    chip_maps = across_chips(chip_maps)
    state_outs = [((DK, DK), bf16)] * pairs
    scratch = [((pairs,) + map_shape, bf16), ((pairs, DK, DK), bf16)]
    if groups == 1:
        starts = call(
            functools.partial(scan_kernel, pairs, False), state_outs, [place] + chip_maps, scratch, 8
        )
    else:

        def run(start):
            return call(
                functools.partial(scan_kernel, pairs, True),
                state_outs + [((DK, DK), f32)],
                [place] + chip_maps + [start],
                scratch,
                8,
            )

        def relay(step_index, start):
            arrived = passed_along(run(start)[pairs], "ctx", heads)
            return jnp.where(ctx_me < heads, 0.0, arrived)

        start = lax.fori_loop(0, groups - 1, relay, jnp.zeros((DK, DK), f32))
        starts = run(start)[:pairs]
    starts = across_chips(starts)
    mine, other = call(
        functools.partial(share_kernel, pairs),
        [((pairs, DK, DK), bf16)] * 2,
        [place, kept, got] + starts,
        limit=8,
    )
    other = trade(other, "ctx", 1, heads)

    share = length // parts
    partials = call(
        functools.partial(project_kernel, parts),
        [((share, width), f32)] + [((share, width), bf16)] * (parts - 1),
        [place, residual, kda_out_weight, reads, intra, mine, other],
        [((length, heads * DK), bf16), ((length, width), f32)],
        16,
    )

    def across_heads(pieces):
        moved = {step: trade(pieces[step], "head", step, parts) for step in far_first(parts)}
        return [pieces[0]] + [moved[step] for step in range(1, parts)]

    partials = across_heads(partials)
    stream_rows, latent_rows = call(
        functools.partial(latent_kernel, parts),
        [((share, width), bf16), ((share, latent_weight.shape[1]), bf16)],
        [norm_gain[None], latent_weight, latent_gain[None]] + partials,
        limit=16,
    )
    latent_parts = across_heads([latent_rows] * parts)
    stream_parts = across_heads([stream_rows] * parts)
    latent = call(
        functools.partial(join_kernel, parts),
        [((length, latent_weight.shape[1]), bf16)],
        [place] + latent_parts,
        limit=8,
    )[0]

    order, latents = [0], [latent]
    for step in far_first(count // 2):
        order.append(2 * step)
        latents.append(trade(latent, "ctx", 2 * step, count))
    for position in range(len(order)):
        order.append(order[position] + 1)
        latents.append(trade(latents[position], "ctx", 1, 2))
    up = up_weight.reshape(up_weight.shape[0], -1)
    heads_mla = query_weight.shape[1] // DH
    stream_out, absorbed = call(
        functools.partial(query_kernel, parts),
        [((length, width), bf16), ((heads_mla * length, up.shape[0]), bf16)],
        [place, norm_gain[None], query_weight, up] + stream_parts,
        limit=16,
    )
    attention_out = call(
        functools.partial(attend_kernel, tuple(order)),
        [((length, heads_mla * DH), bf16)],
        [place, absorbed, up] + latents,
        [
            ((heads_mla * length, count * length), f32),
            ((heads_mla * length, up.shape[0]), f32),
        ],
        12 + count * length * heads_mla * length * 8 // MIB,
    )[0]
    return (stream_out, attention_out)


def solution(mesh):
    in_specs = (
        P(None, "ctx", "head"),
        P("ctx", "head"),
        P("ctx", "head"),
        P(None, None, "head"),
        P("head", None),
        P("ctx", None),
        P(),
        P(),
        P(),
        P(None, "head"),
        P(None, None, "head"),
    )
    out_specs = (P("ctx", None), P("ctx", "head"))
    return jax.shard_map(
        per_device, mesh=mesh, in_specs=in_specs, out_specs=out_specs, check_vma=False
    )
```

time: 93.7 us -> 80.4 us (0.86)
  starting transfers between devices: 44.5 us -> 28.2 us
  waiting for transfers between devices: 26.5 us -> 29.6 us
  Pallas kernels: 15.2 us -> 17.2 us
  local copies, waits for them, and re-layouts: 5.59 us -> 4.17 us
    ppermute x7 -> x1, starting transfers between devices: 14.4 us -> 0.45 us  [passed_along(): lax.ppermute(block, axis, [(i, (i + distance) % count) for i in range(cou...]
    ppermute x23 -> x24, waiting for transfers between devices: 24.8 us -> 28 us  [trade(): return lax.ppermute(block, axis, route)]
    unnamed x22 -> x25, local copies, waits for them, and re-layouts: 5.58 us -> 3.26 us
    ppermute x23 -> x24, starting transfers between devices: 30 us -> 27.7 us  [trade(): return lax.ppermute(block, axis, route)]
    pallas_call x7 -> x10, Pallas kernels: 15.2 us -> 17.2 us  [call(): pl.pallas_call(kernel, out_shape=[jax.ShapeDtypeStruct(shape, dtype) for...]
  transfers between devices with their start and end apart: 30 -> 25, of which waited for: 11 -> 15; matrix products, arithmetic and copies ran while one was open for 0% -> 0% of each run, Pallas kernels for 2% -> 3%
where the time goes in v2:
time: 80.4 us; the launch traced here: 80.1 us
  waiting for transfers between devices  29.6 us (37%)
  starting transfers between devices  28.2 us (35%)
  Pallas kernels  17.2 us (21%)
  local copies, waits for them, and re-layouts  4.17 us (5%)
  between operations  0.84 us (1%)
    ppermute x24, waiting for transfers between devices, trade(): return lax.ppermute(block, axis, route)  28 us
    ppermute x24, starting transfers between devices, trade(): return lax.ppermute(block, axis, route)  27.7 us
    pallas_call x10, Pallas kernels, call(): pl.pallas_call(kernel, out_shape=[jax.ShapeDtypeStruct(shape, dtype) for...  17.2 us
    unnamed x25, local copies, waits for them, and re-layouts  3.26 us
    ppermute x1, waiting for transfers between devices, passed_along(): lax.ppermute(block, axis, [(i, (i + distance) % count) for i in range(cou...  1.64 us
  transfers between devices with their start and end apart: 25, of which 15 were waited for; matrix products, arithmetic and copies ran while one was open for 0% of the time, Pallas kernels for 3%

profile of v2, /device:TPU:0, one launch (start us, length us, event | category | flops | bytes accessed | tf_op | source)
XLA Modules:
  0.0 80.1 jit_solution(17890755222139717321)
XLA Ops:
  0.6 0.9 %slice.3 = bf16[3,16,1024]{2,1,0:T(8,128)(2,1)S(1)} slice(bf16[3,128,1024]{2,1,0:T(8,128)(2,1)} %stored_inputs.1), slice={[0:3], [112:128], [0:1024]} | slice | bytes 196608 | tf_op jit(solution)/shard_map/slice | solution.py:410
  1.5 0.5 collective-permute-start
  2.1 1.1 %copy-done.2 = bf16[3,128,1024]{2,1,0:T(8,128)(2,1)S(1)} copy-done((bf16[3,128,1024]{2,1,0:T(8,128)(2,1)S(1)}, bf16[3,128,1024]{2,1,0:T(8,128)(2,1)}, u32[]{:S(2)}) %copy-start.2) | copy-done | bytes 786456
  3.2 1.0 %copy-done.4 = f32[128,1024]{1,0:T(8,128)S(1)} copy-done((f32[128,1024]{1,0:T(8,128)S(1)}, f32[128,1024]{1,0:T(8,128)}, u32[]{:S(2)}) %copy-start.4) | copy-done | bytes 524312
  4.3 0.8 copy-done.5
  5.1 0.5 shard_map.122
  5.5 1.6 %collective-permute-done.refs_2_ = bf16[3,16,1024]{2,1,0:T(8,128)(2,1)S(1)} collective-permute-done((bf16[3,16,1024]{2,1,0:T(8,128)(2,1)S(1)}, bf16[3,16,1024]{2,1,0:T(8,128)(2,1)S(1)}, u32[]{:S(2)}, u32[]{:S(2)}) %collective-permute-start) | collective-permute-done | bytes 98336 | tf_op jit(solution)/shard_map/ppermute | solution.py:73
  7.2 5.8 %shard_map.123 = (bf16[4,272,128]{2,1,0:T(8,128)(2,1)S(1)}, bf16[4,272,128]{2,1,0:T(8,128)(2,1)S(1)}, bf16[128,1024]{1,0:T(8,128)(2,1)S(1)}, f32[128,1024]{1,0:T(8,128)S(1)}) custom-call(s32[3]{0:T(128)S(1)} %pad_add_fusion.refs_0_.place, bf16[3,128,1024]{2,1,0:T(8,128)(2,1)S(1)} %get-tuple-element.27.refs_1_, ...), custom_call_target="tpu_custom_call" | custom-call | flops 6000000000 | tf_op jit(solution)/shard_map/pallas_call | solution.py:45
  13.0 1.1 %collective-permute-start.1 = (bf16[4,272,128]{2,1,0:T(8,128)(2,1)S(1)}, bf16[4,272,128]{2,1,0:T(8,128)(2,1)S(1)}, u32[]{:S(2)}, u32[]{:S(2)}) collective-permute-start(bf16[4,272,128]{2,1,0:T(8,128)(2,1)S(1)} %get-tuple-element.33), channel_id=1, source_target_pairs={{0,4},{4,0},{8,12},{12,8},{16,20},{20,16},{24,28},{28,24},{1,5},{5... | collective-permute-start | bytes 835592 | tf_op jit(solution)/shard_map/ppermute | solution.py:68
  14.1 1.2 %collective-permute-done.1.got = bf16[4,272,128]{2,1,0:T(8,128)(2,1)S(1)} collective-permute-done((bf16[4,272,128]{2,1,0:T(8,128)(2,1)S(1)}, bf16[4,272,128]{2,1,0:T(8,128)(2,1)S(1)}, u32[]{:S(2)}, u32[]{:S(2)}) %collective-permute-start.1) | collective-permute-done | bytes 278560 | tf_op jit(solution)/shard_map/ppermute | solution.py:68
  15.3 0.8 %shard_map.124 = (bf16[272,128]{1,0:T(8,128)(2,1)S(1)}, bf16[272,128]{1,0:T(8,128)(2,1)S(1)}, bf16[272,128]{1,0:T(8,128)(2,1)S(1)}, bf16[272,128]{1,0:T(8,128)(2,1)S(1)}) custom-call(s32[3]{0:T(128)S(1)} %pad_add_fusion.refs_0_.place, bf16[4,272,128]{2,1,0:T(8,128)(2,1)S(1)} %get-tuple-element.32.kept, bf16[4,272,128]{2,1,0:T(8,128)(2,1)S(1)} %collective-permute-done.1.got), custom_call_target="tpu_custom_call" | custom-call | flops 1000000000 | tf_op jit(solution)/shard_map/pallas_call | solution.py:45
  16.1 1.6 %collective-permute-start.2 = (bf16[272,128]{1,0:T(8,128)(2,1)S(1)}, bf16[272,128]{1,0:T(8,128)(2,1)S(1)}, u32[]{:S(2)}, u32[]{:S(2)}) collective-permute-start(bf16[272,128]{1,0:T(8,128)(2,1)S(1)} %get-tuple-element.35), channel_id=1, source_target_pairs={{0,8},{4,12},{8,0},{12,4},{16,24},{20,28},{24,16},{28,20},{1,9},{5... | collective-permute-start | bytes 208904 | tf_op jit(solution)/shard_map/ppermute | solution.py:68
  17.7 0.7 collective-permute-start.3
  18.4 1.3 %collective-permute-start.4 = (bf16[272,128]{1,0:T(8,128)(2,1)S(1)}, bf16[272,128]{1,0:T(8,128)(2,1)S(1)}, u32[]{:S(2)}, u32[]{:S(2)}) collective-permute-start(bf16[272,128]{1,0:T(8,128)(2,1)S(1)} %get-tuple-element.37), channel_id=1, source_target_pairs={{0,24},{4,28},{8,16},{12,20},{16,8},{20,12},{24,0},{28,4},{1,25},{... | collective-permute-start | bytes 208904 | tf_op jit(solution)/shard_map/ppermute | solution.py:68
  19.7 1.0 %collective-permute-done.2.refs_2_ = bf16[272,128]{1,0:T(8,128)(2,1)S(1)} collective-permute-done((bf16[272,128]{1,0:T(8,128)(2,1)S(1)}, bf16[272,128]{1,0:T(8,128)(2,1)S(1)}, u32[]{:S(2)}, u32[]{:S(2)}) %collective-permute-start.2) | collective-permute-done | bytes 69664 | tf_op jit(solution)/shard_map/ppermute | solution.py:68
  20.6 2.1 %collective-permute-done.3.refs_3_ = bf16[272,128]{1,0:T(8,128)(2,1)S(1)} collective-permute-done((bf16[272,128]{1,0:T(8,128)(2,1)S(1)}, bf16[272,128]{1,0:T(8,128)(2,1)S(1)}, u32[]{:S(2)}, u32[]{:S(2)}) %collective-permute-start.3) | collective-permute-done | bytes 69664 | tf_op jit(solution)/shard_map/ppermute | solution.py:68
  22.8 0.9 %collective-permute-done.4.refs_4_ = bf16[272,128]{1,0:T(8,128)(2,1)S(1)} collective-permute-done((bf16[272,128]{1,0:T(8,128)(2,1)S(1)}, bf16[272,128]{1,0:T(8,128)(2,1)S(1)}, u32[]{:S(2)}, u32[]{:S(2)}) %collective-permute-start.4) | collective-permute-done | bytes 69664 | tf_op jit(solution)/shard_map/ppermute | solution.py:68
  23.6 0.8 %shard_map.125 = (bf16[128,128]{1,0:T(8,128)(2,1)S(1)}, bf16[128,128]{1,0:T(8,128)(2,1)S(1)}, bf16[128,128]{1,0:T(8,128)(2,1)S(1)}, bf16[128,128]{1,0:T(8,128)(2,1)S(1)}) custom-call(s32[3]{0:T(128)S(1)} %pad_add_fusion.refs_0_.place, bf16[272,128]{1,0:T(8,128)(2,1)S(1)} %get-tuple-element.34.refs_1_, bf16[272,128]{1,0:T(8,128)(2,1)S(1)} %collective-permute-done.2.refs_2_, ...), custom_call_target="tpu_custom_call" | custom-call | flops 1000000000 | tf_op jit(solution)/shard_map/pallas_call | solution.py:45
  24.5 1.5 %collective-permute-start.5 = (bf16[128,128]{1,0:T(8,128)(2,1)S(1)}, bf16[128,128]{1,0:T(8,128)(2,1)S(1)}, u32[]{:S(2)}, u32[]{:S(2)}) collective-permute-start(bf16[128,128]{1,0:T(8,128)(2,1)S(1)} %get-tuple-element.39), channel_id=1, source_target_pairs={{0,8},{4,12},{8,0},{12,4},{16,24},{20,28},{24,16},{28,20},{1,9},{5... | collective-permute-start | bytes 98312 | tf_op jit(solution)/shard_map/ppermute | solution.py:68
  26.0 0.6 collective-permute-start.6
  26.6 1.5 %collective-permute-start.7 = (bf16[128,128]{1,0:T(8,128)(2,1)S(1)}, bf16[128,128]{1,0:T(8,128)(2,1)S(1)}, u32[]{:S(2)}, u32[]{:S(2)}) collective-permute-start(bf16[128,128]{1,0:T(8,128)(2,1)S(1)} %get-tuple-element.41), channel_id=1, source_target_pairs={{0,24},{4,28},{8,16},{12,20},{16,8},{20,12},{24,0},{28,4},{1,25},{... | collective-permute-start | bytes 98312 | tf_op jit(solution)/shard_map/ppermute | solution.py:68
  28.1 0.7 collective-permute-done.5.refs_1_
  28.7 1.2 %collective-permute-done.6.refs_2_ = bf16[128,128]{1,0:T(8,128)(2,1)S(1)} collective-permute-done((bf16[128,128]{1,0:T(8,128)(2,1)S(1)}, bf16[128,128]{1,0:T(8,128)(2,1)S(1)}, u32[]{:S(2)}, u32[]{:S(2)}) %collective-permute-start.6) | collective-permute-done | bytes 32800 | tf_op jit(solution)/shard_map/ppermute | solution.py:68
  29.9 1.5 %collective-permute-done.7.refs_3_ = bf16[128,128]{1,0:T(8,128)(2,1)S(1)} collective-permute-done((bf16[128,128]{1,0:T(8,128)(2,1)S(1)}, bf16[128,128]{1,0:T(8,128)(2,1)S(1)}, u32[]{:S(2)}, u32[]{:S(2)}) %collective-permute-start.7) | collective-permute-done | bytes 32800 | tf_op jit(solution)/shard_map/ppermute | solution.py:68
  31.4 0.8 shard_map.126
  32.3 1.3 %collective-permute-done.8.refs_6_ = bf16[4,128,128]{2,1,0:T(8,128)(2,1)S(1)} collective-permute-done((bf16[4,128,128]{2,1,0:T(8,128)(2,1)S(1)}, bf16[4,128,128]{2,1,0:T(8,128)(2,1)S(1)}, u32[]{:S(2)}, u32[]{:S(2)}) %collective-permute-start.8) | collective-permute-done | bytes 131104 | tf_op jit(solution)/shard_map/ppermute | solution.py:68
  33.7 1.8 %shard_map.127 = (f32[32,2304]{1,0:T(8,128)S(1)}, bf16[32,2304]{1,0:T(8,128)(2,1)S(1)}, bf16[32,2304]{1,0:T(8,128)(2,1)S(1)}, bf16[32,2304]{1,0:T(8,128)(2,1)S(1)}) custom-call(s32[3]{0:T(128)S(1)} %pad_add_fusion.refs_0_.place, bf16[128,2304]{1,0:T(8,128)(2,1)S(1)} %copy-done.1, bf16[1024,2304]{1,0:T(8,128)(2,1)S(1)} %bitcast.8, ...), custom_call_target="tpu_custom_call" | custom-call | flops 1000000000 | tf_op jit(solution)/shard_map/pallas_call | solution.py:45
  35.5 2.7 %collective-permute-start.10 = (bf16[32,2304]{1,0:T(8,128)(2,1)S(1)}, bf16[32,2304]{1,0:T(8,128)(2,1)S(1)}, u32[]{:S(2)}, u32[]{:S(2)}) collective-permute-start(bf16[32,2304]{1,0:T(8,128)(2,1)S(1)} %get-tuple-element.46), channel_id=1, source_target_pairs={{0,2},{1,3},{2,0},{3,1},{4,6},{5,7},{6,4},{7,5},{8,10},{9,11},{10,... | collective-permute-start | bytes 442376 | tf_op jit(solution)/shard_map/ppermute | solution.py:68
  38.1 1.3 %collective-permute-start.11 = (bf16[32,2304]{1,0:T(8,128)(2,1)S(1)}, bf16[32,2304]{1,0:T(8,128)(2,1)S(1)}, u32[]{:S(2)}, u32[]{:S(2)}) collective-permute-start(bf16[32,2304]{1,0:T(8,128)(2,1)S(1)} %get-tuple-element.47), channel_id=1, source_target_pairs={{0,3},{1,2},{2,1},{3,0},{4,7},{5,6},{6,5},{7,4},{8,11},{9,10},{10,... | collective-permute-start | bytes 442376 | tf_op jit(solution)/shard_map/ppermute | solution.py:68
  39.7 9.8 %collective-permute-done.10.refs_5_ = bf16[32,2304]{1,0:T(8,128)(2,1)S(1)} collective-permute-done((bf16[32,2304]{1,0:T(8,128)(2,1)S(1)}, bf16[32,2304]{1,0:T(8,128)(2,1)S(1)}, u32[]{:S(2)}, u32[]{:S(2)}) %collective-permute-start.10) | collective-permute-done | bytes 147488 | tf_op jit(solution)/shard_map/ppermute | solution.py:68
  49.5 0.5 collective-permute-done.9.refs_4_
  50.0 0.7 shard_map.128
  50.8 2.6 %collective-permute-start.15 = (bf16[32,512]{1,0:T(8,128)(2,1)S(1)}, bf16[32,512]{1,0:T(8,128)(2,1)S(1)}, u32[]{:S(2)}, u32[]{:S(2)}) collective-permute-start(bf16[32,512]{1,0:T(8,128)(2,1)S(1)} %get-tuple-element.51.refs_1_), channel_id=1, source_target_pairs={{0,1},{1,0},{2,3},{3,2},{4,5},{5,4},{6,7},{7,6},{8,9},{9,8},{10,11... | collective-permute-start | bytes 98312 | tf_op jit(solution)/shard_map/ppermute | solution.py:68
  53.4 2.0 %collective-permute-start.16 = (bf16[32,512]{1,0:T(8,128)(2,1)S(1)}, bf16[32,512]{1,0:T(8,128)(2,1)S(1)}, u32[]{:S(2)}, u32[]{:S(2)}) collective-permute-start(bf16[32,512]{1,0:T(8,128)(2,1)S(1)} %get-tuple-element.51.refs_1_), channel_id=1, source_target_pairs={{0,2},{1,3},{2,0},{3,1},{4,6},{5,7},{6,4},{7,5},{8,10},{9,11},{10,... | collective-permute-start | bytes 98312 | tf_op jit(solution)/shard_map/ppermute | solution.py:68
  55.4 1.9 %collective-permute-start.12 = (bf16[32,2304]{1,0:T(8,128)(2,1)S(1)}, bf16[32,2304]{1,0:T(8,128)(2,1)S(1)}, u32[]{:S(2)}, u32[]{:S(2)}) collective-permute-start(bf16[32,2304]{1,0:T(8,128)(2,1)S(1)} %get-tuple-element.48.refs_4_), channel_id=1, source_target_pairs={{0,1},{1,0},{2,3},{3,2},{4,5},{5,4},{6,7},{7,6},{8,9},{9,8},{10,11... | collective-permute-start | bytes 442376 | tf_op jit(solution)/shard_map/ppermute | solution.py:68
  57.3 0.4 collective-permute-start.17
  57.8 1.1 %collective-permute-start.13 = (bf16[32,2304]{1,0:T(8,128)(2,1)S(1)}, bf16[32,2304]{1,0:T(8,128)(2,1)S(1)}, u32[]{:S(2)}, u32[]{:S(2)}) collective-permute-start(bf16[32,2304]{1,0:T(8,128)(2,1)S(1)} %get-tuple-element.48.refs_4_), channel_id=1, source_target_pairs={{0,2},{1,3},{2,0},{3,1},{4,6},{5,7},{6,4},{7,5},{8,10},{9,11},{10,... | collective-permute-start | bytes 442376 | tf_op jit(solution)/shard_map/ppermute | solution.py:68
  58.9 4.8 %collective-permute-done.17.refs_4_ = bf16[32,512]{1,0:T(8,128)(2,1)S(1)} collective-permute-done((bf16[32,512]{1,0:T(8,128)(2,1)S(1)}, bf16[32,512]{1,0:T(8,128)(2,1)S(1)}, u32[]{:S(2)}, u32[]{:S(2)}) %collective-permute-start.17) | collective-permute-done | bytes 32800 | tf_op jit(solution)/shard_map/ppermute | solution.py:68
  63.6 0.6 shard_map.130.refs_3_
  64.2 1.5 %collective-permute-start.18 = (bf16[128,512]{1,0:T(8,128)(2,1)S(1)}, bf16[128,512]{1,0:T(8,128)(2,1)S(1)}, u32[]{:S(2)}, u32[]{:S(2)}) collective-permute-start(bf16[128,512]{1,0:T(8,128)(2,1)S(1)} %shard_map.130.refs_3_), channel_id=1, source_target_pairs={{0,24},{4,28},{8,16},{12,20},{16,8},{20,12},{24,0},{28,4},{1,25},{... | collective-permute-start | bytes 393224 | tf_op jit(solution)/shard_map/ppermute | solution.py:68
  65.7 1.3 %collective-permute-start.19 = (bf16[128,512]{1,0:T(8,128)(2,1)S(1)}, bf16[128,512]{1,0:T(8,128)(2,1)S(1)}, u32[]{:S(2)}, u32[]{:S(2)}) collective-permute-start(bf16[128,512]{1,0:T(8,128)(2,1)S(1)} %shard_map.130.refs_3_), channel_id=1, source_target_pairs={{0,16},{4,20},{8,24},{12,28},{16,0},{20,4},{24,8},{28,12},{1,17},{... | collective-permute-start | bytes 393224 | tf_op jit(solution)/shard_map/ppermute | solution.py:68
  67.0 0.7 collective-permute-start.20
  67.8 3.1 %collective-permute-start.14 = (bf16[32,2304]{1,0:T(8,128)(2,1)S(1)}, bf16[32,2304]{1,0:T(8,128)(2,1)S(1)}, u32[]{:S(2)}, u32[]{:S(2)}) collective-permute-start(bf16[32,2304]{1,0:T(8,128)(2,1)S(1)} %get-tuple-element.48.refs_4_), channel_id=1, source_target_pairs={{0,3},{1,2},{2,1},{3,0},{4,7},{5,6},{6,5},{7,4},{8,11},{9,10},{10,... | collective-permute-start | bytes 442376 | tf_op jit(solution)/shard_map/ppermute | solution.py:68
  70.8 0.5 collective-permute-start.22
  71.5 0.4 collective-permute-done.20.refs_6_
  72.3 2.4 %collective-permute-done.14.refs_7_ = bf16[32,2304]{1,0:T(8,128)(2,1)S(1)} collective-permute-done((bf16[32,2304]{1,0:T(8,128)(2,1)S(1)}, bf16[32,2304]{1,0:T(8,128)(2,1)S(1)}, u32[]{:S(2)}, u32[]{:S(2)}) %collective-permute-start.14) | collective-permute-done | bytes 147488 | tf_op jit(solution)/shard_map/ppermute | solution.py:68
  74.7 1.5 %shard_map.129 = (bf16[128,2304]{1,0:T(8,128)(2,1)}, bf16[512,512]{1,0:T(8,128)(2,1)S(1)}) custom-call(s32[3]{0:T(128)S(1)} %pad_add_fusion.refs_0_.place, f32[1,2304]{1,0:T(1,128)S(1)} %broadcast_in_dim.7.refs_0_.refs_1_, bf16[2304,512]{1,0:T(8,128)(2,1)S(1)} %copy-done, bf16[512,1024]{1,0:T(8,128)(2,1)S(1)} %bitcast.9, ...), custom_call_target="tpu_custom_call" | custom-call | flops 1000000000 | tf_op jit(solution)/shard_map/pallas_call | solution.py:45
  76.2 3.8 %shard_map.131 = bf16[128,512]{1,0:T(8,128)(2,1)} custom-call(s32[3]{0:T(128)S(1)} %pad_add_fusion.refs_0_.place, bf16[512,512]{1,0:T(8,128)(2,1)S(1)} %get-tuple-element.50.refs_1_, bf16[512,1024]{1,0:T(8,128)(2,1)S(1)} %bitcast.10, bf16[128,512]{1,0:T(8,128)(2,1)S(1)} %shard_map.130.refs_3_, bf16[128,512]{1,0:T(8,128)(2,1)S(1)} %collective-permute-done.18.refs_4_, ...), custom_call_target="tpu_custom_call" | custom-call | flops 1000000000 | tf_op jit(solution)/shard_map/pallas_call | solution.py:45
  (41 shorter events, 1.0 us)
Async XLA Ops:
  0.6 6.6 %copy-start.6 = (f32[128,8]{0,1:T(8,128)S(1)}, f32[128,8]{0,1:T(8,128)}, u32[]{:S(2)}) copy-start(f32[128,8]{0,1:T(8,128)} %param.13) | copy-start | bytes 12292
  1.5 5.6 %collective-permute-start = (bf16[3,16,1024]{2,1,0:T(8,128)(2,1)S(1)}, bf16[3,16,1024]{2,1,0:T(8,128)(2,1)S(1)}, u32[]{:S(2)}, u32[]{:S(2)}) collective-permute-start(bf16[3,16,1024]{2,1,0:T(8,128)(2,1)S(1)} %slice.3), channel_id=1, source_target_pairs={{0,4},{4,8},{8,12},{12,16},{16,20},{20,24},{24,28},{28,0},{1,5},{5... | collective-permute-start | bytes 294920 | tf_op jit(solution)/shard_map/ppermute | solution.py:73
  2.1 1.1 %copy-start.2 = (bf16[3,128,1024]{2,1,0:T(8,128)(2,1)S(1)}, bf16[3,128,1024]{2,1,0:T(8,128)(2,1)}, u32[]{:S(2)}) copy-start(bf16[3,128,1024]{2,1,0:T(8,128)(2,1)} %stored_inputs.1) | copy-start | bytes 2359300
  3.2 1.0 %copy-start.4 = (f32[128,1024]{1,0:T(8,128)S(1)}, f32[128,1024]{1,0:T(8,128)}, u32[]{:S(2)}) copy-start(f32[128,1024]{1,0:T(8,128)} %stored_gate.1) | copy-start | bytes 1572868
  4.3 0.8 copy-start.5
  5.1 28.6 %slice-start = ((s8[4718592]{0:T(1024)(128)(4,1)}), s8[524288]{0:T(1024)(128)(4,1)S(1)}, s32[]{:S(2)}) async-start(s8[4718592]{0:T(1024)(128)(4,1)} %bitcast.7), calls=%async_computation | async-start | bytes 1048576
  7.2 26.4 %slice-start.1 = ((s8[4718592]{0:T(1024)(128)(4,1)}), s8[4194304]{0:T(1024)(128)(4,1)S(1)}, s32[]{:S(2)}) async-start(s8[4718592]{0:T(1024)(128)(4,1)} %bitcast.7), calls=%async_computation.1 | async-start | bytes 8388608
  13.0 2.3 %collective-permute-start.1 = (bf16[4,272,128]{2,1,0:T(8,128)(2,1)S(1)}, bf16[4,272,128]{2,1,0:T(8,128)(2,1)S(1)}, u32[]{:S(2)}, u32[]{:S(2)}) collective-permute-start(bf16[4,272,128]{2,1,0:T(8,128)(2,1)S(1)} %get-tuple-element.33), channel_id=1, source_target_pairs={{0,4},{4,0},{8,12},{12,8},{16,20},{20,16},{24,28},{28,24},{1,5},{5... | collective-permute-start | bytes 835592 | tf_op jit(solution)/shard_map/ppermute | solution.py:68
  16.1 4.5 %collective-permute-start.2 = (bf16[272,128]{1,0:T(8,128)(2,1)S(1)}, bf16[272,128]{1,0:T(8,128)(2,1)S(1)}, u32[]{:S(2)}, u32[]{:S(2)}) collective-permute-start(bf16[272,128]{1,0:T(8,128)(2,1)S(1)} %get-tuple-element.35), channel_id=1, source_target_pairs={{0,8},{4,12},{8,0},{12,4},{16,24},{20,28},{24,16},{28,20},{1,9},{5... | collective-permute-start | bytes 208904 | tf_op jit(solution)/shard_map/ppermute | solution.py:68
  17.7 5.1 %collective-permute-start.3 = (bf16[272,128]{1,0:T(8,128)(2,1)S(1)}, bf16[272,128]{1,0:T(8,128)(2,1)S(1)}, u32[]{:S(2)}, u32[]{:S(2)}) collective-permute-start(bf16[272,128]{1,0:T(8,128)(2,1)S(1)} %get-tuple-element.36), channel_id=1, source_target_pairs={{0,16},{4,20},{8,24},{12,28},{16,0},{20,4},{24,8},{28,12},{1,17},{... | collective-permute-start | bytes 208904 | tf_op jit(solution)/shard_map/ppermute | solution.py:68
  18.4 5.2 %collective-permute-start.4 = (bf16[272,128]{1,0:T(8,128)(2,1)S(1)}, bf16[272,128]{1,0:T(8,128)(2,1)S(1)}, u32[]{:S(2)}, u32[]{:S(2)}) collective-permute-start(bf16[272,128]{1,0:T(8,128)(2,1)S(1)} %get-tuple-element.37), channel_id=1, source_target_pairs={{0,24},{4,28},{8,16},{12,20},{16,8},{20,12},{24,0},{28,4},{1,25},{... | collective-permute-start | bytes 208904 | tf_op jit(solution)/shard_map/ppermute | solution.py:68
  24.5 9.1 %copy-start.1 = (bf16[128,2304]{1,0:T(8,128)(2,1)S(1)}, bf16[128,2304]{1,0:T(8,128)(2,1)}, u32[]{:S(2)}) copy-start(bf16[128,2304]{1,0:T(8,128)(2,1)} %refs_1_.2) | copy-start | bytes 1769476
  24.5 4.2 %collective-permute-start.5 = (bf16[128,128]{1,0:T(8,128)(2,1)S(1)}, bf16[128,128]{1,0:T(8,128)(2,1)S(1)}, u32[]{:S(2)}, u32[]{:S(2)}) collective-permute-start(bf16[128,128]{1,0:T(8,128)(2,1)S(1)} %get-tuple-element.39), channel_id=1, source_target_pairs={{0,8},{4,12},{8,0},{12,4},{16,24},{20,28},{24,16},{28,20},{1,9},{5... | collective-permute-start | bytes 98312 | tf_op jit(solution)/shard_map/ppermute | solution.py:68
  26.0 3.9 %collective-permute-start.6 = (bf16[128,128]{1,0:T(8,128)(2,1)S(1)}, bf16[128,128]{1,0:T(8,128)(2,1)S(1)}, u32[]{:S(2)}, u32[]{:S(2)}) collective-permute-start(bf16[128,128]{1,0:T(8,128)(2,1)S(1)} %get-tuple-element.40), channel_id=1, source_target_pairs={{0,16},{4,20},{8,24},{12,28},{16,0},{20,4},{24,8},{28,12},{1,17},{... | collective-permute-start | bytes 98312 | tf_op jit(solution)/shard_map/ppermute | solution.py:68
  26.6 4.8 %collective-permute-start.7 = (bf16[128,128]{1,0:T(8,128)(2,1)S(1)}, bf16[128,128]{1,0:T(8,128)(2,1)S(1)}, u32[]{:S(2)}, u32[]{:S(2)}) collective-permute-start(bf16[128,128]{1,0:T(8,128)(2,1)S(1)} %get-tuple-element.41), channel_id=1, source_target_pairs={{0,24},{4,28},{8,16},{12,20},{16,8},{20,12},{24,0},{28,4},{1,25},{... | collective-permute-start | bytes 98312 | tf_op jit(solution)/shard_map/ppermute | solution.py:68
  32.2 1.4 %collective-permute-start.8 = (bf16[4,128,128]{2,1,0:T(8,128)(2,1)S(1)}, bf16[4,128,128]{2,1,0:T(8,128)(2,1)S(1)}, u32[]{:S(2)}, u32[]{:S(2)}) collective-permute-start(bf16[4,128,128]{2,1,0:T(8,128)(2,1)S(1)} %get-tuple-element.43), channel_id=1, source_target_pairs={{0,4},{4,0},{8,12},{12,8},{16,20},{20,16},{24,28},{28,24},{1,5},{5... | collective-permute-start | bytes 393224 | tf_op jit(solution)/shard_map/ppermute | solution.py:68
  33.6 6.1 %copy-start.9 = (f32[2304]{0:T(1024)S(1)}, f32[2304]{0:T(1024)}, u32[]{:S(2)}) copy-start(f32[2304]{0:T(1024)} %param.17) | copy-start | bytes 27652
  33.6 16.4 %copy-start.3 = (bf16[2304,512]{1,0:T(8,128)(2,1)S(1)}, bf16[2304,512]{1,0:T(8,128)(2,1)}, u32[]{:S(2)}) copy-start(bf16[2304,512]{1,0:T(8,128)(2,1)} %refs_1_.3) | copy-start | bytes 7077892
  33.6 16.4 %copy-start.7 = (f32[512]{0:T(512)S(1)}, f32[512]{0:T(512)}, u32[]{:S(2)}) copy-start(f32[512]{0:T(512)} %param.19) | copy-start | bytes 6148
  35.5 14.0 %collective-permute-start.10 = (bf16[32,2304]{1,0:T(8,128)(2,1)S(1)}, bf16[32,2304]{1,0:T(8,128)(2,1)S(1)}, u32[]{:S(2)}, u32[]{:S(2)}) collective-permute-start(bf16[32,2304]{1,0:T(8,128)(2,1)S(1)} %get-tuple-element.46), channel_id=1, source_target_pairs={{0,2},{1,3},{2,0},{3,1},{4,6},{5,7},{6,4},{7,5},{8,10},{9,11},{10,... | collective-permute-start | bytes 442376 | tf_op jit(solution)/shard_map/ppermute | solution.py:68
  38.1 11.4 %collective-permute-start.11 = (bf16[32,2304]{1,0:T(8,128)(2,1)S(1)}, bf16[32,2304]{1,0:T(8,128)(2,1)S(1)}, u32[]{:S(2)}, u32[]{:S(2)}) collective-permute-start(bf16[32,2304]{1,0:T(8,128)(2,1)S(1)} %get-tuple-element.47), channel_id=1, source_target_pairs={{0,3},{1,2},{2,1},{3,0},{4,7},{5,6},{6,5},{7,4},{8,11},{9,10},{10,... | collective-permute-start | bytes 442376 | tf_op jit(solution)/shard_map/ppermute | solution.py:68
  39.5 10.6 %collective-permute-start.9 = (bf16[32,2304]{1,0:T(8,128)(2,1)S(1)}, bf16[32,2304]{1,0:T(8,128)(2,1)S(1)}, u32[]{:S(2)}, u32[]{:S(2)}) collective-permute-start(bf16[32,2304]{1,0:T(8,128)(2,1)S(1)} %get-tuple-element.45), channel_id=1, source_target_pairs={{0,1},{1,0},{2,3},{3,2},{4,5},{5,4},{6,7},{7,6},{8,9},{9,8},{10,11... | collective-permute-start | bytes 442376 | tf_op jit(solution)/shard_map/ppermute | solution.py:68
  50.8 21.3 %copy-start.8 = (bf16[512,2,512]{2,1,0:T(2,128)(2,1)S(1)}, bf16[512,2,512]{2,1,0:T(2,128)(2,1)}, u32[]{:S(2)}) copy-start(bf16[512,2,512]{2,1,0:T(2,128)(2,1)} %param.21) | copy-start | bytes 3145732
  50.8 8.1 %collective-permute-start.15 = (bf16[32,512]{1,0:T(8,128)(2,1)S(1)}, bf16[32,512]{1,0:T(8,128)(2,1)S(1)}, u32[]{:S(2)}, u32[]{:S(2)}) collective-permute-start(bf16[32,512]{1,0:T(8,128)(2,1)S(1)} %get-tuple-element.51.refs_1_), channel_id=1, source_target_pairs={{0,1},{1,0},{2,3},{3,2},{4,5},{5,4},{6,7},{7,6},{8,9},{9,8},{10,11... | collective-permute-start | bytes 98312 | tf_op jit(solution)/shard_map/ppermute | solution.py:68
  53.4 5.5 %collective-permute-start.16 = (bf16[32,512]{1,0:T(8,128)(2,1)S(1)}, bf16[32,512]{1,0:T(8,128)(2,1)S(1)}, u32[]{:S(2)}, u32[]{:S(2)}) collective-permute-start(bf16[32,512]{1,0:T(8,128)(2,1)S(1)} %get-tuple-element.51.refs_1_), channel_id=1, source_target_pairs={{0,2},{1,3},{2,0},{3,1},{4,6},{5,7},{6,4},{7,5},{8,10},{9,11},{10,... | collective-permute-start | bytes 98312 | tf_op jit(solution)/shard_map/ppermute | solution.py:68
  55.4 19.3 %copy-start = (bf16[2304,512]{1,0:T(8,128)(2,1)S(1)}, bf16[2304,512]{1,0:T(8,128)(2,1)}, u32[]{:S(2)}) copy-start(bf16[2304,512]{1,0:T(8,128)(2,1)} %refs_2_.3) | copy-start | bytes 7077892
  55.4 12.4 %collective-permute-start.12 = (bf16[32,2304]{1,0:T(8,128)(2,1)S(1)}, bf16[32,2304]{1,0:T(8,128)(2,1)S(1)}, u32[]{:S(2)}, u32[]{:S(2)}) collective-permute-start(bf16[32,2304]{1,0:T(8,128)(2,1)S(1)} %get-tuple-element.48.refs_4_), channel_id=1, source_target_pairs={{0,1},{1,0},{2,3},{3,2},{4,5},{5,4},{6,7},{7,6},{8,9},{9,8},{10,11... | collective-permute-start | bytes 442376 | tf_op jit(solution)/shard_map/ppermute | solution.py:68
  57.3 6.3 %collective-permute-start.17 = (bf16[32,512]{1,0:T(8,128)(2,1)S(1)}, bf16[32,512]{1,0:T(8,128)(2,1)S(1)}, u32[]{:S(2)}, u32[]{:S(2)}) collective-permute-start(bf16[32,512]{1,0:T(8,128)(2,1)S(1)} %get-tuple-element.51.refs_1_), channel_id=1, source_target_pairs={{0,3},{1,2},{2,1},{3,0},{4,7},{5,6},{6,5},{7,4},{8,11},{9,10},{10,... | collective-permute-start | bytes 98312 | tf_op jit(solution)/shard_map/ppermute | solution.py:68
  57.8 13.1 %collective-permute-start.13 = (bf16[32,2304]{1,0:T(8,128)(2,1)S(1)}, bf16[32,2304]{1,0:T(8,128)(2,1)S(1)}, u32[]{:S(2)}, u32[]{:S(2)}) collective-permute-start(bf16[32,2304]{1,0:T(8,128)(2,1)S(1)} %get-tuple-element.48.refs_4_), channel_id=1, source_target_pairs={{0,2},{1,3},{2,0},{3,1},{4,6},{5,7},{6,4},{7,5},{8,10},{9,11},{10,... | collective-permute-start | bytes 442376 | tf_op jit(solution)/shard_map/ppermute | solution.py:68
  64.2 6.6 %collective-permute-start.18 = (bf16[128,512]{1,0:T(8,128)(2,1)S(1)}, bf16[128,512]{1,0:T(8,128)(2,1)S(1)}, u32[]{:S(2)}, u32[]{:S(2)}) collective-permute-start(bf16[128,512]{1,0:T(8,128)(2,1)S(1)} %shard_map.130.refs_3_), channel_id=1, source_target_pairs={{0,24},{4,28},{8,16},{12,20},{16,8},{20,12},{24,0},{28,4},{1,25},{... | collective-permute-start | bytes 393224 | tf_op jit(solution)/shard_map/ppermute | solution.py:68
  65.7 5.8 %collective-permute-start.19 = (bf16[128,512]{1,0:T(8,128)(2,1)S(1)}, bf16[128,512]{1,0:T(8,128)(2,1)S(1)}, u32[]{:S(2)}, u32[]{:S(2)}) collective-permute-start(bf16[128,512]{1,0:T(8,128)(2,1)S(1)} %shard_map.130.refs_3_), channel_id=1, source_target_pairs={{0,16},{4,20},{8,24},{12,28},{16,0},{20,4},{24,8},{28,12},{1,17},{... | collective-permute-start | bytes 393224 | tf_op jit(solution)/shard_map/ppermute | solution.py:68
  67.0 5.0 %collective-permute-start.20 = (bf16[128,512]{1,0:T(8,128)(2,1)S(1)}, bf16[128,512]{1,0:T(8,128)(2,1)S(1)}, u32[]{:S(2)}, u32[]{:S(2)}) collective-permute-start(bf16[128,512]{1,0:T(8,128)(2,1)S(1)} %shard_map.130.refs_3_), channel_id=1, source_target_pairs={{0,8},{4,12},{8,0},{12,4},{16,24},{20,28},{24,16},{28,20},{1,9},{5... | collective-permute-start | bytes 393224 | tf_op jit(solution)/shard_map/ppermute | solution.py:68
  67.8 6.9 %collective-permute-start.14 = (bf16[32,2304]{1,0:T(8,128)(2,1)S(1)}, bf16[32,2304]{1,0:T(8,128)(2,1)S(1)}, u32[]{:S(2)}, u32[]{:S(2)}) collective-permute-start(bf16[32,2304]{1,0:T(8,128)(2,1)S(1)} %get-tuple-element.48.refs_4_), channel_id=1, source_target_pairs={{0,3},{1,2},{2,1},{3,0},{4,7},{5,6},{6,5},{7,4},{8,11},{9,10},{10,... | collective-permute-start | bytes 442376 | tf_op jit(solution)/shard_map/ppermute | solution.py:68
  70.8 5.4 %collective-permute-start.21 = (bf16[128,512]{1,0:T(8,128)(2,1)S(1)}, bf16[128,512]{1,0:T(8,128)(2,1)S(1)}, u32[]{:S(2)}, u32[]{:S(2)}) collective-permute-start(bf16[128,512]{1,0:T(8,128)(2,1)S(1)} %shard_map.130.refs_3_), channel_id=1, source_target_pairs={{0,4},{4,0},{8,12},{12,8},{16,20},{20,16},{24,28},{28,24},{1,5},{5... | collective-permute-start | bytes 393224 | tf_op jit(solution)/shard_map/ppermute | solution.py:68
  70.8 5.4 %collective-permute-start.22 = (bf16[128,512]{1,0:T(8,128)(2,1)S(1)}, bf16[128,512]{1,0:T(8,128)(2,1)S(1)}, u32[]{:S(2)}, u32[]{:S(2)}) collective-permute-start(bf16[128,512]{1,0:T(8,128)(2,1)S(1)} %collective-permute-done.18.refs_4_), channel_id=1, source_target_pairs={{0,4},{4,0},{8,12},{12,8},{16,20},{20,16},{24,28},{28,24},{1,5},{5... | collective-permute-start | bytes 393224 | tf_op jit(solution)/shard_map/ppermute | solution.py:68
  71.5 4.7 %collective-permute-start.23 = (bf16[128,512]{1,0:T(8,128)(2,1)S(1)}, bf16[128,512]{1,0:T(8,128)(2,1)S(1)}, u32[]{:S(2)}, u32[]{:S(2)}) collective-permute-start(bf16[128,512]{1,0:T(8,128)(2,1)S(1)} %collective-permute-done.19.refs_5_), channel_id=1, source_target_pairs={{0,4},{4,0},{8,12},{12,8},{16,20},{20,16},{24,28},{28,24},{1,5},{5... | collective-permute-start | bytes 393224 | tf_op jit(solution)/shard_map/ppermute | solution.py:68
  72.0 4.2 %collective-permute-start.24 = (bf16[128,512]{1,0:T(8,128)(2,1)S(1)}, bf16[128,512]{1,0:T(8,128)(2,1)S(1)}, u32[]{:S(2)}, u32[]{:S(2)}) collective-permute-start(bf16[128,512]{1,0:T(8,128)(2,1)S(1)} %collective-permute-done.20.refs_6_), channel_id=1, source_target_pairs={{0,4},{4,0},{8,12},{12,8},{16,20},{20,16},{24,28},{28,24},{1,5},{5... | collective-permute-start | bytes 393224 | tf_op jit(solution)/shard_map/ppermute | solution.py:68

commit v3 on v2

--- a/solution.py
+++ b/solution.py
@@ -101,64 +101,67 @@
     moves[2].wait()
 
 
-def local_kernel(heads, *refs):
-    place, inputs, halo, logs, beta, taps = refs[:6]
-    kept, sent, reads, intra = refs[6:10]
-    wide, maps = refs[10:]
+def put_wide(wide, place, inputs, halo, own, part):
+    pad = wide.shape[0] - inputs.shape[1]
+    before = halo[part, halo.shape[1] - pad :, own].astype(f32)
+    wide[:pad, :] = jnp.where(place[2] == 0, 0.0, before)
+    wide[pad:, :] = inputs[part, :, own].astype(f32)
+
+
+def convolved(wide, taps, own, part):
+    length = wide.shape[0] - 8
+    total = jnp.zeros((length, DK), f32)
+    for tap in range(CONV):
+        first = 8 - (CONV - 1) + tap
+        total = total + taps[part, tap : tap + 1, own] * wide[first : first + length, :]
+    return total / (1.0 + jnp.exp(-total))
+
+
+def unit(value):
+    return value * lax.rsqrt(jnp.sum(value * value, axis=-1, keepdims=True) + eps_norm)
+
+
+def spans(log):
+    half = log.shape[0] // 2
+    for b in range(2):
+        middle = log[b * half + half // 2 : b * half + half // 2 + 1]
+        yield b, slice(b * half, (b + 1) * half), middle
+
+
+def side_heads(place, pairs):
+    _, core = split_cores(place)
+    return [2 * i + core for i in range(pairs)] + [2 * i + 1 - core for i in range(pairs)]
+
+
+def map_kernel(place, inputs, halo, logs, beta, taps, kept, sent, solutions, shrunk, wide):
     length = logs.shape[0]
-    pad = wide.shape[1] - length
-    before = halo[:, halo.shape[1] - pad :, :].astype(f32)
-    wide[:, :pad, :] = jnp.where(place[2] == 0, 0.0, before)
-    wide[:, pad:, :] = inputs[...].astype(f32)
-
+    pairs = kept.shape[0]
+    chunks = range(2 * pairs)
+    heads = side_heads(place, pairs)
+    lane = [lanes(head) for head in heads]
     rows = lax.broadcasted_iota(jnp.int32, (length, length), 0)
     cols = lax.broadcasted_iota(jnp.int32, (length, length), 1)
     eye = (rows == cols).astype(f32)
-    half = length // 2
-    chunks = range(heads)
-
-    def convolved(part, i):
-        own = slice(i * DK, (i + 1) * DK)
-        total = jnp.zeros((length, DK), f32)
-        for tap in range(CONV):
-            first = pad - (CONV - 1) + tap
-            total = total + taps[part, tap : tap + 1, own] * wide[part, first : first + length, own]
-        return total / (1.0 + jnp.exp(-total))
-
-    def unit(value):
-        return value * lax.rsqrt(jnp.sum(value * value, axis=-1, keepdims=True) + eps_norm)
-
-    coupling, mixing, right, finals, queries_grown, decay = [], [], [], [], [], []
     for i in chunks:
-        own_head = slice(i * DK, (i + 1) * DK)
-        query = (unit(convolved(0, i)) * DK ** (-0.5)).astype(bf16).astype(f32)
-        key = unit(convolved(1, i)).astype(bf16).astype(f32)
-        value = convolved(2, i).astype(bf16)
-        log = logs[:, own_head]
-        rate_row = beta[i : i + 1, :]
+        for part in (1, 2):
+            put_wide(wide.at[i, part - 1], place, inputs, halo, lane[i], part)
+
+    coupling, right, finals, decay = [], [], [], []
+    for i in chunks:
+        key = unit(convolved(wide.at[i, 0], taps, lane[i], 1)).astype(bf16).astype(f32)
+        value = convolved(wide.at[i, 1], taps, lane[i], 2).astype(bf16)
+        log = logs[:, lane[i]]
+        rate_row = beta[pl.ds(heads[i], 1), :]
         rate_column = jnp.sum(rate_row * eye, axis=1, keepdims=True)
         last = log[length - 1 :]
-        kept_parts, mixed_parts = [], []
-        for b in range(2):
-            own = slice(b * half, (b + 1) * half)
-            middle = log[b * half + half // 2 : b * half + half // 2 + 1]
-            row_scale = jnp.exp(log[own] - middle)
-            shrunk = key * jnp.exp(jnp.minimum(middle - log, 75.0))
-            both = jnp.concatenate([query[own] * row_scale, key[own] * row_scale], axis=0)
-            product = mm_nt(both, shrunk)
-            mixed_parts.append(product[:half])
-            kept_parts.append(product[half:])
+        products = []
+        for b, own, middle in spans(log):
+            shrunk[i, b] = (key * jnp.exp(jnp.minimum(middle - log, 75.0))).astype(bf16)
+            products.append(mm_nt(key[own] * jnp.exp(log[own] - middle), shrunk[i, b]))
         coupling.append(
-            jnp.where(rows > cols, jnp.concatenate(kept_parts, axis=0) * rate_row, 0.0).astype(bf16)
+            jnp.where(rows > cols, jnp.concatenate(products, axis=0) * rate_row, 0.0).astype(bf16)
         )
-        mixing.append(
-            jnp.where(rows >= cols, jnp.concatenate(mixed_parts, axis=0) * rate_row, 0.0).astype(
-                bf16
-            )
-        )
-        growth = jnp.exp(log)
-        queries_grown.append(query * growth)
-        right.append(jnp.concatenate([value, (key * growth).astype(bf16)], axis=1))
+        right.append(jnp.concatenate([value, (key * jnp.exp(log)).astype(bf16)], axis=1))
         finals.append((key * jnp.exp(last - log) * rate_column).astype(bf16))
         decay.append(jnp.exp(last))
 
@@ -183,23 +186,41 @@
     first = [mm(short[i], right[i]).astype(bf16) for i in chunks]
     left = [right[i].astype(f32) - first[i].astype(f32) - mm(coupling[i], first[i]) for i in chunks]
     solved = [(first[i].astype(f32) + mm(short[i], left[i])).astype(bf16) for i in chunks]
-
     for i in chunks:
-        own_head = slice(i * DK, (i + 1) * DK)
-        maps[i, : 2 * DK, :] = mm_tn(solved[i], finals[i]).astype(bf16)
-        high = decay[i].astype(bf16)
-        low = (decay[i] - high.astype(f32)).astype(bf16)
-        maps[i, 2 * DK :, :] = jnp.concatenate(
-            [jnp.broadcast_to(high, (EXTRA // 2, DK)), jnp.broadcast_to(low, (EXTRA // 2, DK))],
-            axis=0,
-        )
-        mixes = mm(mixing[i], solved[i])
-        intra[:, own_head] = mixes[:, :DK]
-        reads[:, own_head] = (queries_grown[i] - mixes[:, DK:]).astype(bf16)
-    _, core = split_cores(place)
-    for pair in range(heads // 2):
-        kept[pair] = maps[2 * pair + core]
-        sent[pair] = maps[2 * pair + 1 - core]
+        solutions[i] = solved[i]
+        maps = kept if i < pairs else sent
+        put_map(maps, i % pairs, mm_tn(solved[i], finals[i]), decay[i])
+
+
+def put_map(maps, i, offset_and_move, decay):
+    maps[i, : 2 * DK, :] = offset_and_move.astype(bf16)
+    high = decay.astype(bf16)
+    low = (decay - high.astype(f32)).astype(bf16)
+    maps[i, 2 * DK :, :] = jnp.concatenate(
+        [jnp.broadcast_to(high, (EXTRA // 2, DK)), jnp.broadcast_to(low, (EXTRA // 2, DK))],
+        axis=0,
+    )
+
+
+def read_kernel(place, inputs, halo, logs, beta, taps, solutions, shrunk, reads, intra, wide):
+    length = logs.shape[0]
+    rows = lax.broadcasted_iota(jnp.int32, (length, length), 0)
+    cols = lax.broadcasted_iota(jnp.int32, (length, length), 1)
+    for i, head in enumerate(side_heads(place, solutions.shape[0] // 2)):
+        lane = lanes(head)
+        put_wide(wide.at[i], place, inputs, halo, lane, 0)
+        query = unit(convolved(wide.at[i], taps, lane, 0)) * DK ** (-0.5)
+        query = query.astype(bf16).astype(f32)
+        log = logs[:, lane]
+        products = [
+            mm_nt(query[own] * jnp.exp(log[own] - middle), shrunk[i, b])
+            for b, own, middle in spans(log)
+        ]
+        rate_row = beta[pl.ds(head, 1), :]
+        mixing = jnp.where(rows >= cols, jnp.concatenate(products, axis=0) * rate_row, 0.0)
+        mixes = mm(mixing, solutions[i])
+        intra[:, lane] = mixes[:, :DK]
+        reads[:, lane] = (query * jnp.exp(log) - mixes[:, DK:]).astype(bf16)
 
 
 def parts_of(state_map):
@@ -220,19 +241,9 @@
         offset_b, move_b, decay_b = parts_of(jnp.where(core == 0, other, mine))
         product = mm(jnp.concatenate([offset_a, move_a], axis=0), move_b)
         column = jnp.sum(eye * decay_a, axis=1, keepdims=True)
-        maps[pair, :DK, :] = (
-            offset_a.astype(f32) * decay_b - product[:DK] + offset_b.astype(f32)
-        ).astype(bf16)
-        maps[pair, DK : 2 * DK, :] = (
-            move_a.astype(f32) * decay_b + column * move_b.astype(f32) - product[DK:]
-        ).astype(bf16)
-        decay = decay_a * decay_b
-        high = decay.astype(bf16)
-        low = (decay - high.astype(f32)).astype(bf16)
-        maps[pair, 2 * DK :, :] = jnp.concatenate(
-            [jnp.broadcast_to(high, (EXTRA // 2, DK)), jnp.broadcast_to(low, (EXTRA // 2, DK))],
-            axis=0,
-        )
+        offset = offset_a.astype(f32) * decay_b - product[:DK] + offset_b.astype(f32)
+        move = move_a.astype(f32) * decay_b + column * move_b.astype(f32) - product[DK:]
+        put_map(maps, pair, jnp.concatenate([offset, move], axis=0), decay_a * decay_b)
     for step in range(pairs):
         outs[step][...] = maps[partner(chip, step, pairs)]
 
@@ -267,27 +278,21 @@
         outs[step][...] = starts[partner(chip, step, pairs)]
 
 
-def share_kernel(pairs, place, kept, got, *refs):
-    starts, (mine, other) = refs[:pairs], refs[pairs:]
+def project_kernel(parts, *refs):
+    place, residual, weight, reads, intra, stay, go = refs[:7]
+    refs = refs[7:]
+    pairs = stay.shape[0]
+    mine, other, refs = refs[:pairs], refs[pairs : 2 * pairs], refs[2 * pairs :]
+    outs, (whole, summed) = refs[:parts], refs[parts:]
     chip, core = split_cores(place)
+    head_me = place[1]
     for step in range(pairs):
         pair = partner(chip, step, pairs)
-        state = starts[step][...]
-        later = apply_map(state, jnp.where(core == 0, kept[pair], got[pair])).astype(bf16)
-        mine[pair] = jnp.where(core == 0, state, later)
-        other[pair] = jnp.where(core == 0, later, state)
-
-
-def project_kernel(parts, *refs):
-    place, residual, weight, reads, intra, mine, other = refs[:7]
-    outs = refs[7 : 7 + parts]
-    whole, summed = refs[7 + parts :]
-    _, core = split_cores(place)
-    head_me = place[1]
-    for pair in range(mine.shape[0]):
-        for states, head in ((mine, 2 * pair + core), (other, 2 * pair + 1 - core)):
-            own = lanes(head)
-            whole[:, own] = (intra[:, own] + mm_nt(reads[:, own], states[pair])).astype(bf16)
+        for states, maps, side in ((mine, stay, core), (other, go, 1 - core)):
+            own = lanes(2 * pair + side)
+            state = states[step][...]
+            state = jnp.where(core == 0, state, apply_map(state, maps[pair]).astype(bf16))
+            whole[:, own] = (intra[:, own] + mm_nt(reads[:, own], state)).astype(bf16)
     summed[...] = jnp.dot(whole[...], weight[...], preferred_element_type=f32)
     share = summed.shape[0] // parts
     for step in range(parts):
@@ -305,15 +310,19 @@
 def latent_kernel(parts, *refs):
     gain, latent_weight, latent_gain = refs[:3]
     partials = refs[3 : 3 + parts]
-    stream, latent = refs[3 + parts :]
+    stream, latent, together = refs[3 + parts :]
+    width = stream.shape[1]
     total = partials[0][...]
     for step in range(1, parts):
         total = total + partials[step][...].astype(f32)
     short = total.astype(bf16)
     stream[...] = short
+    together[:, :width] = short
     normed = normalized(short.astype(f32), gain[...]).astype(bf16)
     before = jnp.dot(normed, latent_weight[...], preferred_element_type=f32)
-    latent[...] = normalized(before, latent_gain[...]).astype(bf16)
+    rows = normalized(before, latent_gain[...]).astype(bf16)
+    latent[...] = rows
+    together[:, width:] = rows
 
 
 def join_kernel(parts, *refs):
@@ -323,7 +332,7 @@
     share = out.shape[0] // parts
     for step in range(parts):
         at = pl.ds(pl.multiple_of(partner(place[1], step, parts) * share, share), share)
-        out[at, :] = pieces[step][...]
+        out[at, :] = pieces[step][:, pieces[step].shape[1] - out.shape[1] :]
 
 
 def query_kernel(parts, *refs):
@@ -334,7 +343,7 @@
     share = length // parts
     for step in range(parts):
         at = pl.ds(pl.multiple_of(partner(place[1], step, parts) * share, share), share)
-        stream[at, :] = pieces[step][...]
+        stream[at, :] = pieces[step][:, : stream.shape[1]]
     normed = normalized(stream[...].astype(f32), gain[...]).astype(bf16)
     query = jnp.dot(normed, query_weight[...], preferred_element_type=f32).astype(bf16)
     for head in range(query.shape[1] // DH):
@@ -346,40 +355,35 @@
 
 def attend_kernel(order, *refs):
     place, absorbed, up = refs[:3]
-    latents = refs[3 : 3 + len(order)]
-    out, scores, mixed = refs[3 + len(order) :]
-    length = latents[0].shape[0]
+    blocks = refs[3 : 3 + len(order)]
+    out, latents = refs[3 + len(order) :]
+    length = blocks[0].shape[0]
     heads = absorbed.shape[0] // length
     me = place[2]
-    rows = lax.broadcasted_iota(jnp.int32, (length, length), 0)
-    cols = lax.broadcasted_iota(jnp.int32, (length, length), 1)
-    causal = jnp.concatenate([rows >= cols] * heads, axis=0)
-    peak = None
-    for place_in, distance in enumerate(order):
-        part = mm_nt(absorbed[...], latents[place_in][...])
-        allowed = causal if distance == 0 else (me ^ distance) < me
-        part = jnp.where(allowed, part, -1e30)
-        scores[:, place_in * length : (place_in + 1) * length] = part
-        top = jnp.max(part, axis=-1, keepdims=True)
-        peak = top if peak is None else jnp.maximum(peak, top)
-    total = None
-    for place_in in range(len(order)):
-        weights = jnp.exp(scores[:, place_in * length : (place_in + 1) * length] - peak)
-        added = jnp.sum(weights, axis=-1, keepdims=True)
-        share = mm(weights, latents[place_in][...])
-        if total is None:
-            total = added
-            mixed[...] = share
-        else:
-            total = total + added
-            mixed[...] += share
-    for head in range(heads):
-        own = slice(head * length, (head + 1) * length)
-        value = slice((heads + head) * DH, (heads + head + 1) * DH)
-        spread = (mixed[own, :] / total[own, :]).astype(bf16)
-        out[:, head * DH : (head + 1) * DH] = jnp.dot(
-            spread, up[:, value], preferred_element_type=f32
-        ).astype(bf16)
+    for position in range(len(order)):
+        latents[position * length : (position + 1) * length, :] = blocks[position][...]
+    group = 2 if heads % 2 == 0 else 1
+    rows = lax.broadcasted_iota(jnp.int32, (group * length, length), 0) % length
+    cols = lax.broadcasted_iota(jnp.int32, (group * length, length), 1)
+    allowed = [rows >= cols] + [(me ^ distance) < me for distance in order[1:]]
+    for first in range(0, heads, group):
+        own = slice(first * length, (first + group) * length)
+        scores = mm_nt(absorbed[own, :], latents[...])
+        parts = [
+            jnp.where(allowed[p], scores[:, p * length : (p + 1) * length], -1e30)
+            for p in range(len(order))
+        ]
+        peak = jnp.max(functools.reduce(jnp.maximum, parts), axis=-1, keepdims=True)
+        weights = [jnp.exp(part - peak) for part in parts]
+        total = jnp.sum(functools.reduce(jnp.add, weights), axis=-1, keepdims=True)
+        mixed = mm(jnp.concatenate([w.astype(bf16) for w in weights], axis=1), latents[...])
+        spread = (mixed / total).astype(bf16)
+        for i in range(group):
+            head = first + i
+            value = slice((heads + head) * DH, (heads + head + 1) * DH)
+            out[:, head * DH : (head + 1) * DH] = jnp.dot(
+                spread[i * length : (i + 1) * length], up[:, value], preferred_element_type=f32
+            ).astype(bf16)
 
 
 def far_first(count):
@@ -418,21 +422,31 @@
         copies=3,
     )
     map_shape = (2 * DK + EXTRA, DK)
-    kept, sent, reads, intra = call(
-        functools.partial(local_kernel, heads),
+    arguments = [place, inputs, halo, logs, beta.T, taps]
+    kept, sent, solutions, shrunk = call(
+        map_kernel,
         [
             ((pairs,) + map_shape, bf16),
             ((pairs,) + map_shape, bf16),
-            ((length, heads * DK), bf16),
-            ((length, heads * DK), f32),
+            ((heads, length, 2 * DK), bf16),
+            ((heads, 2, length, DK), bf16),
         ],
-        [place, inputs, halo, logs, beta.T, taps],
-        [((3, length + 8, heads * DK), f32), ((heads,) + map_shape, bf16)],
+        arguments,
+        [((heads, 2, length + 8, DK), f32)],
         16,
-        cost=6.0,
+        cost=5.0,
     )
 
     got = trade(sent, "ctx", 1, heads)
+    got_kept = trade(kept, "ctx", 1, heads)
+    reads, intra = call(
+        read_kernel,
+        [((length, heads * DK), bf16), ((length, heads * DK), f32)],
+        arguments + [solutions, shrunk],
+        [((heads, length + 8, DK), f32)],
+        16,
+        cost=2.0,
+    )
     chip_maps = call(
         functools.partial(compose_kernel, pairs),
         [(map_shape, bf16)] * pairs,
@@ -445,7 +459,7 @@
         moved = {step: trade(pieces[step], "ctx", 2 * step, heads) for step in far_first(pairs)}
         return [pieces[0]] + [moved[step] for step in range(1, pairs)]
 
-    chip_maps = across_chips(chip_maps)
+    chip_maps, reads, intra = lax.optimization_barrier((across_chips(chip_maps), reads, intra))
     state_outs = [((DK, DK), bf16)] * pairs
     scratch = [((pairs,) + map_shape, bf16), ((pairs, DK, DK), bf16)]
     if groups == 1:
@@ -470,19 +484,13 @@
         start = lax.fori_loop(0, groups - 1, relay, jnp.zeros((DK, DK), f32))
         starts = run(start)[:pairs]
     starts = across_chips(starts)
-    mine, other = call(
-        functools.partial(share_kernel, pairs),
-        [((pairs, DK, DK), bf16)] * 2,
-        [place, kept, got] + starts,
-        limit=8,
-    )
-    other = trade(other, "ctx", 1, heads)
+    others = [trade(state, "ctx", 1, heads) for state in starts]
 
     share = length // parts
     partials = call(
         functools.partial(project_kernel, parts),
         [((share, width), f32)] + [((share, width), bf16)] * (parts - 1),
-        [place, residual, kda_out_weight, reads, intra, mine, other],
+        [place, residual, kda_out_weight, reads, intra, got, got_kept] + starts + others,
         [((length, heads * DK), bf16), ((length, width), f32)],
         16,
     )
@@ -492,17 +500,23 @@
         return [pieces[0]] + [moved[step] for step in range(1, parts)]
 
     partials = across_heads(partials)
-    stream_rows, latent_rows = call(
+    latent_width = latent_weight.shape[1]
+    stream_rows, latent_rows, together = call(
         functools.partial(latent_kernel, parts),
-        [((share, width), bf16), ((share, latent_weight.shape[1]), bf16)],
+        [
+            ((share, width), bf16),
+            ((share, latent_width), bf16),
+            ((share, width + latent_width), bf16),
+        ],
         [norm_gain[None], latent_weight, latent_gain[None]] + partials,
         limit=16,
     )
-    latent_parts = across_heads([latent_rows] * parts)
-    stream_parts = across_heads([stream_rows] * parts)
+    latent_parts = across_heads([latent_rows, together] + [latent_rows] * (parts - 2))
+    far_parts = [trade(stream_rows, "head", step, parts) for step in range(2, parts)]
+    stream_parts = [stream_rows, latent_parts[1]] + far_parts
     latent = call(
         functools.partial(join_kernel, parts),
-        [((length, latent_weight.shape[1]), bf16)],
+        [((length, latent_width), bf16)],
         [place] + latent_parts,
         limit=8,
     )[0]
@@ -511,9 +525,6 @@
     for step in far_first(count // 2):
         order.append(2 * step)
         latents.append(trade(latent, "ctx", 2 * step, count))
-    for position in range(len(order)):
-        order.append(order[position] + 1)
-        latents.append(trade(latents[position], "ctx", 1, 2))
     up = up_weight.reshape(up_weight.shape[0], -1)
     heads_mla = query_weight.shape[1] // DH
     stream_out, absorbed = call(
@@ -522,15 +533,17 @@
         [place, norm_gain[None], query_weight, up] + stream_parts,
         limit=16,
     )
+    latents, absorbed = lax.optimization_barrier((latents, absorbed))
+    for position in range(len(order)):
+        order.append(order[position] + 1)
+        latents.append(trade(latents[position], "ctx", 1, 2))
     attention_out = call(
         functools.partial(attend_kernel, tuple(order)),
         [((length, heads_mla * DH), bf16)],
         [place, absorbed, up] + latents,
-        [
-            ((heads_mla * length, count * length), f32),
-            ((heads_mla * length, up.shape[0]), f32),
-        ],
-        12 + count * length * heads_mla * length * 8 // MIB,
+        [((count * length, up.shape[0]), bf16)],
+        12 + count * length * length * 24 // MIB,
+        cost=4.0,
     )[0]
     return (stream_out, attention_out)
 

time: 80.4 us -> 77.5 us (0.964); the launches traced: 80.1 us -> 76.2 us
  starting transfers between devices: 28.2 us -> 26.4 us
  waiting for transfers between devices: 29.6 us -> 27.9 us
    ppermute x24 -> x27, starting transfers between devices: 27.7 us -> 25.9 us  [trade(): return lax.ppermute(block, axis, route)]
    ppermute x24 -> x27, waiting for transfers between devices: 28 us -> 26.2 us  [trade(): return lax.ppermute(block, axis, route)]
  transfers between devices with their start and end apart: 25 -> 28, of which waited for: 15 -> 16; matrix products, arithmetic and copies ran while one was open for 0% -> 0% of each run, Pallas kernels for 3% -> 8%
where the time goes in v3:
time: 77.5 us; the launch traced here: 76.2 us
  waiting for transfers between devices  27.9 us (36%)
  starting transfers between devices  26.4 us (34%)
  Pallas kernels  16.9 us (22%)
  local copies, waits for them, and re-layouts  4.17 us (5%)
  between operations  0.85 us (1%)
    ppermute x27, waiting for transfers between devices, trade(): return lax.ppermute(block, axis, route)  26.2 us
    ppermute x27, starting transfers between devices, trade(): return lax.ppermute(block, axis, route)  25.9 us
    pallas_call x10, Pallas kernels, call(): pl.pallas_call(kernel, out_shape=[jax.ShapeDtypeStruct(shape, dtype) for...  16.9 us
    unnamed x25, local copies, waits for them, and re-layouts  3.25 us
    ppermute x1, waiting for transfers between devices, passed_along(): lax.ppermute(block, axis, [(i, (i + distance) % count) for i in range(cou...  1.64 us
  transfers between devices with their start and end apart: 28, of which 16 were waited for; matrix products, arithmetic and copies ran while one was open for 0% of the time, Pallas kernels for 8%

profile of v3, /device:TPU:0, one launch (start us, length us, event | category | flops | bytes accessed | tf_op | source)
XLA Modules:
  0.0 76.2 jit_solution(3059460749628390648)
XLA Ops:
  0.6 0.9 %slice.3 = bf16[3,16,1024]{2,1,0:T(8,128)(2,1)S(1)} slice(bf16[3,128,1024]{2,1,0:T(8,128)(2,1)} %stored_inputs.1), slice={[0:3], [112:128], [0:1024]} | slice | bytes 196608 | tf_op jit(solution)/shard_map/slice | solution.py:414
  1.5 0.5 collective-permute-start
  2.1 1.1 %copy-done.2 = bf16[3,128,1024]{2,1,0:T(8,128)(2,1)S(1)} copy-done((bf16[3,128,1024]{2,1,0:T(8,128)(2,1)S(1)}, bf16[3,128,1024]{2,1,0:T(8,128)(2,1)}, u32[]{:S(2)}) %copy-start.2) | copy-done | bytes 786456
  3.2 1.0 %copy-done.4 = f32[128,1024]{1,0:T(8,128)S(1)} copy-done((f32[128,1024]{1,0:T(8,128)S(1)}, f32[128,1024]{1,0:T(8,128)}, u32[]{:S(2)}) %copy-start.4) | copy-done | bytes 524312
  4.3 0.8 %copy-done.5 = f32[3,4,1024]{2,1,0:T(4,128)S(1)} copy-done((f32[3,4,1024]{2,1,0:T(4,128)S(1)}, f32[3,4,1024]{2,1,0:T(4,128)}, u32[]{:S(2)}) %copy-start.5) | copy-done | bytes 49176
  5.1 0.5 shard_map.122
  5.5 1.6 %collective-permute-done.halo = bf16[3,16,1024]{2,1,0:T(8,128)(2,1)S(1)} collective-permute-done((bf16[3,16,1024]{2,1,0:T(8,128)(2,1)S(1)}, bf16[3,16,1024]{2,1,0:T(8,128)(2,1)S(1)}, u32[]{:S(2)}, u32[]{:S(2)}) %collective-permute-start) | collective-permute-done | bytes 98336 | tf_op jit(solution)/shard_map/ppermute | solution.py:73
  7.2 4.2 %shard_map.123 = (bf16[4,272,128]{2,1,0:T(8,128)(2,1)S(1)}, bf16[4,272,128]{2,1,0:T(8,128)(2,1)S(1)}, bf16[8,128,256]{2,1,0:T(8,128)(2,1)S(1)}, bf16[8,2,128,128]{3,2,1,0:T(8,128)(2,1)S(1)}) custom-call(s32[3]{0:T(128)S(1)} %pad_add_fusion.place.refs_0_, bf16[3,128,1024]{2,1,0:T(8,128)(2,1)S(1)} %get-tuple-element.39.inputs, ...), custom_call_target="tpu_custom_call" | custom-call | flops 5000000000 | tf_op jit(solution)/shard_map/pallas_call | solution.py:45
  11.4 1.0 %collective-permute-start.1 = (bf16[4,272,128]{2,1,0:T(8,128)(2,1)S(1)}, bf16[4,272,128]{2,1,0:T(8,128)(2,1)S(1)}, u32[]{:S(2)}, u32[]{:S(2)}) collective-permute-start(bf16[4,272,128]{2,1,0:T(8,128)(2,1)S(1)} %get-tuple-element.43), channel_id=1, source_target_pairs={{0,4},{4,0},{8,12},{12,8},{16,20},{20,16},{24,28},{28,24},{1,5},{5... | collective-permute-start | bytes 835592 | tf_op jit(solution)/shard_map/ppermute | solution.py:68
  12.5 1.1 %collective-permute-done.1.got.refs_5_ = bf16[4,272,128]{2,1,0:T(8,128)(2,1)S(1)} collective-permute-done((bf16[4,272,128]{2,1,0:T(8,128)(2,1)S(1)}, bf16[4,272,128]{2,1,0:T(8,128)(2,1)S(1)}, u32[]{:S(2)}, u32[]{:S(2)}) %collective-permute-start.1) | collective-permute-done | bytes 278560 | tf_op jit(solution)/shard_map/ppermute | solution.py:68
  13.6 0.8 %shard_map.124 = (bf16[272,128]{1,0:T(8,128)(2,1)S(1)}, bf16[272,128]{1,0:T(8,128)(2,1)S(1)}, bf16[272,128]{1,0:T(8,128)(2,1)S(1)}, bf16[272,128]{1,0:T(8,128)(2,1)S(1)}) custom-call(s32[3]{0:T(128)S(1)} %pad_add_fusion.place.refs_0_, bf16[4,272,128]{2,1,0:T(8,128)(2,1)S(1)} %get-tuple-element.42.kept, ...), custom_call_target="tpu_custom_call" | custom-call | flops 1000000000 | tf_op jit(solution)/shard_map/pallas_call | solution.py:45
  14.5 1.6 %collective-permute-start.2 = (bf16[272,128]{1,0:T(8,128)(2,1)S(1)}, bf16[272,128]{1,0:T(8,128)(2,1)S(1)}, u32[]{:S(2)}, u32[]{:S(2)}) collective-permute-start(bf16[272,128]{1,0:T(8,128)(2,1)S(1)} %get-tuple-element.45), channel_id=1, source_target_pairs={{0,8},{4,12},{8,0},{12,4},{16,24},{20,28},{24,16},{28,20},{1,9},{5... | collective-permute-start | bytes 208904 | tf_op jit(solution)/shard_map/ppermute | solution.py:68
  16.1 0.7 collective-permute-start.3
  16.8 1.3 %collective-permute-start.4 = (bf16[272,128]{1,0:T(8,128)(2,1)S(1)}, bf16[272,128]{1,0:T(8,128)(2,1)S(1)}, u32[]{:S(2)}, u32[]{:S(2)}) collective-permute-start(bf16[272,128]{1,0:T(8,128)(2,1)S(1)} %get-tuple-element.47), channel_id=1, source_target_pairs={{0,24},{4,28},{8,16},{12,20},{16,8},{20,12},{24,0},{28,4},{1,25},{... | collective-permute-start | bytes 208904 | tf_op jit(solution)/shard_map/ppermute | solution.py:68
  18.1 2.0 %shard_map.125 = (bf16[128,1024]{1,0:T(8,128)(2,1)S(1)}, f32[128,1024]{1,0:T(8,128)S(1)}) custom-call(s32[3]{0:T(128)S(1)} %pad_add_fusion.place.refs_0_, bf16[3,128,1024]{2,1,0:T(8,128)(2,1)S(1)} %get-tuple-element.39.inputs, bf16[3,16,1024]{2,1,0:T(8,128)(2,1)S(1)} %collective-permute-done.halo, f32[128,1024]{1,0:T(8,128)S(1)} %get-tuple-element.40.logs, ...), custom_call_target="tpu_custom_call" | custom-call | flops 2000000000 | tf_op jit(solution)/shard_map/pallas_call | solution.py:45
  20.1 1.1 %collective-permute-done.3.refs_3_ = bf16[272,128]{1,0:T(8,128)(2,1)S(1)} collective-permute-done((bf16[272,128]{1,0:T(8,128)(2,1)S(1)}, bf16[272,128]{1,0:T(8,128)(2,1)S(1)}, u32[]{:S(2)}, u32[]{:S(2)}) %collective-permute-start.3) | collective-permute-done | bytes 69664 | tf_op jit(solution)/shard_map/ppermute | solution.py:68
  21.1 0.9 %collective-permute-done.4.refs_4_ = bf16[272,128]{1,0:T(8,128)(2,1)S(1)} collective-permute-done((bf16[272,128]{1,0:T(8,128)(2,1)S(1)}, bf16[272,128]{1,0:T(8,128)(2,1)S(1)}, u32[]{:S(2)}, u32[]{:S(2)}) %collective-permute-start.4) | collective-permute-done | bytes 69664 | tf_op jit(solution)/shard_map/ppermute | solution.py:68
  22.0 0.8 %shard_map.126 = (bf16[128,128]{1,0:T(8,128)(2,1)S(1)}, bf16[128,128]{1,0:T(8,128)(2,1)S(1)}, bf16[128,128]{1,0:T(8,128)(2,1)S(1)}, bf16[128,128]{1,0:T(8,128)(2,1)S(1)}) custom-call(s32[3]{0:T(128)S(1)} %pad_add_fusion.place.refs_0_, bf16[272,128]{1,0:T(8,128)(2,1)S(1)} %get-tuple-element.54.refs_1_, bf16[272,128]{1,0:T(8,128)(2,1)S(1)} %collective-permute-done.2.refs_2_, ...), custom_call_target="tpu_custom_call" | custom-call | flops 1000000000 | tf_op jit(solution)/shard_map/pallas_call | solution.py:45
  22.9 1.5 %collective-permute-start.6 = (bf16[128,128]{1,0:T(8,128)(2,1)S(1)}, bf16[128,128]{1,0:T(8,128)(2,1)S(1)}, u32[]{:S(2)}, u32[]{:S(2)}) collective-permute-start(bf16[128,128]{1,0:T(8,128)(2,1)S(1)} %get-tuple-element.59), channel_id=1, source_target_pairs={{0,8},{4,12},{8,0},{12,4},{16,24},{20,28},{24,16},{28,20},{1,9},{5... | collective-permute-start | bytes 98312 | tf_op jit(solution)/shard_map/ppermute | solution.py:68
  24.4 0.6 collective-permute-start.7
  25.0 1.4 %collective-permute-start.8 = (bf16[128,128]{1,0:T(8,128)(2,1)S(1)}, bf16[128,128]{1,0:T(8,128)(2,1)S(1)}, u32[]{:S(2)}, u32[]{:S(2)}) collective-permute-start(bf16[128,128]{1,0:T(8,128)(2,1)S(1)} %get-tuple-element.61), channel_id=1, source_target_pairs={{0,24},{4,28},{8,16},{12,20},{16,8},{20,12},{24,0},{28,4},{1,25},{... | collective-permute-start | bytes 98312 | tf_op jit(solution)/shard_map/ppermute | solution.py:68
  26.4 0.7 collective-permute-done.6.refs_8_
  27.1 1.2 %collective-permute-done.7.refs_9_ = bf16[128,128]{1,0:T(8,128)(2,1)S(1)} collective-permute-done((bf16[128,128]{1,0:T(8,128)(2,1)S(1)}, bf16[128,128]{1,0:T(8,128)(2,1)S(1)}, u32[]{:S(2)}, u32[]{:S(2)}) %collective-permute-start.7) | collective-permute-done | bytes 32800 | tf_op jit(solution)/shard_map/ppermute | solution.py:68
  28.3 1.5 %collective-permute-done.8.refs_10_ = bf16[128,128]{1,0:T(8,128)(2,1)S(1)} collective-permute-done((bf16[128,128]{1,0:T(8,128)(2,1)S(1)}, bf16[128,128]{1,0:T(8,128)(2,1)S(1)}, u32[]{:S(2)}, u32[]{:S(2)}) %collective-permute-start.8) | collective-permute-done | bytes 32800 | tf_op jit(solution)/shard_map/ppermute | solution.py:68
  29.8 1.2 %collective-permute-done.12.refs_14_ = bf16[128,128]{1,0:T(8,128)(2,1)S(1)} collective-permute-done((bf16[128,128]{1,0:T(8,128)(2,1)S(1)}, bf16[128,128]{1,0:T(8,128)(2,1)S(1)}, u32[]{:S(2)}, u32[]{:S(2)}) %collective-permute-start.12) | collective-permute-done | bytes 32800 | tf_op jit(solution)/shard_map/ppermute | solution.py:68
  31.0 2.5 %shard_map.127 = (f32[32,2304]{1,0:T(8,128)S(1)}, bf16[32,2304]{1,0:T(8,128)(2,1)S(1)}, bf16[32,2304]{1,0:T(8,128)(2,1)S(1)}, bf16[32,2304]{1,0:T(8,128)(2,1)S(1)}) custom-call(s32[3]{0:T(128)S(1)} %pad_add_fusion.place.refs_0_, bf16[128,2304]{1,0:T(8,128)(2,1)S(1)} %copy-done.1, bf16[1024,2304]{1,0:T(8,128)(2,1)S(1)} %bitcast.8, ...), custom_call_target="tpu_custom_call" | custom-call | flops 1000000000 | tf_op jit(solution)/shard_map/pallas_call | solution.py:45
  33.5 1.6 %collective-permute-start.13 = (bf16[32,2304]{1,0:T(8,128)(2,1)S(1)}, bf16[32,2304]{1,0:T(8,128)(2,1)S(1)}, u32[]{:S(2)}, u32[]{:S(2)}) collective-permute-start(bf16[32,2304]{1,0:T(8,128)(2,1)S(1)} %get-tuple-element.63), channel_id=1, source_target_pairs={{0,1},{1,0},{2,3},{3,2},{4,5},{5,4},{6,7},{7,6},{8,9},{9,8},{10,11... | collective-permute-start | bytes 442376 | tf_op jit(solution)/shard_map/ppermute | solution.py:68
  35.2 2.6 %collective-permute-start.14 = (bf16[32,2304]{1,0:T(8,128)(2,1)S(1)}, bf16[32,2304]{1,0:T(8,128)(2,1)S(1)}, u32[]{:S(2)}, u32[]{:S(2)}) collective-permute-start(bf16[32,2304]{1,0:T(8,128)(2,1)S(1)} %get-tuple-element.64), channel_id=1, source_target_pairs={{0,2},{1,3},{2,0},{3,1},{4,6},{5,7},{6,4},{7,5},{8,10},{9,11},{10,... | collective-permute-start | bytes 442376 | tf_op jit(solution)/shard_map/ppermute | solution.py:68
  38.0 3.9 %collective-permute-done.13.refs_4_ = bf16[32,2304]{1,0:T(8,128)(2,1)S(1)} collective-permute-done((bf16[32,2304]{1,0:T(8,128)(2,1)S(1)}, bf16[32,2304]{1,0:T(8,128)(2,1)S(1)}, u32[]{:S(2)}, u32[]{:S(2)}) %collective-permute-start.13) | collective-permute-done | bytes 147488 | tf_op jit(solution)/shard_map/ppermute | solution.py:68
  41.9 7.2 %collective-permute-done.14.refs_5_ = bf16[32,2304]{1,0:T(8,128)(2,1)S(1)} collective-permute-done((bf16[32,2304]{1,0:T(8,128)(2,1)S(1)}, bf16[32,2304]{1,0:T(8,128)(2,1)S(1)}, u32[]{:S(2)}, u32[]{:S(2)}) %collective-permute-start.14) | collective-permute-done | bytes 147488 | tf_op jit(solution)/shard_map/ppermute | solution.py:68
  49.1 0.8 shard_map.128
  49.9 2.7 %collective-permute-start.16 = (bf16[32,2816]{1,0:T(8,128)(2,1)S(1)}, bf16[32,2816]{1,0:T(8,128)(2,1)S(1)}, u32[]{:S(2)}, u32[]{:S(2)}) collective-permute-start(bf16[32,2816]{1,0:T(8,128)(2,1)S(1)} %get-tuple-element.67), channel_id=1, source_target_pairs={{0,1},{1,0},{2,3},{3,2},{4,5},{5,4},{6,7},{7,6},{8,9},{9,8},{10,11... | collective-permute-start | bytes 540680 | tf_op jit(solution)/shard_map/ppermute | solution.py:68
  52.6 1.1 %collective-permute-start.19 = (bf16[32,512]{1,0:T(8,128)(2,1)S(1)}, bf16[32,512]{1,0:T(8,128)(2,1)S(1)}, u32[]{:S(2)}, u32[]{:S(2)}) collective-permute-start(bf16[32,512]{1,0:T(8,128)(2,1)S(1)} %get-tuple-element.69.refs_1_), channel_id=1, source_target_pairs={{0,2},{1,3},{2,0},{3,1},{4,6},{5,7},{6,4},{7,5},{8,10},{9,11},{10,... | collective-permute-start | bytes 98312 | tf_op jit(solution)/shard_map/ppermute | solution.py:68
  53.7 1.4 %collective-permute-start.20 = (bf16[32,512]{1,0:T(8,128)(2,1)S(1)}, bf16[32,512]{1,0:T(8,128)(2,1)S(1)}, u32[]{:S(2)}, u32[]{:S(2)}) collective-permute-start(bf16[32,512]{1,0:T(8,128)(2,1)S(1)} %get-tuple-element.69.refs_1_), channel_id=1, source_target_pairs={{0,3},{1,2},{2,1},{3,0},{4,7},{5,6},{6,5},{7,4},{8,11},{9,10},{10,... | collective-permute-start | bytes 98312 | tf_op jit(solution)/shard_map/ppermute | solution.py:68
  55.1 2.0 %collective-permute-start.17 = (bf16[32,2304]{1,0:T(8,128)(2,1)S(1)}, bf16[32,2304]{1,0:T(8,128)(2,1)S(1)}, u32[]{:S(2)}, u32[]{:S(2)}) collective-permute-start(bf16[32,2304]{1,0:T(8,128)(2,1)S(1)} %get-tuple-element.66.refs_4_), channel_id=1, source_target_pairs={{0,2},{1,3},{2,0},{3,1},{4,6},{5,7},{6,4},{7,5},{8,10},{9,11},{10,... | collective-permute-start | bytes 442376 | tf_op jit(solution)/shard_map/ppermute | solution.py:68
  57.1 1.3 %collective-permute-start.18 = (bf16[32,2304]{1,0:T(8,128)(2,1)S(1)}, bf16[32,2304]{1,0:T(8,128)(2,1)S(1)}, u32[]{:S(2)}, u32[]{:S(2)}) collective-permute-start(bf16[32,2304]{1,0:T(8,128)(2,1)S(1)} %get-tuple-element.66.refs_4_), channel_id=1, source_target_pairs={{0,3},{1,2},{2,1},{3,0},{4,7},{5,6},{6,5},{7,4},{8,11},{9,10},{10,... | collective-permute-start | bytes 442376 | tf_op jit(solution)/shard_map/ppermute | solution.py:68
  58.5 3.6 %collective-permute-done.20.refs_4_ = bf16[32,512]{1,0:T(8,128)(2,1)S(1)} collective-permute-done((bf16[32,512]{1,0:T(8,128)(2,1)S(1)}, bf16[32,512]{1,0:T(8,128)(2,1)S(1)}, u32[]{:S(2)}, u32[]{:S(2)}) %collective-permute-start.20) | collective-permute-done | bytes 32800 | tf_op jit(solution)/shard_map/ppermute | solution.py:68
  62.1 0.6 shard_map.130.refs_3_
  62.6 1.5 %collective-permute-start.21 = (bf16[128,512]{1,0:T(8,128)(2,1)S(1)}, bf16[128,512]{1,0:T(8,128)(2,1)S(1)}, u32[]{:S(2)}, u32[]{:S(2)}) collective-permute-start(bf16[128,512]{1,0:T(8,128)(2,1)S(1)} %shard_map.130.refs_3_), channel_id=1, source_target_pairs={{0,24},{4,28},{8,16},{12,20},{16,8},{20,12},{24,0},{28,4},{1,25},{... | collective-permute-start | bytes 393224 | tf_op jit(solution)/shard_map/ppermute | solution.py:68
  64.2 1.3 %collective-permute-start.22 = (bf16[128,512]{1,0:T(8,128)(2,1)S(1)}, bf16[128,512]{1,0:T(8,128)(2,1)S(1)}, u32[]{:S(2)}, u32[]{:S(2)}) collective-permute-start(bf16[128,512]{1,0:T(8,128)(2,1)S(1)} %shard_map.130.refs_3_), channel_id=1, source_target_pairs={{0,16},{4,20},{8,24},{12,28},{16,0},{20,4},{24,8},{28,12},{1,17},{... | collective-permute-start | bytes 393224 | tf_op jit(solution)/shard_map/ppermute | solution.py:68
  65.5 0.8 collective-permute-start.23
  66.5 2.9 %collective-permute-done.17.refs_6_ = bf16[32,2304]{1,0:T(8,128)(2,1)S(1)} collective-permute-done((bf16[32,2304]{1,0:T(8,128)(2,1)S(1)}, bf16[32,2304]{1,0:T(8,128)(2,1)S(1)}, u32[]{:S(2)}, u32[]{:S(2)}) %collective-permute-start.17) | collective-permute-done | bytes 147488 | tf_op jit(solution)/shard_map/ppermute | solution.py:68
  69.3 1.5 %shard_map.129 = (bf16[128,2304]{1,0:T(8,128)(2,1)}, bf16[512,512]{1,0:T(8,128)(2,1)S(1)}) custom-call(s32[3]{0:T(128)S(1)} %pad_add_fusion.place.refs_0_, f32[1,2304]{1,0:T(1,128)S(1)} %broadcast_in_dim.7.refs_0_.refs_1_, bf16[2304,512]{1,0:T(8,128)(2,1)S(1)} %copy-done, bf16[512,1024]{1,0:T(8,128)(2,1)S(1)} %bitcast.9, ...), custom_call_target="tpu_custom_call" | custom-call | flops 1000000000 | tf_op jit(solution)/shard_map/pallas_call | solution.py:45
  70.9 0.5 collective-permute-start.25
  71.5 0.4 collective-permute-start.27
  71.9 0.3 collective-permute-done.24.refs_7_
  72.4 0.3 collective-permute-done.26.refs_9_
  72.9 3.3 %shard_map.131 = bf16[128,512]{1,0:T(8,128)(2,1)} custom-call(s32[3]{0:T(128)S(1)} %pad_add_fusion.place.refs_0_, bf16[512,512]{1,0:T(8,128)(2,1)S(1)} %get-tuple-element.71.refs_1_, bf16[512,1024]{1,0:T(8,128)(2,1)S(1)} %bitcast.10, bf16[128,512]{1,0:T(8,128)(2,1)S(1)} %shard_map.130.refs_3_, bf16[128,512]{1,0:T(8,128)(2,1)S(1)} %collective-permute-done.21.refs_4_, ...), custom_call_target="tpu_custom_call" | custom-call | flops 4000000000 | tf_op jit(solution)/shard_map/pallas_call | solution.py:45
  (47 shorter events, 1.2 us)
Async XLA Ops:
  0.6 6.6 %copy-start.6 = (f32[128,8]{0,1:T(8,128)S(1)}, f32[128,8]{0,1:T(8,128)}, u32[]{:S(2)}) copy-start(f32[128,8]{0,1:T(8,128)} %param.13) | copy-start | bytes 12292
  1.5 5.6 %collective-permute-start = (bf16[3,16,1024]{2,1,0:T(8,128)(2,1)S(1)}, bf16[3,16,1024]{2,1,0:T(8,128)(2,1)S(1)}, u32[]{:S(2)}, u32[]{:S(2)}) collective-permute-start(bf16[3,16,1024]{2,1,0:T(8,128)(2,1)S(1)} %slice.3), channel_id=1, source_target_pairs={{0,4},{4,8},{8,12},{12,16},{16,20},{20,24},{24,28},{28,0},{1,5},{5... | collective-permute-start | bytes 294920 | tf_op jit(solution)/shard_map/ppermute | solution.py:73
  2.1 1.1 %copy-start.2 = (bf16[3,128,1024]{2,1,0:T(8,128)(2,1)S(1)}, bf16[3,128,1024]{2,1,0:T(8,128)(2,1)}, u32[]{:S(2)}) copy-start(bf16[3,128,1024]{2,1,0:T(8,128)(2,1)} %stored_inputs.1) | copy-start | bytes 2359300
  3.2 1.0 %copy-start.4 = (f32[128,1024]{1,0:T(8,128)S(1)}, f32[128,1024]{1,0:T(8,128)}, u32[]{:S(2)}) copy-start(f32[128,1024]{1,0:T(8,128)} %stored_gate.1) | copy-start | bytes 1572868
  4.3 0.8 %copy-start.5 = (f32[3,4,1024]{2,1,0:T(4,128)S(1)}, f32[3,4,1024]{2,1,0:T(4,128)}, u32[]{:S(2)}) copy-start(f32[3,4,1024]{2,1,0:T(4,128)} %stored_taps.1) | copy-start | bytes 147460
  11.4 2.2 %collective-permute-start.1 = (bf16[4,272,128]{2,1,0:T(8,128)(2,1)S(1)}, bf16[4,272,128]{2,1,0:T(8,128)(2,1)S(1)}, u32[]{:S(2)}, u32[]{:S(2)}) collective-permute-start(bf16[4,272,128]{2,1,0:T(8,128)(2,1)S(1)} %get-tuple-element.43), channel_id=1, source_target_pairs={{0,4},{4,0},{8,12},{12,8},{16,20},{20,16},{24,28},{28,24},{1,5},{5... | collective-permute-start | bytes 835592 | tf_op jit(solution)/shard_map/ppermute | solution.py:68
  12.5 17.3 %collective-permute-start.5 = (bf16[4,272,128]{2,1,0:T(8,128)(2,1)S(1)}, bf16[4,272,128]{2,1,0:T(8,128)(2,1)S(1)}, u32[]{:S(2)}, u32[]{:S(2)}) collective-permute-start(bf16[4,272,128]{2,1,0:T(8,128)(2,1)S(1)} %get-tuple-element.42.kept), channel_id=1, source_target_pairs={{0,4},{4,0},{8,12},{12,8},{16,20},{20,16},{24,28},{28,24},{1,5},{5... | collective-permute-start | bytes 835592 | tf_op jit(solution)/shard_map/ppermute | solution.py:68
  14.5 5.5 %collective-permute-start.2 = (bf16[272,128]{1,0:T(8,128)(2,1)S(1)}, bf16[272,128]{1,0:T(8,128)(2,1)S(1)}, u32[]{:S(2)}, u32[]{:S(2)}) collective-permute-start(bf16[272,128]{1,0:T(8,128)(2,1)S(1)} %get-tuple-element.45), channel_id=1, source_target_pairs={{0,8},{4,12},{8,0},{12,4},{16,24},{20,28},{24,16},{28,20},{1,9},{5... | collective-permute-start | bytes 208904 | tf_op jit(solution)/shard_map/ppermute | solution.py:68
  16.1 5.1 %collective-permute-start.3 = (bf16[272,128]{1,0:T(8,128)(2,1)S(1)}, bf16[272,128]{1,0:T(8,128)(2,1)S(1)}, u32[]{:S(2)}, u32[]{:S(2)}) collective-permute-start(bf16[272,128]{1,0:T(8,128)(2,1)S(1)} %get-tuple-element.46), channel_id=1, source_target_pairs={{0,16},{4,20},{8,24},{12,28},{16,0},{20,4},{24,8},{28,12},{1,17},{... | collective-permute-start | bytes 208904 | tf_op jit(solution)/shard_map/ppermute | solution.py:68
  16.8 5.2 %collective-permute-start.4 = (bf16[272,128]{1,0:T(8,128)(2,1)S(1)}, bf16[272,128]{1,0:T(8,128)(2,1)S(1)}, u32[]{:S(2)}, u32[]{:S(2)}) collective-permute-start(bf16[272,128]{1,0:T(8,128)(2,1)S(1)} %get-tuple-element.47), channel_id=1, source_target_pairs={{0,24},{4,28},{8,16},{12,20},{16,8},{20,12},{24,0},{28,4},{1,25},{... | collective-permute-start | bytes 208904 | tf_op jit(solution)/shard_map/ppermute | solution.py:68
  18.1 12.9 %slice-start = ((s8[4718592]{0:T(1024)(128)(4,1)}), s8[4194304]{0:T(1024)(128)(4,1)S(1)}, s32[]{:S(2)}) async-start(s8[4718592]{0:T(1024)(128)(4,1)} %bitcast.7), calls=%async_computation | async-start | bytes 8388608
  18.1 12.9 %slice-start.1 = ((s8[4718592]{0:T(1024)(128)(4,1)}), s8[524288]{0:T(1024)(128)(4,1)S(1)}, s32[]{:S(2)}) async-start(s8[4718592]{0:T(1024)(128)(4,1)} %bitcast.7), calls=%async_computation.1 | async-start | bytes 1048576
  20.0 11.0 %copy-start.1 = (bf16[128,2304]{1,0:T(8,128)(2,1)S(1)}, bf16[128,2304]{1,0:T(8,128)(2,1)}, u32[]{:S(2)}) copy-start(bf16[128,2304]{1,0:T(8,128)(2,1)} %refs_1_.2) | copy-start | bytes 1769476
  22.9 4.2 %collective-permute-start.6 = (bf16[128,128]{1,0:T(8,128)(2,1)S(1)}, bf16[128,128]{1,0:T(8,128)(2,1)S(1)}, u32[]{:S(2)}, u32[]{:S(2)}) collective-permute-start(bf16[128,128]{1,0:T(8,128)(2,1)S(1)} %get-tuple-element.59), channel_id=1, source_target_pairs={{0,8},{4,12},{8,0},{12,4},{16,24},{20,28},{24,16},{28,20},{1,9},{5... | collective-permute-start | bytes 98312 | tf_op jit(solution)/shard_map/ppermute | solution.py:68
  24.4 3.9 %collective-permute-start.7 = (bf16[128,128]{1,0:T(8,128)(2,1)S(1)}, bf16[128,128]{1,0:T(8,128)(2,1)S(1)}, u32[]{:S(2)}, u32[]{:S(2)}) collective-permute-start(bf16[128,128]{1,0:T(8,128)(2,1)S(1)} %get-tuple-element.60), channel_id=1, source_target_pairs={{0,16},{4,20},{8,24},{12,28},{16,0},{20,4},{24,8},{28,12},{1,17},{... | collective-permute-start | bytes 98312 | tf_op jit(solution)/shard_map/ppermute | solution.py:68
  25.0 4.8 %collective-permute-start.8 = (bf16[128,128]{1,0:T(8,128)(2,1)S(1)}, bf16[128,128]{1,0:T(8,128)(2,1)S(1)}, u32[]{:S(2)}, u32[]{:S(2)}) collective-permute-start(bf16[128,128]{1,0:T(8,128)(2,1)S(1)} %get-tuple-element.61), channel_id=1, source_target_pairs={{0,24},{4,28},{8,16},{12,20},{16,8},{20,12},{24,0},{28,4},{1,25},{... | collective-permute-start | bytes 98312 | tf_op jit(solution)/shard_map/ppermute | solution.py:68
  26.4 11.6 %copy-start.9 = (f32[2304]{0:T(1024)S(1)}, f32[2304]{0:T(1024)}, u32[]{:S(2)}) copy-start(f32[2304]{0:T(1024)} %param.17) | copy-start | bytes 27652
  26.4 22.7 %copy-start.3 = (bf16[2304,512]{1,0:T(8,128)(2,1)S(1)}, bf16[2304,512]{1,0:T(8,128)(2,1)}, u32[]{:S(2)}) copy-start(bf16[2304,512]{1,0:T(8,128)(2,1)} %refs_1_.3) | copy-start | bytes 7077892
  26.4 22.7 %copy-start.7 = (f32[512]{0:T(512)S(1)}, f32[512]{0:T(512)}, u32[]{:S(2)}) copy-start(f32[512]{0:T(512)} %param.19) | copy-start | bytes 6148
  26.4 3.4 %collective-permute-start.9 = (bf16[128,128]{1,0:T(8,128)(2,1)S(1)}, bf16[128,128]{1,0:T(8,128)(2,1)S(1)}, u32[]{:S(2)}, u32[]{:S(2)}) collective-permute-start(bf16[128,128]{1,0:T(8,128)(2,1)S(1)} %get-tuple-element.58.refs_7_), channel_id=1, source_target_pairs={{0,4},{4,0},{8,12},{12,8},{16,20},{20,16},{24,28},{28,24},{1,5},{5... | collective-permute-start | bytes 98312 | tf_op jit(solution)/shard_map/ppermute | solution.py:68
  27.1 2.7 %collective-permute-start.10 = (bf16[128,128]{1,0:T(8,128)(2,1)S(1)}, bf16[128,128]{1,0:T(8,128)(2,1)S(1)}, u32[]{:S(2)}, u32[]{:S(2)}) collective-permute-start(bf16[128,128]{1,0:T(8,128)(2,1)S(1)} %collective-permute-done.6.refs_8_), channel_id=1, source_target_pairs={{0,4},{4,0},{8,12},{12,8},{16,20},{20,16},{24,28},{28,24},{1,5},{5... | collective-permute-start | bytes 98312 | tf_op jit(solution)/shard_map/ppermute | solution.py:68
  28.3 1.5 %collective-permute-start.11 = (bf16[128,128]{1,0:T(8,128)(2,1)S(1)}, bf16[128,128]{1,0:T(8,128)(2,1)S(1)}, u32[]{:S(2)}, u32[]{:S(2)}) collective-permute-start(bf16[128,128]{1,0:T(8,128)(2,1)S(1)} %collective-permute-done.7.refs_9_), channel_id=1, source_target_pairs={{0,4},{4,0},{8,12},{12,8},{16,20},{20,16},{24,28},{28,24},{1,5},{5... | collective-permute-start | bytes 98312 | tf_op jit(solution)/shard_map/ppermute | solution.py:68
  29.8 1.2 %collective-permute-start.12 = (bf16[128,128]{1,0:T(8,128)(2,1)S(1)}, bf16[128,128]{1,0:T(8,128)(2,1)S(1)}, u32[]{:S(2)}, u32[]{:S(2)}) collective-permute-start(bf16[128,128]{1,0:T(8,128)(2,1)S(1)} %collective-permute-done.8.refs_10_), channel_id=1, source_target_pairs={{0,4},{4,0},{8,12},{12,8},{16,20},{20,16},{24,28},{28,24},{1,5},{5... | collective-permute-start | bytes 98312 | tf_op jit(solution)/shard_map/ppermute | solution.py:68
  33.5 8.4 %collective-permute-start.13 = (bf16[32,2304]{1,0:T(8,128)(2,1)S(1)}, bf16[32,2304]{1,0:T(8,128)(2,1)S(1)}, u32[]{:S(2)}, u32[]{:S(2)}) collective-permute-start(bf16[32,2304]{1,0:T(8,128)(2,1)S(1)} %get-tuple-element.63), channel_id=1, source_target_pairs={{0,1},{1,0},{2,3},{3,2},{4,5},{5,4},{6,7},{7,6},{8,9},{9,8},{10,11... | collective-permute-start | bytes 442376 | tf_op jit(solution)/shard_map/ppermute | solution.py:68
  35.2 14.0 %collective-permute-start.14 = (bf16[32,2304]{1,0:T(8,128)(2,1)S(1)}, bf16[32,2304]{1,0:T(8,128)(2,1)S(1)}, u32[]{:S(2)}, u32[]{:S(2)}) collective-permute-start(bf16[32,2304]{1,0:T(8,128)(2,1)S(1)} %get-tuple-element.64), channel_id=1, source_target_pairs={{0,2},{1,3},{2,0},{3,1},{4,6},{5,7},{6,4},{7,5},{8,10},{9,11},{10,... | collective-permute-start | bytes 442376 | tf_op jit(solution)/shard_map/ppermute | solution.py:68
  37.7 11.4 %collective-permute-start.15 = (bf16[32,2304]{1,0:T(8,128)(2,1)S(1)}, bf16[32,2304]{1,0:T(8,128)(2,1)S(1)}, u32[]{:S(2)}, u32[]{:S(2)}) collective-permute-start(bf16[32,2304]{1,0:T(8,128)(2,1)S(1)} %get-tuple-element.65), channel_id=1, source_target_pairs={{0,3},{1,2},{2,1},{3,0},{4,7},{5,6},{6,5},{7,4},{8,11},{9,10},{10,... | collective-permute-start | bytes 442376 | tf_op jit(solution)/shard_map/ppermute | solution.py:68
  49.9 16.3 %copy-start.8 = (bf16[512,2,512]{2,1,0:T(2,128)(2,1)S(1)}, bf16[512,2,512]{2,1,0:T(2,128)(2,1)}, u32[]{:S(2)}) copy-start(bf16[512,2,512]{2,1,0:T(2,128)(2,1)} %param.21) | copy-start | bytes 3145732
  49.9 12.2 %collective-permute-start.16 = (bf16[32,2816]{1,0:T(8,128)(2,1)S(1)}, bf16[32,2816]{1,0:T(8,128)(2,1)S(1)}, u32[]{:S(2)}, u32[]{:S(2)}) collective-permute-start(bf16[32,2816]{1,0:T(8,128)(2,1)S(1)} %get-tuple-element.67), channel_id=1, source_target_pairs={{0,1},{1,0},{2,3},{3,2},{4,5},{5,4},{6,7},{7,6},{8,9},{9,8},{10,11... | collective-permute-start | bytes 540680 | tf_op jit(solution)/shard_map/ppermute | solution.py:68
  52.6 5.9 %collective-permute-start.19 = (bf16[32,512]{1,0:T(8,128)(2,1)S(1)}, bf16[32,512]{1,0:T(8,128)(2,1)S(1)}, u32[]{:S(2)}, u32[]{:S(2)}) collective-permute-start(bf16[32,512]{1,0:T(8,128)(2,1)S(1)} %get-tuple-element.69.refs_1_), channel_id=1, source_target_pairs={{0,2},{1,3},{2,0},{3,1},{4,6},{5,7},{6,4},{7,5},{8,10},{9,11},{10,... | collective-permute-start | bytes 98312 | tf_op jit(solution)/shard_map/ppermute | solution.py:68
  53.7 8.4 %collective-permute-start.20 = (bf16[32,512]{1,0:T(8,128)(2,1)S(1)}, bf16[32,512]{1,0:T(8,128)(2,1)S(1)}, u32[]{:S(2)}, u32[]{:S(2)}) collective-permute-start(bf16[32,512]{1,0:T(8,128)(2,1)S(1)} %get-tuple-element.69.refs_1_), channel_id=1, source_target_pairs={{0,3},{1,2},{2,1},{3,0},{4,7},{5,6},{6,5},{7,4},{8,11},{9,10},{10,... | collective-permute-start | bytes 98312 | tf_op jit(solution)/shard_map/ppermute | solution.py:68
  55.1 14.2 %copy-start = (bf16[2304,512]{1,0:T(8,128)(2,1)S(1)}, bf16[2304,512]{1,0:T(8,128)(2,1)}, u32[]{:S(2)}) copy-start(bf16[2304,512]{1,0:T(8,128)(2,1)} %refs_2_.3) | copy-start | bytes 7077892
  55.1 14.2 %collective-permute-start.17 = (bf16[32,2304]{1,0:T(8,128)(2,1)S(1)}, bf16[32,2304]{1,0:T(8,128)(2,1)S(1)}, u32[]{:S(2)}, u32[]{:S(2)}) collective-permute-start(bf16[32,2304]{1,0:T(8,128)(2,1)S(1)} %get-tuple-element.66.refs_4_), channel_id=1, source_target_pairs={{0,2},{1,3},{2,0},{3,1},{4,6},{5,7},{6,4},{7,5},{8,10},{9,11},{10,... | collective-permute-start | bytes 442376 | tf_op jit(solution)/shard_map/ppermute | solution.py:68
  57.1 12.2 %collective-permute-start.18 = (bf16[32,2304]{1,0:T(8,128)(2,1)S(1)}, bf16[32,2304]{1,0:T(8,128)(2,1)S(1)}, u32[]{:S(2)}, u32[]{:S(2)}) collective-permute-start(bf16[32,2304]{1,0:T(8,128)(2,1)S(1)} %get-tuple-element.66.refs_4_), channel_id=1, source_target_pairs={{0,3},{1,2},{2,1},{3,0},{4,7},{5,6},{6,5},{7,4},{8,11},{9,10},{10,... | collective-permute-start | bytes 442376 | tf_op jit(solution)/shard_map/ppermute | solution.py:68
  62.6 8.1 %collective-permute-start.21 = (bf16[128,512]{1,0:T(8,128)(2,1)S(1)}, bf16[128,512]{1,0:T(8,128)(2,1)S(1)}, u32[]{:S(2)}, u32[]{:S(2)}) collective-permute-start(bf16[128,512]{1,0:T(8,128)(2,1)S(1)} %shard_map.130.refs_3_), channel_id=1, source_target_pairs={{0,24},{4,28},{8,16},{12,20},{16,8},{20,12},{24,0},{28,4},{1,25},{... | collective-permute-start | bytes 393224 | tf_op jit(solution)/shard_map/ppermute | solution.py:68
  64.2 6.6 %collective-permute-start.22 = (bf16[128,512]{1,0:T(8,128)(2,1)S(1)}, bf16[128,512]{1,0:T(8,128)(2,1)S(1)}, u32[]{:S(2)}, u32[]{:S(2)}) collective-permute-start(bf16[128,512]{1,0:T(8,128)(2,1)S(1)} %shard_map.130.refs_3_), channel_id=1, source_target_pairs={{0,16},{4,20},{8,24},{12,28},{16,0},{20,4},{24,8},{28,12},{1,17},{... | collective-permute-start | bytes 393224 | tf_op jit(solution)/shard_map/ppermute | solution.py:68
  65.5 5.4 %collective-permute-start.23 = (bf16[128,512]{1,0:T(8,128)(2,1)S(1)}, bf16[128,512]{1,0:T(8,128)(2,1)S(1)}, u32[]{:S(2)}, u32[]{:S(2)}) collective-permute-start(bf16[128,512]{1,0:T(8,128)(2,1)S(1)} %shard_map.130.refs_3_), channel_id=1, source_target_pairs={{0,8},{4,12},{8,0},{12,4},{16,24},{20,28},{24,16},{28,20},{1,9},{5... | collective-permute-start | bytes 393224 | tf_op jit(solution)/shard_map/ppermute | solution.py:68
  70.8 1.4 %collective-permute-start.24 = (bf16[128,512]{1,0:T(8,128)(2,1)S(1)}, bf16[128,512]{1,0:T(8,128)(2,1)S(1)}, u32[]{:S(2)}, u32[]{:S(2)}) collective-permute-start(bf16[128,512]{1,0:T(8,128)(2,1)S(1)} %shard_map.130.refs_3_), channel_id=1, source_target_pairs={{0,4},{4,0},{8,12},{12,8},{16,20},{20,16},{24,28},{28,24},{1,5},{5... | collective-permute-start | bytes 393224 | tf_op jit(solution)/shard_map/ppermute | solution.py:68
  70.9 1.5 %collective-permute-start.25 = (bf16[128,512]{1,0:T(8,128)(2,1)S(1)}, bf16[128,512]{1,0:T(8,128)(2,1)S(1)}, u32[]{:S(2)}, u32[]{:S(2)}) collective-permute-start(bf16[128,512]{1,0:T(8,128)(2,1)S(1)} %collective-permute-done.21.refs_4_), channel_id=1, source_target_pairs={{0,4},{4,0},{8,12},{12,8},{16,20},{20,16},{24,28},{28,24},{1,5},{5... | collective-permute-start | bytes 393224 | tf_op jit(solution)/shard_map/ppermute | solution.py:68
  71.4 1.3 %collective-permute-start.26 = (bf16[128,512]{1,0:T(8,128)(2,1)S(1)}, bf16[128,512]{1,0:T(8,128)(2,1)S(1)}, u32[]{:S(2)}, u32[]{:S(2)}) collective-permute-start(bf16[128,512]{1,0:T(8,128)(2,1)S(1)} %collective-permute-done.22.refs_5_), channel_id=1, source_target_pairs={{0,4},{4,0},{8,12},{12,8},{16,20},{20,16},{24,28},{28,24},{1,5},{5... | collective-permute-start | bytes 393224 | tf_op jit(solution)/shard_map/ppermute | solution.py:68
  71.5 1.5 %collective-permute-start.27 = (bf16[128,512]{1,0:T(8,128)(2,1)S(1)}, bf16[128,512]{1,0:T(8,128)(2,1)S(1)}, u32[]{:S(2)}, u32[]{:S(2)}) collective-permute-start(bf16[128,512]{1,0:T(8,128)(2,1)S(1)} %collective-permute-done.23.refs_6_), channel_id=1, source_target_pairs={{0,4},{4,0},{8,12},{12,8},{16,20},{20,16},{24,28},{28,24},{1,5},{5... | collective-permute-start | bytes 393224 | tf_op jit(solution)/shard_map/ppermute | solution.py:68

commit v4 on v3

--- a/solution.py
+++ b/solution.py
@@ -202,11 +202,15 @@
     )
 
 
-def read_kernel(place, inputs, halo, logs, beta, taps, solutions, shrunk, reads, intra, wide):
+def read_kernel(
+    place, inputs, halo, logs, beta, taps, solutions, shrunk, stay, go, reads, intra, wide
+):
     length = logs.shape[0]
+    pairs = stay.shape[0]
+    _, core = split_cores(place)
     rows = lax.broadcasted_iota(jnp.int32, (length, length), 0)
     cols = lax.broadcasted_iota(jnp.int32, (length, length), 1)
-    for i, head in enumerate(side_heads(place, solutions.shape[0] // 2)):
+    for i, head in enumerate(side_heads(place, pairs)):
         lane = lanes(head)
         put_wide(wide.at[i], place, inputs, halo, lane, 0)
         query = unit(convolved(wide.at[i], taps, lane, 0)) * DK ** (-0.5)
@@ -219,8 +223,12 @@
         rate_row = beta[pl.ds(head, 1), :]
         mixing = jnp.where(rows >= cols, jnp.concatenate(products, axis=0) * rate_row, 0.0)
         mixes = mm(mixing, solutions[i])
-        intra[:, lane] = mixes[:, :DK]
-        reads[:, lane] = (query * jnp.exp(log) - mixes[:, DK:]).astype(bf16)
+        read = query * jnp.exp(log) - mixes[:, DK:]
+        offset, move, decay = parts_of((stay if i < pairs else go)[i % pairs])
+        both = mm_nt(read, jnp.concatenate([offset, move], axis=0))
+        second = core == 1
+        intra[:, lane] = mixes[:, :DK] + jnp.where(second, both[:, :DK], 0.0)
+        reads[:, lane] = jnp.where(second, read * decay - both[:, DK:], read).astype(bf16)
 
 
 def parts_of(state_map):
@@ -279,20 +287,18 @@
 
 
 def project_kernel(parts, *refs):
-    place, residual, weight, reads, intra, stay, go = refs[:7]
-    refs = refs[7:]
-    pairs = stay.shape[0]
+    place, residual, weight, reads, intra = refs[:5]
+    refs = refs[5:]
+    pairs = reads.shape[1] // DK // 2
     mine, other, refs = refs[:pairs], refs[pairs : 2 * pairs], refs[2 * pairs :]
     outs, (whole, summed) = refs[:parts], refs[parts:]
     chip, core = split_cores(place)
     head_me = place[1]
     for step in range(pairs):
         pair = partner(chip, step, pairs)
-        for states, maps, side in ((mine, stay, core), (other, go, 1 - core)):
+        for states, side in ((mine, core), (other, 1 - core)):
             own = lanes(2 * pair + side)
-            state = states[step][...]
-            state = jnp.where(core == 0, state, apply_map(state, maps[pair]).astype(bf16))
-            whole[:, own] = (intra[:, own] + mm_nt(reads[:, own], state)).astype(bf16)
+            whole[:, own] = (intra[:, own] + mm_nt(reads[:, own], states[step][...])).astype(bf16)
     summed[...] = jnp.dot(whole[...], weight[...], preferred_element_type=f32)
     share = summed.shape[0] // parts
     for step in range(parts):
@@ -362,7 +368,7 @@
     me = place[2]
     for position in range(len(order)):
         latents[position * length : (position + 1) * length, :] = blocks[position][...]
-    group = 2 if heads % 2 == 0 else 1
+    group = heads
     rows = lax.broadcasted_iota(jnp.int32, (group * length, length), 0) % length
     cols = lax.broadcasted_iota(jnp.int32, (group * length, length), 1)
     allowed = [rows >= cols] + [(me ^ distance) < me for distance in order[1:]]
@@ -442,10 +448,10 @@
     reads, intra = call(
         read_kernel,
         [((length, heads * DK), bf16), ((length, heads * DK), f32)],
-        arguments + [solutions, shrunk],
+        arguments + [solutions, shrunk, got, got_kept],
         [((heads, length + 8, DK), f32)],
         16,
-        cost=2.0,
+        cost=2.5,
     )
     chip_maps = call(
         functools.partial(compose_kernel, pairs),
@@ -490,7 +496,7 @@
     partials = call(
         functools.partial(project_kernel, parts),
         [((share, width), f32)] + [((share, width), bf16)] * (parts - 1),
-        [place, residual, kda_out_weight, reads, intra, got, got_kept] + starts + others,
+        [place, residual, kda_out_weight, reads, intra] + starts + others,
         [((length, heads * DK), bf16), ((length, width), f32)],
         16,
     )
@@ -512,7 +518,10 @@
         limit=16,
     )
     latent_parts = across_heads([latent_rows, together] + [latent_rows] * (parts - 2))
-    far_parts = [trade(stream_rows, "head", step, parts) for step in range(2, parts)]
+    far_parts = []
+    for step in range(2, parts, 2):
+        far_parts.append(trade(stream_rows, "head", step, parts))
+        far_parts.append(trade(far_parts[-1], "head", 1, parts))
     stream_parts = [stream_rows, latent_parts[1]] + far_parts
     latent = call(
         functools.partial(join_kernel, parts),
@@ -525,6 +534,9 @@
     for step in far_first(count // 2):
         order.append(2 * step)
         latents.append(trade(latent, "ctx", 2 * step, count))
+    for position in range(len(order)):
+        order.append(order[position] + 1)
+        latents.append(trade(latents[position], "ctx", 1, 2))
     up = up_weight.reshape(up_weight.shape[0], -1)
     heads_mla = query_weight.shape[1] // DH
     stream_out, absorbed = call(
@@ -533,10 +545,6 @@
         [place, norm_gain[None], query_weight, up] + stream_parts,
         limit=16,
     )
-    latents, absorbed = lax.optimization_barrier((latents, absorbed))
-    for position in range(len(order)):
-        order.append(order[position] + 1)
-        latents.append(trade(latents[position], "ctx", 1, 2))
     attention_out = call(
         functools.partial(attend_kernel, tuple(order)),
         [((length, heads_mla * DH), bf16)],

time: 77.5 us -> 75 us (0.968); the launches traced: 76.2 us -> 74.7 us
  starting transfers between devices: 26.4 us -> 24.2 us
    ppermute x27, starting transfers between devices: 25.9 us -> 23.8 us  [trade(): return lax.ppermute(block, axis, route)]
where the time goes in v4:
time: 75 us; the launch traced here: 74.7 us
  waiting for transfers between devices  28.6 us (38%)
  starting transfers between devices  24.2 us (32%)
  Pallas kernels  16.8 us (22%)
  local copies, waits for them, and re-layouts  4.17 us (6%)
  between operations  0.84 us (1%)
    ppermute x27, waiting for transfers between devices, trade(): return lax.ppermute(block, axis, route)  27 us
    ppermute x27, starting transfers between devices, trade(): return lax.ppermute(block, axis, route)  23.8 us
    pallas_call x10, Pallas kernels, call(): pl.pallas_call(kernel, out_shape=[jax.ShapeDtypeStruct(shape, dtype) for...  16.8 us
    unnamed x25, local copies, waits for them, and re-layouts  3.25 us
    ppermute x1, waiting for transfers between devices, passed_along(): lax.ppermute(block, axis, [(i, (i + distance) % count) for i in range(cou...  1.64 us
  transfers between devices with their start and end apart: 28, of which 16 were waited for; matrix products, arithmetic and copies ran while one was open for 0% of the time, Pallas kernels for 8%

profile of v4, /device:TPU:0, one launch (start us, length us, event | category | flops | bytes accessed | tf_op | source)
XLA Modules:
  0.0 74.7 jit_solution(15957770271007354152)
XLA Ops:
  0.6 0.9 %slice.3 = bf16[3,16,1024]{2,1,0:T(8,128)(2,1)S(1)} slice(bf16[3,128,1024]{2,1,0:T(8,128)(2,1)} %stored_inputs.1), slice={[0:3], [112:128], [0:1024]} | slice | bytes 196608 | tf_op jit(solution)/shard_map/slice | solution.py:420
  1.5 0.5 collective-permute-start
  2.1 1.1 %copy-done.2 = bf16[3,128,1024]{2,1,0:T(8,128)(2,1)S(1)} copy-done((bf16[3,128,1024]{2,1,0:T(8,128)(2,1)S(1)}, bf16[3,128,1024]{2,1,0:T(8,128)(2,1)}, u32[]{:S(2)}) %copy-start.2) | copy-done | bytes 786456
  3.2 1.0 %copy-done.4 = f32[128,1024]{1,0:T(8,128)S(1)} copy-done((f32[128,1024]{1,0:T(8,128)S(1)}, f32[128,1024]{1,0:T(8,128)}, u32[]{:S(2)}) %copy-start.4) | copy-done | bytes 524312
  4.3 0.8 %copy-done.5 = f32[3,4,1024]{2,1,0:T(4,128)S(1)} copy-done((f32[3,4,1024]{2,1,0:T(4,128)S(1)}, f32[3,4,1024]{2,1,0:T(4,128)}, u32[]{:S(2)}) %copy-start.5) | copy-done | bytes 49176
  5.1 0.5 shard_map.122
  5.5 1.6 %collective-permute-done.halo = bf16[3,16,1024]{2,1,0:T(8,128)(2,1)S(1)} collective-permute-done((bf16[3,16,1024]{2,1,0:T(8,128)(2,1)S(1)}, bf16[3,16,1024]{2,1,0:T(8,128)(2,1)S(1)}, u32[]{:S(2)}, u32[]{:S(2)}) %collective-permute-start) | collective-permute-done | bytes 98336 | tf_op jit(solution)/shard_map/ppermute | solution.py:73
  7.2 4.2 %shard_map.123 = (bf16[4,272,128]{2,1,0:T(8,128)(2,1)S(1)}, bf16[4,272,128]{2,1,0:T(8,128)(2,1)S(1)}, bf16[8,128,256]{2,1,0:T(8,128)(2,1)S(1)}, bf16[8,2,128,128]{3,2,1,0:T(8,128)(2,1)S(1)}) custom-call(s32[3]{0:T(128)S(1)} %pad_add_fusion.place.refs_0_, bf16[3,128,1024]{2,1,0:T(8,128)(2,1)S(1)} %get-tuple-element.34.inputs, ...), custom_call_target="tpu_custom_call" | custom-call | flops 5000000000 | tf_op jit(solution)/shard_map/pallas_call | solution.py:45
  11.4 1.0 %collective-permute-start.1 = (bf16[4,272,128]{2,1,0:T(8,128)(2,1)S(1)}, bf16[4,272,128]{2,1,0:T(8,128)(2,1)S(1)}, u32[]{:S(2)}, u32[]{:S(2)}) collective-permute-start(bf16[4,272,128]{2,1,0:T(8,128)(2,1)S(1)} %get-tuple-element.38), channel_id=1, source_target_pairs={{0,4},{4,0},{8,12},{12,8},{16,20},{20,16},{24,28},{28,24},{1,5},{5... | collective-permute-start | bytes 835592 | tf_op jit(solution)/shard_map/ppermute | solution.py:68
  12.5 1.1 %collective-permute-done.1.got.stay = bf16[4,272,128]{2,1,0:T(8,128)(2,1)S(1)} collective-permute-done((bf16[4,272,128]{2,1,0:T(8,128)(2,1)S(1)}, bf16[4,272,128]{2,1,0:T(8,128)(2,1)S(1)}, u32[]{:S(2)}, u32[]{:S(2)}) %collective-permute-start.1) | collective-permute-done | bytes 278560 | tf_op jit(solution)/shard_map/ppermute | solution.py:68
  13.6 0.8 %shard_map.124 = (bf16[272,128]{1,0:T(8,128)(2,1)S(1)}, bf16[272,128]{1,0:T(8,128)(2,1)S(1)}, bf16[272,128]{1,0:T(8,128)(2,1)S(1)}, bf16[272,128]{1,0:T(8,128)(2,1)S(1)}) custom-call(s32[3]{0:T(128)S(1)} %pad_add_fusion.place.refs_0_, bf16[4,272,128]{2,1,0:T(8,128)(2,1)S(1)} %get-tuple-element.37.kept, bf16[4,272,128]{2,1,0:T(8,128)(2,1)S(1)} %collective-permute-done.1.got.stay), custom_call_target="tpu_custom_call" | custom-call | flops 1000000000 | tf_op jit(solution)/shard_map/pallas_call | solution.py:45
  14.5 1.6 %collective-permute-start.2 = (bf16[272,128]{1,0:T(8,128)(2,1)S(1)}, bf16[272,128]{1,0:T(8,128)(2,1)S(1)}, u32[]{:S(2)}, u32[]{:S(2)}) collective-permute-start(bf16[272,128]{1,0:T(8,128)(2,1)S(1)} %get-tuple-element.40), channel_id=1, source_target_pairs={{0,8},{4,12},{8,0},{12,4},{16,24},{20,28},{24,16},{28,20},{1,9},{5... | collective-permute-start | bytes 208904 | tf_op jit(solution)/shard_map/ppermute | solution.py:68
  16.1 0.7 collective-permute-start.3
  16.8 1.3 %collective-permute-start.4 = (bf16[272,128]{1,0:T(8,128)(2,1)S(1)}, bf16[272,128]{1,0:T(8,128)(2,1)S(1)}, u32[]{:S(2)}, u32[]{:S(2)}) collective-permute-start(bf16[272,128]{1,0:T(8,128)(2,1)S(1)} %get-tuple-element.42), channel_id=1, source_target_pairs={{0,24},{4,28},{8,16},{12,20},{16,8},{20,12},{24,0},{28,4},{1,25},{... | collective-permute-start | bytes 208904 | tf_op jit(solution)/shard_map/ppermute | solution.py:68
  18.1 2.9 %shard_map.125 = (bf16[128,1024]{1,0:T(8,128)(2,1)S(1)}, f32[128,1024]{1,0:T(8,128)S(1)}) custom-call(s32[3]{0:T(128)S(1)} %pad_add_fusion.place.refs_0_, bf16[3,128,1024]{2,1,0:T(8,128)(2,1)S(1)} %get-tuple-element.34.inputs, bf16[3,16,1024]{2,1,0:T(8,128)(2,1)S(1)} %collective-permute-done.halo, f32[128,1024]{1,0:T(8,128)S(1)} %get-tuple-element.35.logs, ...), custom_call_target="tpu_custom_call" | custom-call | flops 2500000000 | tf_op jit(solution)/shard_map/pallas_call | solution.py:45
  21.1 0.9 %collective-permute-done.4.refs_4_ = bf16[272,128]{1,0:T(8,128)(2,1)S(1)} collective-permute-done((bf16[272,128]{1,0:T(8,128)(2,1)S(1)}, bf16[272,128]{1,0:T(8,128)(2,1)S(1)}, u32[]{:S(2)}, u32[]{:S(2)}) %collective-permute-start.4) | collective-permute-done | bytes 69664 | tf_op jit(solution)/shard_map/ppermute | solution.py:68
  22.0 0.8 %shard_map.126 = (bf16[128,128]{1,0:T(8,128)(2,1)S(1)}, bf16[128,128]{1,0:T(8,128)(2,1)S(1)}, bf16[128,128]{1,0:T(8,128)(2,1)S(1)}, bf16[128,128]{1,0:T(8,128)(2,1)S(1)}) custom-call(s32[3]{0:T(128)S(1)} %pad_add_fusion.place.refs_0_, bf16[272,128]{1,0:T(8,128)(2,1)S(1)} %get-tuple-element.49.refs_1_, bf16[272,128]{1,0:T(8,128)(2,1)S(1)} %collective-permute-done.2.refs_2_, ...), custom_call_target="tpu_custom_call" | custom-call | flops 1000000000 | tf_op jit(solution)/shard_map/pallas_call | solution.py:45
  22.9 1.5 %collective-permute-start.6 = (bf16[128,128]{1,0:T(8,128)(2,1)S(1)}, bf16[128,128]{1,0:T(8,128)(2,1)S(1)}, u32[]{:S(2)}, u32[]{:S(2)}) collective-permute-start(bf16[128,128]{1,0:T(8,128)(2,1)S(1)} %get-tuple-element.54), channel_id=1, source_target_pairs={{0,8},{4,12},{8,0},{12,4},{16,24},{20,28},{24,16},{28,20},{1,9},{5... | collective-permute-start | bytes 98312 | tf_op jit(solution)/shard_map/ppermute | solution.py:68
  24.4 0.6 collective-permute-start.7
  25.0 1.4 %collective-permute-start.8 = (bf16[128,128]{1,0:T(8,128)(2,1)S(1)}, bf16[128,128]{1,0:T(8,128)(2,1)S(1)}, u32[]{:S(2)}, u32[]{:S(2)}) collective-permute-start(bf16[128,128]{1,0:T(8,128)(2,1)S(1)} %get-tuple-element.56), channel_id=1, source_target_pairs={{0,24},{4,28},{8,16},{12,20},{16,8},{20,12},{24,0},{28,4},{1,25},{... | collective-permute-start | bytes 98312 | tf_op jit(solution)/shard_map/ppermute | solution.py:68
  26.4 0.7 collective-permute-done.6.refs_6_
  27.1 1.2 %collective-permute-done.7.refs_7_ = bf16[128,128]{1,0:T(8,128)(2,1)S(1)} collective-permute-done((bf16[128,128]{1,0:T(8,128)(2,1)S(1)}, bf16[128,128]{1,0:T(8,128)(2,1)S(1)}, u32[]{:S(2)}, u32[]{:S(2)}) %collective-permute-start.7) | collective-permute-done | bytes 32800 | tf_op jit(solution)/shard_map/ppermute | solution.py:68
  28.3 1.5 %collective-permute-done.8.refs_8_ = bf16[128,128]{1,0:T(8,128)(2,1)S(1)} collective-permute-done((bf16[128,128]{1,0:T(8,128)(2,1)S(1)}, bf16[128,128]{1,0:T(8,128)(2,1)S(1)}, u32[]{:S(2)}, u32[]{:S(2)}) %collective-permute-start.8) | collective-permute-done | bytes 32800 | tf_op jit(solution)/shard_map/ppermute | solution.py:68
  29.8 1.2 %collective-permute-done.12.refs_12_ = bf16[128,128]{1,0:T(8,128)(2,1)S(1)} collective-permute-done((bf16[128,128]{1,0:T(8,128)(2,1)S(1)}, bf16[128,128]{1,0:T(8,128)(2,1)S(1)}, u32[]{:S(2)}, u32[]{:S(2)}) %collective-permute-start.12) | collective-permute-done | bytes 32800 | tf_op jit(solution)/shard_map/ppermute | solution.py:68
  31.0 1.8 %shard_map.127 = (f32[32,2304]{1,0:T(8,128)S(1)}, bf16[32,2304]{1,0:T(8,128)(2,1)S(1)}, bf16[32,2304]{1,0:T(8,128)(2,1)S(1)}, bf16[32,2304]{1,0:T(8,128)(2,1)S(1)}) custom-call(s32[3]{0:T(128)S(1)} %pad_add_fusion.place.refs_0_, bf16[128,2304]{1,0:T(8,128)(2,1)S(1)} %copy-done.1, bf16[1024,2304]{1,0:T(8,128)(2,1)S(1)} %bitcast.8, ...), custom_call_target="tpu_custom_call" | custom-call | flops 1000000000 | tf_op jit(solution)/shard_map/pallas_call | solution.py:45
  32.8 1.6 %collective-permute-start.13 = (bf16[32,2304]{1,0:T(8,128)(2,1)S(1)}, bf16[32,2304]{1,0:T(8,128)(2,1)S(1)}, u32[]{:S(2)}, u32[]{:S(2)}) collective-permute-start(bf16[32,2304]{1,0:T(8,128)(2,1)S(1)} %get-tuple-element.58), channel_id=1, source_target_pairs={{0,1},{1,0},{2,3},{3,2},{4,5},{5,4},{6,7},{7,6},{8,9},{9,8},{10,11... | collective-permute-start | bytes 442376 | tf_op jit(solution)/shard_map/ppermute | solution.py:68
  34.5 2.6 %collective-permute-start.14 = (bf16[32,2304]{1,0:T(8,128)(2,1)S(1)}, bf16[32,2304]{1,0:T(8,128)(2,1)S(1)}, u32[]{:S(2)}, u32[]{:S(2)}) collective-permute-start(bf16[32,2304]{1,0:T(8,128)(2,1)S(1)} %get-tuple-element.59), channel_id=1, source_target_pairs={{0,2},{1,3},{2,0},{3,1},{4,6},{5,7},{6,4},{7,5},{8,10},{9,11},{10,... | collective-permute-start | bytes 442376 | tf_op jit(solution)/shard_map/ppermute | solution.py:68
  37.1 0.2 collective-permute-start.15
  37.3 3.9 %collective-permute-done.13.refs_4_ = bf16[32,2304]{1,0:T(8,128)(2,1)S(1)} collective-permute-done((bf16[32,2304]{1,0:T(8,128)(2,1)S(1)}, bf16[32,2304]{1,0:T(8,128)(2,1)S(1)}, u32[]{:S(2)}, u32[]{:S(2)}) %collective-permute-start.13) | collective-permute-done | bytes 147488 | tf_op jit(solution)/shard_map/ppermute | solution.py:68
  41.2 7.2 %collective-permute-done.14.refs_5_ = bf16[32,2304]{1,0:T(8,128)(2,1)S(1)} collective-permute-done((bf16[32,2304]{1,0:T(8,128)(2,1)S(1)}, bf16[32,2304]{1,0:T(8,128)(2,1)S(1)}, u32[]{:S(2)}, u32[]{:S(2)}) %collective-permute-start.14) | collective-permute-done | bytes 147488 | tf_op jit(solution)/shard_map/ppermute | solution.py:68
  48.4 0.8 %shard_map.128 = (bf16[32,2304]{1,0:T(8,128)(2,1)S(1)}, bf16[32,512]{1,0:T(8,128)(2,1)S(1)}, bf16[32,2816]{1,0:T(8,128)(2,1)S(1)}) custom-call(f32[1,2304]{1,0:T(1,128)S(1)} %broadcast_in_dim.7.refs_0_.refs_1_, bf16[2304,512]{1,0:T(8,128)(2,1)S(1)} %copy-done.3, f32[1,512]{1,0:T(1,128)S(1)} %bitcast.13, f32[32,2304]{1,0:T(8,128)S(1)} %get-tuple-element.57.refs_3_, ...), custom_call_target="tpu_custom_call" | custom-call | flops 1000000000 | tf_op jit(solution)/shard_map/pallas_call | solution.py:45
  49.2 2.7 %collective-permute-start.16 = (bf16[32,2816]{1,0:T(8,128)(2,1)S(1)}, bf16[32,2816]{1,0:T(8,128)(2,1)S(1)}, u32[]{:S(2)}, u32[]{:S(2)}) collective-permute-start(bf16[32,2816]{1,0:T(8,128)(2,1)S(1)} %get-tuple-element.62), channel_id=1, source_target_pairs={{0,1},{1,0},{2,3},{3,2},{4,5},{5,4},{6,7},{7,6},{8,9},{9,8},{10,11... | collective-permute-start | bytes 540680 | tf_op jit(solution)/shard_map/ppermute | solution.py:68
  51.9 1.1 %collective-permute-start.19 = (bf16[32,512]{1,0:T(8,128)(2,1)S(1)}, bf16[32,512]{1,0:T(8,128)(2,1)S(1)}, u32[]{:S(2)}, u32[]{:S(2)}) collective-permute-start(bf16[32,512]{1,0:T(8,128)(2,1)S(1)} %get-tuple-element.65.refs_1_), channel_id=1, source_target_pairs={{0,2},{1,3},{2,0},{3,1},{4,6},{5,7},{6,4},{7,5},{8,10},{9,11},{10,... | collective-permute-start | bytes 98312 | tf_op jit(solution)/shard_map/ppermute | solution.py:68
  53.0 1.4 %collective-permute-start.20 = (bf16[32,512]{1,0:T(8,128)(2,1)S(1)}, bf16[32,512]{1,0:T(8,128)(2,1)S(1)}, u32[]{:S(2)}, u32[]{:S(2)}) collective-permute-start(bf16[32,512]{1,0:T(8,128)(2,1)S(1)} %get-tuple-element.65.refs_1_), channel_id=1, source_target_pairs={{0,3},{1,2},{2,1},{3,0},{4,7},{5,6},{6,5},{7,4},{8,11},{9,10},{10,... | collective-permute-start | bytes 98312 | tf_op jit(solution)/shard_map/ppermute | solution.py:68
  54.4 2.0 %collective-permute-start.17 = (bf16[32,2304]{1,0:T(8,128)(2,1)S(1)}, bf16[32,2304]{1,0:T(8,128)(2,1)S(1)}, u32[]{:S(2)}, u32[]{:S(2)}) collective-permute-start(bf16[32,2304]{1,0:T(8,128)(2,1)S(1)} %get-tuple-element.61.refs_4_), channel_id=1, source_target_pairs={{0,2},{1,3},{2,0},{3,1},{4,6},{5,7},{6,4},{7,5},{8,10},{9,11},{10,... | collective-permute-start | bytes 442376 | tf_op jit(solution)/shard_map/ppermute | solution.py:68
  56.4 1.4 %collective-permute-done.19.refs_3_ = bf16[32,512]{1,0:T(8,128)(2,1)S(1)} collective-permute-done((bf16[32,512]{1,0:T(8,128)(2,1)S(1)}, bf16[32,512]{1,0:T(8,128)(2,1)S(1)}, u32[]{:S(2)}, u32[]{:S(2)}) %collective-permute-start.19) | collective-permute-done | bytes 32800 | tf_op jit(solution)/shard_map/ppermute | solution.py:68
  57.8 3.2 %collective-permute-done.20.refs_4_ = bf16[32,512]{1,0:T(8,128)(2,1)S(1)} collective-permute-done((bf16[32,512]{1,0:T(8,128)(2,1)S(1)}, bf16[32,512]{1,0:T(8,128)(2,1)S(1)}, u32[]{:S(2)}, u32[]{:S(2)}) %collective-permute-start.20) | collective-permute-done | bytes 32800 | tf_op jit(solution)/shard_map/ppermute | solution.py:68
  61.0 0.6 shard_map.130.refs_3_
  61.5 1.5 %collective-permute-start.21 = (bf16[128,512]{1,0:T(8,128)(2,1)S(1)}, bf16[128,512]{1,0:T(8,128)(2,1)S(1)}, u32[]{:S(2)}, u32[]{:S(2)}) collective-permute-start(bf16[128,512]{1,0:T(8,128)(2,1)S(1)} %shard_map.130.refs_3_), channel_id=1, source_target_pairs={{0,24},{4,28},{8,16},{12,20},{16,8},{20,12},{24,0},{28,4},{1,25},{... | collective-permute-start | bytes 393224 | tf_op jit(solution)/shard_map/ppermute | solution.py:68
  63.1 1.3 %collective-permute-start.22 = (bf16[128,512]{1,0:T(8,128)(2,1)S(1)}, bf16[128,512]{1,0:T(8,128)(2,1)S(1)}, u32[]{:S(2)}, u32[]{:S(2)}) collective-permute-start(bf16[128,512]{1,0:T(8,128)(2,1)S(1)} %shard_map.130.refs_3_), channel_id=1, source_target_pairs={{0,16},{4,20},{8,24},{12,28},{16,0},{20,4},{24,8},{28,12},{1,17},{... | collective-permute-start | bytes 393224 | tf_op jit(solution)/shard_map/ppermute | solution.py:68
  64.3 0.8 %collective-permute-start.23 = (bf16[128,512]{1,0:T(8,128)(2,1)S(1)}, bf16[128,512]{1,0:T(8,128)(2,1)S(1)}, u32[]{:S(2)}, u32[]{:S(2)}) collective-permute-start(bf16[128,512]{1,0:T(8,128)(2,1)S(1)} %shard_map.130.refs_3_), channel_id=1, source_target_pairs={{0,8},{4,12},{8,0},{12,4},{16,24},{20,28},{24,16},{28,20},{1,9},{5... | collective-permute-start | bytes 393224 | tf_op jit(solution)/shard_map/ppermute | solution.py:68
  65.3 2.2 %collective-permute-done.21.refs_4_ = bf16[128,512]{1,0:T(8,128)(2,1)S(1)} collective-permute-done((bf16[128,512]{1,0:T(8,128)(2,1)S(1)}, bf16[128,512]{1,0:T(8,128)(2,1)S(1)}, u32[]{:S(2)}, u32[]{:S(2)}) %collective-permute-start.21) | collective-permute-done | bytes 131104 | tf_op jit(solution)/shard_map/ppermute | solution.py:68
  67.5 1.3 %collective-permute-done.22.refs_5_ = bf16[128,512]{1,0:T(8,128)(2,1)S(1)} collective-permute-done((bf16[128,512]{1,0:T(8,128)(2,1)S(1)}, bf16[128,512]{1,0:T(8,128)(2,1)S(1)}, u32[]{:S(2)}, u32[]{:S(2)}) %collective-permute-start.22) | collective-permute-done | bytes 131104 | tf_op jit(solution)/shard_map/ppermute | solution.py:68
  68.9 0.4 collective-permute-done.23.refs_6_
  69.4 0.2 copy.13
  69.6 0.6 collective-permute-done.18.refs_7_
  70.2 1.5 %shard_map.129 = (bf16[128,2304]{1,0:T(8,128)(2,1)}, bf16[512,512]{1,0:T(8,128)(2,1)S(1)}) custom-call(s32[3]{0:T(128)S(1)} %pad_add_fusion.place.refs_0_, f32[1,2304]{1,0:T(1,128)S(1)} %broadcast_in_dim.7.refs_0_.refs_1_, bf16[2304,512]{1,0:T(8,128)(2,1)S(1)} %copy-done, bf16[512,1024]{1,0:T(8,128)(2,1)S(1)} %bitcast.9, ...), custom_call_target="tpu_custom_call" | custom-call | flops 1000000000 | tf_op jit(solution)/shard_map/pallas_call | solution.py:45
  71.7 3.0 %shard_map.131 = bf16[128,512]{1,0:T(8,128)(2,1)} custom-call(s32[3]{0:T(128)S(1)} %pad_add_fusion.place.refs_0_, bf16[512,512]{1,0:T(8,128)(2,1)S(1)} %get-tuple-element.64.refs_1_, bf16[512,1024]{1,0:T(8,128)(2,1)S(1)} %bitcast.10, bf16[128,512]{1,0:T(8,128)(2,1)S(1)} %shard_map.130.refs_3_, bf16[128,512]{1,0:T(8,128)(2,1)S(1)} %collective-permute-done.21.refs_4_, ...), custom_call_target="tpu_custom_call" | custom-call | flops 4000000000 | tf_op jit(solution)/shard_map/pallas_call | solution.py:45
  (47 shorter events, 0.7 us)
Async XLA Ops:
  0.6 6.6 %copy-start.6 = (f32[128,8]{0,1:T(8,128)S(1)}, f32[128,8]{0,1:T(8,128)}, u32[]{:S(2)}) copy-start(f32[128,8]{0,1:T(8,128)} %param.13) | copy-start | bytes 12292
  1.5 5.6 %collective-permute-start = (bf16[3,16,1024]{2,1,0:T(8,128)(2,1)S(1)}, bf16[3,16,1024]{2,1,0:T(8,128)(2,1)S(1)}, u32[]{:S(2)}, u32[]{:S(2)}) collective-permute-start(bf16[3,16,1024]{2,1,0:T(8,128)(2,1)S(1)} %slice.3), channel_id=1, source_target_pairs={{0,4},{4,8},{8,12},{12,16},{16,20},{20,24},{24,28},{28,0},{1,5},{5... | collective-permute-start | bytes 294920 | tf_op jit(solution)/shard_map/ppermute | solution.py:73
  2.1 1.1 %copy-start.2 = (bf16[3,128,1024]{2,1,0:T(8,128)(2,1)S(1)}, bf16[3,128,1024]{2,1,0:T(8,128)(2,1)}, u32[]{:S(2)}) copy-start(bf16[3,128,1024]{2,1,0:T(8,128)(2,1)} %stored_inputs.1) | copy-start | bytes 2359300
  3.2 1.0 %copy-start.4 = (f32[128,1024]{1,0:T(8,128)S(1)}, f32[128,1024]{1,0:T(8,128)}, u32[]{:S(2)}) copy-start(f32[128,1024]{1,0:T(8,128)} %stored_gate.1) | copy-start | bytes 1572868
  4.3 0.8 %copy-start.5 = (f32[3,4,1024]{2,1,0:T(4,128)S(1)}, f32[3,4,1024]{2,1,0:T(4,128)}, u32[]{:S(2)}) copy-start(f32[3,4,1024]{2,1,0:T(4,128)} %stored_taps.1) | copy-start | bytes 147460
  11.4 2.2 %collective-permute-start.1 = (bf16[4,272,128]{2,1,0:T(8,128)(2,1)S(1)}, bf16[4,272,128]{2,1,0:T(8,128)(2,1)S(1)}, u32[]{:S(2)}, u32[]{:S(2)}) collective-permute-start(bf16[4,272,128]{2,1,0:T(8,128)(2,1)S(1)} %get-tuple-element.38), channel_id=1, source_target_pairs={{0,4},{4,0},{8,12},{12,8},{16,20},{20,16},{24,28},{28,24},{1,5},{5... | collective-permute-start | bytes 835592 | tf_op jit(solution)/shard_map/ppermute | solution.py:68
  12.5 5.6 %collective-permute-start.5 = (bf16[4,272,128]{2,1,0:T(8,128)(2,1)S(1)}, bf16[4,272,128]{2,1,0:T(8,128)(2,1)S(1)}, u32[]{:S(2)}, u32[]{:S(2)}) collective-permute-start(bf16[4,272,128]{2,1,0:T(8,128)(2,1)S(1)} %get-tuple-element.37.kept), channel_id=1, source_target_pairs={{0,4},{4,0},{8,12},{12,8},{16,20},{20,16},{24,28},{28,24},{1,5},{5... | collective-permute-start | bytes 835592 | tf_op jit(solution)/shard_map/ppermute | solution.py:68
  14.5 6.5 %collective-permute-start.2 = (bf16[272,128]{1,0:T(8,128)(2,1)S(1)}, bf16[272,128]{1,0:T(8,128)(2,1)S(1)}, u32[]{:S(2)}, u32[]{:S(2)}) collective-permute-start(bf16[272,128]{1,0:T(8,128)(2,1)S(1)} %get-tuple-element.40), channel_id=1, source_target_pairs={{0,8},{4,12},{8,0},{12,4},{16,24},{20,28},{24,16},{28,20},{1,9},{5... | collective-permute-start | bytes 208904 | tf_op jit(solution)/shard_map/ppermute | solution.py:68
  16.1 5.1 %collective-permute-start.3 = (bf16[272,128]{1,0:T(8,128)(2,1)S(1)}, bf16[272,128]{1,0:T(8,128)(2,1)S(1)}, u32[]{:S(2)}, u32[]{:S(2)}) collective-permute-start(bf16[272,128]{1,0:T(8,128)(2,1)S(1)} %get-tuple-element.41), channel_id=1, source_target_pairs={{0,16},{4,20},{8,24},{12,28},{16,0},{20,4},{24,8},{28,12},{1,17},{... | collective-permute-start | bytes 208904 | tf_op jit(solution)/shard_map/ppermute | solution.py:68
  16.8 5.2 %collective-permute-start.4 = (bf16[272,128]{1,0:T(8,128)(2,1)S(1)}, bf16[272,128]{1,0:T(8,128)(2,1)S(1)}, u32[]{:S(2)}, u32[]{:S(2)}) collective-permute-start(bf16[272,128]{1,0:T(8,128)(2,1)S(1)} %get-tuple-element.42), channel_id=1, source_target_pairs={{0,24},{4,28},{8,16},{12,20},{16,8},{20,12},{24,0},{28,4},{1,25},{... | collective-permute-start | bytes 208904 | tf_op jit(solution)/shard_map/ppermute | solution.py:68
  18.1 12.9 %slice-start = ((s8[4718592]{0:T(1024)(128)(4,1)}), s8[4194304]{0:T(1024)(128)(4,1)S(1)}, s32[]{:S(2)}) async-start(s8[4718592]{0:T(1024)(128)(4,1)} %bitcast.7), calls=%async_computation | async-start | bytes 8388608
  18.1 12.9 %slice-start.1 = ((s8[4718592]{0:T(1024)(128)(4,1)}), s8[524288]{0:T(1024)(128)(4,1)S(1)}, s32[]{:S(2)}) async-start(s8[4718592]{0:T(1024)(128)(4,1)} %bitcast.7), calls=%async_computation.1 | async-start | bytes 1048576
  20.9 10.1 %copy-start.1 = (bf16[128,2304]{1,0:T(8,128)(2,1)S(1)}, bf16[128,2304]{1,0:T(8,128)(2,1)}, u32[]{:S(2)}) copy-start(bf16[128,2304]{1,0:T(8,128)(2,1)} %refs_1_.2) | copy-start | bytes 1769476
  22.9 4.3 %collective-permute-start.6 = (bf16[128,128]{1,0:T(8,128)(2,1)S(1)}, bf16[128,128]{1,0:T(8,128)(2,1)S(1)}, u32[]{:S(2)}, u32[]{:S(2)}) collective-permute-start(bf16[128,128]{1,0:T(8,128)(2,1)S(1)} %get-tuple-element.54), channel_id=1, source_target_pairs={{0,8},{4,12},{8,0},{12,4},{16,24},{20,28},{24,16},{28,20},{1,9},{5... | collective-permute-start | bytes 98312 | tf_op jit(solution)/shard_map/ppermute | solution.py:68
  24.4 3.9 %collective-permute-start.7 = (bf16[128,128]{1,0:T(8,128)(2,1)S(1)}, bf16[128,128]{1,0:T(8,128)(2,1)S(1)}, u32[]{:S(2)}, u32[]{:S(2)}) collective-permute-start(bf16[128,128]{1,0:T(8,128)(2,1)S(1)} %get-tuple-element.55), channel_id=1, source_target_pairs={{0,16},{4,20},{8,24},{12,28},{16,0},{20,4},{24,8},{28,12},{1,17},{... | collective-permute-start | bytes 98312 | tf_op jit(solution)/shard_map/ppermute | solution.py:68
  25.0 4.8 %collective-permute-start.8 = (bf16[128,128]{1,0:T(8,128)(2,1)S(1)}, bf16[128,128]{1,0:T(8,128)(2,1)S(1)}, u32[]{:S(2)}, u32[]{:S(2)}) collective-permute-start(bf16[128,128]{1,0:T(8,128)(2,1)S(1)} %get-tuple-element.56), channel_id=1, source_target_pairs={{0,24},{4,28},{8,16},{12,20},{16,8},{20,12},{24,0},{28,4},{1,25},{... | collective-permute-start | bytes 98312 | tf_op jit(solution)/shard_map/ppermute | solution.py:68
  26.4 10.9 %copy-start.9 = (f32[2304]{0:T(1024)S(1)}, f32[2304]{0:T(1024)}, u32[]{:S(2)}) copy-start(f32[2304]{0:T(1024)} %param.17) | copy-start | bytes 27652
  26.4 22.0 %copy-start.3 = (bf16[2304,512]{1,0:T(8,128)(2,1)S(1)}, bf16[2304,512]{1,0:T(8,128)(2,1)}, u32[]{:S(2)}) copy-start(bf16[2304,512]{1,0:T(8,128)(2,1)} %refs_1_.3) | copy-start | bytes 7077892
  26.4 22.0 %copy-start.7 = (f32[512]{0:T(512)S(1)}, f32[512]{0:T(512)}, u32[]{:S(2)}) copy-start(f32[512]{0:T(512)} %param.19) | copy-start | bytes 6148
  26.4 3.4 %collective-permute-start.9 = (bf16[128,128]{1,0:T(8,128)(2,1)S(1)}, bf16[128,128]{1,0:T(8,128)(2,1)S(1)}, u32[]{:S(2)}, u32[]{:S(2)}) collective-permute-start(bf16[128,128]{1,0:T(8,128)(2,1)S(1)} %get-tuple-element.53.refs_5_), channel_id=1, source_target_pairs={{0,4},{4,0},{8,12},{12,8},{16,20},{20,16},{24,28},{28,24},{1,5},{5... | collective-permute-start | bytes 98312 | tf_op jit(solution)/shard_map/ppermute | solution.py:68
  27.1 2.7 %collective-permute-start.10 = (bf16[128,128]{1,0:T(8,128)(2,1)S(1)}, bf16[128,128]{1,0:T(8,128)(2,1)S(1)}, u32[]{:S(2)}, u32[]{:S(2)}) collective-permute-start(bf16[128,128]{1,0:T(8,128)(2,1)S(1)} %collective-permute-done.6.refs_6_), channel_id=1, source_target_pairs={{0,4},{4,0},{8,12},{12,8},{16,20},{20,16},{24,28},{28,24},{1,5},{5... | collective-permute-start | bytes 98312 | tf_op jit(solution)/shard_map/ppermute | solution.py:68
  28.3 1.5 %collective-permute-start.11 = (bf16[128,128]{1,0:T(8,128)(2,1)S(1)}, bf16[128,128]{1,0:T(8,128)(2,1)S(1)}, u32[]{:S(2)}, u32[]{:S(2)}) collective-permute-start(bf16[128,128]{1,0:T(8,128)(2,1)S(1)} %collective-permute-done.7.refs_7_), channel_id=1, source_target_pairs={{0,4},{4,0},{8,12},{12,8},{16,20},{20,16},{24,28},{28,24},{1,5},{5... | collective-permute-start | bytes 98312 | tf_op jit(solution)/shard_map/ppermute | solution.py:68
  29.8 1.2 %collective-permute-start.12 = (bf16[128,128]{1,0:T(8,128)(2,1)S(1)}, bf16[128,128]{1,0:T(8,128)(2,1)S(1)}, u32[]{:S(2)}, u32[]{:S(2)}) collective-permute-start(bf16[128,128]{1,0:T(8,128)(2,1)S(1)} %collective-permute-done.8.refs_8_), channel_id=1, source_target_pairs={{0,4},{4,0},{8,12},{12,8},{16,20},{20,16},{24,28},{28,24},{1,5},{5... | collective-permute-start | bytes 98312 | tf_op jit(solution)/shard_map/ppermute | solution.py:68
  32.8 8.4 %collective-permute-start.13 = (bf16[32,2304]{1,0:T(8,128)(2,1)S(1)}, bf16[32,2304]{1,0:T(8,128)(2,1)S(1)}, u32[]{:S(2)}, u32[]{:S(2)}) collective-permute-start(bf16[32,2304]{1,0:T(8,128)(2,1)S(1)} %get-tuple-element.58), channel_id=1, source_target_pairs={{0,1},{1,0},{2,3},{3,2},{4,5},{5,4},{6,7},{7,6},{8,9},{9,8},{10,11... | collective-permute-start | bytes 442376 | tf_op jit(solution)/shard_map/ppermute | solution.py:68
  34.5 13.9 %collective-permute-start.14 = (bf16[32,2304]{1,0:T(8,128)(2,1)S(1)}, bf16[32,2304]{1,0:T(8,128)(2,1)S(1)}, u32[]{:S(2)}, u32[]{:S(2)}) collective-permute-start(bf16[32,2304]{1,0:T(8,128)(2,1)S(1)} %get-tuple-element.59), channel_id=1, source_target_pairs={{0,2},{1,3},{2,0},{3,1},{4,6},{5,7},{6,4},{7,5},{8,10},{9,11},{10,... | collective-permute-start | bytes 442376 | tf_op jit(solution)/shard_map/ppermute | solution.py:68
  37.1 11.4 %collective-permute-start.15 = (bf16[32,2304]{1,0:T(8,128)(2,1)S(1)}, bf16[32,2304]{1,0:T(8,128)(2,1)S(1)}, u32[]{:S(2)}, u32[]{:S(2)}) collective-permute-start(bf16[32,2304]{1,0:T(8,128)(2,1)S(1)} %get-tuple-element.60), channel_id=1, source_target_pairs={{0,3},{1,2},{2,1},{3,0},{4,7},{5,6},{6,5},{7,4},{8,11},{9,10},{10,... | collective-permute-start | bytes 442376 | tf_op jit(solution)/shard_map/ppermute | solution.py:68
  49.2 20.2 %copy-start.8 = (bf16[512,2,512]{2,1,0:T(2,128)(2,1)S(1)}, bf16[512,2,512]{2,1,0:T(2,128)(2,1)}, u32[]{:S(2)}) copy-start(bf16[512,2,512]{2,1,0:T(2,128)(2,1)} %param.21) | copy-start | bytes 3145732
  49.2 11.8 %collective-permute-start.16 = (bf16[32,2816]{1,0:T(8,128)(2,1)S(1)}, bf16[32,2816]{1,0:T(8,128)(2,1)S(1)}, u32[]{:S(2)}, u32[]{:S(2)}) collective-permute-start(bf16[32,2816]{1,0:T(8,128)(2,1)S(1)} %get-tuple-element.62), channel_id=1, source_target_pairs={{0,1},{1,0},{2,3},{3,2},{4,5},{5,4},{6,7},{7,6},{8,9},{9,8},{10,11... | collective-permute-start | bytes 540680 | tf_op jit(solution)/shard_map/ppermute | solution.py:68
  51.9 5.9 %collective-permute-start.19 = (bf16[32,512]{1,0:T(8,128)(2,1)S(1)}, bf16[32,512]{1,0:T(8,128)(2,1)S(1)}, u32[]{:S(2)}, u32[]{:S(2)}) collective-permute-start(bf16[32,512]{1,0:T(8,128)(2,1)S(1)} %get-tuple-element.65.refs_1_), channel_id=1, source_target_pairs={{0,2},{1,3},{2,0},{3,1},{4,6},{5,7},{6,4},{7,5},{8,10},{9,11},{10,... | collective-permute-start | bytes 98312 | tf_op jit(solution)/shard_map/ppermute | solution.py:68
  53.0 8.0 %collective-permute-start.20 = (bf16[32,512]{1,0:T(8,128)(2,1)S(1)}, bf16[32,512]{1,0:T(8,128)(2,1)S(1)}, u32[]{:S(2)}, u32[]{:S(2)}) collective-permute-start(bf16[32,512]{1,0:T(8,128)(2,1)S(1)} %get-tuple-element.65.refs_1_), channel_id=1, source_target_pairs={{0,3},{1,2},{2,1},{3,0},{4,7},{5,6},{6,5},{7,4},{8,11},{9,10},{10,... | collective-permute-start | bytes 98312 | tf_op jit(solution)/shard_map/ppermute | solution.py:68
  54.4 15.8 %copy-start = (bf16[2304,512]{1,0:T(8,128)(2,1)S(1)}, bf16[2304,512]{1,0:T(8,128)(2,1)}, u32[]{:S(2)}) copy-start(bf16[2304,512]{1,0:T(8,128)(2,1)} %refs_2_.3) | copy-start | bytes 7077892
  54.4 10.7 %collective-permute-start.17 = (bf16[32,2304]{1,0:T(8,128)(2,1)S(1)}, bf16[32,2304]{1,0:T(8,128)(2,1)S(1)}, u32[]{:S(2)}, u32[]{:S(2)}) collective-permute-start(bf16[32,2304]{1,0:T(8,128)(2,1)S(1)} %get-tuple-element.61.refs_4_), channel_id=1, source_target_pairs={{0,2},{1,3},{2,0},{3,1},{4,6},{5,7},{6,4},{7,5},{8,10},{9,11},{10,... | collective-permute-start | bytes 442376 | tf_op jit(solution)/shard_map/ppermute | solution.py:68
  61.5 6.0 %collective-permute-start.21 = (bf16[128,512]{1,0:T(8,128)(2,1)S(1)}, bf16[128,512]{1,0:T(8,128)(2,1)S(1)}, u32[]{:S(2)}, u32[]{:S(2)}) collective-permute-start(bf16[128,512]{1,0:T(8,128)(2,1)S(1)} %shard_map.130.refs_3_), channel_id=1, source_target_pairs={{0,24},{4,28},{8,16},{12,20},{16,8},{20,12},{24,0},{28,4},{1,25},{... | collective-permute-start | bytes 393224 | tf_op jit(solution)/shard_map/ppermute | solution.py:68
  63.1 5.8 %collective-permute-start.22 = (bf16[128,512]{1,0:T(8,128)(2,1)S(1)}, bf16[128,512]{1,0:T(8,128)(2,1)S(1)}, u32[]{:S(2)}, u32[]{:S(2)}) collective-permute-start(bf16[128,512]{1,0:T(8,128)(2,1)S(1)} %shard_map.130.refs_3_), channel_id=1, source_target_pairs={{0,16},{4,20},{8,24},{12,28},{16,0},{20,4},{24,8},{28,12},{1,17},{... | collective-permute-start | bytes 393224 | tf_op jit(solution)/shard_map/ppermute | solution.py:68
  64.3 5.0 %collective-permute-start.23 = (bf16[128,512]{1,0:T(8,128)(2,1)S(1)}, bf16[128,512]{1,0:T(8,128)(2,1)S(1)}, u32[]{:S(2)}, u32[]{:S(2)}) collective-permute-start(bf16[128,512]{1,0:T(8,128)(2,1)S(1)} %shard_map.130.refs_3_), channel_id=1, source_target_pairs={{0,8},{4,12},{8,0},{12,4},{16,24},{20,28},{24,16},{28,20},{1,9},{5... | collective-permute-start | bytes 393224 | tf_op jit(solution)/shard_map/ppermute | solution.py:68
  65.1 5.1 %collective-permute-start.18 = (bf16[32,2304]{1,0:T(8,128)(2,1)S(1)}, bf16[32,2304]{1,0:T(8,128)(2,1)S(1)}, u32[]{:S(2)}, u32[]{:S(2)}) collective-permute-start(bf16[32,2304]{1,0:T(8,128)(2,1)S(1)} %collective-permute-done.17.refs_6_), channel_id=1, source_target_pairs={{0,1},{1,0},{2,3},{3,2},{4,5},{5,4},{6,7},{7,6},{8,9},{9,8},{10,11... | collective-permute-start | bytes 442376 | tf_op jit(solution)/shard_map/ppermute | solution.py:68
  65.3 6.4 %collective-permute-start.24 = (bf16[128,512]{1,0:T(8,128)(2,1)S(1)}, bf16[128,512]{1,0:T(8,128)(2,1)S(1)}, u32[]{:S(2)}, u32[]{:S(2)}) collective-permute-start(bf16[128,512]{1,0:T(8,128)(2,1)S(1)} %shard_map.130.refs_3_), channel_id=1, source_target_pairs={{0,4},{4,0},{8,12},{12,8},{16,20},{20,16},{24,28},{28,24},{1,5},{5... | collective-permute-start | bytes 393224 | tf_op jit(solution)/shard_map/ppermute | solution.py:68
  67.5 4.2 %collective-permute-start.25 = (bf16[128,512]{1,0:T(8,128)(2,1)S(1)}, bf16[128,512]{1,0:T(8,128)(2,1)S(1)}, u32[]{:S(2)}, u32[]{:S(2)}) collective-permute-start(bf16[128,512]{1,0:T(8,128)(2,1)S(1)} %collective-permute-done.21.refs_4_), channel_id=1, source_target_pairs={{0,4},{4,0},{8,12},{12,8},{16,20},{20,16},{24,28},{28,24},{1,5},{5... | collective-permute-start | bytes 393224 | tf_op jit(solution)/shard_map/ppermute | solution.py:68
  68.9 2.9 %collective-permute-start.26 = (bf16[128,512]{1,0:T(8,128)(2,1)S(1)}, bf16[128,512]{1,0:T(8,128)(2,1)S(1)}, u32[]{:S(2)}, u32[]{:S(2)}) collective-permute-start(bf16[128,512]{1,0:T(8,128)(2,1)S(1)} %collective-permute-done.22.refs_5_), channel_id=1, source_target_pairs={{0,4},{4,0},{8,12},{12,8},{16,20},{20,16},{24,28},{28,24},{1,5},{5... | collective-permute-start | bytes 393224 | tf_op jit(solution)/shard_map/ppermute | solution.py:68
  69.3 2.4 %collective-permute-start.27 = (bf16[128,512]{1,0:T(8,128)(2,1)S(1)}, bf16[128,512]{1,0:T(8,128)(2,1)S(1)}, u32[]{:S(2)}, u32[]{:S(2)}) collective-permute-start(bf16[128,512]{1,0:T(8,128)(2,1)S(1)} %collective-permute-done.23.refs_6_), channel_id=1, source_target_pairs={{0,4},{4,0},{8,12},{12,8},{16,20},{20,16},{24,28},{28,24},{1,5},{5... | collective-permute-start | bytes 393224 | tf_op jit(solution)/shard_map/ppermute | solution.py:68

commit v5 on v4

--- a/solution.py
+++ b/solution.py
@@ -81,11 +81,31 @@
     return place[0] // 2, place[0] % 2
 
 
-def load_kernel(stored_inputs, stored_gate, stored_taps, inputs, log, taps, gate, sems):
+def convolved(wide, taps, part, count):
+    total = None
+    for tap in range(CONV):
+        first = 8 - (CONV - 1) + tap
+        term = taps[part, tap : tap + 1, :] * wide[first : first + count, :]
+        total = term if total is None else total + term
+    return total / (1.0 + jnp.exp(-total))
+
+
+def finished(activated, part):
+    if part == 2:
+        return activated.astype(bf16)
+    heads = []
+    for first in range(0, activated.shape[1], DK):
+        head = activated[:, first : first + DK]
+        head = head * lax.rsqrt(jnp.sum(head * head, axis=-1, keepdims=True) + eps_norm)
+        heads.append((head * DK ** (-0.5) if part == 0 else head).astype(bf16))
+    return jnp.concatenate(heads, axis=1)
+
+
+def load_kernel(stored_inputs, stored_gate, stored_taps, done, log, taps, gate, inputs, wide, sems):
     moves = [
         pltpu.make_async_copy(stored_gate, gate, sems.at[0]),
-        pltpu.make_async_copy(stored_inputs, inputs, sems.at[1]),
-        pltpu.make_async_copy(stored_taps, taps, sems.at[2]),
+        pltpu.make_async_copy(stored_taps, taps, sems.at[1]),
+        pltpu.make_async_copy(stored_inputs, inputs, sems.at[2]),
     ]
     for move in moves:
         move.start()
@@ -99,26 +119,22 @@
     log[...] = mm(tril, high) + mm(tril, low)
     moves[1].wait()
     moves[2].wait()
-
-
-def put_wide(wide, place, inputs, halo, own, part):
-    pad = wide.shape[0] - inputs.shape[1]
-    before = halo[part, halo.shape[1] - pad :, own].astype(f32)
-    wide[:pad, :] = jnp.where(place[2] == 0, 0.0, before)
-    wide[pad:, :] = inputs[part, :, own].astype(f32)
-
-
-def convolved(wide, taps, own, part):
-    length = wide.shape[0] - 8
-    total = jnp.zeros((length, DK), f32)
-    for tap in range(CONV):
-        first = 8 - (CONV - 1) + tap
-        total = total + taps[part, tap : tap + 1, own] * wide[first : first + length, :]
-    return total / (1.0 + jnp.exp(-total))
-
-
-def unit(value):
-    return value * lax.rsqrt(jnp.sum(value * value, axis=-1, keepdims=True) + eps_norm)
+    for part in range(3):
+        wide[:8, :] = jnp.zeros((8, wide.shape[1]), f32)
+        wide[8:, :] = inputs[part].astype(f32)
+        done[part] = finished(convolved(wide, taps, part, length), part)
+
+
+def first_rows(place, halo, inputs, taps, part, wide):
+    count = halo.shape[1]
+    before = halo[part, count - 8 :, :].astype(f32)
+    wide[:8, :] = jnp.where(place[2] == 0, 0.0, before)
+    wide[8:, :] = inputs[part].astype(f32)
+    return finished(convolved(wide, taps, part, count), part)
+
+
+def whole_head(first, done, part, lane):
+    return jnp.concatenate([first[:, lane], done[part, first.shape[0] :, lane]], axis=0)
 
 
 def spans(log):
@@ -133,7 +149,9 @@
     return [2 * i + core for i in range(pairs)] + [2 * i + 1 - core for i in range(pairs)]
 
 
-def map_kernel(place, inputs, halo, logs, beta, taps, kept, sent, solutions, shrunk, wide):
+def map_kernel(
+    place, done, head_rows, halo, logs, beta, taps, kept, sent, solutions, shrunk, first, wide
+):
     length = logs.shape[0]
     pairs = kept.shape[0]
     chunks = range(2 * pairs)
@@ -142,14 +160,13 @@
     rows = lax.broadcasted_iota(jnp.int32, (length, length), 0)
     cols = lax.broadcasted_iota(jnp.int32, (length, length), 1)
     eye = (rows == cols).astype(f32)
-    for i in chunks:
-        for part in (1, 2):
-            put_wide(wide.at[i, part - 1], place, inputs, halo, lane[i], part)
+    for part in (1, 2):
+        first[part - 1] = first_rows(place, halo, head_rows, taps, part, wide)
 
     coupling, right, finals, decay = [], [], [], []
     for i in chunks:
-        key = unit(convolved(wide.at[i, 0], taps, lane[i], 1)).astype(bf16).astype(f32)
-        value = convolved(wide.at[i, 1], taps, lane[i], 2).astype(bf16)
+        key = whole_head(first.at[0], done, 1, lane[i]).astype(f32)
+        value = whole_head(first.at[1], done, 2, lane[i])
         log = logs[:, lane[i]]
         rate_row = beta[pl.ds(heads[i], 1), :]
         rate_column = jnp.sum(rate_row * eye, axis=1, keepdims=True)
@@ -183,9 +200,9 @@
         size *= 2
 
     short = [inverse[i].astype(bf16) for i in chunks]
-    first = [mm(short[i], right[i]).astype(bf16) for i in chunks]
-    left = [right[i].astype(f32) - first[i].astype(f32) - mm(coupling[i], first[i]) for i in chunks]
-    solved = [(first[i].astype(f32) + mm(short[i], left[i])).astype(bf16) for i in chunks]
+    near = [mm(short[i], right[i]).astype(bf16) for i in chunks]
+    left = [right[i].astype(f32) - near[i].astype(f32) - mm(coupling[i], near[i]) for i in chunks]
+    solved = [(near[i].astype(f32) + mm(short[i], left[i])).astype(bf16) for i in chunks]
     for i in chunks:
         solutions[i] = solved[i]
         maps = kept if i < pairs else sent
@@ -202,19 +219,17 @@
     )
 
 
-def read_kernel(
-    place, inputs, halo, logs, beta, taps, solutions, shrunk, stay, go, reads, intra, wide
-):
+def read_kernel(place, done, head_rows, halo, logs, beta, taps, *refs):
+    solutions, shrunk, stay, go, reads, intra, first, wide = refs
     length = logs.shape[0]
     pairs = stay.shape[0]
     _, core = split_cores(place)
+    first[...] = first_rows(place, halo, head_rows, taps, 0, wide)
     rows = lax.broadcasted_iota(jnp.int32, (length, length), 0)
     cols = lax.broadcasted_iota(jnp.int32, (length, length), 1)
     for i, head in enumerate(side_heads(place, pairs)):
         lane = lanes(head)
-        put_wide(wide.at[i], place, inputs, halo, lane, 0)
-        query = unit(convolved(wide.at[i], taps, lane, 0)) * DK ** (-0.5)
-        query = query.astype(bf16).astype(f32)
+        query = whole_head(first, done, 0, lane).astype(f32)
         log = logs[:, lane]
         products = [
             mm_nt(query[own] * jnp.exp(log[own] - middle), shrunk[i, b])
@@ -222,7 +237,8 @@
         ]
         rate_row = beta[pl.ds(head, 1), :]
         mixing = jnp.where(rows >= cols, jnp.concatenate(products, axis=0) * rate_row, 0.0)
-        mixes = mm(mixing, solutions[i])
+        high = mixing.astype(bf16)
+        mixes = mm(high, solutions[i]) + mm(mixing - high.astype(f32), solutions[i])
         read = query * jnp.exp(log) - mixes[:, DK:]
         offset, move, decay = parts_of((stay if i < pairs else go)[i % pairs])
         both = mm_nt(read, jnp.concatenate([offset, move], axis=0))
@@ -341,55 +357,50 @@
         out[at, :] = pieces[step][:, pieces[step].shape[1] - out.shape[1] :]
 
 
-def query_kernel(parts, *refs):
+def attend_kernel(parts, order, *refs):
     place, gain, query_weight, up = refs[:4]
-    pieces = refs[4 : 4 + parts]
-    stream, absorbed = refs[4 + parts :]
+    pieces, refs = refs[4 : 4 + parts], refs[4 + parts :]
+    blocks, refs = refs[: len(order)], refs[len(order) :]
+    stream, out, absorbed, latents, scores, weights, totals = refs
     length = stream.shape[0]
+    heads = absorbed.shape[0] // length
+    me = place[2]
     share = length // parts
     for step in range(parts):
         at = pl.ds(pl.multiple_of(partner(place[1], step, parts) * share, share), share)
         stream[at, :] = pieces[step][:, : stream.shape[1]]
+    for position in range(len(order)):
+        latents[position * length : (position + 1) * length, :] = blocks[position][...]
     normed = normalized(stream[...].astype(f32), gain[...]).astype(bf16)
     query = jnp.dot(normed, query_weight[...], preferred_element_type=f32).astype(bf16)
-    for head in range(query.shape[1] // DH):
+    for head in range(heads):
         own = slice(head * DH, (head + 1) * DH)
         absorbed[head * length : (head + 1) * length, :] = (
             mm_nt(query[:, own], up[:, own]) * DH ** (-0.5)
         ).astype(bf16)
-
-
-def attend_kernel(order, *refs):
-    place, absorbed, up = refs[:3]
-    blocks = refs[3 : 3 + len(order)]
-    out, latents = refs[3 + len(order) :]
-    length = blocks[0].shape[0]
-    heads = absorbed.shape[0] // length
-    me = place[2]
-    for position in range(len(order)):
-        latents[position * length : (position + 1) * length, :] = blocks[position][...]
-    group = heads
-    rows = lax.broadcasted_iota(jnp.int32, (group * length, length), 0) % length
-    cols = lax.broadcasted_iota(jnp.int32, (group * length, length), 1)
-    allowed = [rows >= cols] + [(me ^ distance) < me for distance in order[1:]]
-    for first in range(0, heads, group):
-        own = slice(first * length, (first + group) * length)
-        scores = mm_nt(absorbed[own, :], latents[...])
-        parts = [
-            jnp.where(allowed[p], scores[:, p * length : (p + 1) * length], -1e30)
+    scores[...] = mm_nt(absorbed[...], latents[...])
+    group = min(length, 32)
+    for first in range(0, heads * length, group):
+        own = slice(first, first + group)
+        rows = lax.broadcasted_iota(jnp.int32, (group, length), 0) + first % length
+        cols = lax.broadcasted_iota(jnp.int32, (group, length), 1)
+        allowed = [rows >= cols] + [(me ^ distance) < me for distance in order[1:]]
+        masked = [
+            jnp.where(allowed[p], scores[own, p * length : (p + 1) * length], -1e30)
             for p in range(len(order))
         ]
-        peak = jnp.max(functools.reduce(jnp.maximum, parts), axis=-1, keepdims=True)
-        weights = [jnp.exp(part - peak) for part in parts]
-        total = jnp.sum(functools.reduce(jnp.add, weights), axis=-1, keepdims=True)
-        mixed = mm(jnp.concatenate([w.astype(bf16) for w in weights], axis=1), latents[...])
-        spread = (mixed / total).astype(bf16)
-        for i in range(group):
-            head = first + i
-            value = slice((heads + head) * DH, (heads + head + 1) * DH)
-            out[:, head * DH : (head + 1) * DH] = jnp.dot(
-                spread[i * length : (i + 1) * length], up[:, value], preferred_element_type=f32
-            ).astype(bf16)
+        peak = jnp.max(functools.reduce(jnp.maximum, masked), axis=-1, keepdims=True)
+        shares = [jnp.exp(part - peak) for part in masked]
+        total = jnp.sum(functools.reduce(jnp.add, shares), axis=-1, keepdims=True)
+        totals[own, :] = jnp.broadcast_to(total, (group, totals.shape[1]))
+        for p in range(len(order)):
+            weights[own, p * length : (p + 1) * length] = shares[p].astype(bf16)
+    mixed = jnp.dot(weights[...], latents[...], preferred_element_type=f32)
+    for head in range(heads):
+        own = slice(head * length, (head + 1) * length)
+        value = slice((heads + head) * DH, (heads + head + 1) * DH)
+        outcome = mm(mixed[own], up[:, value])
+        out[:, head * DH : (head + 1) * DH] = (outcome / totals[own, :]).astype(bf16)
 
 
 def far_first(count):
@@ -418,17 +429,26 @@
     place = jnp.stack([ctx_me % heads, lax.axis_index("head").astype(jnp.int32), ctx_me])
 
     halo = passed_along(kda_inputs[:, length - HALO :, :], "ctx", 1)
-    inputs, logs, taps = call(
+    stored = [
+        pltpu.with_memory_space_constraint(a, pltpu.HBM) for a in (kda_inputs, gate_log, conv_weight)
+    ]
+    done, logs, taps = call(
         load_kernel,
         [(kda_inputs.shape, bf16), (gate_log.shape, f32), (conv_weight.shape, f32)],
-        [kda_inputs, gate_log, conv_weight],
-        [(gate_log.shape, f32)],
+        stored,
+        [
+            (gate_log.shape, f32),
+            (kda_inputs.shape, bf16),
+            ((length + 8, heads * DK), f32),
+        ],
         24,
         stored=(0, 1, 2),
         copies=3,
+        cost=2.0,
     )
     map_shape = (2 * DK + EXTRA, DK)
-    arguments = [place, inputs, halo, logs, beta.T, taps]
+    head_rows = kda_inputs[:, :HALO, :]
+    arguments = [place, done, head_rows, halo, logs, beta.T, taps]
     kept, sent, solutions, shrunk = call(
         map_kernel,
         [
@@ -438,7 +458,7 @@
             ((heads, 2, length, DK), bf16),
         ],
         arguments,
-        [((heads, 2, length + 8, DK), f32)],
+        [((2, HALO, heads * DK), bf16), ((HALO + 8, heads * DK), f32)],
         16,
         cost=5.0,
     )
@@ -449,7 +469,7 @@
         read_kernel,
         [((length, heads * DK), bf16), ((length, heads * DK), f32)],
         arguments + [solutions, shrunk, got, got_kept],
-        [((heads, length + 8, DK), f32)],
+        [((HALO, heads * DK), bf16), ((HALO + 8, heads * DK), f32)],
         16,
         cost=2.5,
     )
@@ -539,20 +559,21 @@
         latents.append(trade(latents[position], "ctx", 1, 2))
     up = up_weight.reshape(up_weight.shape[0], -1)
     heads_mla = query_weight.shape[1] // DH
-    stream_out, absorbed = call(
-        functools.partial(query_kernel, parts),
-        [((length, width), bf16), ((heads_mla * length, up.shape[0]), bf16)],
-        [place, norm_gain[None], query_weight, up] + stream_parts,
-        limit=16,
-    )
-    attention_out = call(
-        functools.partial(attend_kernel, tuple(order)),
-        [((length, heads_mla * DH), bf16)],
-        [place, absorbed, up] + latents,
-        [((count * length, up.shape[0]), bf16)],
-        12 + count * length * length * 24 // MIB,
+    rows, latent_rows = heads_mla * length, count * length
+    stream_out, attention_out = call(
+        functools.partial(attend_kernel, parts, tuple(order)),
+        [((length, width), bf16), ((length, heads_mla * DH), bf16)],
+        [place, norm_gain[None], query_weight, up] + stream_parts + latents,
+        [
+            ((rows, latent_width), bf16),
+            ((latent_rows, latent_width), bf16),
+            ((rows, latent_rows), f32),
+            ((rows, latent_rows), bf16),
+            ((rows, DH), f32),
+        ],
+        16 + rows * latent_rows * 8 // MIB,
         cost=4.0,
-    )[0]
+    )
     return (stream_out, attention_out)
 
 

time: 75 us -> 74.1 us (0.988)
  local copies, waits for them, and re-layouts: 4.17 us -> 1.25 us
  Pallas kernels: 16.8 us -> 18.7 us
    unnamed x25 -> x19, local copies, waits for them, and re-layouts: 3.25 us -> 0.28 us
    pallas_call x10 -> x9, Pallas kernels: 16.8 us -> 18.7 us  [call(): pl.pallas_call(kernel, out_shape=[jax.ShapeDtypeStruct(shape, dtype) for...]
  transfers between devices with their start and end apart: 28 -> 28, of which waited for: 16 -> 16; matrix products, arithmetic and copies ran while one was open for 0% -> 0% of each run, Pallas kernels for 8% -> 10%
where the time goes in v5:
time: 74.1 us; the launch traced here: 73.9 us
  waiting for transfers between devices  29 us (39%)
  starting transfers between devices  24.1 us (33%)
  Pallas kernels  18.7 us (25%)
  local copies, waits for them, and re-layouts  1.25 us (2%)
  between operations  0.81 us (1%)
    ppermute x27, waiting for transfers between devices, trade(): return lax.ppermute(block, axis, route)  26.9 us
    ppermute x27, starting transfers between devices, trade(): return lax.ppermute(block, axis, route)  23.6 us
    pallas_call x9, Pallas kernels, call(): pl.pallas_call(kernel, out_shape=[jax.ShapeDtypeStruct(shape, dtype) for...  18.7 us
    ppermute x1, waiting for transfers between devices, passed_along(): lax.ppermute(block, axis, [(i, (i + distance) % count) for i in range(cou...  2.1 us
  transfers between devices with their start and end apart: 28, of which 16 were waited for; matrix products, arithmetic and copies ran while one was open for 0% of the time, Pallas kernels for 10%

profile of v5, /device:TPU:0, one launch (start us, length us, event | category | flops | bytes accessed | tf_op | source)
XLA Modules:
  0.0 73.9 jit_solution(12985335465198490994)
XLA Ops:
  0.6 1.0 %fusion = (bf16[3,16,1024]{2,1,0:T(8,128)(2,1)S(1)}, bf16[3,16,1024]{2,1,0:T(8,128)(2,1)S(1)}) fusion(bf16[3,128,1024]{2,1,0:T(8,128)(2,1)} %stored_inputs.1), kind=kLoop, calls=%fused_computation.1 | loop fusion | bytes 393216 | tf_op jit(solution)/shard_map/slice | solution.py:431
  1.6 0.5 collective-permute-start
  2.1 3.0 %shard_map.122 = (bf16[3,128,1024]{2,1,0:T(8,128)(2,1)S(1)}, f32[128,1024]{1,0:T(8,128)S(1)}, f32[3,4,1024]{2,1,0:T(4,128)S(1)}) custom-call(bf16[3,128,1024]{2,1,0:T(8,128)(2,1)} %stored_inputs.1, f32[128,1024]{1,0:T(8,128)} %stored_gate.1, f32[3,4,1024]{2,1,0:T(4,128)} %stored_taps.1), custom_call_target="tpu_custom_call" | custom-call | flops 2000000000 | tf_op jit(solution)/shard_map/pallas_call | solution.py:45
  5.1 0.1 pad_add_fusion.place.refs_0_
  5.2 2.1 %collective-permute-done.halo = bf16[3,16,1024]{2,1,0:T(8,128)(2,1)S(1)} collective-permute-done((bf16[3,16,1024]{2,1,0:T(8,128)(2,1)S(1)}, bf16[3,16,1024]{2,1,0:T(8,128)(2,1)S(1)}, u32[]{:S(2)}, u32[]{:S(2)}) %collective-permute-start) | collective-permute-done | bytes 98336 | tf_op jit(solution)/shard_map/ppermute | solution.py:73
  7.3 3.7 %shard_map.123 = (bf16[4,272,128]{2,1,0:T(8,128)(2,1)S(1)}, bf16[4,272,128]{2,1,0:T(8,128)(2,1)S(1)}, bf16[8,128,256]{2,1,0:T(8,128)(2,1)S(1)}, bf16[8,2,128,128]{3,2,1,0:T(8,128)(2,1)S(1)}) custom-call(s32[3]{0:T(128)S(1)} %pad_add_fusion.place.refs_0_, bf16[3,128,1024]{2,1,0:T(8,128)(2,1)S(1)} %get-tuple-element.32.done, ...), custom_call_target="tpu_custom_call" | custom-call | flops 5000000000 | tf_op jit(solution)/shard_map/pallas_call | solution.py:45
  11.0 0.6 collective-permute-start.1
  11.6 0.1 collective-permute-start.5
  11.7 1.1 %collective-permute-done.1.got.refs_2_ = bf16[4,272,128]{2,1,0:T(8,128)(2,1)S(1)} collective-permute-done((bf16[4,272,128]{2,1,0:T(8,128)(2,1)S(1)}, bf16[4,272,128]{2,1,0:T(8,128)(2,1)S(1)}, u32[]{:S(2)}, u32[]{:S(2)}) %collective-permute-start.1) | collective-permute-done | bytes 278560 | tf_op jit(solution)/shard_map/ppermute | solution.py:68
  12.8 0.8 %shard_map.124 = (bf16[272,128]{1,0:T(8,128)(2,1)S(1)}, bf16[272,128]{1,0:T(8,128)(2,1)S(1)}, bf16[272,128]{1,0:T(8,128)(2,1)S(1)}, bf16[272,128]{1,0:T(8,128)(2,1)S(1)}) custom-call(s32[3]{0:T(128)S(1)} %pad_add_fusion.place.refs_0_, bf16[4,272,128]{2,1,0:T(8,128)(2,1)S(1)} %get-tuple-element.35.kept, ...), custom_call_target="tpu_custom_call" | custom-call | flops 1000000000 | tf_op jit(solution)/shard_map/pallas_call | solution.py:45
  13.6 1.6 %collective-permute-start.2 = (bf16[272,128]{1,0:T(8,128)(2,1)S(1)}, bf16[272,128]{1,0:T(8,128)(2,1)S(1)}, u32[]{:S(2)}, u32[]{:S(2)}) collective-permute-start(bf16[272,128]{1,0:T(8,128)(2,1)S(1)} %get-tuple-element.38), channel_id=1, source_target_pairs={{0,8},{4,12},{8,0},{12,4},{16,24},{20,28},{24,16},{28,20},{1,9},{5... | collective-permute-start | bytes 208904 | tf_op jit(solution)/shard_map/ppermute | solution.py:68
  15.2 1.3 %collective-permute-start.3 = (bf16[272,128]{1,0:T(8,128)(2,1)S(1)}, bf16[272,128]{1,0:T(8,128)(2,1)S(1)}, u32[]{:S(2)}, u32[]{:S(2)}) collective-permute-start(bf16[272,128]{1,0:T(8,128)(2,1)S(1)} %get-tuple-element.39), channel_id=1, source_target_pairs={{0,16},{4,20},{8,24},{12,28},{16,0},{20,4},{24,8},{28,12},{1,17},{... | collective-permute-start | bytes 208904 | tf_op jit(solution)/shard_map/ppermute | solution.py:68
  16.4 0.9 %collective-permute-start.4 = (bf16[272,128]{1,0:T(8,128)(2,1)S(1)}, bf16[272,128]{1,0:T(8,128)(2,1)S(1)}, u32[]{:S(2)}, u32[]{:S(2)}) collective-permute-start(bf16[272,128]{1,0:T(8,128)(2,1)S(1)} %get-tuple-element.40), channel_id=1, source_target_pairs={{0,24},{4,28},{8,16},{12,20},{16,8},{20,12},{24,0},{28,4},{1,25},{... | collective-permute-start | bytes 208904 | tf_op jit(solution)/shard_map/ppermute | solution.py:68
  17.3 3.3 %shard_map.125 = (bf16[128,1024]{1,0:T(8,128)(2,1)S(1)}, f32[128,1024]{1,0:T(8,128)S(1)}) custom-call(s32[3]{0:T(128)S(1)} %pad_add_fusion.place.refs_0_, bf16[3,128,1024]{2,1,0:T(8,128)(2,1)S(1)} %get-tuple-element.32.done, bf16[3,16,1024]{2,1,0:T(8,128)(2,1)S(1)} %get-tuple-element.63.head_rows, bf16[3,16,1024]{2,1,0:T(8,128)(2,1)S(1)} %collective-permute-done.halo, ...), custom_call_target="tpu_custom_call" | custom-call | flops 2500000000 | tf_op jit(solution)/shard_map/pallas_call | solution.py:45
  20.7 1.0 %collective-permute-done.4.refs_4_ = bf16[272,128]{1,0:T(8,128)(2,1)S(1)} collective-permute-done((bf16[272,128]{1,0:T(8,128)(2,1)S(1)}, bf16[272,128]{1,0:T(8,128)(2,1)S(1)}, u32[]{:S(2)}, u32[]{:S(2)}) %collective-permute-start.4) | collective-permute-done | bytes 69664 | tf_op jit(solution)/shard_map/ppermute | solution.py:68
  21.6 0.8 %shard_map.126 = (bf16[128,128]{1,0:T(8,128)(2,1)S(1)}, bf16[128,128]{1,0:T(8,128)(2,1)S(1)}, bf16[128,128]{1,0:T(8,128)(2,1)S(1)}, bf16[128,128]{1,0:T(8,128)(2,1)S(1)}) custom-call(s32[3]{0:T(128)S(1)} %pad_add_fusion.place.refs_0_, bf16[272,128]{1,0:T(8,128)(2,1)S(1)} %get-tuple-element.47.refs_1_, bf16[272,128]{1,0:T(8,128)(2,1)S(1)} %collective-permute-done.2.refs_2_, ...), custom_call_target="tpu_custom_call" | custom-call | flops 1000000000 | tf_op jit(solution)/shard_map/pallas_call | solution.py:45
  22.5 1.5 %collective-permute-start.6 = (bf16[128,128]{1,0:T(8,128)(2,1)S(1)}, bf16[128,128]{1,0:T(8,128)(2,1)S(1)}, u32[]{:S(2)}, u32[]{:S(2)}) collective-permute-start(bf16[128,128]{1,0:T(8,128)(2,1)S(1)} %get-tuple-element.52), channel_id=1, source_target_pairs={{0,8},{4,12},{8,0},{12,4},{16,24},{20,28},{24,16},{28,20},{1,9},{5... | collective-permute-start | bytes 98312 | tf_op jit(solution)/shard_map/ppermute | solution.py:68
  24.0 0.4 collective-permute-start.7
  24.4 1.7 %collective-permute-start.8 = (bf16[128,128]{1,0:T(8,128)(2,1)S(1)}, bf16[128,128]{1,0:T(8,128)(2,1)S(1)}, u32[]{:S(2)}, u32[]{:S(2)}) collective-permute-start(bf16[128,128]{1,0:T(8,128)(2,1)S(1)} %get-tuple-element.54), channel_id=1, source_target_pairs={{0,24},{4,28},{8,16},{12,20},{16,8},{20,12},{24,0},{28,4},{1,25},{... | collective-permute-start | bytes 98312 | tf_op jit(solution)/shard_map/ppermute | solution.py:68
  26.1 0.6 collective-permute-done.6.refs_6_
  26.7 1.2 %collective-permute-done.7.refs_7_ = bf16[128,128]{1,0:T(8,128)(2,1)S(1)} collective-permute-done((bf16[128,128]{1,0:T(8,128)(2,1)S(1)}, bf16[128,128]{1,0:T(8,128)(2,1)S(1)}, u32[]{:S(2)}, u32[]{:S(2)}) %collective-permute-start.7) | collective-permute-done | bytes 32800 | tf_op jit(solution)/shard_map/ppermute | solution.py:68
  27.9 1.3 %collective-permute-done.8.refs_8_ = bf16[128,128]{1,0:T(8,128)(2,1)S(1)} collective-permute-done((bf16[128,128]{1,0:T(8,128)(2,1)S(1)}, bf16[128,128]{1,0:T(8,128)(2,1)S(1)}, u32[]{:S(2)}, u32[]{:S(2)}) %collective-permute-start.8) | collective-permute-done | bytes 32800 | tf_op jit(solution)/shard_map/ppermute | solution.py:68
  29.2 1.2 %collective-permute-done.12.refs_12_ = bf16[128,128]{1,0:T(8,128)(2,1)S(1)} collective-permute-done((bf16[128,128]{1,0:T(8,128)(2,1)S(1)}, bf16[128,128]{1,0:T(8,128)(2,1)S(1)}, u32[]{:S(2)}, u32[]{:S(2)}) %collective-permute-start.12) | collective-permute-done | bytes 32800 | tf_op jit(solution)/shard_map/ppermute | solution.py:68
  30.4 1.8 %shard_map.127 = (f32[32,2304]{1,0:T(8,128)S(1)}, bf16[32,2304]{1,0:T(8,128)(2,1)S(1)}, bf16[32,2304]{1,0:T(8,128)(2,1)S(1)}, bf16[32,2304]{1,0:T(8,128)(2,1)S(1)}) custom-call(s32[3]{0:T(128)S(1)} %pad_add_fusion.place.refs_0_, bf16[128,2304]{1,0:T(8,128)(2,1)S(1)} %copy-done, bf16[1024,2304]{1,0:T(8,128)(2,1)S(1)} %bitcast.8, ...), custom_call_target="tpu_custom_call" | custom-call | flops 1000000000 | tf_op jit(solution)/shard_map/pallas_call | solution.py:45
  32.2 1.9 %collective-permute-start.13 = (bf16[32,2304]{1,0:T(8,128)(2,1)S(1)}, bf16[32,2304]{1,0:T(8,128)(2,1)S(1)}, u32[]{:S(2)}, u32[]{:S(2)}) collective-permute-start(bf16[32,2304]{1,0:T(8,128)(2,1)S(1)} %get-tuple-element.56), channel_id=1, source_target_pairs={{0,1},{1,0},{2,3},{3,2},{4,5},{5,4},{6,7},{7,6},{8,9},{9,8},{10,11... | collective-permute-start | bytes 442376 | tf_op jit(solution)/shard_map/ppermute | solution.py:68
  34.1 2.6 %collective-permute-start.14 = (bf16[32,2304]{1,0:T(8,128)(2,1)S(1)}, bf16[32,2304]{1,0:T(8,128)(2,1)S(1)}, u32[]{:S(2)}, u32[]{:S(2)}) collective-permute-start(bf16[32,2304]{1,0:T(8,128)(2,1)S(1)} %get-tuple-element.57), channel_id=1, source_target_pairs={{0,2},{1,3},{2,0},{3,1},{4,6},{5,7},{6,4},{7,5},{8,10},{9,11},{10,... | collective-permute-start | bytes 442376 | tf_op jit(solution)/shard_map/ppermute | solution.py:68
  36.7 3.9 %collective-permute-done.13.refs_4_ = bf16[32,2304]{1,0:T(8,128)(2,1)S(1)} collective-permute-done((bf16[32,2304]{1,0:T(8,128)(2,1)S(1)}, bf16[32,2304]{1,0:T(8,128)(2,1)S(1)}, u32[]{:S(2)}, u32[]{:S(2)}) %collective-permute-start.13) | collective-permute-done | bytes 147488 | tf_op jit(solution)/shard_map/ppermute | solution.py:68
  40.6 7.4 %collective-permute-done.14.refs_5_ = bf16[32,2304]{1,0:T(8,128)(2,1)S(1)} collective-permute-done((bf16[32,2304]{1,0:T(8,128)(2,1)S(1)}, bf16[32,2304]{1,0:T(8,128)(2,1)S(1)}, u32[]{:S(2)}, u32[]{:S(2)}) %collective-permute-start.14) | collective-permute-done | bytes 147488 | tf_op jit(solution)/shard_map/ppermute | solution.py:68
  48.0 0.8 %shard_map.128 = (bf16[32,2304]{1,0:T(8,128)(2,1)S(1)}, bf16[32,512]{1,0:T(8,128)(2,1)S(1)}, bf16[32,2816]{1,0:T(8,128)(2,1)S(1)}) custom-call(f32[1,2304]{1,0:T(1,128)S(1)} %broadcast_in_dim.7.refs_0_.refs_1_, bf16[2304,512]{1,0:T(8,128)(2,1)S(1)} %copy-done.1, f32[1,512]{1,0:T(1,128)S(1)} %bitcast.12, f32[32,2304]{1,0:T(8,128)S(1)} %get-tuple-element.55.refs_3_, ...), custom_call_target="tpu_custom_call" | custom-call | flops 1000000000 | tf_op jit(solution)/shard_map/pallas_call | solution.py:45
  48.8 2.7 %collective-permute-start.16 = (bf16[32,2816]{1,0:T(8,128)(2,1)S(1)}, bf16[32,2816]{1,0:T(8,128)(2,1)S(1)}, u32[]{:S(2)}, u32[]{:S(2)}) collective-permute-start(bf16[32,2816]{1,0:T(8,128)(2,1)S(1)} %get-tuple-element.60), channel_id=1, source_target_pairs={{0,1},{1,0},{2,3},{3,2},{4,5},{5,4},{6,7},{7,6},{8,9},{9,8},{10,11... | collective-permute-start | bytes 540680 | tf_op jit(solution)/shard_map/ppermute | solution.py:68
  51.5 1.1 %collective-permute-start.19 = (bf16[32,512]{1,0:T(8,128)(2,1)S(1)}, bf16[32,512]{1,0:T(8,128)(2,1)S(1)}, u32[]{:S(2)}, u32[]{:S(2)}) collective-permute-start(bf16[32,512]{1,0:T(8,128)(2,1)S(1)} %get-tuple-element.61.refs_1_), channel_id=1, source_target_pairs={{0,2},{1,3},{2,0},{3,1},{4,6},{5,7},{6,4},{7,5},{8,10},{9,11},{10,... | collective-permute-start | bytes 98312 | tf_op jit(solution)/shard_map/ppermute | solution.py:68
  52.6 1.4 %collective-permute-start.20 = (bf16[32,512]{1,0:T(8,128)(2,1)S(1)}, bf16[32,512]{1,0:T(8,128)(2,1)S(1)}, u32[]{:S(2)}, u32[]{:S(2)}) collective-permute-start(bf16[32,512]{1,0:T(8,128)(2,1)S(1)} %get-tuple-element.61.refs_1_), channel_id=1, source_target_pairs={{0,3},{1,2},{2,1},{3,0},{4,7},{5,6},{6,5},{7,4},{8,11},{9,10},{10,... | collective-permute-start | bytes 98312 | tf_op jit(solution)/shard_map/ppermute | solution.py:68
  54.0 2.0 %collective-permute-start.17 = (bf16[32,2304]{1,0:T(8,128)(2,1)S(1)}, bf16[32,2304]{1,0:T(8,128)(2,1)S(1)}, u32[]{:S(2)}, u32[]{:S(2)}) collective-permute-start(bf16[32,2304]{1,0:T(8,128)(2,1)S(1)} %get-tuple-element.59.refs_4_), channel_id=1, source_target_pairs={{0,2},{1,3},{2,0},{3,1},{4,6},{5,7},{6,4},{7,5},{8,10},{9,11},{10,... | collective-permute-start | bytes 442376 | tf_op jit(solution)/shard_map/ppermute | solution.py:68
  56.0 1.4 %collective-permute-done.19.refs_3_ = bf16[32,512]{1,0:T(8,128)(2,1)S(1)} collective-permute-done((bf16[32,512]{1,0:T(8,128)(2,1)S(1)}, bf16[32,512]{1,0:T(8,128)(2,1)S(1)}, u32[]{:S(2)}, u32[]{:S(2)}) %collective-permute-start.19) | collective-permute-done | bytes 32800 | tf_op jit(solution)/shard_map/ppermute | solution.py:68
  57.4 3.2 %collective-permute-done.20.refs_4_ = bf16[32,512]{1,0:T(8,128)(2,1)S(1)} collective-permute-done((bf16[32,512]{1,0:T(8,128)(2,1)S(1)}, bf16[32,512]{1,0:T(8,128)(2,1)S(1)}, u32[]{:S(2)}, u32[]{:S(2)}) %collective-permute-start.20) | collective-permute-done | bytes 32800 | tf_op jit(solution)/shard_map/ppermute | solution.py:68
  60.6 0.6 shard_map.129.refs_8_
  61.2 1.5 %collective-permute-start.21 = (bf16[128,512]{1,0:T(8,128)(2,1)S(1)}, bf16[128,512]{1,0:T(8,128)(2,1)S(1)}, u32[]{:S(2)}, u32[]{:S(2)}) collective-permute-start(bf16[128,512]{1,0:T(8,128)(2,1)S(1)} %shard_map.129.refs_8_), channel_id=1, source_target_pairs={{0,24},{4,28},{8,16},{12,20},{16,8},{20,12},{24,0},{28,4},{1,25},{... | collective-permute-start | bytes 393224 | tf_op jit(solution)/shard_map/ppermute | solution.py:68
  62.7 1.1 %collective-permute-start.22 = (bf16[128,512]{1,0:T(8,128)(2,1)S(1)}, bf16[128,512]{1,0:T(8,128)(2,1)S(1)}, u32[]{:S(2)}, u32[]{:S(2)}) collective-permute-start(bf16[128,512]{1,0:T(8,128)(2,1)S(1)} %shard_map.129.refs_8_), channel_id=1, source_target_pairs={{0,16},{4,20},{8,24},{12,28},{16,0},{20,4},{24,8},{28,12},{1,17},{... | collective-permute-start | bytes 393224 | tf_op jit(solution)/shard_map/ppermute | solution.py:68
  63.8 0.9 %collective-permute-start.23 = (bf16[128,512]{1,0:T(8,128)(2,1)S(1)}, bf16[128,512]{1,0:T(8,128)(2,1)S(1)}, u32[]{:S(2)}, u32[]{:S(2)}) collective-permute-start(bf16[128,512]{1,0:T(8,128)(2,1)S(1)} %shard_map.129.refs_8_), channel_id=1, source_target_pairs={{0,8},{4,12},{8,0},{12,4},{16,24},{20,28},{24,16},{28,20},{1,9},{5... | collective-permute-start | bytes 393224 | tf_op jit(solution)/shard_map/ppermute | solution.py:68
  64.7 0.2 collective-permute-start.18
  64.9 2.2 %collective-permute-done.21.refs_9_ = bf16[128,512]{1,0:T(8,128)(2,1)S(1)} collective-permute-done((bf16[128,512]{1,0:T(8,128)(2,1)S(1)}, bf16[128,512]{1,0:T(8,128)(2,1)S(1)}, u32[]{:S(2)}, u32[]{:S(2)}) %collective-permute-start.21) | collective-permute-done | bytes 131104 | tf_op jit(solution)/shard_map/ppermute | solution.py:68
  67.2 1.3 %collective-permute-done.22.refs_10_ = bf16[128,512]{1,0:T(8,128)(2,1)S(1)} collective-permute-done((bf16[128,512]{1,0:T(8,128)(2,1)S(1)}, bf16[128,512]{1,0:T(8,128)(2,1)S(1)}, u32[]{:S(2)}, u32[]{:S(2)}) %collective-permute-start.22) | collective-permute-done | bytes 131104 | tf_op jit(solution)/shard_map/ppermute | solution.py:68
  68.5 0.2 collective-permute-done.23.refs_11_
  68.7 0.3 collective-permute-start.27
  69.0 0.2 copy.13
  69.3 0.6 collective-permute-done.18.refs_7_
  69.9 0.2 collective-permute-done.27.refs_15_
  70.1 3.8 %shard_map.130 = (bf16[128,2304]{1,0:T(8,128)(2,1)}, bf16[128,512]{1,0:T(8,128)(2,1)}) custom-call(s32[3]{0:T(128)S(1)} %pad_add_fusion.place.refs_0_, f32[1,2304]{1,0:T(1,128)S(1)} %broadcast_in_dim.7.refs_0_.refs_1_, bf16[2304,512]{1,0:T(8,128)(2,1)S(1)} %copy-done.2, bf16[512,1024]{1,0:T(8,128)(2,1)S(1)} %bitcast.9, ...), custom_call_target="tpu_custom_call" | custom-call | flops 4000000000 | tf_op jit(solution)/shard_map/pallas_call | solution.py:45
  (40 shorter events, 0.1 us)
Async XLA Ops:
  1.6 5.7 %collective-permute-start = (bf16[3,16,1024]{2,1,0:T(8,128)(2,1)S(1)}, bf16[3,16,1024]{2,1,0:T(8,128)(2,1)S(1)}, u32[]{:S(2)}, u32[]{:S(2)}) collective-permute-start(bf16[3,16,1024]{2,1,0:T(8,128)(2,1)S(1)} %get-tuple-element.62), channel_id=1, source_target_pairs={{0,4},{4,8},{8,12},{12,16},{16,20},{20,24},{24,28},{28,0},{1,5},{5... | collective-permute-start | bytes 294920 | tf_op jit(solution)/shard_map/ppermute | solution.py:73
  2.1 5.2 %copy-start.3 = (f32[128,8]{0,1:T(8,128)S(1)}, f32[128,8]{0,1:T(8,128)}, u32[]{:S(2)}) copy-start(f32[128,8]{0,1:T(8,128)} %param.13) | copy-start | bytes 12292
  11.0 1.7 %collective-permute-start.1 = (bf16[4,272,128]{2,1,0:T(8,128)(2,1)S(1)}, bf16[4,272,128]{2,1,0:T(8,128)(2,1)S(1)}, u32[]{:S(2)}, u32[]{:S(2)}) collective-permute-start(bf16[4,272,128]{2,1,0:T(8,128)(2,1)S(1)} %get-tuple-element.36), channel_id=1, source_target_pairs={{0,4},{4,0},{8,12},{12,8},{16,20},{20,16},{24,28},{28,24},{1,5},{5... | collective-permute-start | bytes 835592 | tf_op jit(solution)/shard_map/ppermute | solution.py:68
  11.6 5.7 %collective-permute-start.5 = (bf16[4,272,128]{2,1,0:T(8,128)(2,1)S(1)}, bf16[4,272,128]{2,1,0:T(8,128)(2,1)S(1)}, u32[]{:S(2)}, u32[]{:S(2)}) collective-permute-start(bf16[4,272,128]{2,1,0:T(8,128)(2,1)S(1)} %get-tuple-element.35.kept), channel_id=1, source_target_pairs={{0,4},{4,0},{8,12},{12,8},{16,20},{20,16},{24,28},{28,24},{1,5},{5... | collective-permute-start | bytes 835592 | tf_op jit(solution)/shard_map/ppermute | solution.py:68
  13.6 7.1 %collective-permute-start.2 = (bf16[272,128]{1,0:T(8,128)(2,1)S(1)}, bf16[272,128]{1,0:T(8,128)(2,1)S(1)}, u32[]{:S(2)}, u32[]{:S(2)}) collective-permute-start(bf16[272,128]{1,0:T(8,128)(2,1)S(1)} %get-tuple-element.38), channel_id=1, source_target_pairs={{0,8},{4,12},{8,0},{12,4},{16,24},{20,28},{24,16},{28,20},{1,9},{5... | collective-permute-start | bytes 208904 | tf_op jit(solution)/shard_map/ppermute | solution.py:68
  15.2 5.5 %collective-permute-start.3 = (bf16[272,128]{1,0:T(8,128)(2,1)S(1)}, bf16[272,128]{1,0:T(8,128)(2,1)S(1)}, u32[]{:S(2)}, u32[]{:S(2)}) collective-permute-start(bf16[272,128]{1,0:T(8,128)(2,1)S(1)} %get-tuple-element.39), channel_id=1, source_target_pairs={{0,16},{4,20},{8,24},{12,28},{16,0},{20,4},{24,8},{28,12},{1,17},{... | collective-permute-start | bytes 208904 | tf_op jit(solution)/shard_map/ppermute | solution.py:68
  16.4 5.2 %collective-permute-start.4 = (bf16[272,128]{1,0:T(8,128)(2,1)S(1)}, bf16[272,128]{1,0:T(8,128)(2,1)S(1)}, u32[]{:S(2)}, u32[]{:S(2)}) collective-permute-start(bf16[272,128]{1,0:T(8,128)(2,1)S(1)} %get-tuple-element.40), channel_id=1, source_target_pairs={{0,24},{4,28},{8,16},{12,20},{16,8},{20,12},{24,0},{28,4},{1,25},{... | collective-permute-start | bytes 208904 | tf_op jit(solution)/shard_map/ppermute | solution.py:68
  17.3 13.1 %slice-start = ((s8[4718592]{0:T(1024)(128)(4,1)}), s8[4194304]{0:T(1024)(128)(4,1)S(1)}, s32[]{:S(2)}) async-start(s8[4718592]{0:T(1024)(128)(4,1)} %bitcast.7), calls=%async_computation | async-start | bytes 8388608
  17.3 13.1 %slice-start.1 = ((s8[4718592]{0:T(1024)(128)(4,1)}), s8[524288]{0:T(1024)(128)(4,1)S(1)}, s32[]{:S(2)}) async-start(s8[4718592]{0:T(1024)(128)(4,1)} %bitcast.7), calls=%async_computation.1 | async-start | bytes 1048576
  20.6 9.7 %copy-start = (bf16[128,2304]{1,0:T(8,128)(2,1)S(1)}, bf16[128,2304]{1,0:T(8,128)(2,1)}, u32[]{:S(2)}) copy-start(bf16[128,2304]{1,0:T(8,128)(2,1)} %refs_1_.2) | copy-start | bytes 1769476
  22.5 4.2 %collective-permute-start.6 = (bf16[128,128]{1,0:T(8,128)(2,1)S(1)}, bf16[128,128]{1,0:T(8,128)(2,1)S(1)}, u32[]{:S(2)}, u32[]{:S(2)}) collective-permute-start(bf16[128,128]{1,0:T(8,128)(2,1)S(1)} %get-tuple-element.52), channel_id=1, source_target_pairs={{0,8},{4,12},{8,0},{12,4},{16,24},{20,28},{24,16},{28,20},{1,9},{5... | collective-permute-start | bytes 98312 | tf_op jit(solution)/shard_map/ppermute | solution.py:68
  24.0 3.9 %collective-permute-start.7 = (bf16[128,128]{1,0:T(8,128)(2,1)S(1)}, bf16[128,128]{1,0:T(8,128)(2,1)S(1)}, u32[]{:S(2)}, u32[]{:S(2)}) collective-permute-start(bf16[128,128]{1,0:T(8,128)(2,1)S(1)} %get-tuple-element.53), channel_id=1, source_target_pairs={{0,16},{4,20},{8,24},{12,28},{16,0},{20,4},{24,8},{28,12},{1,17},{... | collective-permute-start | bytes 98312 | tf_op jit(solution)/shard_map/ppermute | solution.py:68
  24.4 4.8 %collective-permute-start.8 = (bf16[128,128]{1,0:T(8,128)(2,1)S(1)}, bf16[128,128]{1,0:T(8,128)(2,1)S(1)}, u32[]{:S(2)}, u32[]{:S(2)}) collective-permute-start(bf16[128,128]{1,0:T(8,128)(2,1)S(1)} %get-tuple-element.54), channel_id=1, source_target_pairs={{0,24},{4,28},{8,16},{12,20},{16,8},{20,12},{24,0},{28,4},{1,25},{... | collective-permute-start | bytes 98312 | tf_op jit(solution)/shard_map/ppermute | solution.py:68
  26.0 10.6 %copy-start.6 = (f32[2304]{0:T(1024)S(1)}, f32[2304]{0:T(1024)}, u32[]{:S(2)}) copy-start(f32[2304]{0:T(1024)} %param.17) | copy-start | bytes 27652
  26.0 22.0 %copy-start.1 = (bf16[2304,512]{1,0:T(8,128)(2,1)S(1)}, bf16[2304,512]{1,0:T(8,128)(2,1)}, u32[]{:S(2)}) copy-start(bf16[2304,512]{1,0:T(8,128)(2,1)} %refs_1_.3) | copy-start | bytes 7077892
  26.1 22.0 %copy-start.4 = (f32[512]{0:T(512)S(1)}, f32[512]{0:T(512)}, u32[]{:S(2)}) copy-start(f32[512]{0:T(512)} %param.19) | copy-start | bytes 6148
  26.1 3.1 %collective-permute-start.9 = (bf16[128,128]{1,0:T(8,128)(2,1)S(1)}, bf16[128,128]{1,0:T(8,128)(2,1)S(1)}, u32[]{:S(2)}, u32[]{:S(2)}) collective-permute-start(bf16[128,128]{1,0:T(8,128)(2,1)S(1)} %get-tuple-element.51.refs_5_), channel_id=1, source_target_pairs={{0,4},{4,0},{8,12},{12,8},{16,20},{20,16},{24,28},{28,24},{1,5},{5... | collective-permute-start | bytes 98312 | tf_op jit(solution)/shard_map/ppermute | solution.py:68
  26.7 2.5 %collective-permute-start.10 = (bf16[128,128]{1,0:T(8,128)(2,1)S(1)}, bf16[128,128]{1,0:T(8,128)(2,1)S(1)}, u32[]{:S(2)}, u32[]{:S(2)}) collective-permute-start(bf16[128,128]{1,0:T(8,128)(2,1)S(1)} %collective-permute-done.6.refs_6_), channel_id=1, source_target_pairs={{0,4},{4,0},{8,12},{12,8},{16,20},{20,16},{24,28},{28,24},{1,5},{5... | collective-permute-start | bytes 98312 | tf_op jit(solution)/shard_map/ppermute | solution.py:68
  27.9 1.3 %collective-permute-start.11 = (bf16[128,128]{1,0:T(8,128)(2,1)S(1)}, bf16[128,128]{1,0:T(8,128)(2,1)S(1)}, u32[]{:S(2)}, u32[]{:S(2)}) collective-permute-start(bf16[128,128]{1,0:T(8,128)(2,1)S(1)} %collective-permute-done.7.refs_7_), channel_id=1, source_target_pairs={{0,4},{4,0},{8,12},{12,8},{16,20},{20,16},{24,28},{28,24},{1,5},{5... | collective-permute-start | bytes 98312 | tf_op jit(solution)/shard_map/ppermute | solution.py:68
  29.2 1.2 %collective-permute-start.12 = (bf16[128,128]{1,0:T(8,128)(2,1)S(1)}, bf16[128,128]{1,0:T(8,128)(2,1)S(1)}, u32[]{:S(2)}, u32[]{:S(2)}) collective-permute-start(bf16[128,128]{1,0:T(8,128)(2,1)S(1)} %collective-permute-done.8.refs_8_), channel_id=1, source_target_pairs={{0,4},{4,0},{8,12},{12,8},{16,20},{20,16},{24,28},{28,24},{1,5},{5... | collective-permute-start | bytes 98312 | tf_op jit(solution)/shard_map/ppermute | solution.py:68
  32.2 8.4 %collective-permute-start.13 = (bf16[32,2304]{1,0:T(8,128)(2,1)S(1)}, bf16[32,2304]{1,0:T(8,128)(2,1)S(1)}, u32[]{:S(2)}, u32[]{:S(2)}) collective-permute-start(bf16[32,2304]{1,0:T(8,128)(2,1)S(1)} %get-tuple-element.56), channel_id=1, source_target_pairs={{0,1},{1,0},{2,3},{3,2},{4,5},{5,4},{6,7},{7,6},{8,9},{9,8},{10,11... | collective-permute-start | bytes 442376 | tf_op jit(solution)/shard_map/ppermute | solution.py:68
  34.1 13.9 %collective-permute-start.14 = (bf16[32,2304]{1,0:T(8,128)(2,1)S(1)}, bf16[32,2304]{1,0:T(8,128)(2,1)S(1)}, u32[]{:S(2)}, u32[]{:S(2)}) collective-permute-start(bf16[32,2304]{1,0:T(8,128)(2,1)S(1)} %get-tuple-element.57), channel_id=1, source_target_pairs={{0,2},{1,3},{2,0},{3,1},{4,6},{5,7},{6,4},{7,5},{8,10},{9,11},{10,... | collective-permute-start | bytes 442376 | tf_op jit(solution)/shard_map/ppermute | solution.py:68
  36.7 11.4 %collective-permute-start.15 = (bf16[32,2304]{1,0:T(8,128)(2,1)S(1)}, bf16[32,2304]{1,0:T(8,128)(2,1)S(1)}, u32[]{:S(2)}, u32[]{:S(2)}) collective-permute-start(bf16[32,2304]{1,0:T(8,128)(2,1)S(1)} %get-tuple-element.58), channel_id=1, source_target_pairs={{0,3},{1,2},{2,1},{3,0},{4,7},{5,6},{6,5},{7,4},{8,11},{9,10},{10,... | collective-permute-start | bytes 442376 | tf_op jit(solution)/shard_map/ppermute | solution.py:68
  48.8 20.2 %copy-start.5 = (bf16[512,2,512]{2,1,0:T(2,128)(2,1)S(1)}, bf16[512,2,512]{2,1,0:T(2,128)(2,1)}, u32[]{:S(2)}) copy-start(bf16[512,2,512]{2,1,0:T(2,128)(2,1)} %param.21) | copy-start | bytes 3145732
  48.8 11.8 %collective-permute-start.16 = (bf16[32,2816]{1,0:T(8,128)(2,1)S(1)}, bf16[32,2816]{1,0:T(8,128)(2,1)S(1)}, u32[]{:S(2)}, u32[]{:S(2)}) collective-permute-start(bf16[32,2816]{1,0:T(8,128)(2,1)S(1)} %get-tuple-element.60), channel_id=1, source_target_pairs={{0,1},{1,0},{2,3},{3,2},{4,5},{5,4},{6,7},{7,6},{8,9},{9,8},{10,11... | collective-permute-start | bytes 540680 | tf_op jit(solution)/shard_map/ppermute | solution.py:68
  51.5 5.9 %collective-permute-start.19 = (bf16[32,512]{1,0:T(8,128)(2,1)S(1)}, bf16[32,512]{1,0:T(8,128)(2,1)S(1)}, u32[]{:S(2)}, u32[]{:S(2)}) collective-permute-start(bf16[32,512]{1,0:T(8,128)(2,1)S(1)} %get-tuple-element.61.refs_1_), channel_id=1, source_target_pairs={{0,2},{1,3},{2,0},{3,1},{4,6},{5,7},{6,4},{7,5},{8,10},{9,11},{10,... | collective-permute-start | bytes 98312 | tf_op jit(solution)/shard_map/ppermute | solution.py:68
  52.6 8.0 %collective-permute-start.20 = (bf16[32,512]{1,0:T(8,128)(2,1)S(1)}, bf16[32,512]{1,0:T(8,128)(2,1)S(1)}, u32[]{:S(2)}, u32[]{:S(2)}) collective-permute-start(bf16[32,512]{1,0:T(8,128)(2,1)S(1)} %get-tuple-element.61.refs_1_), channel_id=1, source_target_pairs={{0,3},{1,2},{2,1},{3,0},{4,7},{5,6},{6,5},{7,4},{8,11},{9,10},{10,... | collective-permute-start | bytes 98312 | tf_op jit(solution)/shard_map/ppermute | solution.py:68
  54.0 16.1 %copy-start.2 = (bf16[2304,512]{1,0:T(8,128)(2,1)S(1)}, bf16[2304,512]{1,0:T(8,128)(2,1)}, u32[]{:S(2)}) copy-start(bf16[2304,512]{1,0:T(8,128)(2,1)} %refs_2_.3) | copy-start | bytes 7077892
  54.0 10.7 %collective-permute-start.17 = (bf16[32,2304]{1,0:T(8,128)(2,1)S(1)}, bf16[32,2304]{1,0:T(8,128)(2,1)S(1)}, u32[]{:S(2)}, u32[]{:S(2)}) collective-permute-start(bf16[32,2304]{1,0:T(8,128)(2,1)S(1)} %get-tuple-element.59.refs_4_), channel_id=1, source_target_pairs={{0,2},{1,3},{2,0},{3,1},{4,6},{5,7},{6,4},{7,5},{8,10},{9,11},{10,... | collective-permute-start | bytes 442376 | tf_op jit(solution)/shard_map/ppermute | solution.py:68
  61.2 6.0 %collective-permute-start.21 = (bf16[128,512]{1,0:T(8,128)(2,1)S(1)}, bf16[128,512]{1,0:T(8,128)(2,1)S(1)}, u32[]{:S(2)}, u32[]{:S(2)}) collective-permute-start(bf16[128,512]{1,0:T(8,128)(2,1)S(1)} %shard_map.129.refs_8_), channel_id=1, source_target_pairs={{0,24},{4,28},{8,16},{12,20},{16,8},{20,12},{24,0},{28,4},{1,25},{... | collective-permute-start | bytes 393224 | tf_op jit(solution)/shard_map/ppermute | solution.py:68
  62.7 5.8 %collective-permute-start.22 = (bf16[128,512]{1,0:T(8,128)(2,1)S(1)}, bf16[128,512]{1,0:T(8,128)(2,1)S(1)}, u32[]{:S(2)}, u32[]{:S(2)}) collective-permute-start(bf16[128,512]{1,0:T(8,128)(2,1)S(1)} %shard_map.129.refs_8_), channel_id=1, source_target_pairs={{0,16},{4,20},{8,24},{12,28},{16,0},{20,4},{24,8},{28,12},{1,17},{... | collective-permute-start | bytes 393224 | tf_op jit(solution)/shard_map/ppermute | solution.py:68
  63.8 5.0 %collective-permute-start.23 = (bf16[128,512]{1,0:T(8,128)(2,1)S(1)}, bf16[128,512]{1,0:T(8,128)(2,1)S(1)}, u32[]{:S(2)}, u32[]{:S(2)}) collective-permute-start(bf16[128,512]{1,0:T(8,128)(2,1)S(1)} %shard_map.129.refs_8_), channel_id=1, source_target_pairs={{0,8},{4,12},{8,0},{12,4},{16,24},{20,28},{24,16},{28,20},{1,9},{5... | collective-permute-start | bytes 393224 | tf_op jit(solution)/shard_map/ppermute | solution.py:68
  64.7 5.1 %collective-permute-start.18 = (bf16[32,2304]{1,0:T(8,128)(2,1)S(1)}, bf16[32,2304]{1,0:T(8,128)(2,1)S(1)}, u32[]{:S(2)}, u32[]{:S(2)}) collective-permute-start(bf16[32,2304]{1,0:T(8,128)(2,1)S(1)} %collective-permute-done.17.refs_6_), channel_id=1, source_target_pairs={{0,1},{1,0},{2,3},{3,2},{4,5},{5,4},{6,7},{7,6},{8,9},{9,8},{10,11... | collective-permute-start | bytes 442376 | tf_op jit(solution)/shard_map/ppermute | solution.py:68
  64.9 4.9 %collective-permute-start.24 = (bf16[128,512]{1,0:T(8,128)(2,1)S(1)}, bf16[128,512]{1,0:T(8,128)(2,1)S(1)}, u32[]{:S(2)}, u32[]{:S(2)}) collective-permute-start(bf16[128,512]{1,0:T(8,128)(2,1)S(1)} %shard_map.129.refs_8_), channel_id=1, source_target_pairs={{0,4},{4,0},{8,12},{12,8},{16,20},{20,16},{24,28},{28,24},{1,5},{5... | collective-permute-start | bytes 393224 | tf_op jit(solution)/shard_map/ppermute | solution.py:68
  67.2 2.7 %collective-permute-start.25 = (bf16[128,512]{1,0:T(8,128)(2,1)S(1)}, bf16[128,512]{1,0:T(8,128)(2,1)S(1)}, u32[]{:S(2)}, u32[]{:S(2)}) collective-permute-start(bf16[128,512]{1,0:T(8,128)(2,1)S(1)} %collective-permute-done.21.refs_9_), channel_id=1, source_target_pairs={{0,4},{4,0},{8,12},{12,8},{16,20},{20,16},{24,28},{28,24},{1,5},{5... | collective-permute-start | bytes 393224 | tf_op jit(solution)/shard_map/ppermute | solution.py:68
  68.5 1.4 %collective-permute-start.26 = (bf16[128,512]{1,0:T(8,128)(2,1)S(1)}, bf16[128,512]{1,0:T(8,128)(2,1)S(1)}, u32[]{:S(2)}, u32[]{:S(2)}) collective-permute-start(bf16[128,512]{1,0:T(8,128)(2,1)S(1)} %collective-permute-done.22.refs_10_), channel_id=1, source_target_pairs={{0,4},{4,0},{8,12},{12,8},{16,20},{20,16},{24,28},{28,24},{1,5},{5... | collective-permute-start | bytes 393224 | tf_op jit(solution)/shard_map/ppermute | solution.py:68
  68.7 1.3 %collective-permute-start.27 = (bf16[128,512]{1,0:T(8,128)(2,1)S(1)}, bf16[128,512]{1,0:T(8,128)(2,1)S(1)}, u32[]{:S(2)}, u32[]{:S(2)}) collective-permute-start(bf16[128,512]{1,0:T(8,128)(2,1)S(1)} %collective-permute-done.23.refs_11_), channel_id=1, source_target_pairs={{0,4},{4,0},{8,12},{12,8},{16,20},{20,16},{24,28},{28,24},{1,5},{5... | collective-permute-start | bytes 393224 | tf_op jit(solution)/shard_map/ppermute | solution.py:68

commit v6 on v5

--- a/solution.py
+++ b/solution.py
@@ -278,26 +278,29 @@
 
 
 def scan_kernel(pairs, grouped, *refs):
-    place, blocks, rest = refs[0], refs[1 : 1 + pairs], refs[1 + pairs :]
+    place, refs = refs[0], refs[1:]
+    sides, refs = (refs[:pairs], refs[pairs : 2 * pairs]), refs[2 * pairs :]
     if grouped:
-        start, rest = rest[0], rest[1:]
-    outs, rest = rest[:pairs], rest[pairs:]
+        start, refs = refs[0], refs[1:]
+    outs, refs = refs[:pairs], refs[pairs:]
     if grouped:
-        final, rest = rest[0], rest[1:]
-    maps, starts = rest
+        final, refs = refs[0], refs[1:]
+    maps, starts = refs
     chip, _ = split_cores(place)
-    for step in range(pairs):
-        maps[partner(chip, step, pairs)] = blocks[step][...]
-    state = start[...] if grouped else jnp.zeros((DK, DK), f32)
+    for side in range(2):
+        for step in range(pairs):
+            maps[side, partner(chip, step, pairs)] = sides[side][step][...]
+    states = [start[side] if grouped else jnp.zeros((DK, DK), f32) for side in range(2)]
     for i in range(pairs):
-        starts[i] = state.astype(bf16)
-        if i < pairs - 1 or grouped:
+        for side in range(2):
+            starts[i, side] = states[side].astype(bf16)
             if i == 0 and not grouped:
-                state = maps[i, :DK, :].astype(f32)
-            else:
-                state = apply_map(state, maps[i])
+                states[side] = maps[side, i, :DK, :].astype(f32)
+            elif i < pairs - 1 or grouped:
+                states[side] = apply_map(states[side], maps[side, i])
     if grouped:
-        final[...] = state
+        for side in range(2):
+            final[side] = states[side]
     for step in range(pairs):
         outs[step][...] = starts[partner(chip, step, pairs)]
 
@@ -306,15 +309,15 @@
     place, residual, weight, reads, intra = refs[:5]
     refs = refs[5:]
     pairs = reads.shape[1] // DK // 2
-    mine, other, refs = refs[:pairs], refs[pairs : 2 * pairs], refs[2 * pairs :]
+    starts, refs = refs[:pairs], refs[pairs:]
     outs, (whole, summed) = refs[:parts], refs[parts:]
     chip, core = split_cores(place)
     head_me = place[1]
     for step in range(pairs):
         pair = partner(chip, step, pairs)
-        for states, side in ((mine, core), (other, 1 - core)):
-            own = lanes(2 * pair + side)
-            whole[:, own] = (intra[:, own] + mm_nt(reads[:, own], states[step][...])).astype(bf16)
+        for side, head in enumerate((2 * pair + core, 2 * pair + 1 - core)):
+            own = lanes(head)
+            whole[:, own] = (intra[:, own] + mm_nt(reads[:, own], starts[step][side])).astype(bf16)
     summed[...] = jnp.dot(whole[...], weight[...], preferred_element_type=f32)
     share = summed.shape[0] // parts
     for step in range(parts):
@@ -486,37 +489,36 @@
         return [pieces[0]] + [moved[step] for step in range(1, pairs)]
 
     chip_maps, reads, intra = lax.optimization_barrier((across_chips(chip_maps), reads, intra))
-    state_outs = [((DK, DK), bf16)] * pairs
-    scratch = [((pairs,) + map_shape, bf16), ((pairs, DK, DK), bf16)]
+    other_maps = [trade(one, "ctx", 1, heads) for one in chip_maps]
+    state_outs = [((2, DK, DK), bf16)] * pairs
+    scratch = [((2, pairs) + map_shape, bf16), ((pairs, 2, DK, DK), bf16)]
+
+    def run(*start):
+        return call(
+            functools.partial(scan_kernel, pairs, len(start) > 0),
+            state_outs + [((2, DK, DK), f32)] * len(start),
+            [place] + chip_maps + other_maps + list(start),
+            scratch,
+            8,
+        )
+
     if groups == 1:
-        starts = call(
-            functools.partial(scan_kernel, pairs, False), state_outs, [place] + chip_maps, scratch, 8
-        )
+        starts = run()
     else:
-
-        def run(start):
-            return call(
-                functools.partial(scan_kernel, pairs, True),
-                state_outs + [((DK, DK), f32)],
-                [place] + chip_maps + [start],
-                scratch,
-                8,
-            )
 
         def relay(step_index, start):
             arrived = passed_along(run(start)[pairs], "ctx", heads)
             return jnp.where(ctx_me < heads, 0.0, arrived)
 
-        start = lax.fori_loop(0, groups - 1, relay, jnp.zeros((DK, DK), f32))
+        start = lax.fori_loop(0, groups - 1, relay, jnp.zeros((2, DK, DK), f32))
         starts = run(start)[:pairs]
     starts = across_chips(starts)
-    others = [trade(state, "ctx", 1, heads) for state in starts]
 
     share = length // parts
     partials = call(
         functools.partial(project_kernel, parts),
         [((share, width), f32)] + [((share, width), bf16)] * (parts - 1),
-        [place, residual, kda_out_weight, reads, intra] + starts + others,
+        [place, residual, kda_out_weight, reads, intra] + starts,
         [((length, heads * DK), bf16), ((length, width), f32)],
         16,
     )
@@ -525,7 +527,8 @@
         moved = {step: trade(pieces[step], "head", step, parts) for step in far_first(parts)}
         return [pieces[0]] + [moved[step] for step in range(1, parts)]
 
-    partials = across_heads(partials)
+    up = up_weight.reshape(up_weight.shape[0], -1)
+    partials, up = lax.optimization_barrier((across_heads(partials), up))
     latent_width = latent_weight.shape[1]
     stream_rows, latent_rows, together = call(
         functools.partial(latent_kernel, parts),
@@ -557,7 +560,6 @@
     for position in range(len(order)):
         order.append(order[position] + 1)
         latents.append(trade(latents[position], "ctx", 1, 2))
-    up = up_weight.reshape(up_weight.shape[0], -1)
     heads_mla = query_weight.shape[1] // DH
     rows, latent_rows = heads_mla * length, count * length
     stream_out, attention_out = call(

time: 74.1 us -> 72.8 us (0.982)
  waiting for transfers between devices: 29 us -> 27 us
    ppermute x27, waiting for transfers between devices: 26.9 us -> 24.9 us  [trade(): return lax.ppermute(block, axis, route)]
  transfers between devices with their start and end apart: 28 -> 28, of which waited for: 16 -> 18; matrix products, arithmetic and copies ran while one was open for 0% -> 0% of each run, Pallas kernels for 10% -> 11%
where the time goes in v6:
time: 72.8 us; the launch traced here: 72.7 us
  waiting for transfers between devices  27 us (37%)
  starting transfers between devices  24.8 us (34%)
  Pallas kernels  18.7 us (26%)
  local copies, waits for them, and re-layouts  1.26 us (2%)
  between operations  0.84 us (1%)
    ppermute x27, waiting for transfers between devices, trade(): return lax.ppermute(block, axis, route)  24.9 us
    ppermute x27, starting transfers between devices, trade(): return lax.ppermute(block, axis, route)  24.2 us
    pallas_call x9, Pallas kernels, call(): pl.pallas_call(kernel, out_shape=[jax.ShapeDtypeStruct(shape, dtype) for...  18.7 us
    ppermute x1, waiting for transfers between devices, passed_along(): lax.ppermute(block, axis, [(i, (i + distance) % count) for i in range(cou...  2.1 us
  transfers between devices with their start and end apart: 28, of which 18 were waited for; matrix products, arithmetic and copies ran while one was open for 0% of the time, Pallas kernels for 11%

profile of v6, /device:TPU:0, one launch (start us, length us, event | category | flops | bytes accessed | tf_op | source)
XLA Modules:
  0.0 72.7 jit_solution(14315016512567747202)
XLA Ops:
  0.6 1.0 %fusion = (bf16[3,16,1024]{2,1,0:T(8,128)(2,1)S(1)}, bf16[3,16,1024]{2,1,0:T(8,128)(2,1)S(1)}) fusion(bf16[3,128,1024]{2,1,0:T(8,128)(2,1)} %stored_inputs.1), kind=kLoop, calls=%fused_computation.1 | loop fusion | bytes 393216 | tf_op jit(solution)/shard_map/slice | solution.py:434
  1.6 0.5 collective-permute-start
  2.1 3.0 %shard_map.122 = (bf16[3,128,1024]{2,1,0:T(8,128)(2,1)S(1)}, f32[128,1024]{1,0:T(8,128)S(1)}, f32[3,4,1024]{2,1,0:T(4,128)S(1)}) custom-call(bf16[3,128,1024]{2,1,0:T(8,128)(2,1)} %stored_inputs.1, f32[128,1024]{1,0:T(8,128)} %stored_gate.1, f32[3,4,1024]{2,1,0:T(4,128)} %stored_taps.1), custom_call_target="tpu_custom_call" | custom-call | flops 2000000000 | tf_op jit(solution)/shard_map/pallas_call | solution.py:45
  5.2 2.1 %collective-permute-done.halo = bf16[3,16,1024]{2,1,0:T(8,128)(2,1)S(1)} collective-permute-done((bf16[3,16,1024]{2,1,0:T(8,128)(2,1)S(1)}, bf16[3,16,1024]{2,1,0:T(8,128)(2,1)S(1)}, u32[]{:S(2)}, u32[]{:S(2)}) %collective-permute-start) | collective-permute-done | bytes 98336 | tf_op jit(solution)/shard_map/ppermute | solution.py:73
  7.3 3.7 %shard_map.123 = (bf16[4,272,128]{2,1,0:T(8,128)(2,1)S(1)}, bf16[4,272,128]{2,1,0:T(8,128)(2,1)S(1)}, bf16[8,128,256]{2,1,0:T(8,128)(2,1)S(1)}, bf16[8,2,128,128]{3,2,1,0:T(8,128)(2,1)S(1)}) custom-call(s32[3]{0:T(128)S(1)} %pad_add_fusion.place.refs_0_, bf16[3,128,1024]{2,1,0:T(8,128)(2,1)S(1)} %get-tuple-element.37.done, ...), custom_call_target="tpu_custom_call" | custom-call | flops 5000000000 | tf_op jit(solution)/shard_map/pallas_call | solution.py:45
  11.0 0.6 collective-permute-start.1
  11.7 1.1 %collective-permute-done.1.got.refs_2_ = bf16[4,272,128]{2,1,0:T(8,128)(2,1)S(1)} collective-permute-done((bf16[4,272,128]{2,1,0:T(8,128)(2,1)S(1)}, bf16[4,272,128]{2,1,0:T(8,128)(2,1)S(1)}, u32[]{:S(2)}, u32[]{:S(2)}) %collective-permute-start.1) | collective-permute-done | bytes 278560 | tf_op jit(solution)/shard_map/ppermute | solution.py:68
  12.8 0.8 %shard_map.124 = (bf16[272,128]{1,0:T(8,128)(2,1)S(1)}, bf16[272,128]{1,0:T(8,128)(2,1)S(1)}, bf16[272,128]{1,0:T(8,128)(2,1)S(1)}, bf16[272,128]{1,0:T(8,128)(2,1)S(1)}) custom-call(s32[3]{0:T(128)S(1)} %pad_add_fusion.place.refs_0_, bf16[4,272,128]{2,1,0:T(8,128)(2,1)S(1)} %get-tuple-element.40.kept, ...), custom_call_target="tpu_custom_call" | custom-call | flops 1000000000 | tf_op jit(solution)/shard_map/pallas_call | solution.py:45
  13.6 1.6 %collective-permute-start.2 = (bf16[272,128]{1,0:T(8,128)(2,1)S(1)}, bf16[272,128]{1,0:T(8,128)(2,1)S(1)}, u32[]{:S(2)}, u32[]{:S(2)}) collective-permute-start(bf16[272,128]{1,0:T(8,128)(2,1)S(1)} %get-tuple-element.43), channel_id=1, source_target_pairs={{0,8},{4,12},{8,0},{12,4},{16,24},{20,28},{24,16},{28,20},{1,9},{5... | collective-permute-start | bytes 208904 | tf_op jit(solution)/shard_map/ppermute | solution.py:68
  15.2 1.3 %collective-permute-start.3 = (bf16[272,128]{1,0:T(8,128)(2,1)S(1)}, bf16[272,128]{1,0:T(8,128)(2,1)S(1)}, u32[]{:S(2)}, u32[]{:S(2)}) collective-permute-start(bf16[272,128]{1,0:T(8,128)(2,1)S(1)} %get-tuple-element.44), channel_id=1, source_target_pairs={{0,16},{4,20},{8,24},{12,28},{16,0},{20,4},{24,8},{28,12},{1,17},{... | collective-permute-start | bytes 208904 | tf_op jit(solution)/shard_map/ppermute | solution.py:68
  16.4 0.9 %collective-permute-start.4 = (bf16[272,128]{1,0:T(8,128)(2,1)S(1)}, bf16[272,128]{1,0:T(8,128)(2,1)S(1)}, u32[]{:S(2)}, u32[]{:S(2)}) collective-permute-start(bf16[272,128]{1,0:T(8,128)(2,1)S(1)} %get-tuple-element.45), channel_id=1, source_target_pairs={{0,24},{4,28},{8,16},{12,20},{16,8},{20,12},{24,0},{28,4},{1,25},{... | collective-permute-start | bytes 208904 | tf_op jit(solution)/shard_map/ppermute | solution.py:68
  17.3 3.3 %shard_map.125 = (bf16[128,1024]{1,0:T(8,128)(2,1)S(1)}, f32[128,1024]{1,0:T(8,128)S(1)}) custom-call(s32[3]{0:T(128)S(1)} %pad_add_fusion.place.refs_0_, bf16[3,128,1024]{2,1,0:T(8,128)(2,1)S(1)} %get-tuple-element.37.done, bf16[3,16,1024]{2,1,0:T(8,128)(2,1)S(1)} %get-tuple-element.73.head_rows, bf16[3,16,1024]{2,1,0:T(8,128)(2,1)S(1)} %collective-permute-done.halo, ...), custom_call_target="tpu_custom_call" | custom-call | flops 2500000000 | tf_op jit(solution)/shard_map/pallas_call | solution.py:45
  20.7 1.0 %collective-permute-done.4.refs_4_ = bf16[272,128]{1,0:T(8,128)(2,1)S(1)} collective-permute-done((bf16[272,128]{1,0:T(8,128)(2,1)S(1)}, bf16[272,128]{1,0:T(8,128)(2,1)S(1)}, u32[]{:S(2)}, u32[]{:S(2)}) %collective-permute-start.4) | collective-permute-done | bytes 69664 | tf_op jit(solution)/shard_map/ppermute | solution.py:68
  21.6 0.5 collective-permute-start.7
  22.2 0.5 collective-permute-start.9
  22.7 0.2 collective-permute-done.6.refs_5_
  22.9 0.2 collective-permute-done.7.refs_6_
  23.1 0.4 collective-permute-done.8.refs_7_
  23.4 0.2 collective-permute-done.9.refs_8_
  23.6 0.9 %shard_map.126 = (bf16[2,128,128]{2,1,0:T(8,128)(2,1)S(1)}, bf16[2,128,128]{2,1,0:T(8,128)(2,1)S(1)}, bf16[2,128,128]{2,1,0:T(8,128)(2,1)S(1)}, bf16[2,128,128]{2,1,0:T(8,128)(2,1)S(1)}) custom-call(s32[3]{0:T(128)S(1)} %pad_add_fusion.place.refs_0_, bf16[272,128]{1,0:T(8,128)(2,1)S(1)} %get-tuple-element.52.refs_1_, ...), custom_call_target="tpu_custom_call" | custom-call | flops 1000000000 | tf_op jit(solution)/shard_map/pallas_call | solution.py:45
  24.5 1.5 %collective-permute-start.10 = (bf16[2,128,128]{2,1,0:T(8,128)(2,1)S(1)}, bf16[2,128,128]{2,1,0:T(8,128)(2,1)S(1)}, u32[]{:S(2)}, u32[]{:S(2)}) collective-permute-start(bf16[2,128,128]{2,1,0:T(8,128)(2,1)S(1)} %get-tuple-element.57), channel_id=1, source_target_pairs={{0,8},{4,12},{8,0},{12,4},{16,24},{20,28},{24,16},{28,20},{1,9},{5... | collective-permute-start | bytes 196616 | tf_op jit(solution)/shard_map/ppermute | solution.py:68
  26.0 0.4 collective-permute-start.11
  26.3 1.7 %collective-permute-start.12 = (bf16[2,128,128]{2,1,0:T(8,128)(2,1)S(1)}, bf16[2,128,128]{2,1,0:T(8,128)(2,1)S(1)}, u32[]{:S(2)}, u32[]{:S(2)}) collective-permute-start(bf16[2,128,128]{2,1,0:T(8,128)(2,1)S(1)} %get-tuple-element.59), channel_id=1, source_target_pairs={{0,24},{4,28},{8,16},{12,20},{16,8},{20,12},{24,0},{28,4},{1,25},{... | collective-permute-start | bytes 196616 | tf_op jit(solution)/shard_map/ppermute | solution.py:68
  28.0 0.9 %collective-permute-done.10.refs_6_ = bf16[2,128,128]{2,1,0:T(8,128)(2,1)S(1)} collective-permute-done((bf16[2,128,128]{2,1,0:T(8,128)(2,1)S(1)}, bf16[2,128,128]{2,1,0:T(8,128)(2,1)S(1)}, u32[]{:S(2)}, u32[]{:S(2)}) %collective-permute-start.10) | collective-permute-done | bytes 65568 | tf_op jit(solution)/shard_map/ppermute | solution.py:68
  28.9 2.7 %collective-permute-done.11.refs_7_ = bf16[2,128,128]{2,1,0:T(8,128)(2,1)S(1)} collective-permute-done((bf16[2,128,128]{2,1,0:T(8,128)(2,1)S(1)}, bf16[2,128,128]{2,1,0:T(8,128)(2,1)S(1)}, u32[]{:S(2)}, u32[]{:S(2)}) %collective-permute-start.11) | collective-permute-done | bytes 65568 | tf_op jit(solution)/shard_map/ppermute | solution.py:68
  31.7 1.8 %shard_map.127 = (f32[32,2304]{1,0:T(8,128)S(1)}, bf16[32,2304]{1,0:T(8,128)(2,1)S(1)}, bf16[32,2304]{1,0:T(8,128)(2,1)S(1)}, bf16[32,2304]{1,0:T(8,128)(2,1)S(1)}) custom-call(s32[3]{0:T(128)S(1)} %pad_add_fusion.place.refs_0_, bf16[128,2304]{1,0:T(8,128)(2,1)S(1)} %copy-done, bf16[1024,2304]{1,0:T(8,128)(2,1)S(1)} %bitcast.8, ...), custom_call_target="tpu_custom_call" | custom-call | flops 1000000000 | tf_op jit(solution)/shard_map/pallas_call | solution.py:45
  33.5 1.7 %collective-permute-start.13 = (bf16[32,2304]{1,0:T(8,128)(2,1)S(1)}, bf16[32,2304]{1,0:T(8,128)(2,1)S(1)}, u32[]{:S(2)}, u32[]{:S(2)}) collective-permute-start(bf16[32,2304]{1,0:T(8,128)(2,1)S(1)} %get-tuple-element.61), channel_id=1, source_target_pairs={{0,1},{1,0},{2,3},{3,2},{4,5},{5,4},{6,7},{7,6},{8,9},{9,8},{10,11... | collective-permute-start | bytes 442376 | tf_op jit(solution)/shard_map/ppermute | solution.py:68
  35.2 2.6 %collective-permute-start.14 = (bf16[32,2304]{1,0:T(8,128)(2,1)S(1)}, bf16[32,2304]{1,0:T(8,128)(2,1)S(1)}, u32[]{:S(2)}, u32[]{:S(2)}) collective-permute-start(bf16[32,2304]{1,0:T(8,128)(2,1)S(1)} %get-tuple-element.62), channel_id=1, source_target_pairs={{0,2},{1,3},{2,0},{3,1},{4,6},{5,7},{6,4},{7,5},{8,10},{9,11},{10,... | collective-permute-start | bytes 442376 | tf_op jit(solution)/shard_map/ppermute | solution.py:68
  38.0 0.2 copy.13
  38.2 2.2 %collective-permute-done.13.refs_4_ = bf16[32,2304]{1,0:T(8,128)(2,1)S(1)} collective-permute-done((bf16[32,2304]{1,0:T(8,128)(2,1)S(1)}, bf16[32,2304]{1,0:T(8,128)(2,1)S(1)}, u32[]{:S(2)}, u32[]{:S(2)}) %collective-permute-start.13) | collective-permute-done | bytes 147488 | tf_op jit(solution)/shard_map/ppermute | solution.py:68
  40.5 7.8 %collective-permute-done.14.refs_5_ = bf16[32,2304]{1,0:T(8,128)(2,1)S(1)} collective-permute-done((bf16[32,2304]{1,0:T(8,128)(2,1)S(1)}, bf16[32,2304]{1,0:T(8,128)(2,1)S(1)}, u32[]{:S(2)}, u32[]{:S(2)}) %collective-permute-start.14) | collective-permute-done | bytes 147488 | tf_op jit(solution)/shard_map/ppermute | solution.py:68
  48.3 0.8 %shard_map.128 = (bf16[32,2304]{1,0:T(8,128)(2,1)S(1)}, bf16[32,512]{1,0:T(8,128)(2,1)S(1)}, bf16[32,2816]{1,0:T(8,128)(2,1)S(1)}) custom-call(f32[1,2304]{1,0:T(1,128)S(1)} %broadcast_in_dim.7.refs_0_.refs_1_, bf16[2304,512]{1,0:T(8,128)(2,1)S(1)} %copy-done.1, f32[1,512]{1,0:T(1,128)S(1)} %bitcast.12, f32[32,2304]{1,0:T(8,128)S(1)} %get-tuple-element.65.refs_3_, ...), custom_call_target="tpu_custom_call" | custom-call | flops 1000000000 | tf_op jit(solution)/shard_map/pallas_call | solution.py:45
  49.1 2.2 %collective-permute-start.16 = (bf16[32,2816]{1,0:T(8,128)(2,1)S(1)}, bf16[32,2816]{1,0:T(8,128)(2,1)S(1)}, u32[]{:S(2)}, u32[]{:S(2)}) collective-permute-start(bf16[32,2816]{1,0:T(8,128)(2,1)S(1)} %get-tuple-element.70), channel_id=1, source_target_pairs={{0,1},{1,0},{2,3},{3,2},{4,5},{5,4},{6,7},{7,6},{8,9},{9,8},{10,11... | collective-permute-start | bytes 540680 | tf_op jit(solution)/shard_map/ppermute | solution.py:68
  51.3 1.1 %collective-permute-start.19 = (bf16[32,512]{1,0:T(8,128)(2,1)S(1)}, bf16[32,512]{1,0:T(8,128)(2,1)S(1)}, u32[]{:S(2)}, u32[]{:S(2)}) collective-permute-start(bf16[32,512]{1,0:T(8,128)(2,1)S(1)} %get-tuple-element.71.refs_1_), channel_id=1, source_target_pairs={{0,2},{1,3},{2,0},{3,1},{4,6},{5,7},{6,4},{7,5},{8,10},{9,11},{10,... | collective-permute-start | bytes 98312 | tf_op jit(solution)/shard_map/ppermute | solution.py:68
  52.4 1.4 %collective-permute-start.20 = (bf16[32,512]{1,0:T(8,128)(2,1)S(1)}, bf16[32,512]{1,0:T(8,128)(2,1)S(1)}, u32[]{:S(2)}, u32[]{:S(2)}) collective-permute-start(bf16[32,512]{1,0:T(8,128)(2,1)S(1)} %get-tuple-element.71.refs_1_), channel_id=1, source_target_pairs={{0,3},{1,2},{2,1},{3,0},{4,7},{5,6},{6,5},{7,4},{8,11},{9,10},{10,... | collective-permute-start | bytes 98312 | tf_op jit(solution)/shard_map/ppermute | solution.py:68
  53.8 2.0 %collective-permute-start.17 = (bf16[32,2304]{1,0:T(8,128)(2,1)S(1)}, bf16[32,2304]{1,0:T(8,128)(2,1)S(1)}, u32[]{:S(2)}, u32[]{:S(2)}) collective-permute-start(bf16[32,2304]{1,0:T(8,128)(2,1)S(1)} %get-tuple-element.69.refs_4_), channel_id=1, source_target_pairs={{0,2},{1,3},{2,0},{3,1},{4,6},{5,7},{6,4},{7,5},{8,10},{9,11},{10,... | collective-permute-start | bytes 442376 | tf_op jit(solution)/shard_map/ppermute | solution.py:68
  55.8 1.4 %collective-permute-done.19.refs_3_ = bf16[32,512]{1,0:T(8,128)(2,1)S(1)} collective-permute-done((bf16[32,512]{1,0:T(8,128)(2,1)S(1)}, bf16[32,512]{1,0:T(8,128)(2,1)S(1)}, u32[]{:S(2)}, u32[]{:S(2)}) %collective-permute-start.19) | collective-permute-done | bytes 32800 | tf_op jit(solution)/shard_map/ppermute | solution.py:68
  57.2 2.2 %collective-permute-done.20.refs_4_ = bf16[32,512]{1,0:T(8,128)(2,1)S(1)} collective-permute-done((bf16[32,512]{1,0:T(8,128)(2,1)S(1)}, bf16[32,512]{1,0:T(8,128)(2,1)S(1)}, u32[]{:S(2)}, u32[]{:S(2)}) %collective-permute-start.20) | collective-permute-done | bytes 32800 | tf_op jit(solution)/shard_map/ppermute | solution.py:68
  59.4 0.6 shard_map.129.refs_8_
  60.0 1.4 %collective-permute-start.21 = (bf16[128,512]{1,0:T(8,128)(2,1)S(1)}, bf16[128,512]{1,0:T(8,128)(2,1)S(1)}, u32[]{:S(2)}, u32[]{:S(2)}) collective-permute-start(bf16[128,512]{1,0:T(8,128)(2,1)S(1)} %shard_map.129.refs_8_), channel_id=1, source_target_pairs={{0,24},{4,28},{8,16},{12,20},{16,8},{20,12},{24,0},{28,4},{1,25},{... | collective-permute-start | bytes 393224 | tf_op jit(solution)/shard_map/ppermute | solution.py:68
  61.4 1.0 %collective-permute-start.22 = (bf16[128,512]{1,0:T(8,128)(2,1)S(1)}, bf16[128,512]{1,0:T(8,128)(2,1)S(1)}, u32[]{:S(2)}, u32[]{:S(2)}) collective-permute-start(bf16[128,512]{1,0:T(8,128)(2,1)S(1)} %shard_map.129.refs_8_), channel_id=1, source_target_pairs={{0,16},{4,20},{8,24},{12,28},{16,0},{20,4},{24,8},{28,12},{1,17},{... | collective-permute-start | bytes 393224 | tf_op jit(solution)/shard_map/ppermute | solution.py:68
  62.4 1.1 %collective-permute-start.23 = (bf16[128,512]{1,0:T(8,128)(2,1)S(1)}, bf16[128,512]{1,0:T(8,128)(2,1)S(1)}, u32[]{:S(2)}, u32[]{:S(2)}) collective-permute-start(bf16[128,512]{1,0:T(8,128)(2,1)S(1)} %shard_map.129.refs_8_), channel_id=1, source_target_pairs={{0,8},{4,12},{8,0},{12,4},{16,24},{20,28},{24,16},{28,20},{1,9},{5... | collective-permute-start | bytes 393224 | tf_op jit(solution)/shard_map/ppermute | solution.py:68
  63.5 0.2 collective-permute-start.18
  63.7 2.3 %collective-permute-done.21.refs_9_ = bf16[128,512]{1,0:T(8,128)(2,1)S(1)} collective-permute-done((bf16[128,512]{1,0:T(8,128)(2,1)S(1)}, bf16[128,512]{1,0:T(8,128)(2,1)S(1)}, u32[]{:S(2)}, u32[]{:S(2)}) %collective-permute-start.21) | collective-permute-done | bytes 131104 | tf_op jit(solution)/shard_map/ppermute | solution.py:68
  66.0 1.3 %collective-permute-done.22.refs_10_ = bf16[128,512]{1,0:T(8,128)(2,1)S(1)} collective-permute-done((bf16[128,512]{1,0:T(8,128)(2,1)S(1)}, bf16[128,512]{1,0:T(8,128)(2,1)S(1)}, u32[]{:S(2)}, u32[]{:S(2)}) %collective-permute-start.22) | collective-permute-done | bytes 131104 | tf_op jit(solution)/shard_map/ppermute | solution.py:68
  67.4 0.4 collective-permute-start.27
  67.8 0.9 %collective-permute-done.18.refs_7_ = bf16[32,2304]{1,0:T(8,128)(2,1)S(1)} collective-permute-done((bf16[32,2304]{1,0:T(8,128)(2,1)S(1)}, bf16[32,2304]{1,0:T(8,128)(2,1)S(1)}, u32[]{:S(2)}, u32[]{:S(2)}) %collective-permute-start.18) | collective-permute-done | bytes 147488 | tf_op jit(solution)/shard_map/ppermute | solution.py:68
  68.8 3.8 %shard_map.130 = (bf16[128,2304]{1,0:T(8,128)(2,1)}, bf16[128,512]{1,0:T(8,128)(2,1)}) custom-call(s32[3]{0:T(128)S(1)} %pad_add_fusion.place.refs_0_, f32[1,2304]{1,0:T(1,128)S(1)} %broadcast_in_dim.7.refs_0_.refs_1_, bf16[2304,512]{1,0:T(8,128)(2,1)S(1)} %copy-done.2, bf16[512,1024]{1,0:T(8,128)(2,1)S(1)} %bitcast.9, ...), custom_call_target="tpu_custom_call" | custom-call | flops 4000000000 | tf_op jit(solution)/shard_map/pallas_call | solution.py:45
  (40 shorter events, 0.6 us)
Async XLA Ops:
  1.6 5.7 %collective-permute-start = (bf16[3,16,1024]{2,1,0:T(8,128)(2,1)S(1)}, bf16[3,16,1024]{2,1,0:T(8,128)(2,1)S(1)}, u32[]{:S(2)}, u32[]{:S(2)}) collective-permute-start(bf16[3,16,1024]{2,1,0:T(8,128)(2,1)S(1)} %get-tuple-element.72), channel_id=1, source_target_pairs={{0,4},{4,8},{8,12},{12,16},{16,20},{20,24},{24,28},{28,0},{1,5},{5... | collective-permute-start | bytes 294920 | tf_op jit(solution)/shard_map/ppermute | solution.py:73
  2.1 5.2 %copy-start.3 = (f32[128,8]{0,1:T(8,128)S(1)}, f32[128,8]{0,1:T(8,128)}, u32[]{:S(2)}) copy-start(f32[128,8]{0,1:T(8,128)} %param.13) | copy-start | bytes 12292
  11.0 1.7 %collective-permute-start.1 = (bf16[4,272,128]{2,1,0:T(8,128)(2,1)S(1)}, bf16[4,272,128]{2,1,0:T(8,128)(2,1)S(1)}, u32[]{:S(2)}, u32[]{:S(2)}) collective-permute-start(bf16[4,272,128]{2,1,0:T(8,128)(2,1)S(1)} %get-tuple-element.41), channel_id=1, source_target_pairs={{0,4},{4,0},{8,12},{12,8},{16,20},{20,16},{24,28},{28,24},{1,5},{5... | collective-permute-start | bytes 835592 | tf_op jit(solution)/shard_map/ppermute | solution.py:68
  11.6 5.7 %collective-permute-start.5 = (bf16[4,272,128]{2,1,0:T(8,128)(2,1)S(1)}, bf16[4,272,128]{2,1,0:T(8,128)(2,1)S(1)}, u32[]{:S(2)}, u32[]{:S(2)}) collective-permute-start(bf16[4,272,128]{2,1,0:T(8,128)(2,1)S(1)} %get-tuple-element.40.kept), channel_id=1, source_target_pairs={{0,4},{4,0},{8,12},{12,8},{16,20},{20,16},{24,28},{28,24},{1,5},{5... | collective-permute-start | bytes 835592 | tf_op jit(solution)/shard_map/ppermute | solution.py:68
  13.6 7.1 %collective-permute-start.2 = (bf16[272,128]{1,0:T(8,128)(2,1)S(1)}, bf16[272,128]{1,0:T(8,128)(2,1)S(1)}, u32[]{:S(2)}, u32[]{:S(2)}) collective-permute-start(bf16[272,128]{1,0:T(8,128)(2,1)S(1)} %get-tuple-element.43), channel_id=1, source_target_pairs={{0,8},{4,12},{8,0},{12,4},{16,24},{20,28},{24,16},{28,20},{1,9},{5... | collective-permute-start | bytes 208904 | tf_op jit(solution)/shard_map/ppermute | solution.py:68
  15.2 5.5 %collective-permute-start.3 = (bf16[272,128]{1,0:T(8,128)(2,1)S(1)}, bf16[272,128]{1,0:T(8,128)(2,1)S(1)}, u32[]{:S(2)}, u32[]{:S(2)}) collective-permute-start(bf16[272,128]{1,0:T(8,128)(2,1)S(1)} %get-tuple-element.44), channel_id=1, source_target_pairs={{0,16},{4,20},{8,24},{12,28},{16,0},{20,4},{24,8},{28,12},{1,17},{... | collective-permute-start | bytes 208904 | tf_op jit(solution)/shard_map/ppermute | solution.py:68
  16.4 5.2 %collective-permute-start.4 = (bf16[272,128]{1,0:T(8,128)(2,1)S(1)}, bf16[272,128]{1,0:T(8,128)(2,1)S(1)}, u32[]{:S(2)}, u32[]{:S(2)}) collective-permute-start(bf16[272,128]{1,0:T(8,128)(2,1)S(1)} %get-tuple-element.45), channel_id=1, source_target_pairs={{0,24},{4,28},{8,16},{12,20},{16,8},{20,12},{24,0},{28,4},{1,25},{... | collective-permute-start | bytes 208904 | tf_op jit(solution)/shard_map/ppermute | solution.py:68
  17.3 14.3 %slice-start = ((s8[4718592]{0:T(1024)(128)(4,1)}), s8[4194304]{0:T(1024)(128)(4,1)S(1)}, s32[]{:S(2)}) async-start(s8[4718592]{0:T(1024)(128)(4,1)} %bitcast.7), calls=%async_computation | async-start | bytes 8388608
  17.3 14.3 %slice-start.1 = ((s8[4718592]{0:T(1024)(128)(4,1)}), s8[524288]{0:T(1024)(128)(4,1)S(1)}, s32[]{:S(2)}) async-start(s8[4718592]{0:T(1024)(128)(4,1)} %bitcast.7), calls=%async_computation.1 | async-start | bytes 1048576
  20.6 11.0 %copy-start = (bf16[128,2304]{1,0:T(8,128)(2,1)S(1)}, bf16[128,2304]{1,0:T(8,128)(2,1)}, u32[]{:S(2)}) copy-start(bf16[128,2304]{1,0:T(8,128)(2,1)} %refs_1_.2) | copy-start | bytes 1769476
  21.6 1.3 %collective-permute-start.6 = (bf16[272,128]{1,0:T(8,128)(2,1)S(1)}, bf16[272,128]{1,0:T(8,128)(2,1)S(1)}, u32[]{:S(2)}, u32[]{:S(2)}) collective-permute-start(bf16[272,128]{1,0:T(8,128)(2,1)S(1)} %get-tuple-element.52.refs_1_), channel_id=1, source_target_pairs={{0,4},{4,0},{8,12},{12,8},{16,20},{20,16},{24,28},{28,24},{1,5},{5... | collective-permute-start | bytes 208904 | tf_op jit(solution)/shard_map/ppermute | solution.py:68
  21.6 1.4 %collective-permute-start.7 = (bf16[272,128]{1,0:T(8,128)(2,1)S(1)}, bf16[272,128]{1,0:T(8,128)(2,1)S(1)}, u32[]{:S(2)}, u32[]{:S(2)}) collective-permute-start(bf16[272,128]{1,0:T(8,128)(2,1)S(1)} %collective-permute-done.2.refs_2_), channel_id=1, source_target_pairs={{0,4},{4,0},{8,12},{12,8},{16,20},{20,16},{24,28},{28,24},{1,5},{5... | collective-permute-start | bytes 208904 | tf_op jit(solution)/shard_map/ppermute | solution.py:68
  22.2 1.3 %collective-permute-start.8 = (bf16[272,128]{1,0:T(8,128)(2,1)S(1)}, bf16[272,128]{1,0:T(8,128)(2,1)S(1)}, u32[]{:S(2)}, u32[]{:S(2)}) collective-permute-start(bf16[272,128]{1,0:T(8,128)(2,1)S(1)} %collective-permute-done.3.refs_3_), channel_id=1, source_target_pairs={{0,4},{4,0},{8,12},{12,8},{16,20},{20,16},{24,28},{28,24},{1,5},{5... | collective-permute-start | bytes 208904 | tf_op jit(solution)/shard_map/ppermute | solution.py:68
  22.2 1.4 %collective-permute-start.9 = (bf16[272,128]{1,0:T(8,128)(2,1)S(1)}, bf16[272,128]{1,0:T(8,128)(2,1)S(1)}, u32[]{:S(2)}, u32[]{:S(2)}) collective-permute-start(bf16[272,128]{1,0:T(8,128)(2,1)S(1)} %collective-permute-done.4.refs_4_), channel_id=1, source_target_pairs={{0,4},{4,0},{8,12},{12,8},{16,20},{20,16},{24,28},{28,24},{1,5},{5... | collective-permute-start | bytes 208904 | tf_op jit(solution)/shard_map/ppermute | solution.py:68
  24.5 4.4 %collective-permute-start.10 = (bf16[2,128,128]{2,1,0:T(8,128)(2,1)S(1)}, bf16[2,128,128]{2,1,0:T(8,128)(2,1)S(1)}, u32[]{:S(2)}, u32[]{:S(2)}) collective-permute-start(bf16[2,128,128]{2,1,0:T(8,128)(2,1)S(1)} %get-tuple-element.57), channel_id=1, source_target_pairs={{0,8},{4,12},{8,0},{12,4},{16,24},{20,28},{24,16},{28,20},{1,9},{5... | collective-permute-start | bytes 196616 | tf_op jit(solution)/shard_map/ppermute | solution.py:68
  26.0 5.7 %collective-permute-start.11 = (bf16[2,128,128]{2,1,0:T(8,128)(2,1)S(1)}, bf16[2,128,128]{2,1,0:T(8,128)(2,1)S(1)}, u32[]{:S(2)}, u32[]{:S(2)}) collective-permute-start(bf16[2,128,128]{2,1,0:T(8,128)(2,1)S(1)} %get-tuple-element.58), channel_id=1, source_target_pairs={{0,16},{4,20},{8,24},{12,28},{16,0},{20,4},{24,8},{28,12},{1,17},{... | collective-permute-start | bytes 196616 | tf_op jit(solution)/shard_map/ppermute | solution.py:68
  26.3 5.3 %collective-permute-start.12 = (bf16[2,128,128]{2,1,0:T(8,128)(2,1)S(1)}, bf16[2,128,128]{2,1,0:T(8,128)(2,1)S(1)}, u32[]{:S(2)}, u32[]{:S(2)}) collective-permute-start(bf16[2,128,128]{2,1,0:T(8,128)(2,1)S(1)} %get-tuple-element.59), channel_id=1, source_target_pairs={{0,24},{4,28},{8,16},{12,20},{16,8},{20,12},{24,0},{28,4},{1,25},{... | collective-permute-start | bytes 196616 | tf_op jit(solution)/shard_map/ppermute | solution.py:68
  31.7 6.3 %copy-start.5 = (bf16[512,2,512]{2,1,0:T(2,128)(2,1)S(1)}, bf16[512,2,512]{2,1,0:T(2,128)(2,1)}, u32[]{:S(2)}) copy-start(bf16[512,2,512]{2,1,0:T(2,128)(2,1)} %param.21) | copy-start | bytes 3145732
  31.7 6.5 %copy-start.6 = (f32[2304]{0:T(1024)S(1)}, f32[2304]{0:T(1024)}, u32[]{:S(2)}) copy-start(f32[2304]{0:T(1024)} %param.17) | copy-start | bytes 27652
  31.7 16.6 %copy-start.1 = (bf16[2304,512]{1,0:T(8,128)(2,1)S(1)}, bf16[2304,512]{1,0:T(8,128)(2,1)}, u32[]{:S(2)}) copy-start(bf16[2304,512]{1,0:T(8,128)(2,1)} %refs_1_.3) | copy-start | bytes 7077892
  31.7 16.6 %copy-start.4 = (f32[512]{0:T(512)S(1)}, f32[512]{0:T(512)}, u32[]{:S(2)}) copy-start(f32[512]{0:T(512)} %param.19) | copy-start | bytes 6148
  33.5 6.9 %collective-permute-start.13 = (bf16[32,2304]{1,0:T(8,128)(2,1)S(1)}, bf16[32,2304]{1,0:T(8,128)(2,1)S(1)}, u32[]{:S(2)}, u32[]{:S(2)}) collective-permute-start(bf16[32,2304]{1,0:T(8,128)(2,1)S(1)} %get-tuple-element.61), channel_id=1, source_target_pairs={{0,1},{1,0},{2,3},{3,2},{4,5},{5,4},{6,7},{7,6},{8,9},{9,8},{10,11... | collective-permute-start | bytes 442376 | tf_op jit(solution)/shard_map/ppermute | solution.py:68
  35.2 13.1 %collective-permute-start.14 = (bf16[32,2304]{1,0:T(8,128)(2,1)S(1)}, bf16[32,2304]{1,0:T(8,128)(2,1)S(1)}, u32[]{:S(2)}, u32[]{:S(2)}) collective-permute-start(bf16[32,2304]{1,0:T(8,128)(2,1)S(1)} %get-tuple-element.62), channel_id=1, source_target_pairs={{0,2},{1,3},{2,0},{3,1},{4,6},{5,7},{6,4},{7,5},{8,10},{9,11},{10,... | collective-permute-start | bytes 442376 | tf_op jit(solution)/shard_map/ppermute | solution.py:68
  37.8 10.5 %collective-permute-start.15 = (bf16[32,2304]{1,0:T(8,128)(2,1)S(1)}, bf16[32,2304]{1,0:T(8,128)(2,1)S(1)}, u32[]{:S(2)}, u32[]{:S(2)}) collective-permute-start(bf16[32,2304]{1,0:T(8,128)(2,1)S(1)} %get-tuple-element.63), channel_id=1, source_target_pairs={{0,3},{1,2},{2,1},{3,0},{4,7},{5,6},{6,5},{7,4},{8,11},{9,10},{10,... | collective-permute-start | bytes 442376 | tf_op jit(solution)/shard_map/ppermute | solution.py:68
  49.1 19.7 %copy-start.2 = (bf16[2304,512]{1,0:T(8,128)(2,1)S(1)}, bf16[2304,512]{1,0:T(8,128)(2,1)}, u32[]{:S(2)}) copy-start(bf16[2304,512]{1,0:T(8,128)(2,1)} %refs_2_.3) | copy-start | bytes 7077892
  49.1 10.3 %collective-permute-start.16 = (bf16[32,2816]{1,0:T(8,128)(2,1)S(1)}, bf16[32,2816]{1,0:T(8,128)(2,1)S(1)}, u32[]{:S(2)}, u32[]{:S(2)}) collective-permute-start(bf16[32,2816]{1,0:T(8,128)(2,1)S(1)} %get-tuple-element.70), channel_id=1, source_target_pairs={{0,1},{1,0},{2,3},{3,2},{4,5},{5,4},{6,7},{7,6},{8,9},{9,8},{10,11... | collective-permute-start | bytes 540680 | tf_op jit(solution)/shard_map/ppermute | solution.py:68
  51.3 5.9 %collective-permute-start.19 = (bf16[32,512]{1,0:T(8,128)(2,1)S(1)}, bf16[32,512]{1,0:T(8,128)(2,1)S(1)}, u32[]{:S(2)}, u32[]{:S(2)}) collective-permute-start(bf16[32,512]{1,0:T(8,128)(2,1)S(1)} %get-tuple-element.71.refs_1_), channel_id=1, source_target_pairs={{0,2},{1,3},{2,0},{3,1},{4,6},{5,7},{6,4},{7,5},{8,10},{9,11},{10,... | collective-permute-start | bytes 98312 | tf_op jit(solution)/shard_map/ppermute | solution.py:68
  52.4 7.0 %collective-permute-start.20 = (bf16[32,512]{1,0:T(8,128)(2,1)S(1)}, bf16[32,512]{1,0:T(8,128)(2,1)S(1)}, u32[]{:S(2)}, u32[]{:S(2)}) collective-permute-start(bf16[32,512]{1,0:T(8,128)(2,1)S(1)} %get-tuple-element.71.refs_1_), channel_id=1, source_target_pairs={{0,3},{1,2},{2,1},{3,0},{4,7},{5,6},{6,5},{7,4},{8,11},{9,10},{10,... | collective-permute-start | bytes 98312 | tf_op jit(solution)/shard_map/ppermute | solution.py:68
  53.8 9.7 %collective-permute-start.17 = (bf16[32,2304]{1,0:T(8,128)(2,1)S(1)}, bf16[32,2304]{1,0:T(8,128)(2,1)S(1)}, u32[]{:S(2)}, u32[]{:S(2)}) collective-permute-start(bf16[32,2304]{1,0:T(8,128)(2,1)S(1)} %get-tuple-element.69.refs_4_), channel_id=1, source_target_pairs={{0,2},{1,3},{2,0},{3,1},{4,6},{5,7},{6,4},{7,5},{8,10},{9,11},{10,... | collective-permute-start | bytes 442376 | tf_op jit(solution)/shard_map/ppermute | solution.py:68
  60.0 6.0 %collective-permute-start.21 = (bf16[128,512]{1,0:T(8,128)(2,1)S(1)}, bf16[128,512]{1,0:T(8,128)(2,1)S(1)}, u32[]{:S(2)}, u32[]{:S(2)}) collective-permute-start(bf16[128,512]{1,0:T(8,128)(2,1)S(1)} %shard_map.129.refs_8_), channel_id=1, source_target_pairs={{0,24},{4,28},{8,16},{12,20},{16,8},{20,12},{24,0},{28,4},{1,25},{... | collective-permute-start | bytes 393224 | tf_op jit(solution)/shard_map/ppermute | solution.py:68
  61.4 5.9 %collective-permute-start.22 = (bf16[128,512]{1,0:T(8,128)(2,1)S(1)}, bf16[128,512]{1,0:T(8,128)(2,1)S(1)}, u32[]{:S(2)}, u32[]{:S(2)}) collective-permute-start(bf16[128,512]{1,0:T(8,128)(2,1)S(1)} %shard_map.129.refs_8_), channel_id=1, source_target_pairs={{0,16},{4,20},{8,24},{12,28},{16,0},{20,4},{24,8},{28,12},{1,17},{... | collective-permute-start | bytes 393224 | tf_op jit(solution)/shard_map/ppermute | solution.py:68
  62.4 5.0 %collective-permute-start.23 = (bf16[128,512]{1,0:T(8,128)(2,1)S(1)}, bf16[128,512]{1,0:T(8,128)(2,1)S(1)}, u32[]{:S(2)}, u32[]{:S(2)}) collective-permute-start(bf16[128,512]{1,0:T(8,128)(2,1)S(1)} %shard_map.129.refs_8_), channel_id=1, source_target_pairs={{0,8},{4,12},{8,0},{12,4},{16,24},{20,28},{24,16},{28,20},{1,9},{5... | collective-permute-start | bytes 393224 | tf_op jit(solution)/shard_map/ppermute | solution.py:68
  63.5 5.1 %collective-permute-start.18 = (bf16[32,2304]{1,0:T(8,128)(2,1)S(1)}, bf16[32,2304]{1,0:T(8,128)(2,1)S(1)}, u32[]{:S(2)}, u32[]{:S(2)}) collective-permute-start(bf16[32,2304]{1,0:T(8,128)(2,1)S(1)} %collective-permute-done.17.refs_6_), channel_id=1, source_target_pairs={{0,1},{1,0},{2,3},{3,2},{4,5},{5,4},{6,7},{7,6},{8,9},{9,8},{10,11... | collective-permute-start | bytes 442376 | tf_op jit(solution)/shard_map/ppermute | solution.py:68
  63.7 4.9 %collective-permute-start.24 = (bf16[128,512]{1,0:T(8,128)(2,1)S(1)}, bf16[128,512]{1,0:T(8,128)(2,1)S(1)}, u32[]{:S(2)}, u32[]{:S(2)}) collective-permute-start(bf16[128,512]{1,0:T(8,128)(2,1)S(1)} %shard_map.129.refs_8_), channel_id=1, source_target_pairs={{0,4},{4,0},{8,12},{12,8},{16,20},{20,16},{24,28},{28,24},{1,5},{5... | collective-permute-start | bytes 393224 | tf_op jit(solution)/shard_map/ppermute | solution.py:68
  66.0 2.7 %collective-permute-start.25 = (bf16[128,512]{1,0:T(8,128)(2,1)S(1)}, bf16[128,512]{1,0:T(8,128)(2,1)S(1)}, u32[]{:S(2)}, u32[]{:S(2)}) collective-permute-start(bf16[128,512]{1,0:T(8,128)(2,1)S(1)} %collective-permute-done.21.refs_9_), channel_id=1, source_target_pairs={{0,4},{4,0},{8,12},{12,8},{16,20},{20,16},{24,28},{28,24},{1,5},{5... | collective-permute-start | bytes 393224 | tf_op jit(solution)/shard_map/ppermute | solution.py:68
  67.3 1.4 %collective-permute-start.26 = (bf16[128,512]{1,0:T(8,128)(2,1)S(1)}, bf16[128,512]{1,0:T(8,128)(2,1)S(1)}, u32[]{:S(2)}, u32[]{:S(2)}) collective-permute-start(bf16[128,512]{1,0:T(8,128)(2,1)S(1)} %collective-permute-done.22.refs_10_), channel_id=1, source_target_pairs={{0,4},{4,0},{8,12},{12,8},{16,20},{20,16},{24,28},{28,24},{1,5},{5... | collective-permute-start | bytes 393224 | tf_op jit(solution)/shard_map/ppermute | solution.py:68
  67.4 1.4 %collective-permute-start.27 = (bf16[128,512]{1,0:T(8,128)(2,1)S(1)}, bf16[128,512]{1,0:T(8,128)(2,1)S(1)}, u32[]{:S(2)}, u32[]{:S(2)}) collective-permute-start(bf16[128,512]{1,0:T(8,128)(2,1)S(1)} %collective-permute-done.23.refs_11_), channel_id=1, source_target_pairs={{0,4},{4,0},{8,12},{12,8},{16,20},{20,16},{24,28},{28,24},{1,5},{5... | collective-permute-start | bytes 393224 | tf_op jit(solution)/shard_map/ppermute | solution.py:68

commit v7 on v6

--- a/solution.py
+++ b/solution.py
@@ -18,7 +18,6 @@
 bf16 = jnp.bfloat16
 f32 = jnp.float32
 VMEM = pl.BlockSpec(memory_space=pltpu.VMEM)
-SMEM = pl.BlockSpec(memory_space=pltpu.SMEM)
 HBM = pl.BlockSpec(memory_space=pltpu.HBM)
 
 
@@ -45,10 +44,7 @@
     return pl.pallas_call(
         kernel,
         out_shape=[jax.ShapeDtypeStruct(shape, dtype) for shape, dtype in outs],
-        in_specs=[
-            HBM if i in stored else SMEM if a.dtype == jnp.int32 else VMEM
-            for i, a in enumerate(args)
-        ],
+        in_specs=[HBM if i in stored else VMEM for i in range(len(args))],
         out_specs=[VMEM for _ in outs],
         scratch_shapes=scratch_shapes,
         compiler_params=pltpu.CompilerParams(vmem_limit_bytes=limit * MIB),
@@ -75,6 +71,11 @@
 
 def lanes(block_index, width=128):
     return pl.ds(pl.multiple_of(block_index * width, width), width)
+
+
+def here(heads):
+    token_index = lax.axis_index("ctx")
+    return lax.rem(token_index, heads), lax.axis_index("head"), token_index
 
 
 def split_cores(place):
@@ -150,10 +151,11 @@
 
 
 def map_kernel(
-    place, done, head_rows, halo, logs, beta, taps, kept, sent, solutions, shrunk, first, wide
+    done, head_rows, halo, logs, beta, taps, kept, sent, solutions, shrunk, first, wide
 ):
     length = logs.shape[0]
     pairs = kept.shape[0]
+    place = here(2 * pairs)
     chunks = range(2 * pairs)
     heads = side_heads(place, pairs)
     lane = [lanes(head) for head in heads]
@@ -219,10 +221,11 @@
     )
 
 
-def read_kernel(place, done, head_rows, halo, logs, beta, taps, *refs):
+def read_kernel(done, head_rows, halo, logs, beta, taps, *refs):
     solutions, shrunk, stay, go, reads, intra, first, wide = refs
     length = logs.shape[0]
     pairs = stay.shape[0]
+    place = here(2 * pairs)
     _, core = split_cores(place)
     first[...] = first_rows(place, halo, head_rows, taps, 0, wide)
     rows = lax.broadcasted_iota(jnp.int32, (length, length), 0)
@@ -253,9 +256,9 @@
     return state_map[:DK], state_map[DK : 2 * DK], decay
 
 
-def compose_kernel(pairs, place, kept, got, *refs):
+def compose_kernel(pairs, kept, got, *refs):
     outs, (maps,) = refs[:pairs], refs[pairs:]
-    chip, core = split_cores(place)
+    chip, core = split_cores(here(2 * pairs))
     eye = (
         lax.broadcasted_iota(jnp.int32, (DK, DK), 0) == lax.broadcasted_iota(jnp.int32, (DK, DK), 1)
     ).astype(f32)
@@ -278,7 +281,6 @@
 
 
 def scan_kernel(pairs, grouped, *refs):
-    place, refs = refs[0], refs[1:]
     sides, refs = (refs[:pairs], refs[pairs : 2 * pairs]), refs[2 * pairs :]
     if grouped:
         start, refs = refs[0], refs[1:]
@@ -286,7 +288,7 @@
     if grouped:
         final, refs = refs[0], refs[1:]
     maps, starts = refs
-    chip, _ = split_cores(place)
+    chip, _ = split_cores(here(2 * pairs))
     for side in range(2):
         for step in range(pairs):
             maps[side, partner(chip, step, pairs)] = sides[side][step][...]
@@ -306,9 +308,10 @@
 
 
 def project_kernel(parts, *refs):
-    place, residual, weight, reads, intra = refs[:5]
-    refs = refs[5:]
+    residual, weight, reads, intra = refs[:4]
+    refs = refs[4:]
     pairs = reads.shape[1] // DK // 2
+    place = here(2 * pairs)
     starts, refs = refs[:pairs], refs[pairs:]
     outs, (whole, summed) = refs[:parts], refs[parts:]
     chip, core = split_cores(place)
@@ -351,26 +354,25 @@
 
 
 def join_kernel(parts, *refs):
-    place = refs[0]
-    pieces = refs[1 : 1 + parts]
-    out = refs[1 + parts]
+    pieces = refs[:parts]
+    out = refs[parts]
     share = out.shape[0] // parts
     for step in range(parts):
-        at = pl.ds(pl.multiple_of(partner(place[1], step, parts) * share, share), share)
+        at = pl.ds(pl.multiple_of(partner(lax.axis_index("head"), step, parts) * share, share), share)
         out[at, :] = pieces[step][:, pieces[step].shape[1] - out.shape[1] :]
 
 
 def attend_kernel(parts, order, *refs):
-    place, gain, query_weight, up = refs[:4]
-    pieces, refs = refs[4 : 4 + parts], refs[4 + parts :]
+    gain, query_weight, up = refs[:3]
+    pieces, refs = refs[3 : 3 + parts], refs[3 + parts :]
     blocks, refs = refs[: len(order)], refs[len(order) :]
     stream, out, absorbed, latents, scores, weights, totals = refs
     length = stream.shape[0]
     heads = absorbed.shape[0] // length
-    me = place[2]
+    me = lax.axis_index("ctx")
     share = length // parts
     for step in range(parts):
-        at = pl.ds(pl.multiple_of(partner(place[1], step, parts) * share, share), share)
+        at = pl.ds(pl.multiple_of(partner(lax.axis_index("head"), step, parts) * share, share), share)
         stream[at, :] = pieces[step][:, : stream.shape[1]]
     for position in range(len(order)):
         latents[position * length : (position + 1) * length, :] = blocks[position][...]
@@ -428,8 +430,6 @@
     pairs = heads // 2
     count, parts = lax.axis_size("ctx"), lax.axis_size("head")
     groups = count // heads
-    ctx_me = lax.axis_index("ctx").astype(jnp.int32)
-    place = jnp.stack([ctx_me % heads, lax.axis_index("head").astype(jnp.int32), ctx_me])
 
     halo = passed_along(kda_inputs[:, length - HALO :, :], "ctx", 1)
     stored = [
@@ -451,7 +451,7 @@
     )
     map_shape = (2 * DK + EXTRA, DK)
     head_rows = kda_inputs[:, :HALO, :]
-    arguments = [place, done, head_rows, halo, logs, beta.T, taps]
+    arguments = [done, head_rows, halo, logs, beta.T, taps]
     kept, sent, solutions, shrunk = call(
         map_kernel,
         [
@@ -479,7 +479,7 @@
     chip_maps = call(
         functools.partial(compose_kernel, pairs),
         [(map_shape, bf16)] * pairs,
-        [place, kept, got],
+        [kept, got],
         [((pairs,) + map_shape, bf16)],
         8,
     )
@@ -497,7 +497,7 @@
         return call(
             functools.partial(scan_kernel, pairs, len(start) > 0),
             state_outs + [((2, DK, DK), f32)] * len(start),
-            [place] + chip_maps + other_maps + list(start),
+            chip_maps + other_maps + list(start),
             scratch,
             8,
         )
@@ -508,7 +508,7 @@
 
         def relay(step_index, start):
             arrived = passed_along(run(start)[pairs], "ctx", heads)
-            return jnp.where(ctx_me < heads, 0.0, arrived)
+            return jnp.where(lax.axis_index("ctx") < heads, 0.0, arrived)
 
         start = lax.fori_loop(0, groups - 1, relay, jnp.zeros((2, DK, DK), f32))
         starts = run(start)[:pairs]
@@ -518,7 +518,7 @@
     partials = call(
         functools.partial(project_kernel, parts),
         [((share, width), f32)] + [((share, width), bf16)] * (parts - 1),
-        [place, residual, kda_out_weight, reads, intra] + starts,
+        [residual, kda_out_weight, reads, intra] + starts,
         [((length, heads * DK), bf16), ((length, width), f32)],
         16,
     )
@@ -549,7 +549,7 @@
     latent = call(
         functools.partial(join_kernel, parts),
         [((length, latent_width), bf16)],
-        [place] + latent_parts,
+        latent_parts,
         limit=8,
     )[0]
 
@@ -565,7 +565,7 @@
     stream_out, attention_out = call(
         functools.partial(attend_kernel, parts, tuple(order)),
         [((length, width), bf16), ((length, heads_mla * DH), bf16)],
-        [place, norm_gain[None], query_weight, up] + stream_parts + latents,
+        [norm_gain[None], query_weight, up] + stream_parts + latents,
         [
             ((rows, latent_width), bf16),
             ((latent_rows, latent_width), bf16),

time: 72.8 us -> 69.8 us (0.959)
  Pallas kernels: 18.7 us -> 15.1 us
    pallas_call x9, Pallas kernels: 18.7 us -> 15.1 us  [call(): pl.pallas_call(kernel, out_shape=[jax.ShapeDtypeStruct(shape, dtype) for...]
  transfers between devices with their start and end apart: 28 -> 28, of which waited for: 18 -> 17; matrix products, arithmetic and copies ran while one was open for 0% -> 0% of each run, Pallas kernels for 11% -> 9%
where the time goes in v7:
time: 69.8 us; the launch traced here: 69.6 us
  waiting for transfers between devices  27.5 us (39%)
  starting transfers between devices  24.8 us (36%)
  Pallas kernels  15.1 us (22%)
  local copies, waits for them, and re-layouts  1.26 us (2%)
  between operations  0.84 us (1%)
    ppermute x27, waiting for transfers between devices, trade(): return lax.ppermute(block, axis, route)  25.3 us
    ppermute x27, starting transfers between devices, trade(): return lax.ppermute(block, axis, route)  24.3 us
    pallas_call x9, Pallas kernels, call(): pl.pallas_call(kernel, out_shape=[jax.ShapeDtypeStruct(shape, dtype) for...  15.1 us
    ppermute x1, waiting for transfers between devices, passed_along(): lax.ppermute(block, axis, [(i, (i + distance) % count) for i in range(cou...  2.21 us
  transfers between devices with their start and end apart: 28, of which 17 were waited for; matrix products, arithmetic and copies ran while one was open for 0% of the time, Pallas kernels for 9%

profile of v7, /device:TPU:0, one launch (start us, length us, event | category | flops | bytes accessed | tf_op | source)
XLA Modules:
  0.0 69.6 jit_solution(16781819587370650356)
XLA Ops:
  0.6 1.0 %fusion = (bf16[3,16,1024]{2,1,0:T(8,128)(2,1)S(1)}, bf16[3,16,1024]{2,1,0:T(8,128)(2,1)S(1)}) fusion(bf16[3,128,1024]{2,1,0:T(8,128)(2,1)} %stored_inputs.1), kind=kLoop, calls=%fused_computation | loop fusion | bytes 393216 | tf_op jit(solution)/shard_map/slice | solution.py:434
  1.6 0.5 collective-permute-start
  2.1 3.0 %shard_map.122 = (bf16[3,128,1024]{2,1,0:T(8,128)(2,1)S(1)}, f32[128,1024]{1,0:T(8,128)S(1)}, f32[3,4,1024]{2,1,0:T(4,128)S(1)}) custom-call(bf16[3,128,1024]{2,1,0:T(8,128)(2,1)} %stored_inputs.1, f32[128,1024]{1,0:T(8,128)} %stored_gate.1, f32[3,4,1024]{2,1,0:T(4,128)} %stored_taps.1), custom_call_target="tpu_custom_call" | custom-call | flops 2000000000 | tf_op jit(solution)/shard_map/pallas_call | solution.py:44
  5.1 2.2 %collective-permute-done.halo = bf16[3,16,1024]{2,1,0:T(8,128)(2,1)S(1)} collective-permute-done((bf16[3,16,1024]{2,1,0:T(8,128)(2,1)S(1)}, bf16[3,16,1024]{2,1,0:T(8,128)(2,1)S(1)}, u32[]{:S(2)}, u32[]{:S(2)}) %collective-permute-start) | collective-permute-done | bytes 98336 | tf_op jit(solution)/shard_map/ppermute | solution.py:69
  7.3 3.3 %shard_map.123 = (bf16[4,272,128]{2,1,0:T(8,128)(2,1)S(1)}, bf16[4,272,128]{2,1,0:T(8,128)(2,1)S(1)}, bf16[8,128,256]{2,1,0:T(8,128)(2,1)S(1)}, bf16[8,2,128,128]{3,2,1,0:T(8,128)(2,1)S(1)}) custom-call(bf16[3,128,1024]{2,1,0:T(8,128)(2,1)S(1)} %get-tuple-element.37.done, bf16[3,16,1024]{2,1,0:T(8,128)(2,1)S(1)} %get-tuple-element.73.head_rows, ...), custom_call_target="tpu_custom_call" | custom-call | flops 5000000000 | tf_op jit(solution)/shard_map/pallas_call | solution.py:44
  10.6 0.5 collective-permute-start.1
  11.2 1.1 %collective-permute-done.1.got.refs_2_ = bf16[4,272,128]{2,1,0:T(8,128)(2,1)S(1)} collective-permute-done((bf16[4,272,128]{2,1,0:T(8,128)(2,1)S(1)}, bf16[4,272,128]{2,1,0:T(8,128)(2,1)S(1)}, u32[]{:S(2)}, u32[]{:S(2)}) %collective-permute-start.1) | collective-permute-done | bytes 278560 | tf_op jit(solution)/shard_map/ppermute | solution.py:64
  12.3 0.3 shard_map.124
  12.6 1.6 %collective-permute-start.2 = (bf16[272,128]{1,0:T(8,128)(2,1)S(1)}, bf16[272,128]{1,0:T(8,128)(2,1)S(1)}, u32[]{:S(2)}, u32[]{:S(2)}) collective-permute-start(bf16[272,128]{1,0:T(8,128)(2,1)S(1)} %get-tuple-element.43), channel_id=1, source_target_pairs={{0,8},{4,12},{8,0},{12,4},{16,24},{20,28},{24,16},{28,20},{1,9},{5... | collective-permute-start | bytes 208904 | tf_op jit(solution)/shard_map/ppermute | solution.py:64
  14.2 1.3 %collective-permute-start.3 = (bf16[272,128]{1,0:T(8,128)(2,1)S(1)}, bf16[272,128]{1,0:T(8,128)(2,1)S(1)}, u32[]{:S(2)}, u32[]{:S(2)}) collective-permute-start(bf16[272,128]{1,0:T(8,128)(2,1)S(1)} %get-tuple-element.44), channel_id=1, source_target_pairs={{0,16},{4,20},{8,24},{12,28},{16,0},{20,4},{24,8},{28,12},{1,17},{... | collective-permute-start | bytes 208904 | tf_op jit(solution)/shard_map/ppermute | solution.py:64
  15.5 0.9 %collective-permute-start.4 = (bf16[272,128]{1,0:T(8,128)(2,1)S(1)}, bf16[272,128]{1,0:T(8,128)(2,1)S(1)}, u32[]{:S(2)}, u32[]{:S(2)}) collective-permute-start(bf16[272,128]{1,0:T(8,128)(2,1)S(1)} %get-tuple-element.45), channel_id=1, source_target_pairs={{0,24},{4,28},{8,16},{12,20},{16,8},{20,12},{24,0},{28,4},{1,25},{... | collective-permute-start | bytes 208904 | tf_op jit(solution)/shard_map/ppermute | solution.py:64
  16.3 2.8 %shard_map.125 = (bf16[128,1024]{1,0:T(8,128)(2,1)S(1)}, f32[128,1024]{1,0:T(8,128)S(1)}) custom-call(bf16[3,128,1024]{2,1,0:T(8,128)(2,1)S(1)} %get-tuple-element.37.done, bf16[3,16,1024]{2,1,0:T(8,128)(2,1)S(1)} %get-tuple-element.73.head_rows, bf16[3,16,1024]{2,1,0:T(8,128)(2,1)S(1)} %collective-permute-done.halo, ...), custom_call_target="tpu_custom_call" | custom-call | flops 2500000000 | tf_op jit(solution)/shard_map/pallas_call | solution.py:44
  19.2 1.5 %collective-permute-done.4.refs_3_ = bf16[272,128]{1,0:T(8,128)(2,1)S(1)} collective-permute-done((bf16[272,128]{1,0:T(8,128)(2,1)S(1)}, bf16[272,128]{1,0:T(8,128)(2,1)S(1)}, u32[]{:S(2)}, u32[]{:S(2)}) %collective-permute-start.4) | collective-permute-done | bytes 69664 | tf_op jit(solution)/shard_map/ppermute | solution.py:64
  20.7 0.5 collective-permute-start.7
  21.2 0.5 collective-permute-start.9
  21.7 0.2 collective-permute-done.6.refs_4_
  21.9 0.2 collective-permute-done.7.refs_5_
  22.1 0.4 collective-permute-done.8.refs_6_
  22.4 0.2 collective-permute-done.9.refs_7_
  22.6 0.4 shard_map.126
  23.0 1.5 %collective-permute-start.10 = (bf16[2,128,128]{2,1,0:T(8,128)(2,1)S(1)}, bf16[2,128,128]{2,1,0:T(8,128)(2,1)S(1)}, u32[]{:S(2)}, u32[]{:S(2)}) collective-permute-start(bf16[2,128,128]{2,1,0:T(8,128)(2,1)S(1)} %get-tuple-element.57), channel_id=1, source_target_pairs={{0,8},{4,12},{8,0},{12,4},{16,24},{20,28},{24,16},{28,20},{1,9},{5... | collective-permute-start | bytes 196616 | tf_op jit(solution)/shard_map/ppermute | solution.py:64
  24.5 0.4 collective-permute-start.11
  24.8 1.7 %collective-permute-start.12 = (bf16[2,128,128]{2,1,0:T(8,128)(2,1)S(1)}, bf16[2,128,128]{2,1,0:T(8,128)(2,1)S(1)}, u32[]{:S(2)}, u32[]{:S(2)}) collective-permute-start(bf16[2,128,128]{2,1,0:T(8,128)(2,1)S(1)} %get-tuple-element.59), channel_id=1, source_target_pairs={{0,24},{4,28},{8,16},{12,20},{16,8},{20,12},{24,0},{28,4},{1,25},{... | collective-permute-start | bytes 196616 | tf_op jit(solution)/shard_map/ppermute | solution.py:64
  26.5 0.9 %collective-permute-done.10.refs_5_ = bf16[2,128,128]{2,1,0:T(8,128)(2,1)S(1)} collective-permute-done((bf16[2,128,128]{2,1,0:T(8,128)(2,1)S(1)}, bf16[2,128,128]{2,1,0:T(8,128)(2,1)S(1)}, u32[]{:S(2)}, u32[]{:S(2)}) %collective-permute-start.10) | collective-permute-done | bytes 65568 | tf_op jit(solution)/shard_map/ppermute | solution.py:64
  27.4 2.7 %collective-permute-done.11.refs_6_ = bf16[2,128,128]{2,1,0:T(8,128)(2,1)S(1)} collective-permute-done((bf16[2,128,128]{2,1,0:T(8,128)(2,1)S(1)}, bf16[2,128,128]{2,1,0:T(8,128)(2,1)S(1)}, u32[]{:S(2)}, u32[]{:S(2)}) %collective-permute-start.11) | collective-permute-done | bytes 65568 | tf_op jit(solution)/shard_map/ppermute | solution.py:64
  30.2 1.3 %shard_map.127 = (f32[32,2304]{1,0:T(8,128)S(1)}, bf16[32,2304]{1,0:T(8,128)(2,1)S(1)}, bf16[32,2304]{1,0:T(8,128)(2,1)S(1)}, bf16[32,2304]{1,0:T(8,128)(2,1)S(1)}) custom-call(bf16[128,2304]{1,0:T(8,128)(2,1)S(1)} %copy-done, bf16[1024,2304]{1,0:T(8,128)(2,1)S(1)} %bitcast.5, bf16[128,1024]{1,0:T(8,128)(2,1)S(1)} %get-tuple-element.50.refs_2_, ...), custom_call_target="tpu_custom_call" | custom-call | flops 1000000000 | tf_op jit(solution)/shard_map/pallas_call | solution.py:44
  31.5 1.7 %collective-permute-start.13 = (bf16[32,2304]{1,0:T(8,128)(2,1)S(1)}, bf16[32,2304]{1,0:T(8,128)(2,1)S(1)}, u32[]{:S(2)}, u32[]{:S(2)}) collective-permute-start(bf16[32,2304]{1,0:T(8,128)(2,1)S(1)} %get-tuple-element.61), channel_id=1, source_target_pairs={{0,1},{1,0},{2,3},{3,2},{4,5},{5,4},{6,7},{7,6},{8,9},{9,8},{10,11... | collective-permute-start | bytes 442376 | tf_op jit(solution)/shard_map/ppermute | solution.py:64
  33.2 2.6 %collective-permute-start.14 = (bf16[32,2304]{1,0:T(8,128)(2,1)S(1)}, bf16[32,2304]{1,0:T(8,128)(2,1)S(1)}, u32[]{:S(2)}, u32[]{:S(2)}) collective-permute-start(bf16[32,2304]{1,0:T(8,128)(2,1)S(1)} %get-tuple-element.62), channel_id=1, source_target_pairs={{0,2},{1,3},{2,0},{3,1},{4,6},{5,7},{6,4},{7,5},{8,10},{9,11},{10,... | collective-permute-start | bytes 442376 | tf_op jit(solution)/shard_map/ppermute | solution.py:64
  36.0 0.2 copy.13
  36.3 2.2 %collective-permute-done.13.refs_4_ = bf16[32,2304]{1,0:T(8,128)(2,1)S(1)} collective-permute-done((bf16[32,2304]{1,0:T(8,128)(2,1)S(1)}, bf16[32,2304]{1,0:T(8,128)(2,1)S(1)}, u32[]{:S(2)}, u32[]{:S(2)}) %collective-permute-start.13) | collective-permute-done | bytes 147488 | tf_op jit(solution)/shard_map/ppermute | solution.py:64
  38.5 7.9 %collective-permute-done.14.refs_5_ = bf16[32,2304]{1,0:T(8,128)(2,1)S(1)} collective-permute-done((bf16[32,2304]{1,0:T(8,128)(2,1)S(1)}, bf16[32,2304]{1,0:T(8,128)(2,1)S(1)}, u32[]{:S(2)}, u32[]{:S(2)}) %collective-permute-start.14) | collective-permute-done | bytes 147488 | tf_op jit(solution)/shard_map/ppermute | solution.py:64
  46.3 0.8 %shard_map.128 = (bf16[32,2304]{1,0:T(8,128)(2,1)S(1)}, bf16[32,512]{1,0:T(8,128)(2,1)S(1)}, bf16[32,2816]{1,0:T(8,128)(2,1)S(1)}) custom-call(f32[1,2304]{1,0:T(1,128)S(1)} %broadcast_in_dim.7.refs_0_, bf16[2304,512]{1,0:T(8,128)(2,1)S(1)} %copy-done.1, f32[1,512]{1,0:T(1,128)S(1)} %bitcast.9, f32[32,2304]{1,0:T(8,128)S(1)} %get-tuple-element.65.refs_3_, ...), custom_call_target="tpu_custom_call" | custom-call | flops 1000000000 | tf_op jit(solution)/shard_map/pallas_call | solution.py:44
  47.1 2.2 %collective-permute-start.16 = (bf16[32,2816]{1,0:T(8,128)(2,1)S(1)}, bf16[32,2816]{1,0:T(8,128)(2,1)S(1)}, u32[]{:S(2)}, u32[]{:S(2)}) collective-permute-start(bf16[32,2816]{1,0:T(8,128)(2,1)S(1)} %get-tuple-element.70), channel_id=1, source_target_pairs={{0,1},{1,0},{2,3},{3,2},{4,5},{5,4},{6,7},{7,6},{8,9},{9,8},{10,11... | collective-permute-start | bytes 540680 | tf_op jit(solution)/shard_map/ppermute | solution.py:64
  49.3 1.1 %collective-permute-start.19 = (bf16[32,512]{1,0:T(8,128)(2,1)S(1)}, bf16[32,512]{1,0:T(8,128)(2,1)S(1)}, u32[]{:S(2)}, u32[]{:S(2)}) collective-permute-start(bf16[32,512]{1,0:T(8,128)(2,1)S(1)} %get-tuple-element.71.refs_0_), channel_id=1, source_target_pairs={{0,2},{1,3},{2,0},{3,1},{4,6},{5,7},{6,4},{7,5},{8,10},{9,11},{10,... | collective-permute-start | bytes 98312 | tf_op jit(solution)/shard_map/ppermute | solution.py:64
  50.4 1.4 %collective-permute-start.20 = (bf16[32,512]{1,0:T(8,128)(2,1)S(1)}, bf16[32,512]{1,0:T(8,128)(2,1)S(1)}, u32[]{:S(2)}, u32[]{:S(2)}) collective-permute-start(bf16[32,512]{1,0:T(8,128)(2,1)S(1)} %get-tuple-element.71.refs_0_), channel_id=1, source_target_pairs={{0,3},{1,2},{2,1},{3,0},{4,7},{5,6},{6,5},{7,4},{8,11},{9,10},{10,... | collective-permute-start | bytes 98312 | tf_op jit(solution)/shard_map/ppermute | solution.py:64
  51.8 2.0 %collective-permute-start.17 = (bf16[32,2304]{1,0:T(8,128)(2,1)S(1)}, bf16[32,2304]{1,0:T(8,128)(2,1)S(1)}, u32[]{:S(2)}, u32[]{:S(2)}) collective-permute-start(bf16[32,2304]{1,0:T(8,128)(2,1)S(1)} %get-tuple-element.69.refs_3_), channel_id=1, source_target_pairs={{0,2},{1,3},{2,0},{3,1},{4,6},{5,7},{6,4},{7,5},{8,10},{9,11},{10,... | collective-permute-start | bytes 442376 | tf_op jit(solution)/shard_map/ppermute | solution.py:64
  53.8 1.4 %collective-permute-done.19.refs_2_ = bf16[32,512]{1,0:T(8,128)(2,1)S(1)} collective-permute-done((bf16[32,512]{1,0:T(8,128)(2,1)S(1)}, bf16[32,512]{1,0:T(8,128)(2,1)S(1)}, u32[]{:S(2)}, u32[]{:S(2)}) %collective-permute-start.19) | collective-permute-done | bytes 32800 | tf_op jit(solution)/shard_map/ppermute | solution.py:64
  55.2 2.2 %collective-permute-done.20.refs_3_ = bf16[32,512]{1,0:T(8,128)(2,1)S(1)} collective-permute-done((bf16[32,512]{1,0:T(8,128)(2,1)S(1)}, bf16[32,512]{1,0:T(8,128)(2,1)S(1)}, u32[]{:S(2)}, u32[]{:S(2)}) %collective-permute-start.20) | collective-permute-done | bytes 32800 | tf_op jit(solution)/shard_map/ppermute | solution.py:64
  57.4 1.3 %collective-permute-start.21 = (bf16[128,512]{1,0:T(8,128)(2,1)S(1)}, bf16[128,512]{1,0:T(8,128)(2,1)S(1)}, u32[]{:S(2)}, u32[]{:S(2)}) collective-permute-start(bf16[128,512]{1,0:T(8,128)(2,1)S(1)} %shard_map.129.refs_7_), channel_id=1, source_target_pairs={{0,24},{4,28},{8,16},{12,20},{16,8},{20,12},{24,0},{28,4},{1,25},{... | collective-permute-start | bytes 393224 | tf_op jit(solution)/shard_map/ppermute | solution.py:64
  58.7 0.8 %collective-permute-start.22 = (bf16[128,512]{1,0:T(8,128)(2,1)S(1)}, bf16[128,512]{1,0:T(8,128)(2,1)S(1)}, u32[]{:S(2)}, u32[]{:S(2)}) collective-permute-start(bf16[128,512]{1,0:T(8,128)(2,1)S(1)} %shard_map.129.refs_7_), channel_id=1, source_target_pairs={{0,16},{4,20},{8,24},{12,28},{16,0},{20,4},{24,8},{28,12},{1,17},{... | collective-permute-start | bytes 393224 | tf_op jit(solution)/shard_map/ppermute | solution.py:64
  59.6 1.4 %collective-permute-start.23 = (bf16[128,512]{1,0:T(8,128)(2,1)S(1)}, bf16[128,512]{1,0:T(8,128)(2,1)S(1)}, u32[]{:S(2)}, u32[]{:S(2)}) collective-permute-start(bf16[128,512]{1,0:T(8,128)(2,1)S(1)} %shard_map.129.refs_7_), channel_id=1, source_target_pairs={{0,8},{4,12},{8,0},{12,4},{16,24},{20,28},{24,16},{28,20},{1,9},{5... | collective-permute-start | bytes 393224 | tf_op jit(solution)/shard_map/ppermute | solution.py:64
  61.0 0.2 collective-permute-start.18
  61.2 2.3 %collective-permute-done.21.refs_8_ = bf16[128,512]{1,0:T(8,128)(2,1)S(1)} collective-permute-done((bf16[128,512]{1,0:T(8,128)(2,1)S(1)}, bf16[128,512]{1,0:T(8,128)(2,1)S(1)}, u32[]{:S(2)}, u32[]{:S(2)}) %collective-permute-start.21) | collective-permute-done | bytes 131104 | tf_op jit(solution)/shard_map/ppermute | solution.py:64
  63.5 1.3 %collective-permute-done.22.refs_9_ = bf16[128,512]{1,0:T(8,128)(2,1)S(1)} collective-permute-done((bf16[128,512]{1,0:T(8,128)(2,1)S(1)}, bf16[128,512]{1,0:T(8,128)(2,1)S(1)}, u32[]{:S(2)}, u32[]{:S(2)}) %collective-permute-start.22) | collective-permute-done | bytes 131104 | tf_op jit(solution)/shard_map/ppermute | solution.py:64
  64.8 0.5 collective-permute-start.27
  65.3 0.9 %collective-permute-done.18.refs_6_ = bf16[32,2304]{1,0:T(8,128)(2,1)S(1)} collective-permute-done((bf16[32,2304]{1,0:T(8,128)(2,1)S(1)}, bf16[32,2304]{1,0:T(8,128)(2,1)S(1)}, u32[]{:S(2)}, u32[]{:S(2)}) %collective-permute-start.18) | collective-permute-done | bytes 147488 | tf_op jit(solution)/shard_map/ppermute | solution.py:64
  66.1 0.2 collective-permute-done.27.refs_14_
  66.3 3.3 %shard_map.130 = (bf16[128,2304]{1,0:T(8,128)(2,1)}, bf16[128,512]{1,0:T(8,128)(2,1)}) custom-call(f32[1,2304]{1,0:T(1,128)S(1)} %broadcast_in_dim.7.refs_0_, bf16[2304,512]{1,0:T(8,128)(2,1)S(1)} %copy-done.2, bf16[512,1024]{1,0:T(8,128)(2,1)S(1)} %bitcast.6, bf16[32,2304]{1,0:T(8,128)(2,1)S(1)} %get-tuple-element.69.refs_3_, ...), custom_call_target="tpu_custom_call" | custom-call | flops 4000000000 | tf_op jit(solution)/shard_map/pallas_call | solution.py:44
  (39 shorter events, 0.3 us)
Async XLA Ops:
  1.6 5.7 %copy-start.3 = (f32[128,8]{0,1:T(8,128)S(1)}, f32[128,8]{0,1:T(8,128)}, u32[]{:S(2)}) copy-start(f32[128,8]{0,1:T(8,128)} %param.13) | copy-start | bytes 12292
  1.6 5.7 %collective-permute-start = (bf16[3,16,1024]{2,1,0:T(8,128)(2,1)S(1)}, bf16[3,16,1024]{2,1,0:T(8,128)(2,1)S(1)}, u32[]{:S(2)}, u32[]{:S(2)}) collective-permute-start(bf16[3,16,1024]{2,1,0:T(8,128)(2,1)S(1)} %get-tuple-element.72), channel_id=1, source_target_pairs={{0,4},{4,8},{8,12},{12,16},{16,20},{20,24},{24,28},{28,0},{1,5},{5... | collective-permute-start | bytes 294920 | tf_op jit(solution)/shard_map/ppermute | solution.py:69
  10.6 1.7 %collective-permute-start.1 = (bf16[4,272,128]{2,1,0:T(8,128)(2,1)S(1)}, bf16[4,272,128]{2,1,0:T(8,128)(2,1)S(1)}, u32[]{:S(2)}, u32[]{:S(2)}) collective-permute-start(bf16[4,272,128]{2,1,0:T(8,128)(2,1)S(1)} %get-tuple-element.41), channel_id=1, source_target_pairs={{0,4},{4,0},{8,12},{12,8},{16,20},{20,16},{24,28},{28,24},{1,5},{5... | collective-permute-start | bytes 835592 | tf_op jit(solution)/shard_map/ppermute | solution.py:64
  11.1 5.3 %collective-permute-start.5 = (bf16[4,272,128]{2,1,0:T(8,128)(2,1)S(1)}, bf16[4,272,128]{2,1,0:T(8,128)(2,1)S(1)}, u32[]{:S(2)}, u32[]{:S(2)}) collective-permute-start(bf16[4,272,128]{2,1,0:T(8,128)(2,1)S(1)} %get-tuple-element.40.kept), channel_id=1, source_target_pairs={{0,4},{4,0},{8,12},{12,8},{16,20},{20,16},{24,28},{28,24},{1,5},{5... | collective-permute-start | bytes 835592 | tf_op jit(solution)/shard_map/ppermute | solution.py:64
  12.6 6.6 %collective-permute-start.2 = (bf16[272,128]{1,0:T(8,128)(2,1)S(1)}, bf16[272,128]{1,0:T(8,128)(2,1)S(1)}, u32[]{:S(2)}, u32[]{:S(2)}) collective-permute-start(bf16[272,128]{1,0:T(8,128)(2,1)S(1)} %get-tuple-element.43), channel_id=1, source_target_pairs={{0,8},{4,12},{8,0},{12,4},{16,24},{20,28},{24,16},{28,20},{1,9},{5... | collective-permute-start | bytes 208904 | tf_op jit(solution)/shard_map/ppermute | solution.py:64
  14.2 5.0 %collective-permute-start.3 = (bf16[272,128]{1,0:T(8,128)(2,1)S(1)}, bf16[272,128]{1,0:T(8,128)(2,1)S(1)}, u32[]{:S(2)}, u32[]{:S(2)}) collective-permute-start(bf16[272,128]{1,0:T(8,128)(2,1)S(1)} %get-tuple-element.44), channel_id=1, source_target_pairs={{0,16},{4,20},{8,24},{12,28},{16,0},{20,4},{24,8},{28,12},{1,17},{... | collective-permute-start | bytes 208904 | tf_op jit(solution)/shard_map/ppermute | solution.py:64
  15.5 5.2 %collective-permute-start.4 = (bf16[272,128]{1,0:T(8,128)(2,1)S(1)}, bf16[272,128]{1,0:T(8,128)(2,1)S(1)}, u32[]{:S(2)}, u32[]{:S(2)}) collective-permute-start(bf16[272,128]{1,0:T(8,128)(2,1)S(1)} %get-tuple-element.45), channel_id=1, source_target_pairs={{0,24},{4,28},{8,16},{12,20},{16,8},{20,12},{24,0},{28,4},{1,25},{... | collective-permute-start | bytes 208904 | tf_op jit(solution)/shard_map/ppermute | solution.py:64
  16.3 13.8 %slice-start = ((s8[4718592]{0:T(1024)(128)(4,1)}), s8[4194304]{0:T(1024)(128)(4,1)S(1)}, s32[]{:S(2)}) async-start(s8[4718592]{0:T(1024)(128)(4,1)} %bitcast.4), calls=%async_computation | async-start | bytes 8388608
  16.3 13.8 %slice-start.1 = ((s8[4718592]{0:T(1024)(128)(4,1)}), s8[524288]{0:T(1024)(128)(4,1)S(1)}, s32[]{:S(2)}) async-start(s8[4718592]{0:T(1024)(128)(4,1)} %bitcast.4), calls=%async_computation.1 | async-start | bytes 1048576
  19.1 11.0 %copy-start = (bf16[128,2304]{1,0:T(8,128)(2,1)S(1)}, bf16[128,2304]{1,0:T(8,128)(2,1)}, u32[]{:S(2)}) copy-start(bf16[128,2304]{1,0:T(8,128)(2,1)} %refs_0_.1) | copy-start | bytes 1769476
  20.7 1.3 %collective-permute-start.6 = (bf16[272,128]{1,0:T(8,128)(2,1)S(1)}, bf16[272,128]{1,0:T(8,128)(2,1)S(1)}, u32[]{:S(2)}, u32[]{:S(2)}) collective-permute-start(bf16[272,128]{1,0:T(8,128)(2,1)S(1)} %get-tuple-element.52.refs_0_), channel_id=1, source_target_pairs={{0,4},{4,0},{8,12},{12,8},{16,20},{20,16},{24,28},{28,24},{1,5},{5... | collective-permute-start | bytes 208904 | tf_op jit(solution)/shard_map/ppermute | solution.py:64
  20.7 1.4 %collective-permute-start.7 = (bf16[272,128]{1,0:T(8,128)(2,1)S(1)}, bf16[272,128]{1,0:T(8,128)(2,1)S(1)}, u32[]{:S(2)}, u32[]{:S(2)}) collective-permute-start(bf16[272,128]{1,0:T(8,128)(2,1)S(1)} %collective-permute-done.2.refs_1_), channel_id=1, source_target_pairs={{0,4},{4,0},{8,12},{12,8},{16,20},{20,16},{24,28},{28,24},{1,5},{5... | collective-permute-start | bytes 208904 | tf_op jit(solution)/shard_map/ppermute | solution.py:64
  21.2 1.3 %collective-permute-start.8 = (bf16[272,128]{1,0:T(8,128)(2,1)S(1)}, bf16[272,128]{1,0:T(8,128)(2,1)S(1)}, u32[]{:S(2)}, u32[]{:S(2)}) collective-permute-start(bf16[272,128]{1,0:T(8,128)(2,1)S(1)} %collective-permute-done.3.refs_2_), channel_id=1, source_target_pairs={{0,4},{4,0},{8,12},{12,8},{16,20},{20,16},{24,28},{28,24},{1,5},{5... | collective-permute-start | bytes 208904 | tf_op jit(solution)/shard_map/ppermute | solution.py:64
  21.2 1.4 %collective-permute-start.9 = (bf16[272,128]{1,0:T(8,128)(2,1)S(1)}, bf16[272,128]{1,0:T(8,128)(2,1)S(1)}, u32[]{:S(2)}, u32[]{:S(2)}) collective-permute-start(bf16[272,128]{1,0:T(8,128)(2,1)S(1)} %collective-permute-done.4.refs_3_), channel_id=1, source_target_pairs={{0,4},{4,0},{8,12},{12,8},{16,20},{20,16},{24,28},{28,24},{1,5},{5... | collective-permute-start | bytes 208904 | tf_op jit(solution)/shard_map/ppermute | solution.py:64
  23.0 4.4 %collective-permute-start.10 = (bf16[2,128,128]{2,1,0:T(8,128)(2,1)S(1)}, bf16[2,128,128]{2,1,0:T(8,128)(2,1)S(1)}, u32[]{:S(2)}, u32[]{:S(2)}) collective-permute-start(bf16[2,128,128]{2,1,0:T(8,128)(2,1)S(1)} %get-tuple-element.57), channel_id=1, source_target_pairs={{0,8},{4,12},{8,0},{12,4},{16,24},{20,28},{24,16},{28,20},{1,9},{5... | collective-permute-start | bytes 196616 | tf_op jit(solution)/shard_map/ppermute | solution.py:64
  24.5 5.7 %collective-permute-start.11 = (bf16[2,128,128]{2,1,0:T(8,128)(2,1)S(1)}, bf16[2,128,128]{2,1,0:T(8,128)(2,1)S(1)}, u32[]{:S(2)}, u32[]{:S(2)}) collective-permute-start(bf16[2,128,128]{2,1,0:T(8,128)(2,1)S(1)} %get-tuple-element.58), channel_id=1, source_target_pairs={{0,16},{4,20},{8,24},{12,28},{16,0},{20,4},{24,8},{28,12},{1,17},{... | collective-permute-start | bytes 196616 | tf_op jit(solution)/shard_map/ppermute | solution.py:64
  24.8 5.3 %collective-permute-start.12 = (bf16[2,128,128]{2,1,0:T(8,128)(2,1)S(1)}, bf16[2,128,128]{2,1,0:T(8,128)(2,1)S(1)}, u32[]{:S(2)}, u32[]{:S(2)}) collective-permute-start(bf16[2,128,128]{2,1,0:T(8,128)(2,1)S(1)} %get-tuple-element.59), channel_id=1, source_target_pairs={{0,24},{4,28},{8,16},{12,20},{16,8},{20,12},{24,0},{28,4},{1,25},{... | collective-permute-start | bytes 196616 | tf_op jit(solution)/shard_map/ppermute | solution.py:64
  30.2 5.8 %copy-start.5 = (bf16[512,2,512]{2,1,0:T(2,128)(2,1)S(1)}, bf16[512,2,512]{2,1,0:T(2,128)(2,1)}, u32[]{:S(2)}) copy-start(bf16[512,2,512]{2,1,0:T(2,128)(2,1)} %param.21) | copy-start | bytes 3145732
  30.2 6.1 %copy-start.6 = (f32[2304]{0:T(1024)S(1)}, f32[2304]{0:T(1024)}, u32[]{:S(2)}) copy-start(f32[2304]{0:T(1024)} %param.17) | copy-start | bytes 27652
  30.2 16.1 %copy-start.1 = (bf16[2304,512]{1,0:T(8,128)(2,1)S(1)}, bf16[2304,512]{1,0:T(8,128)(2,1)}, u32[]{:S(2)}) copy-start(bf16[2304,512]{1,0:T(8,128)(2,1)} %refs_1_.4) | copy-start | bytes 7077892
  30.2 16.1 %copy-start.4 = (f32[512]{0:T(512)S(1)}, f32[512]{0:T(512)}, u32[]{:S(2)}) copy-start(f32[512]{0:T(512)} %param.19) | copy-start | bytes 6148
  31.5 6.9 %collective-permute-start.13 = (bf16[32,2304]{1,0:T(8,128)(2,1)S(1)}, bf16[32,2304]{1,0:T(8,128)(2,1)S(1)}, u32[]{:S(2)}, u32[]{:S(2)}) collective-permute-start(bf16[32,2304]{1,0:T(8,128)(2,1)S(1)} %get-tuple-element.61), channel_id=1, source_target_pairs={{0,1},{1,0},{2,3},{3,2},{4,5},{5,4},{6,7},{7,6},{8,9},{9,8},{10,11... | collective-permute-start | bytes 442376 | tf_op jit(solution)/shard_map/ppermute | solution.py:64
  33.2 13.1 %collective-permute-start.14 = (bf16[32,2304]{1,0:T(8,128)(2,1)S(1)}, bf16[32,2304]{1,0:T(8,128)(2,1)S(1)}, u32[]{:S(2)}, u32[]{:S(2)}) collective-permute-start(bf16[32,2304]{1,0:T(8,128)(2,1)S(1)} %get-tuple-element.62), channel_id=1, source_target_pairs={{0,2},{1,3},{2,0},{3,1},{4,6},{5,7},{6,4},{7,5},{8,10},{9,11},{10,... | collective-permute-start | bytes 442376 | tf_op jit(solution)/shard_map/ppermute | solution.py:64
  35.9 10.5 %collective-permute-start.15 = (bf16[32,2304]{1,0:T(8,128)(2,1)S(1)}, bf16[32,2304]{1,0:T(8,128)(2,1)S(1)}, u32[]{:S(2)}, u32[]{:S(2)}) collective-permute-start(bf16[32,2304]{1,0:T(8,128)(2,1)S(1)} %get-tuple-element.63), channel_id=1, source_target_pairs={{0,3},{1,2},{2,1},{3,0},{4,7},{5,6},{6,5},{7,4},{8,11},{9,10},{10,... | collective-permute-start | bytes 442376 | tf_op jit(solution)/shard_map/ppermute | solution.py:64
  47.1 19.2 %copy-start.2 = (bf16[2304,512]{1,0:T(8,128)(2,1)S(1)}, bf16[2304,512]{1,0:T(8,128)(2,1)}, u32[]{:S(2)}) copy-start(bf16[2304,512]{1,0:T(8,128)(2,1)} %refs_1_.5) | copy-start | bytes 7077892
  47.1 10.3 %collective-permute-start.16 = (bf16[32,2816]{1,0:T(8,128)(2,1)S(1)}, bf16[32,2816]{1,0:T(8,128)(2,1)S(1)}, u32[]{:S(2)}, u32[]{:S(2)}) collective-permute-start(bf16[32,2816]{1,0:T(8,128)(2,1)S(1)} %get-tuple-element.70), channel_id=1, source_target_pairs={{0,1},{1,0},{2,3},{3,2},{4,5},{5,4},{6,7},{7,6},{8,9},{9,8},{10,11... | collective-permute-start | bytes 540680 | tf_op jit(solution)/shard_map/ppermute | solution.py:64
  49.3 5.9 %collective-permute-start.19 = (bf16[32,512]{1,0:T(8,128)(2,1)S(1)}, bf16[32,512]{1,0:T(8,128)(2,1)S(1)}, u32[]{:S(2)}, u32[]{:S(2)}) collective-permute-start(bf16[32,512]{1,0:T(8,128)(2,1)S(1)} %get-tuple-element.71.refs_0_), channel_id=1, source_target_pairs={{0,2},{1,3},{2,0},{3,1},{4,6},{5,7},{6,4},{7,5},{8,10},{9,11},{10,... | collective-permute-start | bytes 98312 | tf_op jit(solution)/shard_map/ppermute | solution.py:64
  50.4 7.0 %collective-permute-start.20 = (bf16[32,512]{1,0:T(8,128)(2,1)S(1)}, bf16[32,512]{1,0:T(8,128)(2,1)S(1)}, u32[]{:S(2)}, u32[]{:S(2)}) collective-permute-start(bf16[32,512]{1,0:T(8,128)(2,1)S(1)} %get-tuple-element.71.refs_0_), channel_id=1, source_target_pairs={{0,3},{1,2},{2,1},{3,0},{4,7},{5,6},{6,5},{7,4},{8,11},{9,10},{10,... | collective-permute-start | bytes 98312 | tf_op jit(solution)/shard_map/ppermute | solution.py:64
  51.8 9.2 %collective-permute-start.17 = (bf16[32,2304]{1,0:T(8,128)(2,1)S(1)}, bf16[32,2304]{1,0:T(8,128)(2,1)S(1)}, u32[]{:S(2)}, u32[]{:S(2)}) collective-permute-start(bf16[32,2304]{1,0:T(8,128)(2,1)S(1)} %get-tuple-element.69.refs_3_), channel_id=1, source_target_pairs={{0,2},{1,3},{2,0},{3,1},{4,6},{5,7},{6,4},{7,5},{8,10},{9,11},{10,... | collective-permute-start | bytes 442376 | tf_op jit(solution)/shard_map/ppermute | solution.py:64
  57.4 6.0 %collective-permute-start.21 = (bf16[128,512]{1,0:T(8,128)(2,1)S(1)}, bf16[128,512]{1,0:T(8,128)(2,1)S(1)}, u32[]{:S(2)}, u32[]{:S(2)}) collective-permute-start(bf16[128,512]{1,0:T(8,128)(2,1)S(1)} %shard_map.129.refs_7_), channel_id=1, source_target_pairs={{0,24},{4,28},{8,16},{12,20},{16,8},{20,12},{24,0},{28,4},{1,25},{... | collective-permute-start | bytes 393224 | tf_op jit(solution)/shard_map/ppermute | solution.py:64
  58.7 6.0 %collective-permute-start.22 = (bf16[128,512]{1,0:T(8,128)(2,1)S(1)}, bf16[128,512]{1,0:T(8,128)(2,1)S(1)}, u32[]{:S(2)}, u32[]{:S(2)}) collective-permute-start(bf16[128,512]{1,0:T(8,128)(2,1)S(1)} %shard_map.129.refs_7_), channel_id=1, source_target_pairs={{0,16},{4,20},{8,24},{12,28},{16,0},{20,4},{24,8},{28,12},{1,17},{... | collective-permute-start | bytes 393224 | tf_op jit(solution)/shard_map/ppermute | solution.py:64
  59.6 5.2 %collective-permute-start.23 = (bf16[128,512]{1,0:T(8,128)(2,1)S(1)}, bf16[128,512]{1,0:T(8,128)(2,1)S(1)}, u32[]{:S(2)}, u32[]{:S(2)}) collective-permute-start(bf16[128,512]{1,0:T(8,128)(2,1)S(1)} %shard_map.129.refs_7_), channel_id=1, source_target_pairs={{0,8},{4,12},{8,0},{12,4},{16,24},{20,28},{24,16},{28,20},{1,9},{5... | collective-permute-start | bytes 393224 | tf_op jit(solution)/shard_map/ppermute | solution.py:64
  61.0 5.1 %collective-permute-start.18 = (bf16[32,2304]{1,0:T(8,128)(2,1)S(1)}, bf16[32,2304]{1,0:T(8,128)(2,1)S(1)}, u32[]{:S(2)}, u32[]{:S(2)}) collective-permute-start(bf16[32,2304]{1,0:T(8,128)(2,1)S(1)} %collective-permute-done.17.refs_5_), channel_id=1, source_target_pairs={{0,1},{1,0},{2,3},{3,2},{4,5},{5,4},{6,7},{7,6},{8,9},{9,8},{10,11... | collective-permute-start | bytes 442376 | tf_op jit(solution)/shard_map/ppermute | solution.py:64
  61.2 4.9 %collective-permute-start.24 = (bf16[128,512]{1,0:T(8,128)(2,1)S(1)}, bf16[128,512]{1,0:T(8,128)(2,1)S(1)}, u32[]{:S(2)}, u32[]{:S(2)}) collective-permute-start(bf16[128,512]{1,0:T(8,128)(2,1)S(1)} %shard_map.129.refs_7_), channel_id=1, source_target_pairs={{0,4},{4,0},{8,12},{12,8},{16,20},{20,16},{24,28},{28,24},{1,5},{5... | collective-permute-start | bytes 393224 | tf_op jit(solution)/shard_map/ppermute | solution.py:64
  63.5 2.7 %collective-permute-start.25 = (bf16[128,512]{1,0:T(8,128)(2,1)S(1)}, bf16[128,512]{1,0:T(8,128)(2,1)S(1)}, u32[]{:S(2)}, u32[]{:S(2)}) collective-permute-start(bf16[128,512]{1,0:T(8,128)(2,1)S(1)} %collective-permute-done.21.refs_8_), channel_id=1, source_target_pairs={{0,4},{4,0},{8,12},{12,8},{16,20},{20,16},{24,28},{28,24},{1,5},{5... | collective-permute-start | bytes 393224 | tf_op jit(solution)/shard_map/ppermute | solution.py:64
  64.8 1.4 %collective-permute-start.26 = (bf16[128,512]{1,0:T(8,128)(2,1)S(1)}, bf16[128,512]{1,0:T(8,128)(2,1)S(1)}, u32[]{:S(2)}, u32[]{:S(2)}) collective-permute-start(bf16[128,512]{1,0:T(8,128)(2,1)S(1)} %collective-permute-done.22.refs_9_), channel_id=1, source_target_pairs={{0,4},{4,0},{8,12},{12,8},{16,20},{20,16},{24,28},{28,24},{1,5},{5... | collective-permute-start | bytes 393224 | tf_op jit(solution)/shard_map/ppermute | solution.py:64
  64.8 1.5 %collective-permute-start.27 = (bf16[128,512]{1,0:T(8,128)(2,1)S(1)}, bf16[128,512]{1,0:T(8,128)(2,1)S(1)}, u32[]{:S(2)}, u32[]{:S(2)}) collective-permute-start(bf16[128,512]{1,0:T(8,128)(2,1)S(1)} %collective-permute-done.23.refs_10_), channel_id=1, source_target_pairs={{0,4},{4,0},{8,12},{12,8},{16,20},{20,16},{24,28},{28,24},{1,5},{5... | collective-permute-start | bytes 393224 | tf_op jit(solution)/shard_map/ppermute | solution.py:64

commit v8 on v7

--- a/solution.py
+++ b/solution.py
@@ -102,7 +102,18 @@
     return jnp.concatenate(heads, axis=1)
 
 
-def load_kernel(stored_inputs, stored_gate, stored_taps, done, log, taps, gate, inputs, wide, sems):
+def last_rows_kernel(stored_inputs, rows, sems):
+    length, count = stored_inputs.shape[1], rows.shape[1]
+    move = pltpu.make_async_copy(
+        stored_inputs.at[:, length - count : length, :], rows, sems.at[0]
+    )
+    move.start()
+    move.wait()
+
+
+def load_kernel(
+    stored_inputs, stored_gate, stored_taps, done, head_rows, log, taps, gate, inputs, wide, sems
+):
     moves = [
         pltpu.make_async_copy(stored_gate, gate, sems.at[0]),
         pltpu.make_async_copy(stored_taps, taps, sems.at[1]),
@@ -120,6 +131,7 @@
     log[...] = mm(tril, high) + mm(tril, low)
     moves[1].wait()
     moves[2].wait()
+    head_rows[...] = inputs[:, : head_rows.shape[1], :]
     for part in range(3):
         wide[:8, :] = jnp.zeros((8, wide.shape[1]), f32)
         wide[8:, :] = inputs[part].astype(f32)
@@ -280,26 +292,30 @@
     return state.astype(f32) * decay - mm(state, move) + offset.astype(f32)
 
 
+def stack_kernel(pairs, *refs):
+    blocks, (maps,) = refs[:pairs], refs[pairs:]
+    chip, _ = split_cores(here(2 * pairs))
+    for step in range(pairs):
+        maps[partner(chip, step, pairs)] = blocks[step][...]
+
+
 def scan_kernel(pairs, grouped, *refs):
-    sides, refs = (refs[:pairs], refs[pairs : 2 * pairs]), refs[2 * pairs :]
+    maps, refs = refs[:2], refs[2:]
     if grouped:
         start, refs = refs[0], refs[1:]
     outs, refs = refs[:pairs], refs[pairs:]
     if grouped:
         final, refs = refs[0], refs[1:]
-    maps, starts = refs
+    starts = refs[0]
     chip, _ = split_cores(here(2 * pairs))
-    for side in range(2):
-        for step in range(pairs):
-            maps[side, partner(chip, step, pairs)] = sides[side][step][...]
     states = [start[side] if grouped else jnp.zeros((DK, DK), f32) for side in range(2)]
     for i in range(pairs):
         for side in range(2):
             starts[i, side] = states[side].astype(bf16)
             if i == 0 and not grouped:
-                states[side] = maps[side, i, :DK, :].astype(f32)
+                states[side] = maps[side][i, :DK, :].astype(f32)
             elif i < pairs - 1 or grouped:
-                states[side] = apply_map(states[side], maps[side, i])
+                states[side] = apply_map(states[side], maps[side][i])
     if grouped:
         for side in range(2):
             final[side] = states[side]
@@ -431,13 +447,22 @@
     count, parts = lax.axis_size("ctx"), lax.axis_size("head")
     groups = count // heads
 
-    halo = passed_along(kda_inputs[:, length - HALO :, :], "ctx", 1)
     stored = [
         pltpu.with_memory_space_constraint(a, pltpu.HBM) for a in (kda_inputs, gate_log, conv_weight)
     ]
-    done, logs, taps = call(
+    edge_shape = (kda_inputs.shape[0], HALO, kda_inputs.shape[2])
+    last_rows = call(
+        last_rows_kernel, [(edge_shape, bf16)], stored[:1], limit=8, stored=(0,), copies=1, cost=0.2
+    )[0]
+    halo = passed_along(last_rows, "ctx", 1)
+    done, head_rows, logs, taps = call(
         load_kernel,
-        [(kda_inputs.shape, bf16), (gate_log.shape, f32), (conv_weight.shape, f32)],
+        [
+            (kda_inputs.shape, bf16),
+            (edge_shape, bf16),
+            (gate_log.shape, f32),
+            (conv_weight.shape, f32),
+        ],
         stored,
         [
             (gate_log.shape, f32),
@@ -450,7 +475,6 @@
         cost=2.0,
     )
     map_shape = (2 * DK + EXTRA, DK)
-    head_rows = kda_inputs[:, :HALO, :]
     arguments = [done, head_rows, halo, logs, beta.T, taps]
     kept, sent, solutions, shrunk = call(
         map_kernel,
@@ -489,15 +513,22 @@
         return [pieces[0]] + [moved[step] for step in range(1, pairs)]
 
     chip_maps, reads, intra = lax.optimization_barrier((across_chips(chip_maps), reads, intra))
-    other_maps = [trade(one, "ctx", 1, heads) for one in chip_maps]
+    chip_maps = call(
+        functools.partial(stack_kernel, pairs),
+        [((pairs,) + map_shape, bf16)],
+        chip_maps,
+        limit=8,
+        cost=0.2,
+    )[0]
+    other_maps = trade(chip_maps, "ctx", 1, heads)
     state_outs = [((2, DK, DK), bf16)] * pairs
-    scratch = [((2, pairs) + map_shape, bf16), ((pairs, 2, DK, DK), bf16)]
+    scratch = [((pairs, 2, DK, DK), bf16)]
 
     def run(*start):
         return call(
             functools.partial(scan_kernel, pairs, len(start) > 0),
             state_outs + [((2, DK, DK), f32)] * len(start),
-            chip_maps + other_maps + list(start),
+            [chip_maps, other_maps] + list(start),
             scratch,
             8,
         )

time: 69.8 us -> 69.1 us (0.990)
  local copies, waits for them, and re-layouts: 1.26 us -> 0.3 us
  starting transfers between devices: 24.8 us -> 23.9 us
  Pallas kernels: 15.1 us -> 16 us
    slice x1 -> x0, local copies, waits for them, and re-layouts: 0.96 us -> none  [per_device(): halo = passed_along(kda_inputs[:, length - HALO:, :], 'ctx', 1)]
    ppermute x27 -> x24, starting transfers between devices: 24.3 us -> 23.4 us  [trade(): return lax.ppermute(block, axis, route)]
    pallas_call x9 -> x11, Pallas kernels: 15.1 us -> 16 us  [call(): pl.pallas_call(kernel, out_shape=[jax.ShapeDtypeStruct(shape, dtype) for...]
    ppermute x27 -> x24, waiting for transfers between devices: 25.3 us -> 25.6 us  [trade(): return lax.ppermute(block, axis, route)]
  transfers between devices with their start and end apart: 28 -> 25, of which waited for: 17 -> 15; matrix products, arithmetic and copies ran while one was open for 0% -> 0% of each run, Pallas kernels for 9% -> 9%
where the time goes in v8:
time: 69.1 us; the launch traced here: 69 us
  waiting for transfers between devices  27.8 us (40%)
  starting transfers between devices  23.9 us (35%)
  Pallas kernels  16 us (23%)
  between operations  0.85 us (1%)
    ppermute x24, waiting for transfers between devices, trade(): return lax.ppermute(block, axis, route)  25.6 us
    ppermute x24, starting transfers between devices, trade(): return lax.ppermute(block, axis, route)  23.4 us
    pallas_call x11, Pallas kernels, call(): pl.pallas_call(kernel, out_shape=[jax.ShapeDtypeStruct(shape, dtype) for...  16 us
    ppermute x1, waiting for transfers between devices, passed_along(): lax.ppermute(block, axis, [(i, (i + distance) % count) for i in range(cou...  2.19 us
  transfers between devices with their start and end apart: 25, of which 15 were waited for; matrix products, arithmetic and copies ran while one was open for 0% of the time, Pallas kernels for 9%

profile of v8, /device:TPU:0, one launch (start us, length us, event | category | flops | bytes accessed | tf_op | source)
XLA Modules:
  0.0 69.0 jit_solution(11452241084451935046)
XLA Ops:
  0.6 0.9 %shard_map.123 = bf16[3,16,1024]{2,1,0:T(8,128)(2,1)S(1)} custom-call(bf16[3,128,1024]{2,1,0:T(8,128)(2,1)} %stored_inputs.3), custom_call_target="tpu_custom_call" | custom-call | flops 200000000 | tf_op jit(solution)/shard_map/pallas_call | solution.py:44
  1.5 0.0 copy-start.3
  1.6 0.5 collective-permute-start
  2.1 3.0 %shard_map.122 = (bf16[3,128,1024]{2,1,0:T(8,128)(2,1)S(1)}, bf16[3,16,1024]{2,1,0:T(8,128)(2,1)S(1)}, f32[128,1024]{1,0:T(8,128)S(1)}, f32[3,4,1024]{2,1,0:T(4,128)S(1)}) custom-call(bf16[3,128,1024]{2,1,0:T(8,128)(2,1)} %stored_inputs.3, f32[128,1024]{1,0:T(8,128)} %stored_gate.1, f32[3,4,1024]{2,1,0:T(4,128)} %stored_taps.1), custom_call_target="tpu_custom_call" | custom-call | flops 2000000000 | tf_op jit(solution)/shard_map/pallas_call | solution.py:44
  5.0 2.2 %collective-permute-done.halo = bf16[3,16,1024]{2,1,0:T(8,128)(2,1)S(1)} collective-permute-done((bf16[3,16,1024]{2,1,0:T(8,128)(2,1)S(1)}, bf16[3,16,1024]{2,1,0:T(8,128)(2,1)S(1)}, u32[]{:S(2)}, u32[]{:S(2)}) %collective-permute-start) | collective-permute-done | bytes 98336 | tf_op jit(solution)/shard_map/ppermute | solution.py:69
  7.2 3.3 %shard_map.124 = (bf16[4,272,128]{2,1,0:T(8,128)(2,1)S(1)}, bf16[4,272,128]{2,1,0:T(8,128)(2,1)S(1)}, bf16[8,128,256]{2,1,0:T(8,128)(2,1)S(1)}, bf16[8,2,128,128]{3,2,1,0:T(8,128)(2,1)S(1)}) custom-call(bf16[3,128,1024]{2,1,0:T(8,128)(2,1)S(1)} %get-tuple-element.38.done, bf16[3,16,1024]{2,1,0:T(8,128)(2,1)S(1)} %get-tuple-element.39.head_rows, ...), custom_call_target="tpu_custom_call" | custom-call | flops 5000000000 | tf_op jit(solution)/shard_map/pallas_call | solution.py:44
  10.5 0.5 collective-permute-start.1
  11.0 0.1 collective-permute-start.5
  11.1 1.1 %collective-permute-done.1.got.refs_2_ = bf16[4,272,128]{2,1,0:T(8,128)(2,1)S(1)} collective-permute-done((bf16[4,272,128]{2,1,0:T(8,128)(2,1)S(1)}, bf16[4,272,128]{2,1,0:T(8,128)(2,1)S(1)}, u32[]{:S(2)}, u32[]{:S(2)}) %collective-permute-start.1) | collective-permute-done | bytes 278560 | tf_op jit(solution)/shard_map/ppermute | solution.py:64
  12.2 0.3 shard_map.125
  12.5 1.6 %collective-permute-start.2 = (bf16[272,128]{1,0:T(8,128)(2,1)S(1)}, bf16[272,128]{1,0:T(8,128)(2,1)S(1)}, u32[]{:S(2)}, u32[]{:S(2)}) collective-permute-start(bf16[272,128]{1,0:T(8,128)(2,1)S(1)} %get-tuple-element.45), channel_id=1, source_target_pairs={{0,8},{4,12},{8,0},{12,4},{16,24},{20,28},{24,16},{28,20},{1,9},{5... | collective-permute-start | bytes 208904 | tf_op jit(solution)/shard_map/ppermute | solution.py:64
  14.1 1.3 %collective-permute-start.3 = (bf16[272,128]{1,0:T(8,128)(2,1)S(1)}, bf16[272,128]{1,0:T(8,128)(2,1)S(1)}, u32[]{:S(2)}, u32[]{:S(2)}) collective-permute-start(bf16[272,128]{1,0:T(8,128)(2,1)S(1)} %get-tuple-element.46), channel_id=1, source_target_pairs={{0,16},{4,20},{8,24},{12,28},{16,0},{20,4},{24,8},{28,12},{1,17},{... | collective-permute-start | bytes 208904 | tf_op jit(solution)/shard_map/ppermute | solution.py:64
  15.4 0.9 %collective-permute-start.4 = (bf16[272,128]{1,0:T(8,128)(2,1)S(1)}, bf16[272,128]{1,0:T(8,128)(2,1)S(1)}, u32[]{:S(2)}, u32[]{:S(2)}) collective-permute-start(bf16[272,128]{1,0:T(8,128)(2,1)S(1)} %get-tuple-element.47), channel_id=1, source_target_pairs={{0,24},{4,28},{8,16},{12,20},{16,8},{20,12},{24,0},{28,4},{1,25},{... | collective-permute-start | bytes 208904 | tf_op jit(solution)/shard_map/ppermute | solution.py:64
  16.3 2.8 %shard_map.126 = (bf16[128,1024]{1,0:T(8,128)(2,1)S(1)}, f32[128,1024]{1,0:T(8,128)S(1)}) custom-call(bf16[3,128,1024]{2,1,0:T(8,128)(2,1)S(1)} %get-tuple-element.38.done, bf16[3,16,1024]{2,1,0:T(8,128)(2,1)S(1)} %get-tuple-element.39.head_rows, bf16[3,16,1024]{2,1,0:T(8,128)(2,1)S(1)} %collective-permute-done.halo, ...), custom_call_target="tpu_custom_call" | custom-call | flops 2500000000 | tf_op jit(solution)/shard_map/pallas_call | solution.py:44
  19.1 1.5 %collective-permute-done.4.refs_3_ = bf16[272,128]{1,0:T(8,128)(2,1)S(1)} collective-permute-done((bf16[272,128]{1,0:T(8,128)(2,1)S(1)}, bf16[272,128]{1,0:T(8,128)(2,1)S(1)}, u32[]{:S(2)}, u32[]{:S(2)}) %collective-permute-start.4) | collective-permute-done | bytes 69664 | tf_op jit(solution)/shard_map/ppermute | solution.py:64
  20.7 0.1 collective-permute-start.6
  20.7 1.5 %collective-permute-done.6.refs_1_ = bf16[4,272,128]{2,1,0:T(8,128)(2,1)S(1)} collective-permute-done((bf16[4,272,128]{2,1,0:T(8,128)(2,1)S(1)}, bf16[4,272,128]{2,1,0:T(8,128)(2,1)S(1)}, u32[]{:S(2)}, u32[]{:S(2)}) %collective-permute-start.6) | collective-permute-done | bytes 278560 | tf_op jit(solution)/shard_map/ppermute | solution.py:64
  22.3 0.3 shard_map.128
  22.6 1.5 %collective-permute-start.7 = (bf16[2,128,128]{2,1,0:T(8,128)(2,1)S(1)}, bf16[2,128,128]{2,1,0:T(8,128)(2,1)S(1)}, u32[]{:S(2)}, u32[]{:S(2)}) collective-permute-start(bf16[2,128,128]{2,1,0:T(8,128)(2,1)S(1)} %get-tuple-element.59), channel_id=1, source_target_pairs={{0,8},{4,12},{8,0},{12,4},{16,24},{20,28},{24,16},{28,20},{1,9},{5... | collective-permute-start | bytes 196616 | tf_op jit(solution)/shard_map/ppermute | solution.py:64
  24.1 0.4 collective-permute-start.8
  24.5 1.7 %collective-permute-start.9 = (bf16[2,128,128]{2,1,0:T(8,128)(2,1)S(1)}, bf16[2,128,128]{2,1,0:T(8,128)(2,1)S(1)}, u32[]{:S(2)}, u32[]{:S(2)}) collective-permute-start(bf16[2,128,128]{2,1,0:T(8,128)(2,1)S(1)} %get-tuple-element.61), channel_id=1, source_target_pairs={{0,24},{4,28},{8,16},{12,20},{16,8},{20,12},{24,0},{28,4},{1,25},{... | collective-permute-start | bytes 196616 | tf_op jit(solution)/shard_map/ppermute | solution.py:64
  26.1 0.8 %collective-permute-done.7.refs_5_ = bf16[2,128,128]{2,1,0:T(8,128)(2,1)S(1)} collective-permute-done((bf16[2,128,128]{2,1,0:T(8,128)(2,1)S(1)}, bf16[2,128,128]{2,1,0:T(8,128)(2,1)S(1)}, u32[]{:S(2)}, u32[]{:S(2)}) %collective-permute-start.7) | collective-permute-done | bytes 65568 | tf_op jit(solution)/shard_map/ppermute | solution.py:64
  26.9 2.0 %collective-permute-done.8.refs_6_ = bf16[2,128,128]{2,1,0:T(8,128)(2,1)S(1)} collective-permute-done((bf16[2,128,128]{2,1,0:T(8,128)(2,1)S(1)}, bf16[2,128,128]{2,1,0:T(8,128)(2,1)S(1)}, u32[]{:S(2)}, u32[]{:S(2)}) %collective-permute-start.8) | collective-permute-done | bytes 65568 | tf_op jit(solution)/shard_map/ppermute | solution.py:64
  29.0 0.7 %collective-permute-done.9.refs_7_ = bf16[2,128,128]{2,1,0:T(8,128)(2,1)S(1)} collective-permute-done((bf16[2,128,128]{2,1,0:T(8,128)(2,1)S(1)}, bf16[2,128,128]{2,1,0:T(8,128)(2,1)S(1)}, u32[]{:S(2)}, u32[]{:S(2)}) %collective-permute-start.9) | collective-permute-done | bytes 65568 | tf_op jit(solution)/shard_map/ppermute | solution.py:64
  29.7 1.3 %shard_map.129 = (f32[32,2304]{1,0:T(8,128)S(1)}, bf16[32,2304]{1,0:T(8,128)(2,1)S(1)}, bf16[32,2304]{1,0:T(8,128)(2,1)S(1)}, bf16[32,2304]{1,0:T(8,128)(2,1)S(1)}) custom-call(bf16[128,2304]{1,0:T(8,128)(2,1)S(1)} %copy-done, bf16[1024,2304]{1,0:T(8,128)(2,1)S(1)} %bitcast.5, bf16[128,1024]{1,0:T(8,128)(2,1)S(1)} %get-tuple-element.52.refs_2_, ...), custom_call_target="tpu_custom_call" | custom-call | flops 1000000000 | tf_op jit(solution)/shard_map/pallas_call | solution.py:44
  31.0 1.8 %collective-permute-start.10 = (bf16[32,2304]{1,0:T(8,128)(2,1)S(1)}, bf16[32,2304]{1,0:T(8,128)(2,1)S(1)}, u32[]{:S(2)}, u32[]{:S(2)}) collective-permute-start(bf16[32,2304]{1,0:T(8,128)(2,1)S(1)} %get-tuple-element.63), channel_id=1, source_target_pairs={{0,1},{1,0},{2,3},{3,2},{4,5},{5,4},{6,7},{7,6},{8,9},{9,8},{10,11... | collective-permute-start | bytes 442376 | tf_op jit(solution)/shard_map/ppermute | solution.py:64
  32.9 2.6 %collective-permute-start.11 = (bf16[32,2304]{1,0:T(8,128)(2,1)S(1)}, bf16[32,2304]{1,0:T(8,128)(2,1)S(1)}, u32[]{:S(2)}, u32[]{:S(2)}) collective-permute-start(bf16[32,2304]{1,0:T(8,128)(2,1)S(1)} %get-tuple-element.64), channel_id=1, source_target_pairs={{0,2},{1,3},{2,0},{3,1},{4,6},{5,7},{6,4},{7,5},{8,10},{9,11},{10,... | collective-permute-start | bytes 442376 | tf_op jit(solution)/shard_map/ppermute | solution.py:64
  35.5 0.0 collective-permute-start.12
  35.5 0.2 copy.13
  35.8 2.1 %collective-permute-done.10.refs_4_ = bf16[32,2304]{1,0:T(8,128)(2,1)S(1)} collective-permute-done((bf16[32,2304]{1,0:T(8,128)(2,1)S(1)}, bf16[32,2304]{1,0:T(8,128)(2,1)S(1)}, u32[]{:S(2)}, u32[]{:S(2)}) %collective-permute-start.10) | collective-permute-done | bytes 147488 | tf_op jit(solution)/shard_map/ppermute | solution.py:64
  37.9 7.8 %collective-permute-done.11.refs_5_ = bf16[32,2304]{1,0:T(8,128)(2,1)S(1)} collective-permute-done((bf16[32,2304]{1,0:T(8,128)(2,1)S(1)}, bf16[32,2304]{1,0:T(8,128)(2,1)S(1)}, u32[]{:S(2)}, u32[]{:S(2)}) %collective-permute-start.11) | collective-permute-done | bytes 147488 | tf_op jit(solution)/shard_map/ppermute | solution.py:64
  45.7 0.8 %shard_map.130 = (bf16[32,2304]{1,0:T(8,128)(2,1)S(1)}, bf16[32,512]{1,0:T(8,128)(2,1)S(1)}, bf16[32,2816]{1,0:T(8,128)(2,1)S(1)}) custom-call(f32[1,2304]{1,0:T(1,128)S(1)} %broadcast_in_dim.7.refs_0_, bf16[2304,512]{1,0:T(8,128)(2,1)S(1)} %copy-done.1, f32[1,512]{1,0:T(1,128)S(1)} %bitcast.9, f32[32,2304]{1,0:T(8,128)S(1)} %get-tuple-element.67.refs_3_, ...), custom_call_target="tpu_custom_call" | custom-call | flops 1000000000 | tf_op jit(solution)/shard_map/pallas_call | solution.py:44
  46.5 2.2 %collective-permute-start.13 = (bf16[32,2816]{1,0:T(8,128)(2,1)S(1)}, bf16[32,2816]{1,0:T(8,128)(2,1)S(1)}, u32[]{:S(2)}, u32[]{:S(2)}) collective-permute-start(bf16[32,2816]{1,0:T(8,128)(2,1)S(1)} %get-tuple-element.72), channel_id=1, source_target_pairs={{0,1},{1,0},{2,3},{3,2},{4,5},{5,4},{6,7},{7,6},{8,9},{9,8},{10,11... | collective-permute-start | bytes 540680 | tf_op jit(solution)/shard_map/ppermute | solution.py:64
  48.7 1.1 %collective-permute-start.16 = (bf16[32,512]{1,0:T(8,128)(2,1)S(1)}, bf16[32,512]{1,0:T(8,128)(2,1)S(1)}, u32[]{:S(2)}, u32[]{:S(2)}) collective-permute-start(bf16[32,512]{1,0:T(8,128)(2,1)S(1)} %get-tuple-element.73.refs_0_), channel_id=1, source_target_pairs={{0,2},{1,3},{2,0},{3,1},{4,6},{5,7},{6,4},{7,5},{8,10},{9,11},{10,... | collective-permute-start | bytes 98312 | tf_op jit(solution)/shard_map/ppermute | solution.py:64
  49.8 1.4 %collective-permute-start.17 = (bf16[32,512]{1,0:T(8,128)(2,1)S(1)}, bf16[32,512]{1,0:T(8,128)(2,1)S(1)}, u32[]{:S(2)}, u32[]{:S(2)}) collective-permute-start(bf16[32,512]{1,0:T(8,128)(2,1)S(1)} %get-tuple-element.73.refs_0_), channel_id=1, source_target_pairs={{0,3},{1,2},{2,1},{3,0},{4,7},{5,6},{6,5},{7,4},{8,11},{9,10},{10,... | collective-permute-start | bytes 98312 | tf_op jit(solution)/shard_map/ppermute | solution.py:64
  51.2 2.0 %collective-permute-start.14 = (bf16[32,2304]{1,0:T(8,128)(2,1)S(1)}, bf16[32,2304]{1,0:T(8,128)(2,1)S(1)}, u32[]{:S(2)}, u32[]{:S(2)}) collective-permute-start(bf16[32,2304]{1,0:T(8,128)(2,1)S(1)} %get-tuple-element.71.refs_3_), channel_id=1, source_target_pairs={{0,2},{1,3},{2,0},{3,1},{4,6},{5,7},{6,4},{7,5},{8,10},{9,11},{10,... | collective-permute-start | bytes 442376 | tf_op jit(solution)/shard_map/ppermute | solution.py:64
  53.2 1.3 %collective-permute-done.16.refs_2_ = bf16[32,512]{1,0:T(8,128)(2,1)S(1)} collective-permute-done((bf16[32,512]{1,0:T(8,128)(2,1)S(1)}, bf16[32,512]{1,0:T(8,128)(2,1)S(1)}, u32[]{:S(2)}, u32[]{:S(2)}) %collective-permute-start.16) | collective-permute-done | bytes 32800 | tf_op jit(solution)/shard_map/ppermute | solution.py:64
  54.5 2.2 %collective-permute-done.17.refs_3_ = bf16[32,512]{1,0:T(8,128)(2,1)S(1)} collective-permute-done((bf16[32,512]{1,0:T(8,128)(2,1)S(1)}, bf16[32,512]{1,0:T(8,128)(2,1)S(1)}, u32[]{:S(2)}, u32[]{:S(2)}) %collective-permute-start.17) | collective-permute-done | bytes 32800 | tf_op jit(solution)/shard_map/ppermute | solution.py:64
  56.7 1.4 %collective-permute-start.18 = (bf16[128,512]{1,0:T(8,128)(2,1)S(1)}, bf16[128,512]{1,0:T(8,128)(2,1)S(1)}, u32[]{:S(2)}, u32[]{:S(2)}) collective-permute-start(bf16[128,512]{1,0:T(8,128)(2,1)S(1)} %shard_map.131.refs_7_), channel_id=1, source_target_pairs={{0,24},{4,28},{8,16},{12,20},{16,8},{20,12},{24,0},{28,4},{1,25},{... | collective-permute-start | bytes 393224 | tf_op jit(solution)/shard_map/ppermute | solution.py:64
  58.2 0.8 %collective-permute-start.19 = (bf16[128,512]{1,0:T(8,128)(2,1)S(1)}, bf16[128,512]{1,0:T(8,128)(2,1)S(1)}, u32[]{:S(2)}, u32[]{:S(2)}) collective-permute-start(bf16[128,512]{1,0:T(8,128)(2,1)S(1)} %shard_map.131.refs_7_), channel_id=1, source_target_pairs={{0,16},{4,20},{8,24},{12,28},{16,0},{20,4},{24,8},{28,12},{1,17},{... | collective-permute-start | bytes 393224 | tf_op jit(solution)/shard_map/ppermute | solution.py:64
  59.0 1.3 %collective-permute-start.20 = (bf16[128,512]{1,0:T(8,128)(2,1)S(1)}, bf16[128,512]{1,0:T(8,128)(2,1)S(1)}, u32[]{:S(2)}, u32[]{:S(2)}) collective-permute-start(bf16[128,512]{1,0:T(8,128)(2,1)S(1)} %shard_map.131.refs_7_), channel_id=1, source_target_pairs={{0,8},{4,12},{8,0},{12,4},{16,24},{20,28},{24,16},{28,20},{1,9},{5... | collective-permute-start | bytes 393224 | tf_op jit(solution)/shard_map/ppermute | solution.py:64
  60.3 0.2 collective-permute-start.15
  60.5 2.3 %collective-permute-done.18.refs_8_ = bf16[128,512]{1,0:T(8,128)(2,1)S(1)} collective-permute-done((bf16[128,512]{1,0:T(8,128)(2,1)S(1)}, bf16[128,512]{1,0:T(8,128)(2,1)S(1)}, u32[]{:S(2)}, u32[]{:S(2)}) %collective-permute-start.18) | collective-permute-done | bytes 131104 | tf_op jit(solution)/shard_map/ppermute | solution.py:64
  62.8 1.3 %collective-permute-done.19.refs_9_ = bf16[128,512]{1,0:T(8,128)(2,1)S(1)} collective-permute-done((bf16[128,512]{1,0:T(8,128)(2,1)S(1)}, bf16[128,512]{1,0:T(8,128)(2,1)S(1)}, u32[]{:S(2)}, u32[]{:S(2)}) %collective-permute-start.19) | collective-permute-done | bytes 131104 | tf_op jit(solution)/shard_map/ppermute | solution.py:64
  64.1 0.5 collective-permute-start.24
  64.6 0.9 %collective-permute-done.15.refs_6_ = bf16[32,2304]{1,0:T(8,128)(2,1)S(1)} collective-permute-done((bf16[32,2304]{1,0:T(8,128)(2,1)S(1)}, bf16[32,2304]{1,0:T(8,128)(2,1)S(1)}, u32[]{:S(2)}, u32[]{:S(2)}) %collective-permute-start.15) | collective-permute-done | bytes 147488 | tf_op jit(solution)/shard_map/ppermute | solution.py:64
  65.5 0.2 collective-permute-done.24.refs_14_
  65.6 3.4 %shard_map.132 = (bf16[128,2304]{1,0:T(8,128)(2,1)}, bf16[128,512]{1,0:T(8,128)(2,1)}) custom-call(f32[1,2304]{1,0:T(1,128)S(1)} %broadcast_in_dim.7.refs_0_, bf16[2304,512]{1,0:T(8,128)(2,1)S(1)} %copy-done.2, bf16[512,1024]{1,0:T(8,128)(2,1)S(1)} %bitcast.6, bf16[32,2304]{1,0:T(8,128)(2,1)S(1)} %get-tuple-element.71.refs_3_, ...), custom_call_target="tpu_custom_call" | custom-call | flops 4000000000 | tf_op jit(solution)/shard_map/pallas_call | solution.py:44
  (34 shorter events, 0.1 us)
Async XLA Ops:
  1.5 5.7 %copy-start.3 = (f32[128,8]{0,1:T(8,128)S(1)}, f32[128,8]{0,1:T(8,128)}, u32[]{:S(2)}) copy-start(f32[128,8]{0,1:T(8,128)} %param.13) | copy-start | bytes 12292
  1.6 5.7 %collective-permute-start = (bf16[3,16,1024]{2,1,0:T(8,128)(2,1)S(1)}, bf16[3,16,1024]{2,1,0:T(8,128)(2,1)S(1)}, u32[]{:S(2)}, u32[]{:S(2)}) collective-permute-start(bf16[3,16,1024]{2,1,0:T(8,128)(2,1)S(1)} %shard_map.123), channel_id=1, source_target_pairs={{0,4},{4,8},{8,12},{12,16},{16,20},{20,24},{24,28},{28,0},{1,5},{5... | collective-permute-start | bytes 294920 | tf_op jit(solution)/shard_map/ppermute | solution.py:69
  10.5 1.7 %collective-permute-start.1 = (bf16[4,272,128]{2,1,0:T(8,128)(2,1)S(1)}, bf16[4,272,128]{2,1,0:T(8,128)(2,1)S(1)}, u32[]{:S(2)}, u32[]{:S(2)}) collective-permute-start(bf16[4,272,128]{2,1,0:T(8,128)(2,1)S(1)} %get-tuple-element.43), channel_id=1, source_target_pairs={{0,4},{4,0},{8,12},{12,8},{16,20},{20,16},{24,28},{28,24},{1,5},{5... | collective-permute-start | bytes 835592 | tf_op jit(solution)/shard_map/ppermute | solution.py:64
  11.0 5.3 %collective-permute-start.5 = (bf16[4,272,128]{2,1,0:T(8,128)(2,1)S(1)}, bf16[4,272,128]{2,1,0:T(8,128)(2,1)S(1)}, u32[]{:S(2)}, u32[]{:S(2)}) collective-permute-start(bf16[4,272,128]{2,1,0:T(8,128)(2,1)S(1)} %get-tuple-element.42.kept), channel_id=1, source_target_pairs={{0,4},{4,0},{8,12},{12,8},{16,20},{20,16},{24,28},{28,24},{1,5},{5... | collective-permute-start | bytes 835592 | tf_op jit(solution)/shard_map/ppermute | solution.py:64
  12.5 6.6 %collective-permute-start.2 = (bf16[272,128]{1,0:T(8,128)(2,1)S(1)}, bf16[272,128]{1,0:T(8,128)(2,1)S(1)}, u32[]{:S(2)}, u32[]{:S(2)}) collective-permute-start(bf16[272,128]{1,0:T(8,128)(2,1)S(1)} %get-tuple-element.45), channel_id=1, source_target_pairs={{0,8},{4,12},{8,0},{12,4},{16,24},{20,28},{24,16},{28,20},{1,9},{5... | collective-permute-start | bytes 208904 | tf_op jit(solution)/shard_map/ppermute | solution.py:64
  14.1 5.0 %collective-permute-start.3 = (bf16[272,128]{1,0:T(8,128)(2,1)S(1)}, bf16[272,128]{1,0:T(8,128)(2,1)S(1)}, u32[]{:S(2)}, u32[]{:S(2)}) collective-permute-start(bf16[272,128]{1,0:T(8,128)(2,1)S(1)} %get-tuple-element.46), channel_id=1, source_target_pairs={{0,16},{4,20},{8,24},{12,28},{16,0},{20,4},{24,8},{28,12},{1,17},{... | collective-permute-start | bytes 208904 | tf_op jit(solution)/shard_map/ppermute | solution.py:64
  15.4 5.2 %collective-permute-start.4 = (bf16[272,128]{1,0:T(8,128)(2,1)S(1)}, bf16[272,128]{1,0:T(8,128)(2,1)S(1)}, u32[]{:S(2)}, u32[]{:S(2)}) collective-permute-start(bf16[272,128]{1,0:T(8,128)(2,1)S(1)} %get-tuple-element.47), channel_id=1, source_target_pairs={{0,24},{4,28},{8,16},{12,20},{16,8},{20,12},{24,0},{28,4},{1,25},{... | collective-permute-start | bytes 208904 | tf_op jit(solution)/shard_map/ppermute | solution.py:64
  16.3 13.4 %slice-start = ((s8[4718592]{0:T(1024)(128)(4,1)}), s8[4194304]{0:T(1024)(128)(4,1)S(1)}, s32[]{:S(2)}) async-start(s8[4718592]{0:T(1024)(128)(4,1)} %bitcast.4), calls=%async_computation | async-start | bytes 8388608
  16.3 13.4 %slice-start.1 = ((s8[4718592]{0:T(1024)(128)(4,1)}), s8[524288]{0:T(1024)(128)(4,1)S(1)}, s32[]{:S(2)}) async-start(s8[4718592]{0:T(1024)(128)(4,1)} %bitcast.4), calls=%async_computation.1 | async-start | bytes 1048576
  19.1 10.6 %copy-start = (bf16[128,2304]{1,0:T(8,128)(2,1)S(1)}, bf16[128,2304]{1,0:T(8,128)(2,1)}, u32[]{:S(2)}) copy-start(bf16[128,2304]{1,0:T(8,128)(2,1)} %refs_0_.1) | copy-start | bytes 1769476
  20.7 1.6 %collective-permute-start.6 = (bf16[4,272,128]{2,1,0:T(8,128)(2,1)S(1)}, bf16[4,272,128]{2,1,0:T(8,128)(2,1)S(1)}, u32[]{:S(2)}, u32[]{:S(2)}) collective-permute-start(bf16[4,272,128]{2,1,0:T(8,128)(2,1)S(1)} %shard_map.127.refs_0_), channel_id=1, source_target_pairs={{0,4},{4,0},{8,12},{12,8},{16,20},{20,16},{24,28},{28,24},{1,5},{5... | collective-permute-start | bytes 835592 | tf_op jit(solution)/shard_map/ppermute | solution.py:64
  22.6 4.3 %collective-permute-start.7 = (bf16[2,128,128]{2,1,0:T(8,128)(2,1)S(1)}, bf16[2,128,128]{2,1,0:T(8,128)(2,1)S(1)}, u32[]{:S(2)}, u32[]{:S(2)}) collective-permute-start(bf16[2,128,128]{2,1,0:T(8,128)(2,1)S(1)} %get-tuple-element.59), channel_id=1, source_target_pairs={{0,8},{4,12},{8,0},{12,4},{16,24},{20,28},{24,16},{28,20},{1,9},{5... | collective-permute-start | bytes 196616 | tf_op jit(solution)/shard_map/ppermute | solution.py:64
  24.1 4.9 %collective-permute-start.8 = (bf16[2,128,128]{2,1,0:T(8,128)(2,1)S(1)}, bf16[2,128,128]{2,1,0:T(8,128)(2,1)S(1)}, u32[]{:S(2)}, u32[]{:S(2)}) collective-permute-start(bf16[2,128,128]{2,1,0:T(8,128)(2,1)S(1)} %get-tuple-element.60), channel_id=1, source_target_pairs={{0,16},{4,20},{8,24},{12,28},{16,0},{20,4},{24,8},{28,12},{1,17},{... | collective-permute-start | bytes 196616 | tf_op jit(solution)/shard_map/ppermute | solution.py:64
  24.5 5.2 %collective-permute-start.9 = (bf16[2,128,128]{2,1,0:T(8,128)(2,1)S(1)}, bf16[2,128,128]{2,1,0:T(8,128)(2,1)S(1)}, u32[]{:S(2)}, u32[]{:S(2)}) collective-permute-start(bf16[2,128,128]{2,1,0:T(8,128)(2,1)S(1)} %get-tuple-element.61), channel_id=1, source_target_pairs={{0,24},{4,28},{8,16},{12,20},{16,8},{20,12},{24,0},{28,4},{1,25},{... | collective-permute-start | bytes 196616 | tf_op jit(solution)/shard_map/ppermute | solution.py:64
  29.7 5.8 %copy-start.5 = (bf16[512,2,512]{2,1,0:T(2,128)(2,1)S(1)}, bf16[512,2,512]{2,1,0:T(2,128)(2,1)}, u32[]{:S(2)}) copy-start(bf16[512,2,512]{2,1,0:T(2,128)(2,1)} %param.21) | copy-start | bytes 3145732
  29.7 6.1 %copy-start.6 = (f32[2304]{0:T(1024)S(1)}, f32[2304]{0:T(1024)}, u32[]{:S(2)}) copy-start(f32[2304]{0:T(1024)} %param.17) | copy-start | bytes 27652
  29.7 16.0 %copy-start.1 = (bf16[2304,512]{1,0:T(8,128)(2,1)S(1)}, bf16[2304,512]{1,0:T(8,128)(2,1)}, u32[]{:S(2)}) copy-start(bf16[2304,512]{1,0:T(8,128)(2,1)} %refs_1_.4) | copy-start | bytes 7077892
  29.7 16.0 %copy-start.4 = (f32[512]{0:T(512)S(1)}, f32[512]{0:T(512)}, u32[]{:S(2)}) copy-start(f32[512]{0:T(512)} %param.19) | copy-start | bytes 6148
  31.0 6.8 %collective-permute-start.10 = (bf16[32,2304]{1,0:T(8,128)(2,1)S(1)}, bf16[32,2304]{1,0:T(8,128)(2,1)S(1)}, u32[]{:S(2)}, u32[]{:S(2)}) collective-permute-start(bf16[32,2304]{1,0:T(8,128)(2,1)S(1)} %get-tuple-element.63), channel_id=1, source_target_pairs={{0,1},{1,0},{2,3},{3,2},{4,5},{5,4},{6,7},{7,6},{8,9},{9,8},{10,11... | collective-permute-start | bytes 442376 | tf_op jit(solution)/shard_map/ppermute | solution.py:64
  32.9 12.8 %collective-permute-start.11 = (bf16[32,2304]{1,0:T(8,128)(2,1)S(1)}, bf16[32,2304]{1,0:T(8,128)(2,1)S(1)}, u32[]{:S(2)}, u32[]{:S(2)}) collective-permute-start(bf16[32,2304]{1,0:T(8,128)(2,1)S(1)} %get-tuple-element.64), channel_id=1, source_target_pairs={{0,2},{1,3},{2,0},{3,1},{4,6},{5,7},{6,4},{7,5},{8,10},{9,11},{10,... | collective-permute-start | bytes 442376 | tf_op jit(solution)/shard_map/ppermute | solution.py:64
  35.5 10.2 %collective-permute-start.12 = (bf16[32,2304]{1,0:T(8,128)(2,1)S(1)}, bf16[32,2304]{1,0:T(8,128)(2,1)S(1)}, u32[]{:S(2)}, u32[]{:S(2)}) collective-permute-start(bf16[32,2304]{1,0:T(8,128)(2,1)S(1)} %get-tuple-element.65), channel_id=1, source_target_pairs={{0,3},{1,2},{2,1},{3,0},{4,7},{5,6},{6,5},{7,4},{8,11},{9,10},{10,... | collective-permute-start | bytes 442376 | tf_op jit(solution)/shard_map/ppermute | solution.py:64
  46.5 19.2 %copy-start.2 = (bf16[2304,512]{1,0:T(8,128)(2,1)S(1)}, bf16[2304,512]{1,0:T(8,128)(2,1)}, u32[]{:S(2)}) copy-start(bf16[2304,512]{1,0:T(8,128)(2,1)} %refs_1_.5) | copy-start | bytes 7077892
  46.5 10.2 %collective-permute-start.13 = (bf16[32,2816]{1,0:T(8,128)(2,1)S(1)}, bf16[32,2816]{1,0:T(8,128)(2,1)S(1)}, u32[]{:S(2)}, u32[]{:S(2)}) collective-permute-start(bf16[32,2816]{1,0:T(8,128)(2,1)S(1)} %get-tuple-element.72), channel_id=1, source_target_pairs={{0,1},{1,0},{2,3},{3,2},{4,5},{5,4},{6,7},{7,6},{8,9},{9,8},{10,11... | collective-permute-start | bytes 540680 | tf_op jit(solution)/shard_map/ppermute | solution.py:64
  48.7 5.9 %collective-permute-start.16 = (bf16[32,512]{1,0:T(8,128)(2,1)S(1)}, bf16[32,512]{1,0:T(8,128)(2,1)S(1)}, u32[]{:S(2)}, u32[]{:S(2)}) collective-permute-start(bf16[32,512]{1,0:T(8,128)(2,1)S(1)} %get-tuple-element.73.refs_0_), channel_id=1, source_target_pairs={{0,2},{1,3},{2,0},{3,1},{4,6},{5,7},{6,4},{7,5},{8,10},{9,11},{10,... | collective-permute-start | bytes 98312 | tf_op jit(solution)/shard_map/ppermute | solution.py:64
  49.8 6.9 %collective-permute-start.17 = (bf16[32,512]{1,0:T(8,128)(2,1)S(1)}, bf16[32,512]{1,0:T(8,128)(2,1)S(1)}, u32[]{:S(2)}, u32[]{:S(2)}) collective-permute-start(bf16[32,512]{1,0:T(8,128)(2,1)S(1)} %get-tuple-element.73.refs_0_), channel_id=1, source_target_pairs={{0,3},{1,2},{2,1},{3,0},{4,7},{5,6},{6,5},{7,4},{8,11},{9,10},{10,... | collective-permute-start | bytes 98312 | tf_op jit(solution)/shard_map/ppermute | solution.py:64
  51.2 9.1 %collective-permute-start.14 = (bf16[32,2304]{1,0:T(8,128)(2,1)S(1)}, bf16[32,2304]{1,0:T(8,128)(2,1)S(1)}, u32[]{:S(2)}, u32[]{:S(2)}) collective-permute-start(bf16[32,2304]{1,0:T(8,128)(2,1)S(1)} %get-tuple-element.71.refs_3_), channel_id=1, source_target_pairs={{0,2},{1,3},{2,0},{3,1},{4,6},{5,7},{6,4},{7,5},{8,10},{9,11},{10,... | collective-permute-start | bytes 442376 | tf_op jit(solution)/shard_map/ppermute | solution.py:64
  56.7 6.0 %collective-permute-start.18 = (bf16[128,512]{1,0:T(8,128)(2,1)S(1)}, bf16[128,512]{1,0:T(8,128)(2,1)S(1)}, u32[]{:S(2)}, u32[]{:S(2)}) collective-permute-start(bf16[128,512]{1,0:T(8,128)(2,1)S(1)} %shard_map.131.refs_7_), channel_id=1, source_target_pairs={{0,24},{4,28},{8,16},{12,20},{16,8},{20,12},{24,0},{28,4},{1,25},{... | collective-permute-start | bytes 393224 | tf_op jit(solution)/shard_map/ppermute | solution.py:64
  58.2 5.9 %collective-permute-start.19 = (bf16[128,512]{1,0:T(8,128)(2,1)S(1)}, bf16[128,512]{1,0:T(8,128)(2,1)S(1)}, u32[]{:S(2)}, u32[]{:S(2)}) collective-permute-start(bf16[128,512]{1,0:T(8,128)(2,1)S(1)} %shard_map.131.refs_7_), channel_id=1, source_target_pairs={{0,16},{4,20},{8,24},{12,28},{16,0},{20,4},{24,8},{28,12},{1,17},{... | collective-permute-start | bytes 393224 | tf_op jit(solution)/shard_map/ppermute | solution.py:64
  59.0 5.1 %collective-permute-start.20 = (bf16[128,512]{1,0:T(8,128)(2,1)S(1)}, bf16[128,512]{1,0:T(8,128)(2,1)S(1)}, u32[]{:S(2)}, u32[]{:S(2)}) collective-permute-start(bf16[128,512]{1,0:T(8,128)(2,1)S(1)} %shard_map.131.refs_7_), channel_id=1, source_target_pairs={{0,8},{4,12},{8,0},{12,4},{16,24},{20,28},{24,16},{28,20},{1,9},{5... | collective-permute-start | bytes 393224 | tf_op jit(solution)/shard_map/ppermute | solution.py:64
  60.3 5.1 %collective-permute-start.15 = (bf16[32,2304]{1,0:T(8,128)(2,1)S(1)}, bf16[32,2304]{1,0:T(8,128)(2,1)S(1)}, u32[]{:S(2)}, u32[]{:S(2)}) collective-permute-start(bf16[32,2304]{1,0:T(8,128)(2,1)S(1)} %collective-permute-done.14.refs_5_), channel_id=1, source_target_pairs={{0,1},{1,0},{2,3},{3,2},{4,5},{5,4},{6,7},{7,6},{8,9},{9,8},{10,11... | collective-permute-start | bytes 442376 | tf_op jit(solution)/shard_map/ppermute | solution.py:64
  60.5 4.9 %collective-permute-start.21 = (bf16[128,512]{1,0:T(8,128)(2,1)S(1)}, bf16[128,512]{1,0:T(8,128)(2,1)S(1)}, u32[]{:S(2)}, u32[]{:S(2)}) collective-permute-start(bf16[128,512]{1,0:T(8,128)(2,1)S(1)} %shard_map.131.refs_7_), channel_id=1, source_target_pairs={{0,4},{4,0},{8,12},{12,8},{16,20},{20,16},{24,28},{28,24},{1,5},{5... | collective-permute-start | bytes 393224 | tf_op jit(solution)/shard_map/ppermute | solution.py:64
  62.8 2.7 %collective-permute-start.22 = (bf16[128,512]{1,0:T(8,128)(2,1)S(1)}, bf16[128,512]{1,0:T(8,128)(2,1)S(1)}, u32[]{:S(2)}, u32[]{:S(2)}) collective-permute-start(bf16[128,512]{1,0:T(8,128)(2,1)S(1)} %collective-permute-done.18.refs_8_), channel_id=1, source_target_pairs={{0,4},{4,0},{8,12},{12,8},{16,20},{20,16},{24,28},{28,24},{1,5},{5... | collective-permute-start | bytes 393224 | tf_op jit(solution)/shard_map/ppermute | solution.py:64
  64.1 1.4 %collective-permute-start.23 = (bf16[128,512]{1,0:T(8,128)(2,1)S(1)}, bf16[128,512]{1,0:T(8,128)(2,1)S(1)}, u32[]{:S(2)}, u32[]{:S(2)}) collective-permute-start(bf16[128,512]{1,0:T(8,128)(2,1)S(1)} %collective-permute-done.19.refs_9_), channel_id=1, source_target_pairs={{0,4},{4,0},{8,12},{12,8},{16,20},{20,16},{24,28},{28,24},{1,5},{5... | collective-permute-start | bytes 393224 | tf_op jit(solution)/shard_map/ppermute | solution.py:64
  64.1 1.5 %collective-permute-start.24 = (bf16[128,512]{1,0:T(8,128)(2,1)S(1)}, bf16[128,512]{1,0:T(8,128)(2,1)S(1)}, u32[]{:S(2)}, u32[]{:S(2)}) collective-permute-start(bf16[128,512]{1,0:T(8,128)(2,1)S(1)} %collective-permute-done.20.refs_10_), channel_id=1, source_target_pairs={{0,4},{4,0},{8,12},{12,8},{16,20},{20,16},{24,28},{28,24},{1,5},{5... | collective-permute-start | bytes 393224 | tf_op jit(solution)/shard_map/ppermute | solution.py:64

commit v9 on v8

--- a/solution.py
+++ b/solution.py
@@ -102,13 +102,17 @@
     return jnp.concatenate(heads, axis=1)
 
 
-def last_rows_kernel(stored_inputs, rows, sems):
+def last_rows_kernel(stored_inputs, packed, rows, sems):
     length, count = stored_inputs.shape[1], rows.shape[1]
     move = pltpu.make_async_copy(
         stored_inputs.at[:, length - count : length, :], rows, sems.at[0]
     )
     move.start()
     move.wait()
+    reach = CONV - 1
+    last = [rows[part].astype(f32)[count - reach :] for part in range(rows.shape[0])]
+    spare = jnp.zeros((packed.shape[0] - reach * len(last), packed.shape[1]), f32)
+    packed[...] = jnp.concatenate(last + [spare], axis=0).astype(bf16)
 
 
 def load_kernel(
@@ -139,9 +143,9 @@
 
 
 def first_rows(place, halo, inputs, taps, part, wide):
-    count = halo.shape[1]
-    before = halo[part, count - 8 :, :].astype(f32)
-    wide[:8, :] = jnp.where(place[2] == 0, 0.0, before)
+    count, reach = inputs.shape[1], CONV - 1
+    before = halo[...].astype(f32)[part * reach : (part + 1) * reach]
+    wide[8 - reach : 8, :] = jnp.where(place[2] == 0, 0.0, before)
     wide[8:, :] = inputs[part].astype(f32)
     return finished(convolved(wide, taps, part, count), part)
 
@@ -452,7 +456,14 @@
     ]
     edge_shape = (kda_inputs.shape[0], HALO, kda_inputs.shape[2])
     last_rows = call(
-        last_rows_kernel, [(edge_shape, bf16)], stored[:1], limit=8, stored=(0,), copies=1, cost=0.2
+        last_rows_kernel,
+        [(edge_shape[1:], bf16)],
+        stored[:1],
+        [(edge_shape, bf16)],
+        8,
+        stored=(0,),
+        copies=1,
+        cost=0.2,
     )[0]
     halo = passed_along(last_rows, "ctx", 1)
     done, head_rows, logs, taps = call(

time: 69.1 us -> 68.7 us (level)
  transfers between devices with their start and end apart: 25 -> 25, of which waited for: 15 -> 17; matrix products, arithmetic and copies ran while one was open for 0% -> 0% of each run, Pallas kernels for 9% -> 9%
where the time goes in v9:
time: 68.7 us; the launch traced here: 68.5 us
  waiting for transfers between devices  27.3 us (40%)
  starting transfers between devices  24 us (35%)
  Pallas kernels  16 us (23%)
  between operations  0.85 us (1%)
    ppermute x24, waiting for transfers between devices, trade(): return lax.ppermute(block, axis, route)  25.8 us
    ppermute x24, starting transfers between devices, trade(): return lax.ppermute(block, axis, route)  23.5 us
    pallas_call x11, Pallas kernels, call(): pl.pallas_call(kernel, out_shape=[jax.ShapeDtypeStruct(shape, dtype) for...  16 us
    ppermute x1, waiting for transfers between devices, passed_along(): lax.ppermute(block, axis, [(i, (i + distance) % count) for i in range(cou...  1.5 us
  transfers between devices with their start and end apart: 25, of which 17 were waited for; matrix products, arithmetic and copies ran while one was open for 0% of the time, Pallas kernels for 9%

profile of v9, /device:TPU:0, one launch (start us, length us, event | category | flops | bytes accessed | tf_op | source)
XLA Modules:
  0.0 68.5 jit_solution(4050441671114738961)
XLA Ops:
  0.6 0.9 %shard_map.123 = bf16[16,1024]{1,0:T(8,128)(2,1)S(1)} custom-call(bf16[3,128,1024]{2,1,0:T(8,128)(2,1)} %stored_inputs.3), custom_call_target="tpu_custom_call" | custom-call | flops 200000000 | tf_op jit(solution)/shard_map/pallas_call | solution.py:44
  1.6 0.5 collective-permute-start
  2.1 3.0 %shard_map.122 = (bf16[3,128,1024]{2,1,0:T(8,128)(2,1)S(1)}, bf16[3,16,1024]{2,1,0:T(8,128)(2,1)S(1)}, f32[128,1024]{1,0:T(8,128)S(1)}, f32[3,4,1024]{2,1,0:T(4,128)S(1)}) custom-call(bf16[3,128,1024]{2,1,0:T(8,128)(2,1)} %stored_inputs.3, f32[128,1024]{1,0:T(8,128)} %stored_gate.1, f32[3,4,1024]{2,1,0:T(4,128)} %stored_taps.1), custom_call_target="tpu_custom_call" | custom-call | flops 2000000000 | tf_op jit(solution)/shard_map/pallas_call | solution.py:44
  5.0 1.5 %collective-permute-done.halo = bf16[16,1024]{1,0:T(8,128)(2,1)S(1)} collective-permute-done((bf16[16,1024]{1,0:T(8,128)(2,1)S(1)}, bf16[16,1024]{1,0:T(8,128)(2,1)S(1)}, u32[]{:S(2)}, u32[]{:S(2)}) %collective-permute-start) | collective-permute-done | bytes 32800 | tf_op jit(solution)/shard_map/ppermute | solution.py:69
  6.6 3.3 %shard_map.124 = (bf16[4,272,128]{2,1,0:T(8,128)(2,1)S(1)}, bf16[4,272,128]{2,1,0:T(8,128)(2,1)S(1)}, bf16[8,128,256]{2,1,0:T(8,128)(2,1)S(1)}, bf16[8,2,128,128]{3,2,1,0:T(8,128)(2,1)S(1)}) custom-call(bf16[3,128,1024]{2,1,0:T(8,128)(2,1)S(1)} %get-tuple-element.38.done, bf16[3,16,1024]{2,1,0:T(8,128)(2,1)S(1)} %get-tuple-element.39.head_rows, ...), custom_call_target="tpu_custom_call" | custom-call | flops 5000000000 | tf_op jit(solution)/shard_map/pallas_call | solution.py:44
  9.8 1.2 %collective-permute-start.1 = (bf16[4,272,128]{2,1,0:T(8,128)(2,1)S(1)}, bf16[4,272,128]{2,1,0:T(8,128)(2,1)S(1)}, u32[]{:S(2)}, u32[]{:S(2)}) collective-permute-start(bf16[4,272,128]{2,1,0:T(8,128)(2,1)S(1)} %get-tuple-element.43), channel_id=1, source_target_pairs={{0,4},{4,0},{8,12},{12,8},{16,20},{20,16},{24,28},{28,24},{1,5},{5... | collective-permute-start | bytes 835592 | tf_op jit(solution)/shard_map/ppermute | solution.py:64
  11.0 0.1 collective-permute-start.5
  11.1 1.1 %collective-permute-done.1.got.refs_2_ = bf16[4,272,128]{2,1,0:T(8,128)(2,1)S(1)} collective-permute-done((bf16[4,272,128]{2,1,0:T(8,128)(2,1)S(1)}, bf16[4,272,128]{2,1,0:T(8,128)(2,1)S(1)}, u32[]{:S(2)}, u32[]{:S(2)}) %collective-permute-start.1) | collective-permute-done | bytes 278560 | tf_op jit(solution)/shard_map/ppermute | solution.py:64
  12.2 0.3 shard_map.125
  12.5 1.6 %collective-permute-start.2 = (bf16[272,128]{1,0:T(8,128)(2,1)S(1)}, bf16[272,128]{1,0:T(8,128)(2,1)S(1)}, u32[]{:S(2)}, u32[]{:S(2)}) collective-permute-start(bf16[272,128]{1,0:T(8,128)(2,1)S(1)} %get-tuple-element.45), channel_id=1, source_target_pairs={{0,8},{4,12},{8,0},{12,4},{16,24},{20,28},{24,16},{28,20},{1,9},{5... | collective-permute-start | bytes 208904 | tf_op jit(solution)/shard_map/ppermute | solution.py:64
  14.1 0.6 collective-permute-start.3
  14.7 1.4 %collective-permute-start.4 = (bf16[272,128]{1,0:T(8,128)(2,1)S(1)}, bf16[272,128]{1,0:T(8,128)(2,1)S(1)}, u32[]{:S(2)}, u32[]{:S(2)}) collective-permute-start(bf16[272,128]{1,0:T(8,128)(2,1)S(1)} %get-tuple-element.47), channel_id=1, source_target_pairs={{0,24},{4,28},{8,16},{12,20},{16,8},{20,12},{24,0},{28,4},{1,25},{... | collective-permute-start | bytes 208904 | tf_op jit(solution)/shard_map/ppermute | solution.py:64
  16.1 2.8 %shard_map.126 = (bf16[128,1024]{1,0:T(8,128)(2,1)S(1)}, f32[128,1024]{1,0:T(8,128)S(1)}) custom-call(bf16[3,128,1024]{2,1,0:T(8,128)(2,1)S(1)} %get-tuple-element.38.done, bf16[3,16,1024]{2,1,0:T(8,128)(2,1)S(1)} %get-tuple-element.39.head_rows, bf16[16,1024]{1,0:T(8,128)(2,1)S(1)} %collective-permute-done.halo, f32[128,1024]{1,0:T(8,128)S(1)} %get-tuple-element.40.logs, ...), custom_call_target="tpu_custom_call" | custom-call | flops 2500000000 | tf_op jit(solution)/shard_map/pallas_call | solution.py:44
  18.9 0.2 collective-permute-done.3.refs_2_
  19.1 0.8 %collective-permute-done.4.refs_3_ = bf16[272,128]{1,0:T(8,128)(2,1)S(1)} collective-permute-done((bf16[272,128]{1,0:T(8,128)(2,1)S(1)}, bf16[272,128]{1,0:T(8,128)(2,1)S(1)}, u32[]{:S(2)}, u32[]{:S(2)}) %collective-permute-start.4) | collective-permute-done | bytes 69664 | tf_op jit(solution)/shard_map/ppermute | solution.py:64
  20.0 1.5 %collective-permute-done.6.refs_1_ = bf16[4,272,128]{2,1,0:T(8,128)(2,1)S(1)} collective-permute-done((bf16[4,272,128]{2,1,0:T(8,128)(2,1)S(1)}, bf16[4,272,128]{2,1,0:T(8,128)(2,1)S(1)}, u32[]{:S(2)}, u32[]{:S(2)}) %collective-permute-start.6) | collective-permute-done | bytes 278560 | tf_op jit(solution)/shard_map/ppermute | solution.py:64
  21.6 0.3 shard_map.128
  21.9 1.5 %collective-permute-start.7 = (bf16[2,128,128]{2,1,0:T(8,128)(2,1)S(1)}, bf16[2,128,128]{2,1,0:T(8,128)(2,1)S(1)}, u32[]{:S(2)}, u32[]{:S(2)}) collective-permute-start(bf16[2,128,128]{2,1,0:T(8,128)(2,1)S(1)} %get-tuple-element.59), channel_id=1, source_target_pairs={{0,8},{4,12},{8,0},{12,4},{16,24},{20,28},{24,16},{28,20},{1,9},{5... | collective-permute-start | bytes 196616 | tf_op jit(solution)/shard_map/ppermute | solution.py:64
  23.4 0.6 collective-permute-start.8
  24.0 1.4 %collective-permute-start.9 = (bf16[2,128,128]{2,1,0:T(8,128)(2,1)S(1)}, bf16[2,128,128]{2,1,0:T(8,128)(2,1)S(1)}, u32[]{:S(2)}, u32[]{:S(2)}) collective-permute-start(bf16[2,128,128]{2,1,0:T(8,128)(2,1)S(1)} %get-tuple-element.61), channel_id=1, source_target_pairs={{0,24},{4,28},{8,16},{12,20},{16,8},{20,12},{24,0},{28,4},{1,25},{... | collective-permute-start | bytes 196616 | tf_op jit(solution)/shard_map/ppermute | solution.py:64
  25.4 0.8 %collective-permute-done.7.refs_5_ = bf16[2,128,128]{2,1,0:T(8,128)(2,1)S(1)} collective-permute-done((bf16[2,128,128]{2,1,0:T(8,128)(2,1)S(1)}, bf16[2,128,128]{2,1,0:T(8,128)(2,1)S(1)}, u32[]{:S(2)}, u32[]{:S(2)}) %collective-permute-start.7) | collective-permute-done | bytes 65568 | tf_op jit(solution)/shard_map/ppermute | solution.py:64
  26.2 2.2 %collective-permute-done.8.refs_6_ = bf16[2,128,128]{2,1,0:T(8,128)(2,1)S(1)} collective-permute-done((bf16[2,128,128]{2,1,0:T(8,128)(2,1)S(1)}, bf16[2,128,128]{2,1,0:T(8,128)(2,1)S(1)}, u32[]{:S(2)}, u32[]{:S(2)}) %collective-permute-start.8) | collective-permute-done | bytes 65568 | tf_op jit(solution)/shard_map/ppermute | solution.py:64
  28.4 0.8 %collective-permute-done.9.refs_7_ = bf16[2,128,128]{2,1,0:T(8,128)(2,1)S(1)} collective-permute-done((bf16[2,128,128]{2,1,0:T(8,128)(2,1)S(1)}, bf16[2,128,128]{2,1,0:T(8,128)(2,1)S(1)}, u32[]{:S(2)}, u32[]{:S(2)}) %collective-permute-start.9) | collective-permute-done | bytes 65568 | tf_op jit(solution)/shard_map/ppermute | solution.py:64
  29.2 1.3 %shard_map.129 = (f32[32,2304]{1,0:T(8,128)S(1)}, bf16[32,2304]{1,0:T(8,128)(2,1)S(1)}, bf16[32,2304]{1,0:T(8,128)(2,1)S(1)}, bf16[32,2304]{1,0:T(8,128)(2,1)S(1)}) custom-call(bf16[128,2304]{1,0:T(8,128)(2,1)S(1)} %copy-done, bf16[1024,2304]{1,0:T(8,128)(2,1)S(1)} %bitcast.5, bf16[128,1024]{1,0:T(8,128)(2,1)S(1)} %get-tuple-element.52.refs_2_, ...), custom_call_target="tpu_custom_call" | custom-call | flops 1000000000 | tf_op jit(solution)/shard_map/pallas_call | solution.py:44
  30.5 1.6 %collective-permute-start.10 = (bf16[32,2304]{1,0:T(8,128)(2,1)S(1)}, bf16[32,2304]{1,0:T(8,128)(2,1)S(1)}, u32[]{:S(2)}, u32[]{:S(2)}) collective-permute-start(bf16[32,2304]{1,0:T(8,128)(2,1)S(1)} %get-tuple-element.63), channel_id=1, source_target_pairs={{0,1},{1,0},{2,3},{3,2},{4,5},{5,4},{6,7},{7,6},{8,9},{9,8},{10,11... | collective-permute-start | bytes 442376 | tf_op jit(solution)/shard_map/ppermute | solution.py:64
  32.2 2.6 %collective-permute-start.11 = (bf16[32,2304]{1,0:T(8,128)(2,1)S(1)}, bf16[32,2304]{1,0:T(8,128)(2,1)S(1)}, u32[]{:S(2)}, u32[]{:S(2)}) collective-permute-start(bf16[32,2304]{1,0:T(8,128)(2,1)S(1)} %get-tuple-element.64), channel_id=1, source_target_pairs={{0,2},{1,3},{2,0},{3,1},{4,6},{5,7},{6,4},{7,5},{8,10},{9,11},{10,... | collective-permute-start | bytes 442376 | tf_op jit(solution)/shard_map/ppermute | solution.py:64
  34.8 0.2 collective-permute-start.12
  35.0 0.2 copy.13
  35.3 1.9 %collective-permute-done.10.refs_4_ = bf16[32,2304]{1,0:T(8,128)(2,1)S(1)} collective-permute-done((bf16[32,2304]{1,0:T(8,128)(2,1)S(1)}, bf16[32,2304]{1,0:T(8,128)(2,1)S(1)}, u32[]{:S(2)}, u32[]{:S(2)}) %collective-permute-start.10) | collective-permute-done | bytes 147488 | tf_op jit(solution)/shard_map/ppermute | solution.py:64
  37.2 7.8 %collective-permute-done.11.refs_5_ = bf16[32,2304]{1,0:T(8,128)(2,1)S(1)} collective-permute-done((bf16[32,2304]{1,0:T(8,128)(2,1)S(1)}, bf16[32,2304]{1,0:T(8,128)(2,1)S(1)}, u32[]{:S(2)}, u32[]{:S(2)}) %collective-permute-start.11) | collective-permute-done | bytes 147488 | tf_op jit(solution)/shard_map/ppermute | solution.py:64
  45.0 0.8 %shard_map.130 = (bf16[32,2304]{1,0:T(8,128)(2,1)S(1)}, bf16[32,512]{1,0:T(8,128)(2,1)S(1)}, bf16[32,2816]{1,0:T(8,128)(2,1)S(1)}) custom-call(f32[1,2304]{1,0:T(1,128)S(1)} %broadcast_in_dim.7.refs_0_, bf16[2304,512]{1,0:T(8,128)(2,1)S(1)} %copy-done.1, f32[1,512]{1,0:T(1,128)S(1)} %bitcast.9, f32[32,2304]{1,0:T(8,128)S(1)} %get-tuple-element.67.refs_3_, ...), custom_call_target="tpu_custom_call" | custom-call | flops 1000000000 | tf_op jit(solution)/shard_map/pallas_call | solution.py:44
  45.8 2.2 %collective-permute-start.13 = (bf16[32,2816]{1,0:T(8,128)(2,1)S(1)}, bf16[32,2816]{1,0:T(8,128)(2,1)S(1)}, u32[]{:S(2)}, u32[]{:S(2)}) collective-permute-start(bf16[32,2816]{1,0:T(8,128)(2,1)S(1)} %get-tuple-element.72), channel_id=1, source_target_pairs={{0,1},{1,0},{2,3},{3,2},{4,5},{5,4},{6,7},{7,6},{8,9},{9,8},{10,11... | collective-permute-start | bytes 540680 | tf_op jit(solution)/shard_map/ppermute | solution.py:64
  48.0 1.1 %collective-permute-start.16 = (bf16[32,512]{1,0:T(8,128)(2,1)S(1)}, bf16[32,512]{1,0:T(8,128)(2,1)S(1)}, u32[]{:S(2)}, u32[]{:S(2)}) collective-permute-start(bf16[32,512]{1,0:T(8,128)(2,1)S(1)} %get-tuple-element.73.refs_0_), channel_id=1, source_target_pairs={{0,2},{1,3},{2,0},{3,1},{4,6},{5,7},{6,4},{7,5},{8,10},{9,11},{10,... | collective-permute-start | bytes 98312 | tf_op jit(solution)/shard_map/ppermute | solution.py:64
  49.1 1.4 %collective-permute-start.17 = (bf16[32,512]{1,0:T(8,128)(2,1)S(1)}, bf16[32,512]{1,0:T(8,128)(2,1)S(1)}, u32[]{:S(2)}, u32[]{:S(2)}) collective-permute-start(bf16[32,512]{1,0:T(8,128)(2,1)S(1)} %get-tuple-element.73.refs_0_), channel_id=1, source_target_pairs={{0,3},{1,2},{2,1},{3,0},{4,7},{5,6},{6,5},{7,4},{8,11},{9,10},{10,... | collective-permute-start | bytes 98312 | tf_op jit(solution)/shard_map/ppermute | solution.py:64
  50.5 2.0 %collective-permute-start.14 = (bf16[32,2304]{1,0:T(8,128)(2,1)S(1)}, bf16[32,2304]{1,0:T(8,128)(2,1)S(1)}, u32[]{:S(2)}, u32[]{:S(2)}) collective-permute-start(bf16[32,2304]{1,0:T(8,128)(2,1)S(1)} %get-tuple-element.71.refs_3_), channel_id=1, source_target_pairs={{0,2},{1,3},{2,0},{3,1},{4,6},{5,7},{6,4},{7,5},{8,10},{9,11},{10,... | collective-permute-start | bytes 442376 | tf_op jit(solution)/shard_map/ppermute | solution.py:64
  52.5 1.3 %collective-permute-done.16.refs_2_ = bf16[32,512]{1,0:T(8,128)(2,1)S(1)} collective-permute-done((bf16[32,512]{1,0:T(8,128)(2,1)S(1)}, bf16[32,512]{1,0:T(8,128)(2,1)S(1)}, u32[]{:S(2)}, u32[]{:S(2)}) %collective-permute-start.16) | collective-permute-done | bytes 32800 | tf_op jit(solution)/shard_map/ppermute | solution.py:64
  53.8 2.2 %collective-permute-done.17.refs_3_ = bf16[32,512]{1,0:T(8,128)(2,1)S(1)} collective-permute-done((bf16[32,512]{1,0:T(8,128)(2,1)S(1)}, bf16[32,512]{1,0:T(8,128)(2,1)S(1)}, u32[]{:S(2)}, u32[]{:S(2)}) %collective-permute-start.17) | collective-permute-done | bytes 32800 | tf_op jit(solution)/shard_map/ppermute | solution.py:64
  56.0 1.5 %collective-permute-start.18 = (bf16[128,512]{1,0:T(8,128)(2,1)S(1)}, bf16[128,512]{1,0:T(8,128)(2,1)S(1)}, u32[]{:S(2)}, u32[]{:S(2)}) collective-permute-start(bf16[128,512]{1,0:T(8,128)(2,1)S(1)} %shard_map.131.refs_7_), channel_id=1, source_target_pairs={{0,24},{4,28},{8,16},{12,20},{16,8},{20,12},{24,0},{28,4},{1,25},{... | collective-permute-start | bytes 393224 | tf_op jit(solution)/shard_map/ppermute | solution.py:64
  57.6 1.3 %collective-permute-start.19 = (bf16[128,512]{1,0:T(8,128)(2,1)S(1)}, bf16[128,512]{1,0:T(8,128)(2,1)S(1)}, u32[]{:S(2)}, u32[]{:S(2)}) collective-permute-start(bf16[128,512]{1,0:T(8,128)(2,1)S(1)} %shard_map.131.refs_7_), channel_id=1, source_target_pairs={{0,16},{4,20},{8,24},{12,28},{16,0},{20,4},{24,8},{28,12},{1,17},{... | collective-permute-start | bytes 393224 | tf_op jit(solution)/shard_map/ppermute | solution.py:64
  58.8 0.8 %collective-permute-start.20 = (bf16[128,512]{1,0:T(8,128)(2,1)S(1)}, bf16[128,512]{1,0:T(8,128)(2,1)S(1)}, u32[]{:S(2)}, u32[]{:S(2)}) collective-permute-start(bf16[128,512]{1,0:T(8,128)(2,1)S(1)} %shard_map.131.refs_7_), channel_id=1, source_target_pairs={{0,8},{4,12},{8,0},{12,4},{16,24},{20,28},{24,16},{28,20},{1,9},{5... | collective-permute-start | bytes 393224 | tf_op jit(solution)/shard_map/ppermute | solution.py:64
  59.6 0.2 collective-permute-start.15
  59.8 2.2 %collective-permute-done.18.refs_8_ = bf16[128,512]{1,0:T(8,128)(2,1)S(1)} collective-permute-done((bf16[128,512]{1,0:T(8,128)(2,1)S(1)}, bf16[128,512]{1,0:T(8,128)(2,1)S(1)}, u32[]{:S(2)}, u32[]{:S(2)}) %collective-permute-start.18) | collective-permute-done | bytes 131104 | tf_op jit(solution)/shard_map/ppermute | solution.py:64
  62.1 1.3 %collective-permute-done.19.refs_9_ = bf16[128,512]{1,0:T(8,128)(2,1)S(1)} collective-permute-done((bf16[128,512]{1,0:T(8,128)(2,1)S(1)}, bf16[128,512]{1,0:T(8,128)(2,1)S(1)}, u32[]{:S(2)}, u32[]{:S(2)}) %collective-permute-start.19) | collective-permute-done | bytes 131104 | tf_op jit(solution)/shard_map/ppermute | solution.py:64
  63.4 0.4 collective-permute-done.20.refs_10_
  63.8 0.1 collective-permute-start.24
  63.9 0.9 %collective-permute-done.15.refs_6_ = bf16[32,2304]{1,0:T(8,128)(2,1)S(1)} collective-permute-done((bf16[32,2304]{1,0:T(8,128)(2,1)S(1)}, bf16[32,2304]{1,0:T(8,128)(2,1)S(1)}, u32[]{:S(2)}, u32[]{:S(2)}) %collective-permute-start.15) | collective-permute-done | bytes 147488 | tf_op jit(solution)/shard_map/ppermute | solution.py:64
  64.8 0.4 collective-permute-done.24.refs_14_
  65.2 3.3 %shard_map.132 = (bf16[128,2304]{1,0:T(8,128)(2,1)}, bf16[128,512]{1,0:T(8,128)(2,1)}) custom-call(f32[1,2304]{1,0:T(1,128)S(1)} %broadcast_in_dim.7.refs_0_, bf16[2304,512]{1,0:T(8,128)(2,1)S(1)} %copy-done.2, bf16[512,1024]{1,0:T(8,128)(2,1)S(1)} %bitcast.6, bf16[32,2304]{1,0:T(8,128)(2,1)S(1)} %get-tuple-element.71.refs_3_, ...), custom_call_target="tpu_custom_call" | custom-call | flops 4000000000 | tf_op jit(solution)/shard_map/pallas_call | solution.py:44
  (34 shorter events, 0.2 us)
Async XLA Ops:
  1.6 5.0 %copy-start.3 = (f32[128,8]{0,1:T(8,128)S(1)}, f32[128,8]{0,1:T(8,128)}, u32[]{:S(2)}) copy-start(f32[128,8]{0,1:T(8,128)} %param.13) | copy-start | bytes 12292
  1.6 5.0 %collective-permute-start = (bf16[16,1024]{1,0:T(8,128)(2,1)S(1)}, bf16[16,1024]{1,0:T(8,128)(2,1)S(1)}, u32[]{:S(2)}, u32[]{:S(2)}) collective-permute-start(bf16[16,1024]{1,0:T(8,128)(2,1)S(1)} %shard_map.123), channel_id=1, source_target_pairs={{0,4},{4,8},{8,12},{12,16},{16,20},{20,24},{24,28},{28,0},{1,5},{5... | collective-permute-start | bytes 98312 | tf_op jit(solution)/shard_map/ppermute | solution.py:69
  9.8 2.4 %collective-permute-start.1 = (bf16[4,272,128]{2,1,0:T(8,128)(2,1)S(1)}, bf16[4,272,128]{2,1,0:T(8,128)(2,1)S(1)}, u32[]{:S(2)}, u32[]{:S(2)}) collective-permute-start(bf16[4,272,128]{2,1,0:T(8,128)(2,1)S(1)} %get-tuple-element.43), channel_id=1, source_target_pairs={{0,4},{4,0},{8,12},{12,8},{16,20},{20,16},{24,28},{28,24},{1,5},{5... | collective-permute-start | bytes 835592 | tf_op jit(solution)/shard_map/ppermute | solution.py:64
  11.0 5.1 %collective-permute-start.5 = (bf16[4,272,128]{2,1,0:T(8,128)(2,1)S(1)}, bf16[4,272,128]{2,1,0:T(8,128)(2,1)S(1)}, u32[]{:S(2)}, u32[]{:S(2)}) collective-permute-start(bf16[4,272,128]{2,1,0:T(8,128)(2,1)S(1)} %get-tuple-element.42.kept), channel_id=1, source_target_pairs={{0,4},{4,0},{8,12},{12,8},{16,20},{20,16},{24,28},{28,24},{1,5},{5... | collective-permute-start | bytes 835592 | tf_op jit(solution)/shard_map/ppermute | solution.py:64
  12.5 6.4 %collective-permute-start.2 = (bf16[272,128]{1,0:T(8,128)(2,1)S(1)}, bf16[272,128]{1,0:T(8,128)(2,1)S(1)}, u32[]{:S(2)}, u32[]{:S(2)}) collective-permute-start(bf16[272,128]{1,0:T(8,128)(2,1)S(1)} %get-tuple-element.45), channel_id=1, source_target_pairs={{0,8},{4,12},{8,0},{12,4},{16,24},{20,28},{24,16},{28,20},{1,9},{5... | collective-permute-start | bytes 208904 | tf_op jit(solution)/shard_map/ppermute | solution.py:64
  14.1 5.1 %collective-permute-start.3 = (bf16[272,128]{1,0:T(8,128)(2,1)S(1)}, bf16[272,128]{1,0:T(8,128)(2,1)S(1)}, u32[]{:S(2)}, u32[]{:S(2)}) collective-permute-start(bf16[272,128]{1,0:T(8,128)(2,1)S(1)} %get-tuple-element.46), channel_id=1, source_target_pairs={{0,16},{4,20},{8,24},{12,28},{16,0},{20,4},{24,8},{28,12},{1,17},{... | collective-permute-start | bytes 208904 | tf_op jit(solution)/shard_map/ppermute | solution.py:64
  14.7 5.2 %collective-permute-start.4 = (bf16[272,128]{1,0:T(8,128)(2,1)S(1)}, bf16[272,128]{1,0:T(8,128)(2,1)S(1)}, u32[]{:S(2)}, u32[]{:S(2)}) collective-permute-start(bf16[272,128]{1,0:T(8,128)(2,1)S(1)} %get-tuple-element.47), channel_id=1, source_target_pairs={{0,24},{4,28},{8,16},{12,20},{16,8},{20,12},{24,0},{28,4},{1,25},{... | collective-permute-start | bytes 208904 | tf_op jit(solution)/shard_map/ppermute | solution.py:64
  16.1 13.1 %slice-start = ((s8[4718592]{0:T(1024)(128)(4,1)}), s8[4194304]{0:T(1024)(128)(4,1)S(1)}, s32[]{:S(2)}) async-start(s8[4718592]{0:T(1024)(128)(4,1)} %bitcast.4), calls=%async_computation | async-start | bytes 8388608
  16.1 13.1 %slice-start.1 = ((s8[4718592]{0:T(1024)(128)(4,1)}), s8[524288]{0:T(1024)(128)(4,1)S(1)}, s32[]{:S(2)}) async-start(s8[4718592]{0:T(1024)(128)(4,1)} %bitcast.4), calls=%async_computation.1 | async-start | bytes 1048576
  18.9 10.3 %copy-start = (bf16[128,2304]{1,0:T(8,128)(2,1)S(1)}, bf16[128,2304]{1,0:T(8,128)(2,1)}, u32[]{:S(2)}) copy-start(bf16[128,2304]{1,0:T(8,128)(2,1)} %refs_0_.1) | copy-start | bytes 1769476
  19.9 1.6 %collective-permute-start.6 = (bf16[4,272,128]{2,1,0:T(8,128)(2,1)S(1)}, bf16[4,272,128]{2,1,0:T(8,128)(2,1)S(1)}, u32[]{:S(2)}, u32[]{:S(2)}) collective-permute-start(bf16[4,272,128]{2,1,0:T(8,128)(2,1)S(1)} %shard_map.127.refs_0_), channel_id=1, source_target_pairs={{0,4},{4,0},{8,12},{12,8},{16,20},{20,16},{24,28},{28,24},{1,5},{5... | collective-permute-start | bytes 835592 | tf_op jit(solution)/shard_map/ppermute | solution.py:64
  21.9 4.3 %collective-permute-start.7 = (bf16[2,128,128]{2,1,0:T(8,128)(2,1)S(1)}, bf16[2,128,128]{2,1,0:T(8,128)(2,1)S(1)}, u32[]{:S(2)}, u32[]{:S(2)}) collective-permute-start(bf16[2,128,128]{2,1,0:T(8,128)(2,1)S(1)} %get-tuple-element.59), channel_id=1, source_target_pairs={{0,8},{4,12},{8,0},{12,4},{16,24},{20,28},{24,16},{28,20},{1,9},{5... | collective-permute-start | bytes 196616 | tf_op jit(solution)/shard_map/ppermute | solution.py:64
  23.4 5.0 %collective-permute-start.8 = (bf16[2,128,128]{2,1,0:T(8,128)(2,1)S(1)}, bf16[2,128,128]{2,1,0:T(8,128)(2,1)S(1)}, u32[]{:S(2)}, u32[]{:S(2)}) collective-permute-start(bf16[2,128,128]{2,1,0:T(8,128)(2,1)S(1)} %get-tuple-element.60), channel_id=1, source_target_pairs={{0,16},{4,20},{8,24},{12,28},{16,0},{20,4},{24,8},{28,12},{1,17},{... | collective-permute-start | bytes 196616 | tf_op jit(solution)/shard_map/ppermute | solution.py:64
  24.0 5.2 %collective-permute-start.9 = (bf16[2,128,128]{2,1,0:T(8,128)(2,1)S(1)}, bf16[2,128,128]{2,1,0:T(8,128)(2,1)S(1)}, u32[]{:S(2)}, u32[]{:S(2)}) collective-permute-start(bf16[2,128,128]{2,1,0:T(8,128)(2,1)S(1)} %get-tuple-element.61), channel_id=1, source_target_pairs={{0,24},{4,28},{8,16},{12,20},{16,8},{20,12},{24,0},{28,4},{1,25},{... | collective-permute-start | bytes 196616 | tf_op jit(solution)/shard_map/ppermute | solution.py:64
  29.2 5.8 %copy-start.5 = (bf16[512,2,512]{2,1,0:T(2,128)(2,1)S(1)}, bf16[512,2,512]{2,1,0:T(2,128)(2,1)}, u32[]{:S(2)}) copy-start(bf16[512,2,512]{2,1,0:T(2,128)(2,1)} %param.21) | copy-start | bytes 3145732
  29.2 6.1 %copy-start.6 = (f32[2304]{0:T(1024)S(1)}, f32[2304]{0:T(1024)}, u32[]{:S(2)}) copy-start(f32[2304]{0:T(1024)} %param.17) | copy-start | bytes 27652
  29.2 15.8 %copy-start.1 = (bf16[2304,512]{1,0:T(8,128)(2,1)S(1)}, bf16[2304,512]{1,0:T(8,128)(2,1)}, u32[]{:S(2)}) copy-start(bf16[2304,512]{1,0:T(8,128)(2,1)} %refs_1_.4) | copy-start | bytes 7077892
  29.2 15.8 %copy-start.4 = (f32[512]{0:T(512)S(1)}, f32[512]{0:T(512)}, u32[]{:S(2)}) copy-start(f32[512]{0:T(512)} %param.19) | copy-start | bytes 6148
  30.5 6.6 %collective-permute-start.10 = (bf16[32,2304]{1,0:T(8,128)(2,1)S(1)}, bf16[32,2304]{1,0:T(8,128)(2,1)S(1)}, u32[]{:S(2)}, u32[]{:S(2)}) collective-permute-start(bf16[32,2304]{1,0:T(8,128)(2,1)S(1)} %get-tuple-element.63), channel_id=1, source_target_pairs={{0,1},{1,0},{2,3},{3,2},{4,5},{5,4},{6,7},{7,6},{8,9},{9,8},{10,11... | collective-permute-start | bytes 442376 | tf_op jit(solution)/shard_map/ppermute | solution.py:64
  32.2 12.8 %collective-permute-start.11 = (bf16[32,2304]{1,0:T(8,128)(2,1)S(1)}, bf16[32,2304]{1,0:T(8,128)(2,1)S(1)}, u32[]{:S(2)}, u32[]{:S(2)}) collective-permute-start(bf16[32,2304]{1,0:T(8,128)(2,1)S(1)} %get-tuple-element.64), channel_id=1, source_target_pairs={{0,2},{1,3},{2,0},{3,1},{4,6},{5,7},{6,4},{7,5},{8,10},{9,11},{10,... | collective-permute-start | bytes 442376 | tf_op jit(solution)/shard_map/ppermute | solution.py:64
  34.8 10.2 %collective-permute-start.12 = (bf16[32,2304]{1,0:T(8,128)(2,1)S(1)}, bf16[32,2304]{1,0:T(8,128)(2,1)S(1)}, u32[]{:S(2)}, u32[]{:S(2)}) collective-permute-start(bf16[32,2304]{1,0:T(8,128)(2,1)S(1)} %get-tuple-element.65), channel_id=1, source_target_pairs={{0,3},{1,2},{2,1},{3,0},{4,7},{5,6},{6,5},{7,4},{8,11},{9,10},{10,... | collective-permute-start | bytes 442376 | tf_op jit(solution)/shard_map/ppermute | solution.py:64
  45.8 19.4 %copy-start.2 = (bf16[2304,512]{1,0:T(8,128)(2,1)S(1)}, bf16[2304,512]{1,0:T(8,128)(2,1)}, u32[]{:S(2)}) copy-start(bf16[2304,512]{1,0:T(8,128)(2,1)} %refs_1_.5) | copy-start | bytes 7077892
  45.8 10.2 %collective-permute-start.13 = (bf16[32,2816]{1,0:T(8,128)(2,1)S(1)}, bf16[32,2816]{1,0:T(8,128)(2,1)S(1)}, u32[]{:S(2)}, u32[]{:S(2)}) collective-permute-start(bf16[32,2816]{1,0:T(8,128)(2,1)S(1)} %get-tuple-element.72), channel_id=1, source_target_pairs={{0,1},{1,0},{2,3},{3,2},{4,5},{5,4},{6,7},{7,6},{8,9},{9,8},{10,11... | collective-permute-start | bytes 540680 | tf_op jit(solution)/shard_map/ppermute | solution.py:64
  48.0 5.9 %collective-permute-start.16 = (bf16[32,512]{1,0:T(8,128)(2,1)S(1)}, bf16[32,512]{1,0:T(8,128)(2,1)S(1)}, u32[]{:S(2)}, u32[]{:S(2)}) collective-permute-start(bf16[32,512]{1,0:T(8,128)(2,1)S(1)} %get-tuple-element.73.refs_0_), channel_id=1, source_target_pairs={{0,2},{1,3},{2,0},{3,1},{4,6},{5,7},{6,4},{7,5},{8,10},{9,11},{10,... | collective-permute-start | bytes 98312 | tf_op jit(solution)/shard_map/ppermute | solution.py:64
  49.1 6.9 %collective-permute-start.17 = (bf16[32,512]{1,0:T(8,128)(2,1)S(1)}, bf16[32,512]{1,0:T(8,128)(2,1)S(1)}, u32[]{:S(2)}, u32[]{:S(2)}) collective-permute-start(bf16[32,512]{1,0:T(8,128)(2,1)S(1)} %get-tuple-element.73.refs_0_), channel_id=1, source_target_pairs={{0,3},{1,2},{2,1},{3,0},{4,7},{5,6},{6,5},{7,4},{8,11},{9,10},{10,... | collective-permute-start | bytes 98312 | tf_op jit(solution)/shard_map/ppermute | solution.py:64
  50.5 9.1 %collective-permute-start.14 = (bf16[32,2304]{1,0:T(8,128)(2,1)S(1)}, bf16[32,2304]{1,0:T(8,128)(2,1)S(1)}, u32[]{:S(2)}, u32[]{:S(2)}) collective-permute-start(bf16[32,2304]{1,0:T(8,128)(2,1)S(1)} %get-tuple-element.71.refs_3_), channel_id=1, source_target_pairs={{0,2},{1,3},{2,0},{3,1},{4,6},{5,7},{6,4},{7,5},{8,10},{9,11},{10,... | collective-permute-start | bytes 442376 | tf_op jit(solution)/shard_map/ppermute | solution.py:64
  56.0 6.0 %collective-permute-start.18 = (bf16[128,512]{1,0:T(8,128)(2,1)S(1)}, bf16[128,512]{1,0:T(8,128)(2,1)S(1)}, u32[]{:S(2)}, u32[]{:S(2)}) collective-permute-start(bf16[128,512]{1,0:T(8,128)(2,1)S(1)} %shard_map.131.refs_7_), channel_id=1, source_target_pairs={{0,24},{4,28},{8,16},{12,20},{16,8},{20,12},{24,0},{28,4},{1,25},{... | collective-permute-start | bytes 393224 | tf_op jit(solution)/shard_map/ppermute | solution.py:64
  57.6 5.8 %collective-permute-start.19 = (bf16[128,512]{1,0:T(8,128)(2,1)S(1)}, bf16[128,512]{1,0:T(8,128)(2,1)S(1)}, u32[]{:S(2)}, u32[]{:S(2)}) collective-permute-start(bf16[128,512]{1,0:T(8,128)(2,1)S(1)} %shard_map.131.refs_7_), channel_id=1, source_target_pairs={{0,16},{4,20},{8,24},{12,28},{16,0},{20,4},{24,8},{28,12},{1,17},{... | collective-permute-start | bytes 393224 | tf_op jit(solution)/shard_map/ppermute | solution.py:64
  58.8 5.0 %collective-permute-start.20 = (bf16[128,512]{1,0:T(8,128)(2,1)S(1)}, bf16[128,512]{1,0:T(8,128)(2,1)S(1)}, u32[]{:S(2)}, u32[]{:S(2)}) collective-permute-start(bf16[128,512]{1,0:T(8,128)(2,1)S(1)} %shard_map.131.refs_7_), channel_id=1, source_target_pairs={{0,8},{4,12},{8,0},{12,4},{16,24},{20,28},{24,16},{28,20},{1,9},{5... | collective-permute-start | bytes 393224 | tf_op jit(solution)/shard_map/ppermute | solution.py:64
  59.6 5.1 %collective-permute-start.15 = (bf16[32,2304]{1,0:T(8,128)(2,1)S(1)}, bf16[32,2304]{1,0:T(8,128)(2,1)S(1)}, u32[]{:S(2)}, u32[]{:S(2)}) collective-permute-start(bf16[32,2304]{1,0:T(8,128)(2,1)S(1)} %collective-permute-done.14.refs_5_), channel_id=1, source_target_pairs={{0,1},{1,0},{2,3},{3,2},{4,5},{5,4},{6,7},{7,6},{8,9},{9,8},{10,11... | collective-permute-start | bytes 442376 | tf_op jit(solution)/shard_map/ppermute | solution.py:64
  59.8 4.9 %collective-permute-start.21 = (bf16[128,512]{1,0:T(8,128)(2,1)S(1)}, bf16[128,512]{1,0:T(8,128)(2,1)S(1)}, u32[]{:S(2)}, u32[]{:S(2)}) collective-permute-start(bf16[128,512]{1,0:T(8,128)(2,1)S(1)} %shard_map.131.refs_7_), channel_id=1, source_target_pairs={{0,4},{4,0},{8,12},{12,8},{16,20},{20,16},{24,28},{28,24},{1,5},{5... | collective-permute-start | bytes 393224 | tf_op jit(solution)/shard_map/ppermute | solution.py:64
  62.1 2.7 %collective-permute-start.22 = (bf16[128,512]{1,0:T(8,128)(2,1)S(1)}, bf16[128,512]{1,0:T(8,128)(2,1)S(1)}, u32[]{:S(2)}, u32[]{:S(2)}) collective-permute-start(bf16[128,512]{1,0:T(8,128)(2,1)S(1)} %collective-permute-done.18.refs_8_), channel_id=1, source_target_pairs={{0,4},{4,0},{8,12},{12,8},{16,20},{20,16},{24,28},{28,24},{1,5},{5... | collective-permute-start | bytes 393224 | tf_op jit(solution)/shard_map/ppermute | solution.py:64
  63.4 1.4 %collective-permute-start.23 = (bf16[128,512]{1,0:T(8,128)(2,1)S(1)}, bf16[128,512]{1,0:T(8,128)(2,1)S(1)}, u32[]{:S(2)}, u32[]{:S(2)}) collective-permute-start(bf16[128,512]{1,0:T(8,128)(2,1)S(1)} %collective-permute-done.19.refs_9_), channel_id=1, source_target_pairs={{0,4},{4,0},{8,12},{12,8},{16,20},{20,16},{24,28},{28,24},{1,5},{5... | collective-permute-start | bytes 393224 | tf_op jit(solution)/shard_map/ppermute | solution.py:64
  63.8 1.3 %collective-permute-start.24 = (bf16[128,512]{1,0:T(8,128)(2,1)S(1)}, bf16[128,512]{1,0:T(8,128)(2,1)S(1)}, u32[]{:S(2)}, u32[]{:S(2)}) collective-permute-start(bf16[128,512]{1,0:T(8,128)(2,1)S(1)} %collective-permute-done.20.refs_10_), channel_id=1, source_target_pairs={{0,4},{4,0},{8,12},{12,8},{16,20},{20,16},{24,28},{28,24},{1,5},{5... | collective-permute-start | bytes 393224 | tf_op jit(solution)/shard_map/ppermute | solution.py:64

commit v10 on v9

--- a/solution.py
+++ b/solution.py
@@ -403,8 +403,10 @@
         absorbed[head * length : (head + 1) * length, :] = (
             mm_nt(query[:, own], up[:, own]) * DH ** (-0.5)
         ).astype(bf16)
-    scores[...] = mm_nt(absorbed[...], latents[...])
-    group = min(length, 32)
+    span = min(2, heads) * length
+    for first in range(0, heads * length, span):
+        scores[first : first + span, :] = mm_nt(absorbed[first : first + span, :], latents[...])
+    group = min(length, 16)
     for first in range(0, heads * length, group):
         own = slice(first, first + group)
         rows = lax.broadcasted_iota(jnp.int32, (group, length), 0) + first % length

time: 68.7 us -> 68.6 us (level)
  no operation moved by 1% of the time
where the time goes in v10:
time: 68.6 us; the launch traced here: 68.4 us
  waiting for transfers between devices  27.3 us (40%)
  starting transfers between devices  24 us (35%)
  Pallas kernels  15.9 us (23%)
  between operations  0.85 us (1%)
    ppermute x24, waiting for transfers between devices, trade(): return lax.ppermute(block, axis, route)  25.8 us
    ppermute x24, starting transfers between devices, trade(): return lax.ppermute(block, axis, route)  23.5 us
    pallas_call x11, Pallas kernels, call(): pl.pallas_call(kernel, out_shape=[jax.ShapeDtypeStruct(shape, dtype) for...  15.9 us
    ppermute x1, waiting for transfers between devices, passed_along(): lax.ppermute(block, axis, [(i, (i + distance) % count) for i in range(cou...  1.5 us
  transfers between devices with their start and end apart: 25, of which 17 were waited for; matrix products, arithmetic and copies ran while one was open for 0% of the time, Pallas kernels for 9%

profile of v10, /device:TPU:0, one launch (start us, length us, event | category | flops | bytes accessed | tf_op | source)
XLA Modules:
  0.0 68.4 jit_solution(1170949325029264541)
XLA Ops:
  0.6 0.9 %shard_map.123 = bf16[16,1024]{1,0:T(8,128)(2,1)S(1)} custom-call(bf16[3,128,1024]{2,1,0:T(8,128)(2,1)} %stored_inputs.3), custom_call_target="tpu_custom_call" | custom-call | flops 200000000 | tf_op jit(solution)/shard_map/pallas_call | solution.py:44
  1.6 0.5 collective-permute-start
  2.1 3.0 %shard_map.122 = (bf16[3,128,1024]{2,1,0:T(8,128)(2,1)S(1)}, bf16[3,16,1024]{2,1,0:T(8,128)(2,1)S(1)}, f32[128,1024]{1,0:T(8,128)S(1)}, f32[3,4,1024]{2,1,0:T(4,128)S(1)}) custom-call(bf16[3,128,1024]{2,1,0:T(8,128)(2,1)} %stored_inputs.3, f32[128,1024]{1,0:T(8,128)} %stored_gate.1, f32[3,4,1024]{2,1,0:T(4,128)} %stored_taps.1), custom_call_target="tpu_custom_call" | custom-call | flops 2000000000 | tf_op jit(solution)/shard_map/pallas_call | solution.py:44
  5.0 1.5 %collective-permute-done.halo = bf16[16,1024]{1,0:T(8,128)(2,1)S(1)} collective-permute-done((bf16[16,1024]{1,0:T(8,128)(2,1)S(1)}, bf16[16,1024]{1,0:T(8,128)(2,1)S(1)}, u32[]{:S(2)}, u32[]{:S(2)}) %collective-permute-start) | collective-permute-done | bytes 32800 | tf_op jit(solution)/shard_map/ppermute | solution.py:69
  6.6 3.3 %shard_map.124 = (bf16[4,272,128]{2,1,0:T(8,128)(2,1)S(1)}, bf16[4,272,128]{2,1,0:T(8,128)(2,1)S(1)}, bf16[8,128,256]{2,1,0:T(8,128)(2,1)S(1)}, bf16[8,2,128,128]{3,2,1,0:T(8,128)(2,1)S(1)}) custom-call(bf16[3,128,1024]{2,1,0:T(8,128)(2,1)S(1)} %get-tuple-element.38.done, bf16[3,16,1024]{2,1,0:T(8,128)(2,1)S(1)} %get-tuple-element.39.head_rows, ...), custom_call_target="tpu_custom_call" | custom-call | flops 5000000000 | tf_op jit(solution)/shard_map/pallas_call | solution.py:44
  9.8 1.2 %collective-permute-start.1 = (bf16[4,272,128]{2,1,0:T(8,128)(2,1)S(1)}, bf16[4,272,128]{2,1,0:T(8,128)(2,1)S(1)}, u32[]{:S(2)}, u32[]{:S(2)}) collective-permute-start(bf16[4,272,128]{2,1,0:T(8,128)(2,1)S(1)} %get-tuple-element.43), channel_id=1, source_target_pairs={{0,4},{4,0},{8,12},{12,8},{16,20},{20,16},{24,28},{28,24},{1,5},{5... | collective-permute-start | bytes 835592 | tf_op jit(solution)/shard_map/ppermute | solution.py:64
  11.0 0.1 collective-permute-start.5
  11.1 1.1 %collective-permute-done.1.got.refs_2_ = bf16[4,272,128]{2,1,0:T(8,128)(2,1)S(1)} collective-permute-done((bf16[4,272,128]{2,1,0:T(8,128)(2,1)S(1)}, bf16[4,272,128]{2,1,0:T(8,128)(2,1)S(1)}, u32[]{:S(2)}, u32[]{:S(2)}) %collective-permute-start.1) | collective-permute-done | bytes 278560 | tf_op jit(solution)/shard_map/ppermute | solution.py:64
  12.2 0.3 shard_map.125
  12.5 1.6 %collective-permute-start.2 = (bf16[272,128]{1,0:T(8,128)(2,1)S(1)}, bf16[272,128]{1,0:T(8,128)(2,1)S(1)}, u32[]{:S(2)}, u32[]{:S(2)}) collective-permute-start(bf16[272,128]{1,0:T(8,128)(2,1)S(1)} %get-tuple-element.45), channel_id=1, source_target_pairs={{0,8},{4,12},{8,0},{12,4},{16,24},{20,28},{24,16},{28,20},{1,9},{5... | collective-permute-start | bytes 208904 | tf_op jit(solution)/shard_map/ppermute | solution.py:64
  14.1 0.6 collective-permute-start.3
  14.7 1.4 %collective-permute-start.4 = (bf16[272,128]{1,0:T(8,128)(2,1)S(1)}, bf16[272,128]{1,0:T(8,128)(2,1)S(1)}, u32[]{:S(2)}, u32[]{:S(2)}) collective-permute-start(bf16[272,128]{1,0:T(8,128)(2,1)S(1)} %get-tuple-element.47), channel_id=1, source_target_pairs={{0,24},{4,28},{8,16},{12,20},{16,8},{20,12},{24,0},{28,4},{1,25},{... | collective-permute-start | bytes 208904 | tf_op jit(solution)/shard_map/ppermute | solution.py:64
  16.1 2.8 %shard_map.126 = (bf16[128,1024]{1,0:T(8,128)(2,1)S(1)}, f32[128,1024]{1,0:T(8,128)S(1)}) custom-call(bf16[3,128,1024]{2,1,0:T(8,128)(2,1)S(1)} %get-tuple-element.38.done, bf16[3,16,1024]{2,1,0:T(8,128)(2,1)S(1)} %get-tuple-element.39.head_rows, bf16[16,1024]{1,0:T(8,128)(2,1)S(1)} %collective-permute-done.halo, f32[128,1024]{1,0:T(8,128)S(1)} %get-tuple-element.40.logs, ...), custom_call_target="tpu_custom_call" | custom-call | flops 2500000000 | tf_op jit(solution)/shard_map/pallas_call | solution.py:44
  18.9 0.2 collective-permute-done.3.refs_2_
  19.1 0.8 %collective-permute-done.4.refs_3_ = bf16[272,128]{1,0:T(8,128)(2,1)S(1)} collective-permute-done((bf16[272,128]{1,0:T(8,128)(2,1)S(1)}, bf16[272,128]{1,0:T(8,128)(2,1)S(1)}, u32[]{:S(2)}, u32[]{:S(2)}) %collective-permute-start.4) | collective-permute-done | bytes 69664 | tf_op jit(solution)/shard_map/ppermute | solution.py:64
  20.0 1.5 %collective-permute-done.6.refs_1_ = bf16[4,272,128]{2,1,0:T(8,128)(2,1)S(1)} collective-permute-done((bf16[4,272,128]{2,1,0:T(8,128)(2,1)S(1)}, bf16[4,272,128]{2,1,0:T(8,128)(2,1)S(1)}, u32[]{:S(2)}, u32[]{:S(2)}) %collective-permute-start.6) | collective-permute-done | bytes 278560 | tf_op jit(solution)/shard_map/ppermute | solution.py:64
  21.6 0.3 shard_map.128
  21.9 1.5 %collective-permute-start.7 = (bf16[2,128,128]{2,1,0:T(8,128)(2,1)S(1)}, bf16[2,128,128]{2,1,0:T(8,128)(2,1)S(1)}, u32[]{:S(2)}, u32[]{:S(2)}) collective-permute-start(bf16[2,128,128]{2,1,0:T(8,128)(2,1)S(1)} %get-tuple-element.59), channel_id=1, source_target_pairs={{0,8},{4,12},{8,0},{12,4},{16,24},{20,28},{24,16},{28,20},{1,9},{5... | collective-permute-start | bytes 196616 | tf_op jit(solution)/shard_map/ppermute | solution.py:64
  23.4 0.6 collective-permute-start.8
  24.0 1.4 %collective-permute-start.9 = (bf16[2,128,128]{2,1,0:T(8,128)(2,1)S(1)}, bf16[2,128,128]{2,1,0:T(8,128)(2,1)S(1)}, u32[]{:S(2)}, u32[]{:S(2)}) collective-permute-start(bf16[2,128,128]{2,1,0:T(8,128)(2,1)S(1)} %get-tuple-element.61), channel_id=1, source_target_pairs={{0,24},{4,28},{8,16},{12,20},{16,8},{20,12},{24,0},{28,4},{1,25},{... | collective-permute-start | bytes 196616 | tf_op jit(solution)/shard_map/ppermute | solution.py:64
  25.4 0.8 %collective-permute-done.7.refs_5_ = bf16[2,128,128]{2,1,0:T(8,128)(2,1)S(1)} collective-permute-done((bf16[2,128,128]{2,1,0:T(8,128)(2,1)S(1)}, bf16[2,128,128]{2,1,0:T(8,128)(2,1)S(1)}, u32[]{:S(2)}, u32[]{:S(2)}) %collective-permute-start.7) | collective-permute-done | bytes 65568 | tf_op jit(solution)/shard_map/ppermute | solution.py:64
  26.2 2.2 %collective-permute-done.8.refs_6_ = bf16[2,128,128]{2,1,0:T(8,128)(2,1)S(1)} collective-permute-done((bf16[2,128,128]{2,1,0:T(8,128)(2,1)S(1)}, bf16[2,128,128]{2,1,0:T(8,128)(2,1)S(1)}, u32[]{:S(2)}, u32[]{:S(2)}) %collective-permute-start.8) | collective-permute-done | bytes 65568 | tf_op jit(solution)/shard_map/ppermute | solution.py:64
  28.4 0.8 %collective-permute-done.9.refs_7_ = bf16[2,128,128]{2,1,0:T(8,128)(2,1)S(1)} collective-permute-done((bf16[2,128,128]{2,1,0:T(8,128)(2,1)S(1)}, bf16[2,128,128]{2,1,0:T(8,128)(2,1)S(1)}, u32[]{:S(2)}, u32[]{:S(2)}) %collective-permute-start.9) | collective-permute-done | bytes 65568 | tf_op jit(solution)/shard_map/ppermute | solution.py:64
  29.2 1.3 %shard_map.129 = (f32[32,2304]{1,0:T(8,128)S(1)}, bf16[32,2304]{1,0:T(8,128)(2,1)S(1)}, bf16[32,2304]{1,0:T(8,128)(2,1)S(1)}, bf16[32,2304]{1,0:T(8,128)(2,1)S(1)}) custom-call(bf16[128,2304]{1,0:T(8,128)(2,1)S(1)} %copy-done, bf16[1024,2304]{1,0:T(8,128)(2,1)S(1)} %bitcast.5, bf16[128,1024]{1,0:T(8,128)(2,1)S(1)} %get-tuple-element.52.refs_2_, ...), custom_call_target="tpu_custom_call" | custom-call | flops 1000000000 | tf_op jit(solution)/shard_map/pallas_call | solution.py:44
  30.5 1.6 %collective-permute-start.10 = (bf16[32,2304]{1,0:T(8,128)(2,1)S(1)}, bf16[32,2304]{1,0:T(8,128)(2,1)S(1)}, u32[]{:S(2)}, u32[]{:S(2)}) collective-permute-start(bf16[32,2304]{1,0:T(8,128)(2,1)S(1)} %get-tuple-element.63), channel_id=1, source_target_pairs={{0,1},{1,0},{2,3},{3,2},{4,5},{5,4},{6,7},{7,6},{8,9},{9,8},{10,11... | collective-permute-start | bytes 442376 | tf_op jit(solution)/shard_map/ppermute | solution.py:64
  32.2 2.6 %collective-permute-start.11 = (bf16[32,2304]{1,0:T(8,128)(2,1)S(1)}, bf16[32,2304]{1,0:T(8,128)(2,1)S(1)}, u32[]{:S(2)}, u32[]{:S(2)}) collective-permute-start(bf16[32,2304]{1,0:T(8,128)(2,1)S(1)} %get-tuple-element.64), channel_id=1, source_target_pairs={{0,2},{1,3},{2,0},{3,1},{4,6},{5,7},{6,4},{7,5},{8,10},{9,11},{10,... | collective-permute-start | bytes 442376 | tf_op jit(solution)/shard_map/ppermute | solution.py:64
  34.8 0.2 collective-permute-start.12
  35.0 0.2 copy.13
  35.3 1.9 %collective-permute-done.10.refs_4_ = bf16[32,2304]{1,0:T(8,128)(2,1)S(1)} collective-permute-done((bf16[32,2304]{1,0:T(8,128)(2,1)S(1)}, bf16[32,2304]{1,0:T(8,128)(2,1)S(1)}, u32[]{:S(2)}, u32[]{:S(2)}) %collective-permute-start.10) | collective-permute-done | bytes 147488 | tf_op jit(solution)/shard_map/ppermute | solution.py:64
  37.2 7.8 %collective-permute-done.11.refs_5_ = bf16[32,2304]{1,0:T(8,128)(2,1)S(1)} collective-permute-done((bf16[32,2304]{1,0:T(8,128)(2,1)S(1)}, bf16[32,2304]{1,0:T(8,128)(2,1)S(1)}, u32[]{:S(2)}, u32[]{:S(2)}) %collective-permute-start.11) | collective-permute-done | bytes 147488 | tf_op jit(solution)/shard_map/ppermute | solution.py:64
  45.0 0.8 %shard_map.130 = (bf16[32,2304]{1,0:T(8,128)(2,1)S(1)}, bf16[32,512]{1,0:T(8,128)(2,1)S(1)}, bf16[32,2816]{1,0:T(8,128)(2,1)S(1)}) custom-call(f32[1,2304]{1,0:T(1,128)S(1)} %broadcast_in_dim.7.refs_0_, bf16[2304,512]{1,0:T(8,128)(2,1)S(1)} %copy-done.1, f32[1,512]{1,0:T(1,128)S(1)} %bitcast.9, f32[32,2304]{1,0:T(8,128)S(1)} %get-tuple-element.67.refs_3_, ...), custom_call_target="tpu_custom_call" | custom-call | flops 1000000000 | tf_op jit(solution)/shard_map/pallas_call | solution.py:44
  45.8 2.2 %collective-permute-start.13 = (bf16[32,2816]{1,0:T(8,128)(2,1)S(1)}, bf16[32,2816]{1,0:T(8,128)(2,1)S(1)}, u32[]{:S(2)}, u32[]{:S(2)}) collective-permute-start(bf16[32,2816]{1,0:T(8,128)(2,1)S(1)} %get-tuple-element.72), channel_id=1, source_target_pairs={{0,1},{1,0},{2,3},{3,2},{4,5},{5,4},{6,7},{7,6},{8,9},{9,8},{10,11... | collective-permute-start | bytes 540680 | tf_op jit(solution)/shard_map/ppermute | solution.py:64
  48.0 1.1 %collective-permute-start.16 = (bf16[32,512]{1,0:T(8,128)(2,1)S(1)}, bf16[32,512]{1,0:T(8,128)(2,1)S(1)}, u32[]{:S(2)}, u32[]{:S(2)}) collective-permute-start(bf16[32,512]{1,0:T(8,128)(2,1)S(1)} %get-tuple-element.73.refs_0_), channel_id=1, source_target_pairs={{0,2},{1,3},{2,0},{3,1},{4,6},{5,7},{6,4},{7,5},{8,10},{9,11},{10,... | collective-permute-start | bytes 98312 | tf_op jit(solution)/shard_map/ppermute | solution.py:64
  49.1 1.4 %collective-permute-start.17 = (bf16[32,512]{1,0:T(8,128)(2,1)S(1)}, bf16[32,512]{1,0:T(8,128)(2,1)S(1)}, u32[]{:S(2)}, u32[]{:S(2)}) collective-permute-start(bf16[32,512]{1,0:T(8,128)(2,1)S(1)} %get-tuple-element.73.refs_0_), channel_id=1, source_target_pairs={{0,3},{1,2},{2,1},{3,0},{4,7},{5,6},{6,5},{7,4},{8,11},{9,10},{10,... | collective-permute-start | bytes 98312 | tf_op jit(solution)/shard_map/ppermute | solution.py:64
  50.5 2.0 %collective-permute-start.14 = (bf16[32,2304]{1,0:T(8,128)(2,1)S(1)}, bf16[32,2304]{1,0:T(8,128)(2,1)S(1)}, u32[]{:S(2)}, u32[]{:S(2)}) collective-permute-start(bf16[32,2304]{1,0:T(8,128)(2,1)S(1)} %get-tuple-element.71.refs_3_), channel_id=1, source_target_pairs={{0,2},{1,3},{2,0},{3,1},{4,6},{5,7},{6,4},{7,5},{8,10},{9,11},{10,... | collective-permute-start | bytes 442376 | tf_op jit(solution)/shard_map/ppermute | solution.py:64
  52.5 1.3 %collective-permute-done.16.refs_2_ = bf16[32,512]{1,0:T(8,128)(2,1)S(1)} collective-permute-done((bf16[32,512]{1,0:T(8,128)(2,1)S(1)}, bf16[32,512]{1,0:T(8,128)(2,1)S(1)}, u32[]{:S(2)}, u32[]{:S(2)}) %collective-permute-start.16) | collective-permute-done | bytes 32800 | tf_op jit(solution)/shard_map/ppermute | solution.py:64
  53.8 2.2 %collective-permute-done.17.refs_3_ = bf16[32,512]{1,0:T(8,128)(2,1)S(1)} collective-permute-done((bf16[32,512]{1,0:T(8,128)(2,1)S(1)}, bf16[32,512]{1,0:T(8,128)(2,1)S(1)}, u32[]{:S(2)}, u32[]{:S(2)}) %collective-permute-start.17) | collective-permute-done | bytes 32800 | tf_op jit(solution)/shard_map/ppermute | solution.py:64
  56.0 1.5 %collective-permute-start.18 = (bf16[128,512]{1,0:T(8,128)(2,1)S(1)}, bf16[128,512]{1,0:T(8,128)(2,1)S(1)}, u32[]{:S(2)}, u32[]{:S(2)}) collective-permute-start(bf16[128,512]{1,0:T(8,128)(2,1)S(1)} %shard_map.131.refs_7_), channel_id=1, source_target_pairs={{0,24},{4,28},{8,16},{12,20},{16,8},{20,12},{24,0},{28,4},{1,25},{... | collective-permute-start | bytes 393224 | tf_op jit(solution)/shard_map/ppermute | solution.py:64
  57.6 1.3 %collective-permute-start.19 = (bf16[128,512]{1,0:T(8,128)(2,1)S(1)}, bf16[128,512]{1,0:T(8,128)(2,1)S(1)}, u32[]{:S(2)}, u32[]{:S(2)}) collective-permute-start(bf16[128,512]{1,0:T(8,128)(2,1)S(1)} %shard_map.131.refs_7_), channel_id=1, source_target_pairs={{0,16},{4,20},{8,24},{12,28},{16,0},{20,4},{24,8},{28,12},{1,17},{... | collective-permute-start | bytes 393224 | tf_op jit(solution)/shard_map/ppermute | solution.py:64
  58.8 0.8 %collective-permute-start.20 = (bf16[128,512]{1,0:T(8,128)(2,1)S(1)}, bf16[128,512]{1,0:T(8,128)(2,1)S(1)}, u32[]{:S(2)}, u32[]{:S(2)}) collective-permute-start(bf16[128,512]{1,0:T(8,128)(2,1)S(1)} %shard_map.131.refs_7_), channel_id=1, source_target_pairs={{0,8},{4,12},{8,0},{12,4},{16,24},{20,28},{24,16},{28,20},{1,9},{5... | collective-permute-start | bytes 393224 | tf_op jit(solution)/shard_map/ppermute | solution.py:64
  59.6 0.2 collective-permute-start.15
  59.8 2.2 %collective-permute-done.18.refs_8_ = bf16[128,512]{1,0:T(8,128)(2,1)S(1)} collective-permute-done((bf16[128,512]{1,0:T(8,128)(2,1)S(1)}, bf16[128,512]{1,0:T(8,128)(2,1)S(1)}, u32[]{:S(2)}, u32[]{:S(2)}) %collective-permute-start.18) | collective-permute-done | bytes 131104 | tf_op jit(solution)/shard_map/ppermute | solution.py:64
  62.1 1.3 %collective-permute-done.19.refs_9_ = bf16[128,512]{1,0:T(8,128)(2,1)S(1)} collective-permute-done((bf16[128,512]{1,0:T(8,128)(2,1)S(1)}, bf16[128,512]{1,0:T(8,128)(2,1)S(1)}, u32[]{:S(2)}, u32[]{:S(2)}) %collective-permute-start.19) | collective-permute-done | bytes 131104 | tf_op jit(solution)/shard_map/ppermute | solution.py:64
  63.4 0.4 collective-permute-done.20.refs_10_
  63.8 0.1 collective-permute-start.24
  63.9 0.9 %collective-permute-done.15.refs_6_ = bf16[32,2304]{1,0:T(8,128)(2,1)S(1)} collective-permute-done((bf16[32,2304]{1,0:T(8,128)(2,1)S(1)}, bf16[32,2304]{1,0:T(8,128)(2,1)S(1)}, u32[]{:S(2)}, u32[]{:S(2)}) %collective-permute-start.15) | collective-permute-done | bytes 147488 | tf_op jit(solution)/shard_map/ppermute | solution.py:64
  64.8 0.4 collective-permute-done.24.refs_14_
  65.2 3.2 %shard_map.132 = (bf16[128,2304]{1,0:T(8,128)(2,1)}, bf16[128,512]{1,0:T(8,128)(2,1)}) custom-call(f32[1,2304]{1,0:T(1,128)S(1)} %broadcast_in_dim.7.refs_0_, bf16[2304,512]{1,0:T(8,128)(2,1)S(1)} %copy-done.2, bf16[512,1024]{1,0:T(8,128)(2,1)S(1)} %bitcast.6, bf16[32,2304]{1,0:T(8,128)(2,1)S(1)} %get-tuple-element.71.refs_3_, ...), custom_call_target="tpu_custom_call" | custom-call | flops 4000000000 | tf_op jit(solution)/shard_map/pallas_call | solution.py:44
  (34 shorter events, 0.2 us)
Async XLA Ops:
  1.6 5.0 %copy-start.3 = (f32[128,8]{0,1:T(8,128)S(1)}, f32[128,8]{0,1:T(8,128)}, u32[]{:S(2)}) copy-start(f32[128,8]{0,1:T(8,128)} %param.13) | copy-start | bytes 12292
  1.6 5.0 %collective-permute-start = (bf16[16,1024]{1,0:T(8,128)(2,1)S(1)}, bf16[16,1024]{1,0:T(8,128)(2,1)S(1)}, u32[]{:S(2)}, u32[]{:S(2)}) collective-permute-start(bf16[16,1024]{1,0:T(8,128)(2,1)S(1)} %shard_map.123), channel_id=1, source_target_pairs={{0,4},{4,8},{8,12},{12,16},{16,20},{20,24},{24,28},{28,0},{1,5},{5... | collective-permute-start | bytes 98312 | tf_op jit(solution)/shard_map/ppermute | solution.py:69
  9.8 2.4 %collective-permute-start.1 = (bf16[4,272,128]{2,1,0:T(8,128)(2,1)S(1)}, bf16[4,272,128]{2,1,0:T(8,128)(2,1)S(1)}, u32[]{:S(2)}, u32[]{:S(2)}) collective-permute-start(bf16[4,272,128]{2,1,0:T(8,128)(2,1)S(1)} %get-tuple-element.43), channel_id=1, source_target_pairs={{0,4},{4,0},{8,12},{12,8},{16,20},{20,16},{24,28},{28,24},{1,5},{5... | collective-permute-start | bytes 835592 | tf_op jit(solution)/shard_map/ppermute | solution.py:64
  11.0 5.1 %collective-permute-start.5 = (bf16[4,272,128]{2,1,0:T(8,128)(2,1)S(1)}, bf16[4,272,128]{2,1,0:T(8,128)(2,1)S(1)}, u32[]{:S(2)}, u32[]{:S(2)}) collective-permute-start(bf16[4,272,128]{2,1,0:T(8,128)(2,1)S(1)} %get-tuple-element.42.kept), channel_id=1, source_target_pairs={{0,4},{4,0},{8,12},{12,8},{16,20},{20,16},{24,28},{28,24},{1,5},{5... | collective-permute-start | bytes 835592 | tf_op jit(solution)/shard_map/ppermute | solution.py:64
  12.5 6.4 %collective-permute-start.2 = (bf16[272,128]{1,0:T(8,128)(2,1)S(1)}, bf16[272,128]{1,0:T(8,128)(2,1)S(1)}, u32[]{:S(2)}, u32[]{:S(2)}) collective-permute-start(bf16[272,128]{1,0:T(8,128)(2,1)S(1)} %get-tuple-element.45), channel_id=1, source_target_pairs={{0,8},{4,12},{8,0},{12,4},{16,24},{20,28},{24,16},{28,20},{1,9},{5... | collective-permute-start | bytes 208904 | tf_op jit(solution)/shard_map/ppermute | solution.py:64
  14.1 5.1 %collective-permute-start.3 = (bf16[272,128]{1,0:T(8,128)(2,1)S(1)}, bf16[272,128]{1,0:T(8,128)(2,1)S(1)}, u32[]{:S(2)}, u32[]{:S(2)}) collective-permute-start(bf16[272,128]{1,0:T(8,128)(2,1)S(1)} %get-tuple-element.46), channel_id=1, source_target_pairs={{0,16},{4,20},{8,24},{12,28},{16,0},{20,4},{24,8},{28,12},{1,17},{... | collective-permute-start | bytes 208904 | tf_op jit(solution)/shard_map/ppermute | solution.py:64
  14.7 5.2 %collective-permute-start.4 = (bf16[272,128]{1,0:T(8,128)(2,1)S(1)}, bf16[272,128]{1,0:T(8,128)(2,1)S(1)}, u32[]{:S(2)}, u32[]{:S(2)}) collective-permute-start(bf16[272,128]{1,0:T(8,128)(2,1)S(1)} %get-tuple-element.47), channel_id=1, source_target_pairs={{0,24},{4,28},{8,16},{12,20},{16,8},{20,12},{24,0},{28,4},{1,25},{... | collective-permute-start | bytes 208904 | tf_op jit(solution)/shard_map/ppermute | solution.py:64
  16.1 13.1 %slice-start = ((s8[4718592]{0:T(1024)(128)(4,1)}), s8[4194304]{0:T(1024)(128)(4,1)S(1)}, s32[]{:S(2)}) async-start(s8[4718592]{0:T(1024)(128)(4,1)} %bitcast.4), calls=%async_computation | async-start | bytes 8388608
  16.1 13.1 %slice-start.1 = ((s8[4718592]{0:T(1024)(128)(4,1)}), s8[524288]{0:T(1024)(128)(4,1)S(1)}, s32[]{:S(2)}) async-start(s8[4718592]{0:T(1024)(128)(4,1)} %bitcast.4), calls=%async_computation.1 | async-start | bytes 1048576
  18.9 10.3 %copy-start = (bf16[128,2304]{1,0:T(8,128)(2,1)S(1)}, bf16[128,2304]{1,0:T(8,128)(2,1)}, u32[]{:S(2)}) copy-start(bf16[128,2304]{1,0:T(8,128)(2,1)} %refs_0_.1) | copy-start | bytes 1769476
  19.9 1.6 %collective-permute-start.6 = (bf16[4,272,128]{2,1,0:T(8,128)(2,1)S(1)}, bf16[4,272,128]{2,1,0:T(8,128)(2,1)S(1)}, u32[]{:S(2)}, u32[]{:S(2)}) collective-permute-start(bf16[4,272,128]{2,1,0:T(8,128)(2,1)S(1)} %shard_map.127.refs_0_), channel_id=1, source_target_pairs={{0,4},{4,0},{8,12},{12,8},{16,20},{20,16},{24,28},{28,24},{1,5},{5... | collective-permute-start | bytes 835592 | tf_op jit(solution)/shard_map/ppermute | solution.py:64
  21.9 4.3 %collective-permute-start.7 = (bf16[2,128,128]{2,1,0:T(8,128)(2,1)S(1)}, bf16[2,128,128]{2,1,0:T(8,128)(2,1)S(1)}, u32[]{:S(2)}, u32[]{:S(2)}) collective-permute-start(bf16[2,128,128]{2,1,0:T(8,128)(2,1)S(1)} %get-tuple-element.59), channel_id=1, source_target_pairs={{0,8},{4,12},{8,0},{12,4},{16,24},{20,28},{24,16},{28,20},{1,9},{5... | collective-permute-start | bytes 196616 | tf_op jit(solution)/shard_map/ppermute | solution.py:64
  23.4 5.0 %collective-permute-start.8 = (bf16[2,128,128]{2,1,0:T(8,128)(2,1)S(1)}, bf16[2,128,128]{2,1,0:T(8,128)(2,1)S(1)}, u32[]{:S(2)}, u32[]{:S(2)}) collective-permute-start(bf16[2,128,128]{2,1,0:T(8,128)(2,1)S(1)} %get-tuple-element.60), channel_id=1, source_target_pairs={{0,16},{4,20},{8,24},{12,28},{16,0},{20,4},{24,8},{28,12},{1,17},{... | collective-permute-start | bytes 196616 | tf_op jit(solution)/shard_map/ppermute | solution.py:64
  24.0 5.2 %collective-permute-start.9 = (bf16[2,128,128]{2,1,0:T(8,128)(2,1)S(1)}, bf16[2,128,128]{2,1,0:T(8,128)(2,1)S(1)}, u32[]{:S(2)}, u32[]{:S(2)}) collective-permute-start(bf16[2,128,128]{2,1,0:T(8,128)(2,1)S(1)} %get-tuple-element.61), channel_id=1, source_target_pairs={{0,24},{4,28},{8,16},{12,20},{16,8},{20,12},{24,0},{28,4},{1,25},{... | collective-permute-start | bytes 196616 | tf_op jit(solution)/shard_map/ppermute | solution.py:64
  29.2 5.8 %copy-start.5 = (bf16[512,2,512]{2,1,0:T(2,128)(2,1)S(1)}, bf16[512,2,512]{2,1,0:T(2,128)(2,1)}, u32[]{:S(2)}) copy-start(bf16[512,2,512]{2,1,0:T(2,128)(2,1)} %param.21) | copy-start | bytes 3145732
  29.2 6.1 %copy-start.6 = (f32[2304]{0:T(1024)S(1)}, f32[2304]{0:T(1024)}, u32[]{:S(2)}) copy-start(f32[2304]{0:T(1024)} %param.17) | copy-start | bytes 27652
  29.2 15.8 %copy-start.1 = (bf16[2304,512]{1,0:T(8,128)(2,1)S(1)}, bf16[2304,512]{1,0:T(8,128)(2,1)}, u32[]{:S(2)}) copy-start(bf16[2304,512]{1,0:T(8,128)(2,1)} %refs_1_.4) | copy-start | bytes 7077892
  29.2 15.8 %copy-start.4 = (f32[512]{0:T(512)S(1)}, f32[512]{0:T(512)}, u32[]{:S(2)}) copy-start(f32[512]{0:T(512)} %param.19) | copy-start | bytes 6148
  30.5 6.6 %collective-permute-start.10 = (bf16[32,2304]{1,0:T(8,128)(2,1)S(1)}, bf16[32,2304]{1,0:T(8,128)(2,1)S(1)}, u32[]{:S(2)}, u32[]{:S(2)}) collective-permute-start(bf16[32,2304]{1,0:T(8,128)(2,1)S(1)} %get-tuple-element.63), channel_id=1, source_target_pairs={{0,1},{1,0},{2,3},{3,2},{4,5},{5,4},{6,7},{7,6},{8,9},{9,8},{10,11... | collective-permute-start | bytes 442376 | tf_op jit(solution)/shard_map/ppermute | solution.py:64
  32.2 12.8 %collective-permute-start.11 = (bf16[32,2304]{1,0:T(8,128)(2,1)S(1)}, bf16[32,2304]{1,0:T(8,128)(2,1)S(1)}, u32[]{:S(2)}, u32[]{:S(2)}) collective-permute-start(bf16[32,2304]{1,0:T(8,128)(2,1)S(1)} %get-tuple-element.64), channel_id=1, source_target_pairs={{0,2},{1,3},{2,0},{3,1},{4,6},{5,7},{6,4},{7,5},{8,10},{9,11},{10,... | collective-permute-start | bytes 442376 | tf_op jit(solution)/shard_map/ppermute | solution.py:64
  34.8 10.2 %collective-permute-start.12 = (bf16[32,2304]{1,0:T(8,128)(2,1)S(1)}, bf16[32,2304]{1,0:T(8,128)(2,1)S(1)}, u32[]{:S(2)}, u32[]{:S(2)}) collective-permute-start(bf16[32,2304]{1,0:T(8,128)(2,1)S(1)} %get-tuple-element.65), channel_id=1, source_target_pairs={{0,3},{1,2},{2,1},{3,0},{4,7},{5,6},{6,5},{7,4},{8,11},{9,10},{10,... | collective-permute-start | bytes 442376 | tf_op jit(solution)/shard_map/ppermute | solution.py:64
  45.8 19.4 %copy-start.2 = (bf16[2304,512]{1,0:T(8,128)(2,1)S(1)}, bf16[2304,512]{1,0:T(8,128)(2,1)}, u32[]{:S(2)}) copy-start(bf16[2304,512]{1,0:T(8,128)(2,1)} %refs_1_.5) | copy-start | bytes 7077892
  45.8 10.2 %collective-permute-start.13 = (bf16[32,2816]{1,0:T(8,128)(2,1)S(1)}, bf16[32,2816]{1,0:T(8,128)(2,1)S(1)}, u32[]{:S(2)}, u32[]{:S(2)}) collective-permute-start(bf16[32,2816]{1,0:T(8,128)(2,1)S(1)} %get-tuple-element.72), channel_id=1, source_target_pairs={{0,1},{1,0},{2,3},{3,2},{4,5},{5,4},{6,7},{7,6},{8,9},{9,8},{10,11... | collective-permute-start | bytes 540680 | tf_op jit(solution)/shard_map/ppermute | solution.py:64
  48.0 5.9 %collective-permute-start.16 = (bf16[32,512]{1,0:T(8,128)(2,1)S(1)}, bf16[32,512]{1,0:T(8,128)(2,1)S(1)}, u32[]{:S(2)}, u32[]{:S(2)}) collective-permute-start(bf16[32,512]{1,0:T(8,128)(2,1)S(1)} %get-tuple-element.73.refs_0_), channel_id=1, source_target_pairs={{0,2},{1,3},{2,0},{3,1},{4,6},{5,7},{6,4},{7,5},{8,10},{9,11},{10,... | collective-permute-start | bytes 98312 | tf_op jit(solution)/shard_map/ppermute | solution.py:64
  49.1 6.9 %collective-permute-start.17 = (bf16[32,512]{1,0:T(8,128)(2,1)S(1)}, bf16[32,512]{1,0:T(8,128)(2,1)S(1)}, u32[]{:S(2)}, u32[]{:S(2)}) collective-permute-start(bf16[32,512]{1,0:T(8,128)(2,1)S(1)} %get-tuple-element.73.refs_0_), channel_id=1, source_target_pairs={{0,3},{1,2},{2,1},{3,0},{4,7},{5,6},{6,5},{7,4},{8,11},{9,10},{10,... | collective-permute-start | bytes 98312 | tf_op jit(solution)/shard_map/ppermute | solution.py:64
  50.5 9.1 %collective-permute-start.14 = (bf16[32,2304]{1,0:T(8,128)(2,1)S(1)}, bf16[32,2304]{1,0:T(8,128)(2,1)S(1)}, u32[]{:S(2)}, u32[]{:S(2)}) collective-permute-start(bf16[32,2304]{1,0:T(8,128)(2,1)S(1)} %get-tuple-element.71.refs_3_), channel_id=1, source_target_pairs={{0,2},{1,3},{2,0},{3,1},{4,6},{5,7},{6,4},{7,5},{8,10},{9,11},{10,... | collective-permute-start | bytes 442376 | tf_op jit(solution)/shard_map/ppermute | solution.py:64
  56.0 6.0 %collective-permute-start.18 = (bf16[128,512]{1,0:T(8,128)(2,1)S(1)}, bf16[128,512]{1,0:T(8,128)(2,1)S(1)}, u32[]{:S(2)}, u32[]{:S(2)}) collective-permute-start(bf16[128,512]{1,0:T(8,128)(2,1)S(1)} %shard_map.131.refs_7_), channel_id=1, source_target_pairs={{0,24},{4,28},{8,16},{12,20},{16,8},{20,12},{24,0},{28,4},{1,25},{... | collective-permute-start | bytes 393224 | tf_op jit(solution)/shard_map/ppermute | solution.py:64
  57.6 5.8 %collective-permute-start.19 = (bf16[128,512]{1,0:T(8,128)(2,1)S(1)}, bf16[128,512]{1,0:T(8,128)(2,1)S(1)}, u32[]{:S(2)}, u32[]{:S(2)}) collective-permute-start(bf16[128,512]{1,0:T(8,128)(2,1)S(1)} %shard_map.131.refs_7_), channel_id=1, source_target_pairs={{0,16},{4,20},{8,24},{12,28},{16,0},{20,4},{24,8},{28,12},{1,17},{... | collective-permute-start | bytes 393224 | tf_op jit(solution)/shard_map/ppermute | solution.py:64
  58.8 5.0 %collective-permute-start.20 = (bf16[128,512]{1,0:T(8,128)(2,1)S(1)}, bf16[128,512]{1,0:T(8,128)(2,1)S(1)}, u32[]{:S(2)}, u32[]{:S(2)}) collective-permute-start(bf16[128,512]{1,0:T(8,128)(2,1)S(1)} %shard_map.131.refs_7_), channel_id=1, source_target_pairs={{0,8},{4,12},{8,0},{12,4},{16,24},{20,28},{24,16},{28,20},{1,9},{5... | collective-permute-start | bytes 393224 | tf_op jit(solution)/shard_map/ppermute | solution.py:64
  59.6 5.1 %collective-permute-start.15 = (bf16[32,2304]{1,0:T(8,128)(2,1)S(1)}, bf16[32,2304]{1,0:T(8,128)(2,1)S(1)}, u32[]{:S(2)}, u32[]{:S(2)}) collective-permute-start(bf16[32,2304]{1,0:T(8,128)(2,1)S(1)} %collective-permute-done.14.refs_5_), channel_id=1, source_target_pairs={{0,1},{1,0},{2,3},{3,2},{4,5},{5,4},{6,7},{7,6},{8,9},{9,8},{10,11... | collective-permute-start | bytes 442376 | tf_op jit(solution)/shard_map/ppermute | solution.py:64
  59.8 4.9 %collective-permute-start.21 = (bf16[128,512]{1,0:T(8,128)(2,1)S(1)}, bf16[128,512]{1,0:T(8,128)(2,1)S(1)}, u32[]{:S(2)}, u32[]{:S(2)}) collective-permute-start(bf16[128,512]{1,0:T(8,128)(2,1)S(1)} %shard_map.131.refs_7_), channel_id=1, source_target_pairs={{0,4},{4,0},{8,12},{12,8},{16,20},{20,16},{24,28},{28,24},{1,5},{5... | collective-permute-start | bytes 393224 | tf_op jit(solution)/shard_map/ppermute | solution.py:64
  62.1 2.7 %collective-permute-start.22 = (bf16[128,512]{1,0:T(8,128)(2,1)S(1)}, bf16[128,512]{1,0:T(8,128)(2,1)S(1)}, u32[]{:S(2)}, u32[]{:S(2)}) collective-permute-start(bf16[128,512]{1,0:T(8,128)(2,1)S(1)} %collective-permute-done.18.refs_8_), channel_id=1, source_target_pairs={{0,4},{4,0},{8,12},{12,8},{16,20},{20,16},{24,28},{28,24},{1,5},{5... | collective-permute-start | bytes 393224 | tf_op jit(solution)/shard_map/ppermute | solution.py:64
  63.4 1.4 %collective-permute-start.23 = (bf16[128,512]{1,0:T(8,128)(2,1)S(1)}, bf16[128,512]{1,0:T(8,128)(2,1)S(1)}, u32[]{:S(2)}, u32[]{:S(2)}) collective-permute-start(bf16[128,512]{1,0:T(8,128)(2,1)S(1)} %collective-permute-done.19.refs_9_), channel_id=1, source_target_pairs={{0,4},{4,0},{8,12},{12,8},{16,20},{20,16},{24,28},{28,24},{1,5},{5... | collective-permute-start | bytes 393224 | tf_op jit(solution)/shard_map/ppermute | solution.py:64
  63.8 1.3 %collective-permute-start.24 = (bf16[128,512]{1,0:T(8,128)(2,1)S(1)}, bf16[128,512]{1,0:T(8,128)(2,1)S(1)}, u32[]{:S(2)}, u32[]{:S(2)}) collective-permute-start(bf16[128,512]{1,0:T(8,128)(2,1)S(1)} %collective-permute-done.20.refs_10_), channel_id=1, source_target_pairs={{0,4},{4,0},{8,12},{12,8},{16,20},{20,16},{24,28},{28,24},{1,5},{5... | collective-permute-start | bytes 393224 | tf_op jit(solution)/shard_map/ppermute | solution.py:64

commit v11 on v10

--- a/solution.py
+++ b/solution.py
@@ -37,7 +37,7 @@
     )
 
 
-def call(kernel, outs, args, scratch=(), limit=32, stored=(), copies=0, cost=1.0):
+def call(kernel, outs, args, scratch=(), limit=32, stored=(), copies=0, cost=1.0, results=False):
     scratch_shapes = [pltpu.VMEM(shape, dtype) for shape, dtype in scratch]
     if copies:
         scratch_shapes.append(pltpu.SemaphoreType.DMA((copies,)))
@@ -45,7 +45,7 @@
         kernel,
         out_shape=[jax.ShapeDtypeStruct(shape, dtype) for shape, dtype in outs],
         in_specs=[HBM if i in stored else VMEM for i in range(len(args))],
-        out_specs=[VMEM for _ in outs],
+        out_specs=[HBM if results else VMEM for _ in outs],
         scratch_shapes=scratch_shapes,
         compiler_params=pltpu.CompilerParams(vmem_limit_bytes=limit * MIB),
         cost_estimate=pl.CostEstimate(flops=int(cost * 1e9), bytes_accessed=0, transcendentals=0),
@@ -386,7 +386,9 @@
     gain, query_weight, up = refs[:3]
     pieces, refs = refs[3 : 3 + parts], refs[3 + parts :]
     blocks, refs = refs[: len(order)], refs[len(order) :]
-    stream, out, absorbed, latents, scores, weights, totals = refs
+    stored_stream, stored_out, stream, out, absorbed, latents, scores, weights, totals, sems = refs
+    save_stream = pltpu.make_async_copy(stream, stored_stream, sems.at[0])
+    save_out = pltpu.make_async_copy(out, stored_out, sems.at[1])
     length = stream.shape[0]
     heads = absorbed.shape[0] // length
     me = lax.axis_index("ctx")
@@ -394,6 +396,7 @@
     for step in range(parts):
         at = pl.ds(pl.multiple_of(partner(lax.axis_index("head"), step, parts) * share, share), share)
         stream[at, :] = pieces[step][:, : stream.shape[1]]
+    save_stream.start()
     for position in range(len(order)):
         latents[position * length : (position + 1) * length, :] = blocks[position][...]
     normed = normalized(stream[...].astype(f32), gain[...]).astype(bf16)
@@ -428,6 +431,9 @@
         value = slice((heads + head) * DH, (heads + head + 1) * DH)
         outcome = mm(mixed[own], up[:, value])
         out[:, head * DH : (head + 1) * DH] = (outcome / totals[own, :]).astype(bf16)
+    save_out.start()
+    save_stream.wait()
+    save_out.wait()
 
 
 def far_first(count):
@@ -611,6 +617,8 @@
         [((length, width), bf16), ((length, heads_mla * DH), bf16)],
         [norm_gain[None], query_weight, up] + stream_parts + latents,
         [
+            ((length, width), bf16),
+            ((length, heads_mla * DH), bf16),
             ((rows, latent_width), bf16),
             ((latent_rows, latent_width), bf16),
             ((rows, latent_rows), f32),
@@ -618,7 +626,9 @@
             ((rows, DH), f32),
         ],
         16 + rows * latent_rows * 8 // MIB,
+        copies=2,
         cost=4.0,
+        results=True,
     )
     return (stream_out, attention_out)
 

time: 68.6 us -> 68.6 us (level)
  no operation moved by 1% of the time
where the time goes in v11:
time: 68.6 us; the launch traced here: 68.4 us
  waiting for transfers between devices  27.3 us (40%)
  starting transfers between devices  24 us (35%)
  Pallas kernels  15.9 us (23%)
  between operations  0.85 us (1%)
    ppermute x24, waiting for transfers between devices, trade(): return lax.ppermute(block, axis, route)  25.8 us
    ppermute x24, starting transfers between devices, trade(): return lax.ppermute(block, axis, route)  23.5 us
    pallas_call x11, Pallas kernels, call(): pl.pallas_call(kernel, out_shape=[jax.ShapeDtypeStruct(shape, dtype) for...  15.9 us
    ppermute x1, waiting for transfers between devices, passed_along(): lax.ppermute(block, axis, [(i, (i + distance) % count) for i in range(cou...  1.5 us
  transfers between devices with their start and end apart: 25, of which 17 were waited for; matrix products, arithmetic and copies ran while one was open for 0% of the time, Pallas kernels for 9%

profile of v11, /device:TPU:0, one launch (start us, length us, event | category | flops | bytes accessed | tf_op | source)
XLA Modules:
  0.0 68.4 jit_solution(10132304973799228513)
XLA Ops:
  0.6 0.9 %shard_map.123 = bf16[16,1024]{1,0:T(8,128)(2,1)S(1)} custom-call(bf16[3,128,1024]{2,1,0:T(8,128)(2,1)} %stored_inputs.3), custom_call_target="tpu_custom_call" | custom-call | flops 200000000 | tf_op jit(solution)/shard_map/pallas_call | solution.py:44
  1.6 0.5 collective-permute-start
  2.1 3.0 %shard_map.122 = (bf16[3,128,1024]{2,1,0:T(8,128)(2,1)S(1)}, bf16[3,16,1024]{2,1,0:T(8,128)(2,1)S(1)}, f32[128,1024]{1,0:T(8,128)S(1)}, f32[3,4,1024]{2,1,0:T(4,128)S(1)}) custom-call(bf16[3,128,1024]{2,1,0:T(8,128)(2,1)} %stored_inputs.3, f32[128,1024]{1,0:T(8,128)} %stored_gate.1, f32[3,4,1024]{2,1,0:T(4,128)} %stored_taps.1), custom_call_target="tpu_custom_call" | custom-call | flops 2000000000 | tf_op jit(solution)/shard_map/pallas_call | solution.py:44
  5.0 1.5 %collective-permute-done.halo = bf16[16,1024]{1,0:T(8,128)(2,1)S(1)} collective-permute-done((bf16[16,1024]{1,0:T(8,128)(2,1)S(1)}, bf16[16,1024]{1,0:T(8,128)(2,1)S(1)}, u32[]{:S(2)}, u32[]{:S(2)}) %collective-permute-start) | collective-permute-done | bytes 32800 | tf_op jit(solution)/shard_map/ppermute | solution.py:69
  6.6 3.3 %shard_map.124 = (bf16[4,272,128]{2,1,0:T(8,128)(2,1)S(1)}, bf16[4,272,128]{2,1,0:T(8,128)(2,1)S(1)}, bf16[8,128,256]{2,1,0:T(8,128)(2,1)S(1)}, bf16[8,2,128,128]{3,2,1,0:T(8,128)(2,1)S(1)}) custom-call(bf16[3,128,1024]{2,1,0:T(8,128)(2,1)S(1)} %get-tuple-element.38.done, bf16[3,16,1024]{2,1,0:T(8,128)(2,1)S(1)} %get-tuple-element.39.head_rows, ...), custom_call_target="tpu_custom_call" | custom-call | flops 5000000000 | tf_op jit(solution)/shard_map/pallas_call | solution.py:44
  9.8 1.2 %collective-permute-start.1 = (bf16[4,272,128]{2,1,0:T(8,128)(2,1)S(1)}, bf16[4,272,128]{2,1,0:T(8,128)(2,1)S(1)}, u32[]{:S(2)}, u32[]{:S(2)}) collective-permute-start(bf16[4,272,128]{2,1,0:T(8,128)(2,1)S(1)} %get-tuple-element.43), channel_id=1, source_target_pairs={{0,4},{4,0},{8,12},{12,8},{16,20},{20,16},{24,28},{28,24},{1,5},{5... | collective-permute-start | bytes 835592 | tf_op jit(solution)/shard_map/ppermute | solution.py:64
  11.0 0.1 collective-permute-start.5
  11.1 1.1 %collective-permute-done.1.got.refs_2_ = bf16[4,272,128]{2,1,0:T(8,128)(2,1)S(1)} collective-permute-done((bf16[4,272,128]{2,1,0:T(8,128)(2,1)S(1)}, bf16[4,272,128]{2,1,0:T(8,128)(2,1)S(1)}, u32[]{:S(2)}, u32[]{:S(2)}) %collective-permute-start.1) | collective-permute-done | bytes 278560 | tf_op jit(solution)/shard_map/ppermute | solution.py:64
  12.2 0.3 shard_map.125
  12.5 1.6 %collective-permute-start.2 = (bf16[272,128]{1,0:T(8,128)(2,1)S(1)}, bf16[272,128]{1,0:T(8,128)(2,1)S(1)}, u32[]{:S(2)}, u32[]{:S(2)}) collective-permute-start(bf16[272,128]{1,0:T(8,128)(2,1)S(1)} %get-tuple-element.45), channel_id=1, source_target_pairs={{0,8},{4,12},{8,0},{12,4},{16,24},{20,28},{24,16},{28,20},{1,9},{5... | collective-permute-start | bytes 208904 | tf_op jit(solution)/shard_map/ppermute | solution.py:64
  14.1 0.6 collective-permute-start.3
  14.7 1.4 %collective-permute-start.4 = (bf16[272,128]{1,0:T(8,128)(2,1)S(1)}, bf16[272,128]{1,0:T(8,128)(2,1)S(1)}, u32[]{:S(2)}, u32[]{:S(2)}) collective-permute-start(bf16[272,128]{1,0:T(8,128)(2,1)S(1)} %get-tuple-element.47), channel_id=1, source_target_pairs={{0,24},{4,28},{8,16},{12,20},{16,8},{20,12},{24,0},{28,4},{1,25},{... | collective-permute-start | bytes 208904 | tf_op jit(solution)/shard_map/ppermute | solution.py:64
  16.1 2.8 %shard_map.126 = (bf16[128,1024]{1,0:T(8,128)(2,1)S(1)}, f32[128,1024]{1,0:T(8,128)S(1)}) custom-call(bf16[3,128,1024]{2,1,0:T(8,128)(2,1)S(1)} %get-tuple-element.38.done, bf16[3,16,1024]{2,1,0:T(8,128)(2,1)S(1)} %get-tuple-element.39.head_rows, bf16[16,1024]{1,0:T(8,128)(2,1)S(1)} %collective-permute-done.halo, f32[128,1024]{1,0:T(8,128)S(1)} %get-tuple-element.40.logs, ...), custom_call_target="tpu_custom_call" | custom-call | flops 2500000000 | tf_op jit(solution)/shard_map/pallas_call | solution.py:44
  18.9 0.2 collective-permute-done.3.refs_2_
  19.1 0.8 %collective-permute-done.4.refs_3_ = bf16[272,128]{1,0:T(8,128)(2,1)S(1)} collective-permute-done((bf16[272,128]{1,0:T(8,128)(2,1)S(1)}, bf16[272,128]{1,0:T(8,128)(2,1)S(1)}, u32[]{:S(2)}, u32[]{:S(2)}) %collective-permute-start.4) | collective-permute-done | bytes 69664 | tf_op jit(solution)/shard_map/ppermute | solution.py:64
  20.0 1.5 %collective-permute-done.6.refs_1_ = bf16[4,272,128]{2,1,0:T(8,128)(2,1)S(1)} collective-permute-done((bf16[4,272,128]{2,1,0:T(8,128)(2,1)S(1)}, bf16[4,272,128]{2,1,0:T(8,128)(2,1)S(1)}, u32[]{:S(2)}, u32[]{:S(2)}) %collective-permute-start.6) | collective-permute-done | bytes 278560 | tf_op jit(solution)/shard_map/ppermute | solution.py:64
  21.6 0.3 shard_map.128
  21.9 1.5 %collective-permute-start.7 = (bf16[2,128,128]{2,1,0:T(8,128)(2,1)S(1)}, bf16[2,128,128]{2,1,0:T(8,128)(2,1)S(1)}, u32[]{:S(2)}, u32[]{:S(2)}) collective-permute-start(bf16[2,128,128]{2,1,0:T(8,128)(2,1)S(1)} %get-tuple-element.59), channel_id=1, source_target_pairs={{0,8},{4,12},{8,0},{12,4},{16,24},{20,28},{24,16},{28,20},{1,9},{5... | collective-permute-start | bytes 196616 | tf_op jit(solution)/shard_map/ppermute | solution.py:64
  23.4 0.6 collective-permute-start.8
  24.0 1.4 %collective-permute-start.9 = (bf16[2,128,128]{2,1,0:T(8,128)(2,1)S(1)}, bf16[2,128,128]{2,1,0:T(8,128)(2,1)S(1)}, u32[]{:S(2)}, u32[]{:S(2)}) collective-permute-start(bf16[2,128,128]{2,1,0:T(8,128)(2,1)S(1)} %get-tuple-element.61), channel_id=1, source_target_pairs={{0,24},{4,28},{8,16},{12,20},{16,8},{20,12},{24,0},{28,4},{1,25},{... | collective-permute-start | bytes 196616 | tf_op jit(solution)/shard_map/ppermute | solution.py:64
  25.4 0.8 %collective-permute-done.7.refs_5_ = bf16[2,128,128]{2,1,0:T(8,128)(2,1)S(1)} collective-permute-done((bf16[2,128,128]{2,1,0:T(8,128)(2,1)S(1)}, bf16[2,128,128]{2,1,0:T(8,128)(2,1)S(1)}, u32[]{:S(2)}, u32[]{:S(2)}) %collective-permute-start.7) | collective-permute-done | bytes 65568 | tf_op jit(solution)/shard_map/ppermute | solution.py:64
  26.2 2.2 %collective-permute-done.8.refs_6_ = bf16[2,128,128]{2,1,0:T(8,128)(2,1)S(1)} collective-permute-done((bf16[2,128,128]{2,1,0:T(8,128)(2,1)S(1)}, bf16[2,128,128]{2,1,0:T(8,128)(2,1)S(1)}, u32[]{:S(2)}, u32[]{:S(2)}) %collective-permute-start.8) | collective-permute-done | bytes 65568 | tf_op jit(solution)/shard_map/ppermute | solution.py:64
  28.4 0.8 %collective-permute-done.9.refs_7_ = bf16[2,128,128]{2,1,0:T(8,128)(2,1)S(1)} collective-permute-done((bf16[2,128,128]{2,1,0:T(8,128)(2,1)S(1)}, bf16[2,128,128]{2,1,0:T(8,128)(2,1)S(1)}, u32[]{:S(2)}, u32[]{:S(2)}) %collective-permute-start.9) | collective-permute-done | bytes 65568 | tf_op jit(solution)/shard_map/ppermute | solution.py:64
  29.2 1.3 %shard_map.129 = (f32[32,2304]{1,0:T(8,128)S(1)}, bf16[32,2304]{1,0:T(8,128)(2,1)S(1)}, bf16[32,2304]{1,0:T(8,128)(2,1)S(1)}, bf16[32,2304]{1,0:T(8,128)(2,1)S(1)}) custom-call(bf16[128,2304]{1,0:T(8,128)(2,1)S(1)} %copy-done, bf16[1024,2304]{1,0:T(8,128)(2,1)S(1)} %bitcast.5, bf16[128,1024]{1,0:T(8,128)(2,1)S(1)} %get-tuple-element.52.refs_2_, ...), custom_call_target="tpu_custom_call" | custom-call | flops 1000000000 | tf_op jit(solution)/shard_map/pallas_call | solution.py:44
  30.5 1.6 %collective-permute-start.10 = (bf16[32,2304]{1,0:T(8,128)(2,1)S(1)}, bf16[32,2304]{1,0:T(8,128)(2,1)S(1)}, u32[]{:S(2)}, u32[]{:S(2)}) collective-permute-start(bf16[32,2304]{1,0:T(8,128)(2,1)S(1)} %get-tuple-element.63), channel_id=1, source_target_pairs={{0,1},{1,0},{2,3},{3,2},{4,5},{5,4},{6,7},{7,6},{8,9},{9,8},{10,11... | collective-permute-start | bytes 442376 | tf_op jit(solution)/shard_map/ppermute | solution.py:64
  32.2 2.6 %collective-permute-start.11 = (bf16[32,2304]{1,0:T(8,128)(2,1)S(1)}, bf16[32,2304]{1,0:T(8,128)(2,1)S(1)}, u32[]{:S(2)}, u32[]{:S(2)}) collective-permute-start(bf16[32,2304]{1,0:T(8,128)(2,1)S(1)} %get-tuple-element.64), channel_id=1, source_target_pairs={{0,2},{1,3},{2,0},{3,1},{4,6},{5,7},{6,4},{7,5},{8,10},{9,11},{10,... | collective-permute-start | bytes 442376 | tf_op jit(solution)/shard_map/ppermute | solution.py:64
  34.8 0.2 collective-permute-start.12
  35.0 0.2 copy.13
  35.3 1.9 %collective-permute-done.10.refs_4_ = bf16[32,2304]{1,0:T(8,128)(2,1)S(1)} collective-permute-done((bf16[32,2304]{1,0:T(8,128)(2,1)S(1)}, bf16[32,2304]{1,0:T(8,128)(2,1)S(1)}, u32[]{:S(2)}, u32[]{:S(2)}) %collective-permute-start.10) | collective-permute-done | bytes 147488 | tf_op jit(solution)/shard_map/ppermute | solution.py:64
  37.2 7.8 %collective-permute-done.11.refs_5_ = bf16[32,2304]{1,0:T(8,128)(2,1)S(1)} collective-permute-done((bf16[32,2304]{1,0:T(8,128)(2,1)S(1)}, bf16[32,2304]{1,0:T(8,128)(2,1)S(1)}, u32[]{:S(2)}, u32[]{:S(2)}) %collective-permute-start.11) | collective-permute-done | bytes 147488 | tf_op jit(solution)/shard_map/ppermute | solution.py:64
  45.0 0.8 %shard_map.130 = (bf16[32,2304]{1,0:T(8,128)(2,1)S(1)}, bf16[32,512]{1,0:T(8,128)(2,1)S(1)}, bf16[32,2816]{1,0:T(8,128)(2,1)S(1)}) custom-call(f32[1,2304]{1,0:T(1,128)S(1)} %broadcast_in_dim.7.refs_0_, bf16[2304,512]{1,0:T(8,128)(2,1)S(1)} %copy-done.1, f32[1,512]{1,0:T(1,128)S(1)} %bitcast.9, f32[32,2304]{1,0:T(8,128)S(1)} %get-tuple-element.67.refs_3_, ...), custom_call_target="tpu_custom_call" | custom-call | flops 1000000000 | tf_op jit(solution)/shard_map/pallas_call | solution.py:44
  45.8 2.2 %collective-permute-start.13 = (bf16[32,2816]{1,0:T(8,128)(2,1)S(1)}, bf16[32,2816]{1,0:T(8,128)(2,1)S(1)}, u32[]{:S(2)}, u32[]{:S(2)}) collective-permute-start(bf16[32,2816]{1,0:T(8,128)(2,1)S(1)} %get-tuple-element.72), channel_id=1, source_target_pairs={{0,1},{1,0},{2,3},{3,2},{4,5},{5,4},{6,7},{7,6},{8,9},{9,8},{10,11... | collective-permute-start | bytes 540680 | tf_op jit(solution)/shard_map/ppermute | solution.py:64
  48.0 1.1 %collective-permute-start.16 = (bf16[32,512]{1,0:T(8,128)(2,1)S(1)}, bf16[32,512]{1,0:T(8,128)(2,1)S(1)}, u32[]{:S(2)}, u32[]{:S(2)}) collective-permute-start(bf16[32,512]{1,0:T(8,128)(2,1)S(1)} %get-tuple-element.73.refs_0_), channel_id=1, source_target_pairs={{0,2},{1,3},{2,0},{3,1},{4,6},{5,7},{6,4},{7,5},{8,10},{9,11},{10,... | collective-permute-start | bytes 98312 | tf_op jit(solution)/shard_map/ppermute | solution.py:64
  49.1 1.4 %collective-permute-start.17 = (bf16[32,512]{1,0:T(8,128)(2,1)S(1)}, bf16[32,512]{1,0:T(8,128)(2,1)S(1)}, u32[]{:S(2)}, u32[]{:S(2)}) collective-permute-start(bf16[32,512]{1,0:T(8,128)(2,1)S(1)} %get-tuple-element.73.refs_0_), channel_id=1, source_target_pairs={{0,3},{1,2},{2,1},{3,0},{4,7},{5,6},{6,5},{7,4},{8,11},{9,10},{10,... | collective-permute-start | bytes 98312 | tf_op jit(solution)/shard_map/ppermute | solution.py:64
  50.5 2.0 %collective-permute-start.14 = (bf16[32,2304]{1,0:T(8,128)(2,1)S(1)}, bf16[32,2304]{1,0:T(8,128)(2,1)S(1)}, u32[]{:S(2)}, u32[]{:S(2)}) collective-permute-start(bf16[32,2304]{1,0:T(8,128)(2,1)S(1)} %get-tuple-element.71.refs_3_), channel_id=1, source_target_pairs={{0,2},{1,3},{2,0},{3,1},{4,6},{5,7},{6,4},{7,5},{8,10},{9,11},{10,... | collective-permute-start | bytes 442376 | tf_op jit(solution)/shard_map/ppermute | solution.py:64
  52.5 1.3 %collective-permute-done.16.refs_2_ = bf16[32,512]{1,0:T(8,128)(2,1)S(1)} collective-permute-done((bf16[32,512]{1,0:T(8,128)(2,1)S(1)}, bf16[32,512]{1,0:T(8,128)(2,1)S(1)}, u32[]{:S(2)}, u32[]{:S(2)}) %collective-permute-start.16) | collective-permute-done | bytes 32800 | tf_op jit(solution)/shard_map/ppermute | solution.py:64
  53.8 2.2 %collective-permute-done.17.refs_3_ = bf16[32,512]{1,0:T(8,128)(2,1)S(1)} collective-permute-done((bf16[32,512]{1,0:T(8,128)(2,1)S(1)}, bf16[32,512]{1,0:T(8,128)(2,1)S(1)}, u32[]{:S(2)}, u32[]{:S(2)}) %collective-permute-start.17) | collective-permute-done | bytes 32800 | tf_op jit(solution)/shard_map/ppermute | solution.py:64
  56.0 1.5 %collective-permute-start.18 = (bf16[128,512]{1,0:T(8,128)(2,1)S(1)}, bf16[128,512]{1,0:T(8,128)(2,1)S(1)}, u32[]{:S(2)}, u32[]{:S(2)}) collective-permute-start(bf16[128,512]{1,0:T(8,128)(2,1)S(1)} %shard_map.131.refs_7_), channel_id=1, source_target_pairs={{0,24},{4,28},{8,16},{12,20},{16,8},{20,12},{24,0},{28,4},{1,25},{... | collective-permute-start | bytes 393224 | tf_op jit(solution)/shard_map/ppermute | solution.py:64
  57.6 1.3 %collective-permute-start.19 = (bf16[128,512]{1,0:T(8,128)(2,1)S(1)}, bf16[128,512]{1,0:T(8,128)(2,1)S(1)}, u32[]{:S(2)}, u32[]{:S(2)}) collective-permute-start(bf16[128,512]{1,0:T(8,128)(2,1)S(1)} %shard_map.131.refs_7_), channel_id=1, source_target_pairs={{0,16},{4,20},{8,24},{12,28},{16,0},{20,4},{24,8},{28,12},{1,17},{... | collective-permute-start | bytes 393224 | tf_op jit(solution)/shard_map/ppermute | solution.py:64
  58.8 0.8 %collective-permute-start.20 = (bf16[128,512]{1,0:T(8,128)(2,1)S(1)}, bf16[128,512]{1,0:T(8,128)(2,1)S(1)}, u32[]{:S(2)}, u32[]{:S(2)}) collective-permute-start(bf16[128,512]{1,0:T(8,128)(2,1)S(1)} %shard_map.131.refs_7_), channel_id=1, source_target_pairs={{0,8},{4,12},{8,0},{12,4},{16,24},{20,28},{24,16},{28,20},{1,9},{5... | collective-permute-start | bytes 393224 | tf_op jit(solution)/shard_map/ppermute | solution.py:64
  59.6 0.2 collective-permute-start.15
  59.8 2.2 %collective-permute-done.18.refs_8_ = bf16[128,512]{1,0:T(8,128)(2,1)S(1)} collective-permute-done((bf16[128,512]{1,0:T(8,128)(2,1)S(1)}, bf16[128,512]{1,0:T(8,128)(2,1)S(1)}, u32[]{:S(2)}, u32[]{:S(2)}) %collective-permute-start.18) | collective-permute-done | bytes 131104 | tf_op jit(solution)/shard_map/ppermute | solution.py:64
  62.1 1.3 %collective-permute-done.19.refs_9_ = bf16[128,512]{1,0:T(8,128)(2,1)S(1)} collective-permute-done((bf16[128,512]{1,0:T(8,128)(2,1)S(1)}, bf16[128,512]{1,0:T(8,128)(2,1)S(1)}, u32[]{:S(2)}, u32[]{:S(2)}) %collective-permute-start.19) | collective-permute-done | bytes 131104 | tf_op jit(solution)/shard_map/ppermute | solution.py:64
  63.4 0.4 collective-permute-done.20.refs_10_
  63.8 0.1 collective-permute-start.24
  63.9 0.9 %collective-permute-done.15.refs_6_ = bf16[32,2304]{1,0:T(8,128)(2,1)S(1)} collective-permute-done((bf16[32,2304]{1,0:T(8,128)(2,1)S(1)}, bf16[32,2304]{1,0:T(8,128)(2,1)S(1)}, u32[]{:S(2)}, u32[]{:S(2)}) %collective-permute-start.15) | collective-permute-done | bytes 147488 | tf_op jit(solution)/shard_map/ppermute | solution.py:64
  64.8 0.4 collective-permute-done.24.refs_14_
  65.2 3.3 %shard_map.132 = (bf16[128,2304]{1,0:T(8,128)(2,1)}, bf16[128,512]{1,0:T(8,128)(2,1)}) custom-call(f32[1,2304]{1,0:T(1,128)S(1)} %broadcast_in_dim.7.refs_0_, bf16[2304,512]{1,0:T(8,128)(2,1)S(1)} %copy-done.2, bf16[512,1024]{1,0:T(8,128)(2,1)S(1)} %bitcast.6, bf16[32,2304]{1,0:T(8,128)(2,1)S(1)} %get-tuple-element.71.refs_3_, ...), custom_call_target="tpu_custom_call" | custom-call | flops 4000000000 | tf_op jit(solution)/shard_map/pallas_call | solution.py:44
  (34 shorter events, 0.2 us)
Async XLA Ops:
  1.6 5.0 %copy-start.3 = (f32[128,8]{0,1:T(8,128)S(1)}, f32[128,8]{0,1:T(8,128)}, u32[]{:S(2)}) copy-start(f32[128,8]{0,1:T(8,128)} %param.13) | copy-start | bytes 12292
  1.6 5.0 %collective-permute-start = (bf16[16,1024]{1,0:T(8,128)(2,1)S(1)}, bf16[16,1024]{1,0:T(8,128)(2,1)S(1)}, u32[]{:S(2)}, u32[]{:S(2)}) collective-permute-start(bf16[16,1024]{1,0:T(8,128)(2,1)S(1)} %shard_map.123), channel_id=1, source_target_pairs={{0,4},{4,8},{8,12},{12,16},{16,20},{20,24},{24,28},{28,0},{1,5},{5... | collective-permute-start | bytes 98312 | tf_op jit(solution)/shard_map/ppermute | solution.py:69
  9.8 2.4 %collective-permute-start.1 = (bf16[4,272,128]{2,1,0:T(8,128)(2,1)S(1)}, bf16[4,272,128]{2,1,0:T(8,128)(2,1)S(1)}, u32[]{:S(2)}, u32[]{:S(2)}) collective-permute-start(bf16[4,272,128]{2,1,0:T(8,128)(2,1)S(1)} %get-tuple-element.43), channel_id=1, source_target_pairs={{0,4},{4,0},{8,12},{12,8},{16,20},{20,16},{24,28},{28,24},{1,5},{5... | collective-permute-start | bytes 835592 | tf_op jit(solution)/shard_map/ppermute | solution.py:64
  11.0 5.1 %collective-permute-start.5 = (bf16[4,272,128]{2,1,0:T(8,128)(2,1)S(1)}, bf16[4,272,128]{2,1,0:T(8,128)(2,1)S(1)}, u32[]{:S(2)}, u32[]{:S(2)}) collective-permute-start(bf16[4,272,128]{2,1,0:T(8,128)(2,1)S(1)} %get-tuple-element.42.kept), channel_id=1, source_target_pairs={{0,4},{4,0},{8,12},{12,8},{16,20},{20,16},{24,28},{28,24},{1,5},{5... | collective-permute-start | bytes 835592 | tf_op jit(solution)/shard_map/ppermute | solution.py:64
  12.5 6.4 %collective-permute-start.2 = (bf16[272,128]{1,0:T(8,128)(2,1)S(1)}, bf16[272,128]{1,0:T(8,128)(2,1)S(1)}, u32[]{:S(2)}, u32[]{:S(2)}) collective-permute-start(bf16[272,128]{1,0:T(8,128)(2,1)S(1)} %get-tuple-element.45), channel_id=1, source_target_pairs={{0,8},{4,12},{8,0},{12,4},{16,24},{20,28},{24,16},{28,20},{1,9},{5... | collective-permute-start | bytes 208904 | tf_op jit(solution)/shard_map/ppermute | solution.py:64
  14.1 5.1 %collective-permute-start.3 = (bf16[272,128]{1,0:T(8,128)(2,1)S(1)}, bf16[272,128]{1,0:T(8,128)(2,1)S(1)}, u32[]{:S(2)}, u32[]{:S(2)}) collective-permute-start(bf16[272,128]{1,0:T(8,128)(2,1)S(1)} %get-tuple-element.46), channel_id=1, source_target_pairs={{0,16},{4,20},{8,24},{12,28},{16,0},{20,4},{24,8},{28,12},{1,17},{... | collective-permute-start | bytes 208904 | tf_op jit(solution)/shard_map/ppermute | solution.py:64
  14.7 5.2 %collective-permute-start.4 = (bf16[272,128]{1,0:T(8,128)(2,1)S(1)}, bf16[272,128]{1,0:T(8,128)(2,1)S(1)}, u32[]{:S(2)}, u32[]{:S(2)}) collective-permute-start(bf16[272,128]{1,0:T(8,128)(2,1)S(1)} %get-tuple-element.47), channel_id=1, source_target_pairs={{0,24},{4,28},{8,16},{12,20},{16,8},{20,12},{24,0},{28,4},{1,25},{... | collective-permute-start | bytes 208904 | tf_op jit(solution)/shard_map/ppermute | solution.py:64
  16.1 13.1 %slice-start = ((s8[4718592]{0:T(1024)(128)(4,1)}), s8[4194304]{0:T(1024)(128)(4,1)S(1)}, s32[]{:S(2)}) async-start(s8[4718592]{0:T(1024)(128)(4,1)} %bitcast.4), calls=%async_computation | async-start | bytes 8388608
  16.1 13.1 %slice-start.1 = ((s8[4718592]{0:T(1024)(128)(4,1)}), s8[524288]{0:T(1024)(128)(4,1)S(1)}, s32[]{:S(2)}) async-start(s8[4718592]{0:T(1024)(128)(4,1)} %bitcast.4), calls=%async_computation.1 | async-start | bytes 1048576
  18.9 10.3 %copy-start = (bf16[128,2304]{1,0:T(8,128)(2,1)S(1)}, bf16[128,2304]{1,0:T(8,128)(2,1)}, u32[]{:S(2)}) copy-start(bf16[128,2304]{1,0:T(8,128)(2,1)} %refs_0_.1) | copy-start | bytes 1769476
  19.9 1.6 %collective-permute-start.6 = (bf16[4,272,128]{2,1,0:T(8,128)(2,1)S(1)}, bf16[4,272,128]{2,1,0:T(8,128)(2,1)S(1)}, u32[]{:S(2)}, u32[]{:S(2)}) collective-permute-start(bf16[4,272,128]{2,1,0:T(8,128)(2,1)S(1)} %shard_map.127.refs_0_), channel_id=1, source_target_pairs={{0,4},{4,0},{8,12},{12,8},{16,20},{20,16},{24,28},{28,24},{1,5},{5... | collective-permute-start | bytes 835592 | tf_op jit(solution)/shard_map/ppermute | solution.py:64
  21.9 4.3 %collective-permute-start.7 = (bf16[2,128,128]{2,1,0:T(8,128)(2,1)S(1)}, bf16[2,128,128]{2,1,0:T(8,128)(2,1)S(1)}, u32[]{:S(2)}, u32[]{:S(2)}) collective-permute-start(bf16[2,128,128]{2,1,0:T(8,128)(2,1)S(1)} %get-tuple-element.59), channel_id=1, source_target_pairs={{0,8},{4,12},{8,0},{12,4},{16,24},{20,28},{24,16},{28,20},{1,9},{5... | collective-permute-start | bytes 196616 | tf_op jit(solution)/shard_map/ppermute | solution.py:64
  23.4 5.0 %collective-permute-start.8 = (bf16[2,128,128]{2,1,0:T(8,128)(2,1)S(1)}, bf16[2,128,128]{2,1,0:T(8,128)(2,1)S(1)}, u32[]{:S(2)}, u32[]{:S(2)}) collective-permute-start(bf16[2,128,128]{2,1,0:T(8,128)(2,1)S(1)} %get-tuple-element.60), channel_id=1, source_target_pairs={{0,16},{4,20},{8,24},{12,28},{16,0},{20,4},{24,8},{28,12},{1,17},{... | collective-permute-start | bytes 196616 | tf_op jit(solution)/shard_map/ppermute | solution.py:64
  24.0 5.2 %collective-permute-start.9 = (bf16[2,128,128]{2,1,0:T(8,128)(2,1)S(1)}, bf16[2,128,128]{2,1,0:T(8,128)(2,1)S(1)}, u32[]{:S(2)}, u32[]{:S(2)}) collective-permute-start(bf16[2,128,128]{2,1,0:T(8,128)(2,1)S(1)} %get-tuple-element.61), channel_id=1, source_target_pairs={{0,24},{4,28},{8,16},{12,20},{16,8},{20,12},{24,0},{28,4},{1,25},{... | collective-permute-start | bytes 196616 | tf_op jit(solution)/shard_map/ppermute | solution.py:64
  29.2 5.8 %copy-start.5 = (bf16[512,2,512]{2,1,0:T(2,128)(2,1)S(1)}, bf16[512,2,512]{2,1,0:T(2,128)(2,1)}, u32[]{:S(2)}) copy-start(bf16[512,2,512]{2,1,0:T(2,128)(2,1)} %param.21) | copy-start | bytes 3145732
  29.2 6.1 %copy-start.6 = (f32[2304]{0:T(1024)S(1)}, f32[2304]{0:T(1024)}, u32[]{:S(2)}) copy-start(f32[2304]{0:T(1024)} %param.17) | copy-start | bytes 27652
  29.2 15.8 %copy-start.1 = (bf16[2304,512]{1,0:T(8,128)(2,1)S(1)}, bf16[2304,512]{1,0:T(8,128)(2,1)}, u32[]{:S(2)}) copy-start(bf16[2304,512]{1,0:T(8,128)(2,1)} %refs_1_.4) | copy-start | bytes 7077892
  29.2 15.8 %copy-start.4 = (f32[512]{0:T(512)S(1)}, f32[512]{0:T(512)}, u32[]{:S(2)}) copy-start(f32[512]{0:T(512)} %param.19) | copy-start | bytes 6148
  30.5 6.6 %collective-permute-start.10 = (bf16[32,2304]{1,0:T(8,128)(2,1)S(1)}, bf16[32,2304]{1,0:T(8,128)(2,1)S(1)}, u32[]{:S(2)}, u32[]{:S(2)}) collective-permute-start(bf16[32,2304]{1,0:T(8,128)(2,1)S(1)} %get-tuple-element.63), channel_id=1, source_target_pairs={{0,1},{1,0},{2,3},{3,2},{4,5},{5,4},{6,7},{7,6},{8,9},{9,8},{10,11... | collective-permute-start | bytes 442376 | tf_op jit(solution)/shard_map/ppermute | solution.py:64
  32.2 12.8 %collective-permute-start.11 = (bf16[32,2304]{1,0:T(8,128)(2,1)S(1)}, bf16[32,2304]{1,0:T(8,128)(2,1)S(1)}, u32[]{:S(2)}, u32[]{:S(2)}) collective-permute-start(bf16[32,2304]{1,0:T(8,128)(2,1)S(1)} %get-tuple-element.64), channel_id=1, source_target_pairs={{0,2},{1,3},{2,0},{3,1},{4,6},{5,7},{6,4},{7,5},{8,10},{9,11},{10,... | collective-permute-start | bytes 442376 | tf_op jit(solution)/shard_map/ppermute | solution.py:64
  34.8 10.2 %collective-permute-start.12 = (bf16[32,2304]{1,0:T(8,128)(2,1)S(1)}, bf16[32,2304]{1,0:T(8,128)(2,1)S(1)}, u32[]{:S(2)}, u32[]{:S(2)}) collective-permute-start(bf16[32,2304]{1,0:T(8,128)(2,1)S(1)} %get-tuple-element.65), channel_id=1, source_target_pairs={{0,3},{1,2},{2,1},{3,0},{4,7},{5,6},{6,5},{7,4},{8,11},{9,10},{10,... | collective-permute-start | bytes 442376 | tf_op jit(solution)/shard_map/ppermute | solution.py:64
  45.8 19.4 %copy-start.2 = (bf16[2304,512]{1,0:T(8,128)(2,1)S(1)}, bf16[2304,512]{1,0:T(8,128)(2,1)}, u32[]{:S(2)}) copy-start(bf16[2304,512]{1,0:T(8,128)(2,1)} %refs_1_.5) | copy-start | bytes 7077892
  45.8 10.2 %collective-permute-start.13 = (bf16[32,2816]{1,0:T(8,128)(2,1)S(1)}, bf16[32,2816]{1,0:T(8,128)(2,1)S(1)}, u32[]{:S(2)}, u32[]{:S(2)}) collective-permute-start(bf16[32,2816]{1,0:T(8,128)(2,1)S(1)} %get-tuple-element.72), channel_id=1, source_target_pairs={{0,1},{1,0},{2,3},{3,2},{4,5},{5,4},{6,7},{7,6},{8,9},{9,8},{10,11... | collective-permute-start | bytes 540680 | tf_op jit(solution)/shard_map/ppermute | solution.py:64
  48.0 5.9 %collective-permute-start.16 = (bf16[32,512]{1,0:T(8,128)(2,1)S(1)}, bf16[32,512]{1,0:T(8,128)(2,1)S(1)}, u32[]{:S(2)}, u32[]{:S(2)}) collective-permute-start(bf16[32,512]{1,0:T(8,128)(2,1)S(1)} %get-tuple-element.73.refs_0_), channel_id=1, source_target_pairs={{0,2},{1,3},{2,0},{3,1},{4,6},{5,7},{6,4},{7,5},{8,10},{9,11},{10,... | collective-permute-start | bytes 98312 | tf_op jit(solution)/shard_map/ppermute | solution.py:64
  49.1 6.9 %collective-permute-start.17 = (bf16[32,512]{1,0:T(8,128)(2,1)S(1)}, bf16[32,512]{1,0:T(8,128)(2,1)S(1)}, u32[]{:S(2)}, u32[]{:S(2)}) collective-permute-start(bf16[32,512]{1,0:T(8,128)(2,1)S(1)} %get-tuple-element.73.refs_0_), channel_id=1, source_target_pairs={{0,3},{1,2},{2,1},{3,0},{4,7},{5,6},{6,5},{7,4},{8,11},{9,10},{10,... | collective-permute-start | bytes 98312 | tf_op jit(solution)/shard_map/ppermute | solution.py:64
  50.5 9.1 %collective-permute-start.14 = (bf16[32,2304]{1,0:T(8,128)(2,1)S(1)}, bf16[32,2304]{1,0:T(8,128)(2,1)S(1)}, u32[]{:S(2)}, u32[]{:S(2)}) collective-permute-start(bf16[32,2304]{1,0:T(8,128)(2,1)S(1)} %get-tuple-element.71.refs_3_), channel_id=1, source_target_pairs={{0,2},{1,3},{2,0},{3,1},{4,6},{5,7},{6,4},{7,5},{8,10},{9,11},{10,... | collective-permute-start | bytes 442376 | tf_op jit(solution)/shard_map/ppermute | solution.py:64
  56.0 6.0 %collective-permute-start.18 = (bf16[128,512]{1,0:T(8,128)(2,1)S(1)}, bf16[128,512]{1,0:T(8,128)(2,1)S(1)}, u32[]{:S(2)}, u32[]{:S(2)}) collective-permute-start(bf16[128,512]{1,0:T(8,128)(2,1)S(1)} %shard_map.131.refs_7_), channel_id=1, source_target_pairs={{0,24},{4,28},{8,16},{12,20},{16,8},{20,12},{24,0},{28,4},{1,25},{... | collective-permute-start | bytes 393224 | tf_op jit(solution)/shard_map/ppermute | solution.py:64
  57.6 5.8 %collective-permute-start.19 = (bf16[128,512]{1,0:T(8,128)(2,1)S(1)}, bf16[128,512]{1,0:T(8,128)(2,1)S(1)}, u32[]{:S(2)}, u32[]{:S(2)}) collective-permute-start(bf16[128,512]{1,0:T(8,128)(2,1)S(1)} %shard_map.131.refs_7_), channel_id=1, source_target_pairs={{0,16},{4,20},{8,24},{12,28},{16,0},{20,4},{24,8},{28,12},{1,17},{... | collective-permute-start | bytes 393224 | tf_op jit(solution)/shard_map/ppermute | solution.py:64
  58.8 5.0 %collective-permute-start.20 = (bf16[128,512]{1,0:T(8,128)(2,1)S(1)}, bf16[128,512]{1,0:T(8,128)(2,1)S(1)}, u32[]{:S(2)}, u32[]{:S(2)}) collective-permute-start(bf16[128,512]{1,0:T(8,128)(2,1)S(1)} %shard_map.131.refs_7_), channel_id=1, source_target_pairs={{0,8},{4,12},{8,0},{12,4},{16,24},{20,28},{24,16},{28,20},{1,9},{5... | collective-permute-start | bytes 393224 | tf_op jit(solution)/shard_map/ppermute | solution.py:64
  59.6 5.1 %collective-permute-start.15 = (bf16[32,2304]{1,0:T(8,128)(2,1)S(1)}, bf16[32,2304]{1,0:T(8,128)(2,1)S(1)}, u32[]{:S(2)}, u32[]{:S(2)}) collective-permute-start(bf16[32,2304]{1,0:T(8,128)(2,1)S(1)} %collective-permute-done.14.refs_5_), channel_id=1, source_target_pairs={{0,1},{1,0},{2,3},{3,2},{4,5},{5,4},{6,7},{7,6},{8,9},{9,8},{10,11... | collective-permute-start | bytes 442376 | tf_op jit(solution)/shard_map/ppermute | solution.py:64
  59.8 4.9 %collective-permute-start.21 = (bf16[128,512]{1,0:T(8,128)(2,1)S(1)}, bf16[128,512]{1,0:T(8,128)(2,1)S(1)}, u32[]{:S(2)}, u32[]{:S(2)}) collective-permute-start(bf16[128,512]{1,0:T(8,128)(2,1)S(1)} %shard_map.131.refs_7_), channel_id=1, source_target_pairs={{0,4},{4,0},{8,12},{12,8},{16,20},{20,16},{24,28},{28,24},{1,5},{5... | collective-permute-start | bytes 393224 | tf_op jit(solution)/shard_map/ppermute | solution.py:64
  62.1 2.7 %collective-permute-start.22 = (bf16[128,512]{1,0:T(8,128)(2,1)S(1)}, bf16[128,512]{1,0:T(8,128)(2,1)S(1)}, u32[]{:S(2)}, u32[]{:S(2)}) collective-permute-start(bf16[128,512]{1,0:T(8,128)(2,1)S(1)} %collective-permute-done.18.refs_8_), channel_id=1, source_target_pairs={{0,4},{4,0},{8,12},{12,8},{16,20},{20,16},{24,28},{28,24},{1,5},{5... | collective-permute-start | bytes 393224 | tf_op jit(solution)/shard_map/ppermute | solution.py:64
  63.4 1.4 %collective-permute-start.23 = (bf16[128,512]{1,0:T(8,128)(2,1)S(1)}, bf16[128,512]{1,0:T(8,128)(2,1)S(1)}, u32[]{:S(2)}, u32[]{:S(2)}) collective-permute-start(bf16[128,512]{1,0:T(8,128)(2,1)S(1)} %collective-permute-done.19.refs_9_), channel_id=1, source_target_pairs={{0,4},{4,0},{8,12},{12,8},{16,20},{20,16},{24,28},{28,24},{1,5},{5... | collective-permute-start | bytes 393224 | tf_op jit(solution)/shard_map/ppermute | solution.py:64
  63.8 1.3 %collective-permute-start.24 = (bf16[128,512]{1,0:T(8,128)(2,1)S(1)}, bf16[128,512]{1,0:T(8,128)(2,1)S(1)}, u32[]{:S(2)}, u32[]{:S(2)}) collective-permute-start(bf16[128,512]{1,0:T(8,128)(2,1)S(1)} %collective-permute-done.20.refs_10_), channel_id=1, source_target_pairs={{0,4},{4,0},{8,12},{12,8},{16,20},{20,16},{24,28},{28,24},{1,5},{5... | collective-permute-start | bytes 393224 | tf_op jit(solution)/shard_map/ppermute | solution.py:64
